TPU v7x, 32 devices: a whole 2x2x4 slice. The times are simulated.
32 devices in a mesh: tm: 8 (over y, x, core), space: 4 (over z).
Axes of the slice: x: 2, y: 2, z: 4, core: 2. Of those that a mesh axis runs over, the one named last changes fastest.
Arguments:
- frames_in: bfloat16 [64, 32, 64, 256], P('tm', 'space'), may hold values from -6 to 6
- cotangent: bfloat16 [64, 32, 64, 256], P('tm', 'space'), may hold values from -6 to 6
- spatial: bfloat16 [3, 3, 256, 256], replicated, may hold values from -0.125 to 0.125
- temporal: bfloat16 [3, 256, 256], replicated, may hold values from -0.375 to 0.375
- norm_gain: float32 [256], replicated, may hold values from 0.5 to 2
- norm_shift: float32 [256], replicated, may hold values from -3 to 3
- clip_frames: int32 [2], replicated, may hold values from 8 to 48, as said below
- dilation: int32 [2], replicated, may hold values from 1 to 8, as said below
Outputs:
- out_frames: bfloat16 [64, 32, 64, 256], P('tm', 'space')
- in_grad: bfloat16 [64, 32, 64, 256], P('tm', 'space')
- spatial_grad: float32 [3, 3, 256, 256], replicated
- temporal_grad: float32 [3, 256, 256], replicated
Inputs may be any that keep to these rules, and one draw needn't show every extreme that they name: `clip_frames`: the two clips are packed in order from slot 0 and fill at least 56 and at most 64 slots together; one of them has exactly 48 frames. One of the two clips has dilation 8.
All inputs are finite; a program needn't handle non-finite values.
Results may differ from a plain program's by a relative error of at most 0.0055.
Values may be sent and summed in bfloat16 or wider, within the bound.
No kernel may reach another device: no remote copies, remote signals or barrier semaphores. Data moves between devices by JAX's collectives and lax.ppermute only.
A program may use at most 128 MiB of HBM per device.

v0:
```python
import functools

import jax
import jax.numpy as jnp
from jax import lax
from jax.experimental import pallas as pl
from jax.experimental.pallas import tpu as pltpu
from jax.sharding import PartitionSpec as P

GROUPS = 32
NORM_EPS = 1e-05
BF16 = jnp.bfloat16
F32 = jnp.float32
MIB = 2**20


def call(kernel, name, operands, out_shape, flops=0, moved=0, scratch=(), grant=14):
    vmem = pl.BlockSpec(memory_space=pltpu.VMEM)
    smem = pl.BlockSpec(memory_space=pltpu.SMEM)
    return pl.pallas_call(
        kernel,
        in_specs=[smem if x.dtype == jnp.int32 else vmem for x in operands],
        out_specs=jax.tree.map(lambda _: vmem, out_shape),
        out_shape=out_shape,
        scratch_shapes=list(scratch),
        compiler_params=pltpu.CompilerParams(vmem_limit_bytes=grant * MIB),
        cost_estimate=pl.CostEstimate(flops=int(flops), bytes_accessed=int(moved), transcendentals=0),
        name=name,
    )(*operands)


def dot(a, b):
    return jnp.dot(a, b, preferred_element_type=F32)


def dot_rows(a, b):
    return lax.dot_general(a, b, (((0,), (0,)), ((), ())), preferred_element_type=F32)


def group_total(row, group_size):
    channels = row.shape[-1]
    lane = lax.broadcasted_iota(jnp.int32, row.shape, 1)
    step = 1
    while step < group_size:
        up = pltpu.roll(row, channels - step, axis=1)
        down = pltpu.roll(row, step, axis=1)
        row = row + jnp.where((lane & step) == 0, up, down)
        step *= 2
    return row


def frame_stats(part_refs, f, entries, group_size):
    total = part_refs[0][f]
    for ref in part_refs[1:]:
        total = total + ref[f]
    return group_total(total, group_size) / entries


def mean_and_inv(part_refs, f, entries, group_size):
    both = frame_stats(part_refs, f, entries, group_size)
    mean = both[0:1]
    inv = lax.rsqrt(both[1:2] - mean * mean + NORM_EPS)
    return mean, inv


def column_sums(first, second):
    return jnp.concatenate(
        [jnp.sum(first, axis=0, keepdims=True), jnp.sum(second, axis=0, keepdims=True)], axis=0
    )


def put_windows(above, mid, below, lhs_ref, at, order):
    width, (pixels, channels) = above.shape[0], mid.shape
    first, mid_at, last = (slice(k * channels, (k + 1) * channels) for k in order)
    lhs_ref[at : at + width, first] = above
    lhs_ref[at + width : at + pixels, first] = mid[: pixels - width]
    lhs_ref[at : at + pixels, mid_at] = mid
    lhs_ref[at : at + pixels - width, last] = mid[width:]
    lhs_ref[at + pixels - width : at + pixels, last] = below


def from_left(y, width):
    col = lax.broadcasted_iota(jnp.int32, y.shape, 0) & (width - 1)
    return jnp.where(col == 0, 0.0, pltpu.roll(y, 1, axis=0))


def from_right(y, width):
    col = lax.broadcasted_iota(jnp.int32, y.shape, 0) & (width - 1)
    return jnp.where(col == width - 1, 0.0, pltpu.roll(y, y.shape[0] - 1, axis=0))


def slot_sources(clip_ref, dil_ref, local, frames):
    slot = lax.axis_index("tm") * frames + local
    start1 = clip_ref[0]
    filled = start1 + clip_ref[1]
    in_first = slot < start1
    d = jnp.where(in_first, dil_ref[0], dil_ref[1])
    low = jnp.where(in_first, 0, start1)
    high = jnp.where(in_first, start1, filled)
    used = slot < filled
    later, earlier = local + d, local - d
    later_live = used & (slot + d < high)
    earlier_live = used & (slot - d >= low)
    later_which = jnp.where(later_live, jnp.where(later < frames, 1, 2), 0)
    earlier_which = jnp.where(earlier_live, jnp.where(earlier >= 0, 1, 2), 0)
    return (later, later_which), (earlier, earlier_which), used


def gather_taps(clip_ref, dil_ref, local, own, nxt, prv, corner, cat_ref, at, up_slot):
    frames, pixels, channels = own.shape
    later, earlier, used = slot_sources(clip_ref, dil_ref, local, frames)
    me, half = lax.axis_index("tm"), frames // 2

    def put(slot, ref, index):
        cat_ref[pl.ds(at, pixels), slot * channels : (slot + 1) * channels] = ref[index]

    def clear(slot):
        cat_ref[pl.ds(at, pixels), slot * channels : (slot + 1) * channels] = jnp.zeros((pixels, channels), BF16)

    for slot, (index, which), other, shift, turn in (
        (up_slot, later, nxt, -frames, 3),
        (2 - up_slot, earlier, prv, frames, 4),
    ):
        beyond = which == 2
        there = jnp.clip(index + shift, 0, frames - 1)
        pl.when(which == 0)(functools.partial(clear, slot))
        pl.when(which == 1)(functools.partial(put, slot, own, jnp.clip(index, 0, frames - 1)))
        if corner:
            by_corner = beyond & (me == turn)
            low, high = by_corner & (there < half), by_corner & (there >= half)
            pl.when(low)(functools.partial(put, slot, corner[0], jnp.minimum(there, half - 1)))
            pl.when(high)(functools.partial(put, slot, corner[1], jnp.maximum(there - half, 0)))
            beyond = beyond & (me != turn)
        pl.when(beyond)(functools.partial(put, slot, other, there))
    pl.when(used)(functools.partial(put, 1, own, local))
    pl.when(jnp.logical_not(used))(functools.partial(clear, 1))


def loop(count, body):
    def step(k, carry):
        body(k)
        return carry

    lax.fori_loop(0, count, step, 0)


def conv_kernel(x_ref, above_ref, below_ref, w_ref, out_ref, sums_ref, lhs_ref):
    frames, rows, width, channels = x_ref.shape
    pixels = rows * width

    def body(pair):
        for b in range(2):
            f = 2 * pair + b
            mid = x_ref[f].reshape(pixels, channels)
            put_windows(above_ref[f, 0], mid, below_ref[f, 0], lhs_ref, b * pixels, (0, 1, 2))
        lhs = lhs_ref[...]
        y = [dot(lhs, w_ref[:, j].reshape(3 * channels, channels)) for j in range(3)]
        out = y[1] + from_left(y[0], width) + from_right(y[2], width)
        for b in range(2):
            one = out[b * pixels : (b + 1) * pixels]
            out_ref[2 * pair + b] = one
            sums_ref[2 * pair + b] = column_sums(one, one * one)

    loop(frames // 2, body)


def silu_parts(normed, half_gain, half_shift):
    h = normed * half_gain + half_shift
    t = jnp.tanh(h)
    rise = 1.0 + t
    return h, rise, rise * (1.0 + h * (1.0 - t)) * half_gain


def act_kernel(n, entries, group_size, clip_ref, *refs):
    parts, refs = refs[:n], refs[n:]
    conv_ref, gain_ref, shift_ref, act_ref, normed_ref, slope_ref = refs
    frames = conv_ref.shape[0]
    first = lax.axis_index("tm") * frames
    filled = clip_ref[0] + clip_ref[1]
    half_gain, half_shift = 0.5 * gain_ref[...], 0.5 * shift_ref[...]

    def body(f):
        mean, inv = mean_and_inv(parts, f, entries, group_size)
        normed = (conv_ref[f] - mean) * inv
        h, rise, slope = silu_parts(normed, half_gain, half_shift)
        act_ref[f] = jnp.where(first + f < filled, h * rise, 0.0).astype(BF16)
        normed_ref[f] = normed.astype(BF16)
        slope_ref[f] = slope.astype(BF16)

    loop(frames, body)


def turn_kernel(x_ref, above_ref, below_ref, xt_ref, lhs_ref):
    frames, rows, width, channels = x_ref.shape
    pixels = rows * width

    def body(f):
        mid = x_ref[f].reshape(pixels, channels)
        put_windows(above_ref[f, 0], mid, below_ref[f, 0], lhs_ref, 0, (0, 1, 2))
        lanes = pl.ds(pl.multiple_of(f * pixels, pixels), pixels)
        for i in range(3):
            block = slice(i * channels, (i + 1) * channels)
            xt_ref[block, lanes] = lhs_ref[:, block].T

    loop(frames, body)


def turn_weights_kernel(spatial_ref, temporal_ref, back_ref, out_ref):
    channels = spatial_ref.shape[-1]
    for i in range(3):
        rows = slice(i * channels, (i + 1) * channels)
        out_ref[rows] = temporal_ref[i].T
        for j in range(3):
            back_ref[j, rows] = spatial_ref[i, j].T


def grad_act_kernel(corners, clip_ref, dil_ref, own, nxt, prv, *refs):
    corner, (tw_ref, normed_ref, slope_ref, ga_ref, cat_ref, sums_ref) = refs[:corners], refs[corners:]
    frames, pixels, _ = own.shape

    def body(pair):
        rows = pl.ds(pl.multiple_of(2 * pair * pixels, 2 * pixels), 2 * pixels)
        for b in range(2):
            at = pl.multiple_of((2 * pair + b) * pixels, pixels)
            gather_taps(clip_ref, dil_ref, 2 * pair + b, own, nxt, prv, corner, cat_ref, at, 0)
        grad_act = dot(cat_ref[rows], tw_ref[...]).astype(BF16)
        for b in range(2):
            f = 2 * pair + b
            one = grad_act[b * pixels : (b + 1) * pixels]
            ga_ref[f] = one
            gn = one.astype(F32) * slope_ref[f].astype(F32)
            sums_ref[f] = column_sums(gn, gn * normed_ref[f].astype(F32))

    loop(frames // 2, body)


def temporal_grad_kernel(act_ref, cat_ref, out_ref):
    frames, pixels, channels = act_ref.shape
    out_ref[...] = dot_rows(act_ref[...].reshape(frames * pixels, channels), cat_ref[...])


def norm_back_kernel(n, m, entries, group_size, normed_ref, slope_ref, ga_ref, *refs):
    parts, grad_parts = refs[:n], refs[n : n + m]
    g_ref, first_ref, last_ref, moved_ref = refs[n + m :]
    _, pixels, channels = normed_ref.shape
    width = first_ref.shape[2]

    def body(f):
        _, inv = mean_and_inv(parts, f, entries, group_size)
        means = frame_stats(grad_parts, f, entries, group_size)
        gn = ga_ref[f].astype(F32) * slope_ref[f].astype(F32)
        wide = inv * (gn - means[0:1] - normed_ref[f].astype(F32) * means[1:2])
        grad = wide.astype(BF16)
        g_ref[f] = grad
        first_ref[f, 0] = grad[:width]
        last_ref[f, 0] = grad[pixels - width :]
        here = pl.ds(pl.multiple_of(f * pixels, pixels), pixels)
        moved_ref[here, :channels] = from_right(wide, width).astype(BF16)
        moved_ref[here, channels : 2 * channels] = grad
        moved_ref[here, 2 * channels :] = from_left(wide, width).astype(BF16)

    loop(normed_ref.shape[0], body)


def weight_grad_kernel(xt_ref, moved_ref, temporal_ref, out_ref):
    channels = temporal_ref.shape[0]
    for j in range(3):
        lanes = slice(j * channels, (j + 1) * channels)
        out_ref[: 3 * channels, lanes] = dot(xt_ref[...], moved_ref[:, lanes])
    out_ref[3 * channels :, :] = temporal_ref[...]


def hand_out_kernel(acc_ref, send_ref, keep_ref):
    chips, depth, block, _ = keep_ref.shape
    half = chips * depth * block
    core = lax.axis_index("tm") & 1

    def hand_out(kept, sent):
        for p in range(chips):
            for z in range(depth):
                at = (p * depth + z) * block
                keep_ref[p, z] = acc_ref[kept + at : kept + at + block]
                send_ref[p, z] = acc_ref[sent + at : sent + at + block].astype(BF16)

    pl.when(core == 0)(functools.partial(hand_out, 0, half))
    pl.when(core == 1)(functools.partial(hand_out, half, 0))


def conv_back_kernel(g_ref, above_ref, below_ref, cot_ref, w_ref, out_ref, lhs_ref):
    frames, rows, width, channels = cot_ref.shape
    pixels = rows * width

    def body(pair):
        for b in range(2):
            f = 2 * pair + b
            put_windows(above_ref[f, 0], g_ref[f], below_ref[f, 0], lhs_ref, b * pixels, (2, 1, 0))
        lhs = lhs_ref[...]
        z = [dot(lhs, w_ref[j]) for j in range(3)]
        out = z[1] + from_right(z[0], width) + from_left(z[2], width)
        for b in range(2):
            one = out[b * pixels : (b + 1) * pixels].reshape(rows, width, channels)
            out_ref[2 * pair + b] = (one + cot_ref[2 * pair + b].astype(F32)).astype(BF16)

    loop(frames // 2, body)


def out_kernel(clip_ref, dil_ref, own, nxt, prv, tw_ref, x_ref, out_ref, cat_ref):
    frames, rows, width, channels = x_ref.shape
    pixels = rows * width

    def body(pair):
        for b in range(2):
            gather_taps(clip_ref, dil_ref, 2 * pair + b, own, nxt, prv, (), cat_ref, b * pixels, 2)
        temporal_out = dot(cat_ref[...], tw_ref[...]).astype(BF16).astype(F32)
        for b in range(2):
            one = temporal_out[b * pixels : (b + 1) * pixels].reshape(rows, width, channels)
            out_ref[2 * pair + b] = (x_ref[2 * pair + b].astype(F32) + one).astype(BF16)

    loop(frames // 2, body)


def core_sum_kernel(keep_ref, got_ref, own_ref, *send_refs):
    chip = lax.axis_index("tm") >> 1
    own_ref[...] = keep_ref[chip] + got_ref[chip].astype(F32)
    for s, ref in enumerate(send_refs, 1):
        ref[...] = (keep_ref[chip ^ s] + got_ref[chip ^ s].astype(F32)).astype(BF16)


def sum_kernel(count, own_ref, *refs):
    total = own_ref[...]
    for ref in refs[:count]:
        total = total + ref[...].astype(F32)
    refs[count][...] = total.astype(BF16)


def sum_split_kernel(count, own_ref, *refs):
    got, (mine_ref, *send_refs) = refs[:count], refs[count:]
    deep = lax.axis_index("space")

    def block(k):
        total = own_ref[k]
        for ref in got:
            total = total + ref[k].astype(F32)
        return total

    mine_ref[...] = block(deep)
    for s, ref in enumerate(send_refs, 1):
        ref[...] = block(deep ^ s).astype(BF16)


def place_kernel(axis, shift, *refs):
    me = lax.axis_index(axis) >> shift
    for s, ref in enumerate(refs[:-1]):
        refs[-1][me ^ s] = ref[...]


def finish_kernel(mine_ref, got_ref, spatial_ref, temporal_ref):
    chips, depth, block, _ = mine_ref.shape
    channels = spatial_ref.shape[-1]

    def write(pair):
        for c in range(2):
            for p in range(chips):
                for z in range(depth):
                    row = ((c * chips + p) * depth + z) * block
                    values = pair[c][p, z].astype(F32)
                    i, at = row // channels, row % channels
                    for k in range(3):
                        lanes = values[:, k * channels : (k + 1) * channels]
                        if i < 3:
                            spatial_ref[i, k, at : at + block] = lanes
                        else:
                            temporal_ref[k, at : at + block] = lanes

    core = lax.axis_index("tm") & 1
    pl.when(core == 0)(functools.partial(write, (mine_ref, got_ref)))
    pl.when(core == 1)(functools.partial(write, (got_ref, mine_ref)))


def neighbours(axis, low, high, but=None):
    size = lax.axis_size(axis)
    up = [(i, i + 1) for i in range(size - 1) if i != but]
    down = [(j, i) for i, j in up]
    return lax.ppermute(high, axis, up), lax.ppermute(low, axis, down)


def spread_sums(part, axis):
    size = lax.axis_size(axis)
    step, got = 1, None
    while step < size:
        if got is not None:
            part = part + got
        got = lax.ppermute(part, axis, [(i, i ^ step) for i in range(size)])
        step *= 2
    return [part, got]


def per_device(frames_in, cotangent, spatial, temporal, norm_gain, norm_shift, clip_frames, dilation):
    frames, rows, width, channels = frames_in.shape
    pixels = rows * width
    n, tm = lax.axis_size("space"), lax.axis_size("tm")
    chips = tm // 2
    group_size = channels // GROUPS
    entries = float(rows * n * width * group_size)
    gain, shift = norm_gain[None], norm_shift[None]
    big = frames * pixels * channels
    shape = jax.ShapeDtypeStruct
    per_px = (frames, pixels, channels)
    windows = pltpu.VMEM((2 * pixels, 3 * channels), BF16)

    cot = cotangent.reshape(per_px)
    by_corner = tm == 8
    cot_prev, cot_next = neighbours("tm", cot, cot, 3 if by_corner else None)
    cot_corner = []
    if by_corner:
        relayed = lax.ppermute(cot, "tm", [(3, 7), (4, 0)])
    above, below = neighbours("space", frames_in[:, :1], frames_in[:, rows - 1 :])
    back_weights, back_taps = call(
        turn_weights_kernel, "turn_weights", [spatial, temporal],
        [shape((3, 3 * channels, channels), BF16), shape((3 * channels, channels), BF16)], 0, big,
    )
    conv_out, sums = call(
        conv_kernel, "conv_forward", [frames_in, above, below, spatial],
        [shape(per_px, F32), shape((frames, 2, channels), F32)],
        18 * big * channels, 8 * big, [windows], 18,
    )
    if by_corner:
        sums, straight = lax.optimization_barrier((sums, cot))
        cot_corner.append(lax.ppermute(straight[: frames // 2], "tm", [(3, 4), (4, 3)]))
    parts = spread_sums(sums, "space")
    if by_corner:
        parts[0], relayed = lax.optimization_barrier((parts[0], relayed))
        cot_corner.append(lax.ppermute(relayed[frames // 2 :], "tm", [(7, 4), (0, 3)]))
    x_turned = call(
        turn_kernel, "turned", [frames_in, above, below], shape((3 * channels, frames * pixels), BF16),
        0, 8 * big, [pltpu.VMEM((pixels, 3 * channels), BF16)],
    )
    x_turned, *parts = lax.optimization_barrier((x_turned, *parts))
    act, normed, slope = call(
        functools.partial(act_kernel, len(parts), entries, group_size), "activation",
        [clip_frames, *parts, conv_out, gain, shift], [shape(per_px, BF16)] * 3, 10 * big, 10 * big,
    )
    act_prev, act_next = neighbours("tm", act, act)

    grad_act, cot_cat, grad_sums = call(
        functools.partial(grad_act_kernel, len(cot_corner)), "grad_activation",
        [clip_frames, dilation, cot, cot_next, cot_prev, *cot_corner, back_taps, normed, slope],
        [shape(per_px, BF16), shape((frames * pixels, 3 * channels), BF16), shape((frames, 2, channels), F32)],
        6 * big * channels, 16 * big,
    )
    grad_parts = spread_sums(grad_sums, "space")
    temporal_part = call(
        temporal_grad_kernel, "temporal_grad", [act, cot_cat],
        shape((channels, 3 * channels), F32), 6 * big * channels, 8 * big,
    )
    lanes = 3 * channels
    grad_conv, first_rows, last_rows, moved = call(
        functools.partial(norm_back_kernel, len(parts), len(grad_parts), entries, group_size), "norm_backward",
        [normed, slope, grad_act, *parts, *grad_parts],
        [shape(per_px, BF16)] + [shape((frames, 1, width, channels), BF16)] * 2
        + [shape((frames * pixels, lanes), BF16)],
        0, 12 * big,
    )
    grad_above, grad_below = neighbours("space", first_rows, last_rows)
    sums = call(
        weight_grad_kernel, "weight_grad", [x_turned, moved, temporal_part], shape((4 * channels, lanes), F32),
        18 * big * channels, 12 * big,
    )
    sums, grad_above, grad_below = lax.optimization_barrier((sums, grad_above, grad_below))
    block = 2 * channels // (chips * n)
    send, keep = call(
        hand_out_kernel, "hand_out", [sums],
        [shape((chips, n, block, lanes), BF16), shape((chips, n, block, lanes), F32)], 0, big,
    )
    def other_chip(s):
        return [(i, i ^ (2 * s)) for i in range(tm)]

    def other_plane(s):
        return [(i, i ^ s) for i in range(n)]

    other_core = [(i, i ^ 1) for i in range(tm)]
    got = lax.ppermute(send, "tm", other_core)
    own, *sends = call(
        core_sum_kernel, "core_sum", [keep, got],
        [shape((n, block, lanes), F32)] + [shape((n, block, lanes), BF16)] * (chips - 1), 0, 4 * big,
    )
    gots = [lax.ppermute(x, "tm", other_chip(s)) for s, x in enumerate(sends, 1)]

    in_grad = call(
        conv_back_kernel, "conv_backward", [grad_conv, grad_above, grad_below, cotangent, back_weights],
        shape(frames_in.shape, BF16), 18 * big * channels, 8 * big, [windows], 20,
    )
    own, in_grad, act_prev, act_next = lax.optimization_barrier((own, in_grad, act_prev, act_next))

    own, *sends = call(
        functools.partial(sum_split_kernel, chips - 1), "plane_sum", [own, *gots],
        [shape((block, lanes), F32)] + [shape((block, lanes), BF16)] * (n - 1), 0, big,
    )
    gots = [lax.ppermute(x, "space", other_plane(s)) for s, x in enumerate(sends, 1)]
    own = call(
        functools.partial(sum_kernel, n - 1), "line_sum", [own, *gots], shape((block, lanes), BF16), 0, big
    )
    gots = [lax.ppermute(own, "space", other_plane(s)) for s in range(1, n)]
    own = call(
        functools.partial(place_kernel, "space", 0), "line_place", [own, *gots], shape((n, block, lanes), BF16), 0, big
    )
    gots = [lax.ppermute(own, "tm", other_chip(s)) for s in range(1, chips)]

    out_frames = call(
        out_kernel, "temporal_forward",
        [clip_frames, dilation, act, act_next, act_prev, temporal.reshape(3 * channels, channels), frames_in],
        shape(frames_in.shape, BF16), 6 * big * channels, 10 * big, [windows],
    )
    own, out_frames = lax.optimization_barrier((own, out_frames))

    own = call(
        functools.partial(place_kernel, "tm", 1), "plane_place", [own, *gots], shape((chips, n, block, lanes), BF16), 0, big
    )
    got = lax.ppermute(own, "tm", other_core)
    spatial_grad, temporal_grad = call(
        finish_kernel, "finish", [own, got], [shape(spatial.shape, F32), shape(temporal.shape, F32)], 0, 4 * big
    )
    return (out_frames, in_grad, spatial_grad, temporal_grad)


def solution(mesh):
    tiles = P("tm", "space", None, None)
    return jax.shard_map(
        per_device,
        mesh=mesh,
        in_specs=(tiles, tiles, P(), P(), P(), P(), P(), P()),
        out_specs=(tiles, tiles, P(), P()),
        check_vma=False,
    )
```

profile of v0, /device:TPU:0, one launch (start us, length us, event | category | flops | bytes accessed | tf_op | source)
XLA Modules:
  0.0 140.9 jit_solution(6081887458101658660)
XLA Ops:
  0.6 1.3 collective-permute-start.3
  1.9 1.3 collective-permute-start.5
  3.2 3.2 %collective-permute-start.6 = (bf16[8,512,256]{2,1,0:T(8,128)(2,1)}, bf16[8,512,256]{2,1,0:T(8,128)(2,1)S(1)}, u32[]{:S(2)}, u32[]{:S(2)}) collective-permute-start(bf16[8,512,256]{2,1,0:T(8,128)(2,1)} %bitcast.6), channel_id=1, source_target_pairs={{0,4},{4,8},{8,12},{16,20},{20,24},{24,28},{1,5},{5,9},{9,13},{17,... | collective-permute-start | bytes 6291464 | tf_op jit(solution)/shard_map/ppermute | solution.py:384
  6.4 1.1 fusion
  7.5 4.9 %collective-permute-start = (bf16[8,1,64,256]{3,2,1,0:T(8,128)(2,1)S(1)}, bf16[8,1,64,256]{3,2,1,0:T(8,128)(2,1)S(1)}, u32[]{:S(2)}, u32[]{:S(2)}) collective-permute-start(bf16[8,1,64,256]{3,2,1,0:T(8,128)(2,1)S(1)} %get-tuple-element.89), channel_id=1, source_target_pairs={{0,1},{1,2},{2,3},{4,5},{5,6},{6,7},{8,9},{9,10},{10,11},{12,13},{... | collective-permute-start | bytes 786440 | tf_op jit(solution)/shard_map/ppermute | solution.py:384
  12.4 1.3 collective-permute-start.1
  13.7 4.9 %collective-permute-done.above_ref = bf16[8,1,64,256]{3,2,1,0:T(8,128)(2,1)S(1)} collective-permute-done((bf16[8,1,64,256]{3,2,1,0:T(8,128)(2,1)S(1)}, bf16[8,1,64,256]{3,2,1,0:T(8,128)(2,1)S(1)}, u32[]{:S(2)}, u32[]{:S(2)}) %collective-permute-start) | collective-permute-done | bytes 262176 | tf_op jit(solution)/shard_map/ppermute | solution.py:384
  18.6 4.1 %collective-permute-done.1.below_ref = bf16[8,1,64,256]{3,2,1,0:T(8,128)(2,1)S(1)} collective-permute-done((bf16[8,1,64,256]{3,2,1,0:T(8,128)(2,1)S(1)}, bf16[8,1,64,256]{3,2,1,0:T(8,128)(2,1)S(1)}, u32[]{:S(2)}, u32[]{:S(2)}) %collective-permute-start.1) | collective-permute-done | bytes 262176 | tf_op jit(solution)/shard_map/ppermute | solution.py:384
  22.8 1.6 %copy-done = bf16[8,8,64,256]{3,2,1,0:T(8,128)(2,1)S(1)} copy-done((bf16[8,8,64,256]{3,2,1,0:T(8,128)(2,1)S(1)}, bf16[8,8,64,256]{3,2,1,0:T(8,128)(2,1)}, u32[]{:S(2)}) %copy-start) | copy-done | bytes 2097176
  24.3 1.3 copy-done.4
  25.6 5.6 %conv_forward.1 = (f32[8,512,256]{2,1,0:T(8,128)S(1)}, f32[8,2,256]{2,1,0:T(2,128)S(1)}) custom-call(bf16[8,8,64,256]{3,2,1,0:T(8,128)(2,1)S(1)} %copy-done, bf16[8,1,64,256]{3,2,1,0:T(8,128)(2,1)S(1)} %collective-permute-done.above_ref, bf16[8,1,64,256]{3,2,1,0:T(8,128)(2,1)S(1)} %collective-permute-done.1.below_ref, bf16[3,3,256,256]{3,2,1,0:T(8,128)(2,1)S(1)} %copy-done.4), custom_call_target="tpu_custom_call" | custom-call | flops 4831838208 | bytes 8388608 | tf_op jit(solution)/shard_map/conv_forward/pallas_call | solution.py:20
  31.3 0.1 slice.14
  31.3 0.9 collective-permute-start.7
  32.2 1.6 %collective-permute-start.2 = (f32[8,2,256]{2,1,0:T(2,128)S(1)}, f32[8,2,256]{2,1,0:T(2,128)S(1)}, u32[]{:S(2)}, u32[]{:S(2)}) collective-permute-start(f32[8,2,256]{2,1,0:T(2,128)S(1)} %get-tuple-element.47), channel_id=1, source_target_pairs={{0,1},{1,0},{2,3},{3,2},{4,5},{5,4},{6,7},{7,6},{8,9},{9,8},{10,11... | collective-permute-start | bytes 49160 | tf_op jit(solution)/shard_map/ppermute | solution.py:393
  33.8 2.2 %collective-permute-done.2 = f32[8,2,256]{2,1,0:T(2,128)S(1)} collective-permute-done((f32[8,2,256]{2,1,0:T(2,128)S(1)}, f32[8,2,256]{2,1,0:T(2,128)S(1)}, u32[]{:S(2)}, u32[]{:S(2)}) %collective-permute-start.2) | collective-permute-done | bytes 16416 | tf_op jit(solution)/shard_map/ppermute | solution.py:393
  36.0 0.1 slice.15
  36.1 5.5 %collective-permute-start.8 = (bf16[4,512,256]{2,1,0:T(8,128)(2,1)S(1)}, bf16[4,512,256]{2,1,0:T(8,128)(2,1)S(1)}, u32[]{:S(2)}, u32[]{:S(2)}) collective-permute-start(bf16[4,512,256]{2,1,0:T(8,128)(2,1)S(1)} %slice.15), channel_id=1, source_target_pairs={{28,16},{0,12},{29,17},{1,13},{30,18},{2,14},{31,19},{3,15}} | collective-permute-start | bytes 3145736 | tf_op jit(solution)/shard_map/ppermute | solution.py:433
  41.6 2.6 %collective-permute-start.4 = (f32[8,2,256]{2,1,0:T(2,128)S(1)}, f32[8,2,256]{2,1,0:T(2,128)S(1)}, u32[]{:S(2)}, u32[]{:S(2)}) collective-permute-start(f32[8,2,256]{2,1,0:T(2,128)S(1)} %add.6.refs_0_), channel_id=1, source_target_pairs={{0,2},{1,3},{2,0},{3,1},{4,6},{5,7},{6,4},{7,5},{8,10},{9,11},{10,... | collective-permute-start | bytes 49160 | tf_op jit(solution)/shard_map/ppermute | solution.py:393
  44.3 2.2 %turned.1.xt_ref = bf16[768,4096]{1,0:T(8,128)(2,1)S(1)} custom-call(bf16[8,8,64,256]{3,2,1,0:T(8,128)(2,1)S(1)} %copy-done.1, bf16[8,1,64,256]{3,2,1,0:T(8,128)(2,1)S(1)} %collective-permute-done.above_ref, bf16[8,1,64,256]{3,2,1,0:T(8,128)(2,1)S(1)} %collective-permute-done.1.below_ref), custom_call_target="tpu_custom_call" | custom-call | bytes 8388608 | tf_op jit(solution)/shard_map/turned/pallas_call | solution.py:20
  46.5 6.0 %activation.1 = (bf16[8,512,256]{2,1,0:T(8,128)(2,1)S(1)}, bf16[8,512,256]{2,1,0:T(8,128)(2,1)S(1)}, bf16[8,512,256]{2,1,0:T(8,128)(2,1)S(1)}) custom-call(s32[2]{0:T(128)S(1)} %copy-done.5, f32[8,2,256]{2,1,0:T(2,128)S(1)} %add.6.refs_0_, f32[8,2,256]{2,1,0:T(2,128)S(1)} %collective-permute-done.4.refs_1_, f32[8,512,256]{2,1,0:T(8,128)S(1)} %get-tuple-element.52.refs_2_, ...), custom_call_target="tpu_custom_call" | custom-call | flops 10485760 | bytes 10485760 | tf_op jit(solution)/shard_map/activation/pallas_call | solution.py:20
  52.6 1.4 %collective-permute-start.14 = (bf16[8,512,256]{2,1,0:T(8,128)(2,1)S(1)}, bf16[8,512,256]{2,1,0:T(8,128)(2,1)S(1)}, u32[]{:S(2)}, u32[]{:S(2)}) collective-permute-start(bf16[8,512,256]{2,1,0:T(8,128)(2,1)S(1)} %get-tuple-element.61.act_ref.own), channel_id=1, source_target_pairs={{0,4},{4,8},{8,12},{12,16},{16,20},{20,24},{24,28},{1,5},{5,9},{9,... | collective-permute-start | bytes 6291464 | tf_op jit(solution)/shard_map/ppermute | solution.py:384
  54.0 1.3 collective-permute-start.15
  55.3 0.5 turn_weights.1
  55.8 0.5 collective-permute-done.8.refs_1_
  56.3 4.1 %grad_activation.1 = (bf16[8,512,256]{2,1,0:T(8,128)(2,1)S(1)}, bf16[4096,768]{1,0:T(8,128)(2,1)S(1)}, f32[8,2,256]{2,1,0:T(2,128)S(1)}) custom-call(s32[2]{0:T(128)S(1)} %copy-done.5, s32[2]{0:T(128)S(1)} %copy-done.6, bf16[8,512,256]{2,1,0:T(8,128)(2,1)S(1)} %bitcast.8, bf16[8,512,256]{2,1,0:T(8,128)(2,1)S(1)} %collective-permute-done.5.nxt, ...), custom_call_target="tpu_custom_call" | custom-call | flops 1610612736 | bytes 16777216 | tf_op jit(solution)/shard_map/grad_activation/pallas_call | solution.py:20
  60.4 1.8 %collective-permute-start.9 = (f32[8,2,256]{2,1,0:T(2,128)S(1)}, f32[8,2,256]{2,1,0:T(2,128)S(1)}, u32[]{:S(2)}, u32[]{:S(2)}) collective-permute-start(f32[8,2,256]{2,1,0:T(2,128)S(1)} %get-tuple-element.59), channel_id=1, source_target_pairs={{0,1},{1,0},{2,3},{3,2},{4,5},{5,4},{6,7},{7,6},{8,9},{9,8},{10,11... | collective-permute-start | bytes 49160 | tf_op jit(solution)/shard_map/ppermute | solution.py:393
  62.2 2.0 %collective-permute-done.9 = f32[8,2,256]{2,1,0:T(2,128)S(1)} collective-permute-done((f32[8,2,256]{2,1,0:T(2,128)S(1)}, f32[8,2,256]{2,1,0:T(2,128)S(1)}, u32[]{:S(2)}, u32[]{:S(2)}) %collective-permute-start.9) | collective-permute-done | bytes 16416 | tf_op jit(solution)/shard_map/ppermute | solution.py:393
  64.2 2.8 %collective-permute-start.10 = (f32[8,2,256]{2,1,0:T(2,128)S(1)}, f32[8,2,256]{2,1,0:T(2,128)S(1)}, u32[]{:S(2)}, u32[]{:S(2)}) collective-permute-start(f32[8,2,256]{2,1,0:T(2,128)S(1)} %add.7.refs_2_), channel_id=1, source_target_pairs={{0,2},{1,3},{2,0},{3,1},{4,6},{5,7},{6,4},{7,5},{8,10},{9,11},{10,... | collective-permute-start | bytes 49160 | tf_op jit(solution)/shard_map/ppermute | solution.py:393
  67.0 1.9 %temporal_grad.1.temporal_ref = f32[256,768]{1,0:T(8,128)S(1)} custom-call(bf16[8,512,256]{2,1,0:T(8,128)(2,1)S(1)} %get-tuple-element.61.act_ref.own, bf16[4096,768]{1,0:T(8,128)(2,1)S(1)} %get-tuple-element.62.cat_ref), custom_call_target="tpu_custom_call" | custom-call | flops 1610612736 | bytes 8388608 | tf_op jit(solution)/shard_map/temporal_grad/pallas_call | solution.py:20
  68.9 0.0 collective-permute-done.10.refs_3_
  68.9 4.6 %norm_backward.1 = (bf16[8,512,256]{2,1,0:T(8,128)(2,1)S(1)}, bf16[8,1,64,256]{3,2,1,0:T(8,128)(2,1)S(1)}, bf16[8,1,64,256]{3,2,1,0:T(8,128)(2,1)S(1)}, bf16[4096,768]{1,0:T(8,128)(2,1)S(1)}) custom-call(bf16[8,512,256]{2,1,0:T(8,128)(2,1)S(1)} %get-tuple-element.53.refs_3_.normed_ref, bf16[8,512,256]{2,1,0:T(8,128)(2,1)S(1)} %get-tuple-element.54.refs_4_.slope_ref, ...), custom_call_target="tpu_custom_call" | custom-call | bytes 12582912 | tf_op jit(solution)/shard_map/norm_backward/pallas_call | solution.py:20
  73.5 3.6 %collective-permute-start.11 = (bf16[8,1,64,256]{3,2,1,0:T(8,128)(2,1)S(1)}, bf16[8,1,64,256]{3,2,1,0:T(8,128)(2,1)S(1)}, u32[]{:S(2)}, u32[]{:S(2)}) collective-permute-start(bf16[8,1,64,256]{3,2,1,0:T(8,128)(2,1)S(1)} %get-tuple-element.63), channel_id=1, source_target_pairs={{0,1},{1,2},{2,3},{4,5},{5,6},{6,7},{8,9},{9,10},{10,11},{12,13},{... | collective-permute-start | bytes 786440 | tf_op jit(solution)/shard_map/ppermute | solution.py:384
  77.2 1.3 collective-permute-start.12
  78.5 5.1 %weight_grad.1.acc_ref = f32[1024,768]{1,0:T(8,128)S(1)} custom-call(bf16[768,4096]{1,0:T(8,128)(2,1)S(1)} %turned.1.xt_ref, bf16[4096,768]{1,0:T(8,128)(2,1)S(1)} %get-tuple-element.60.moved_ref, f32[256,768]{1,0:T(8,128)S(1)} %temporal_grad.1.temporal_ref), custom_call_target="tpu_custom_call" | custom-call | flops 4831838208 | bytes 12582912 | tf_op jit(solution)/shard_map/weight_grad/pallas_call | solution.py:20
  83.6 1.8 %collective-permute-done.12.below_ref = bf16[8,1,64,256]{3,2,1,0:T(8,128)(2,1)S(1)} collective-permute-done((bf16[8,1,64,256]{3,2,1,0:T(8,128)(2,1)S(1)}, bf16[8,1,64,256]{3,2,1,0:T(8,128)(2,1)S(1)}, u32[]{:S(2)}, u32[]{:S(2)}) %collective-permute-start.12) | collective-permute-done | bytes 262176 | tf_op jit(solution)/shard_map/ppermute | solution.py:384
  85.4 0.4 hand_out.1
  85.8 0.1 collective-permute-start.13
  85.9 2.3 %collective-permute-done.13.got_ref = bf16[4,4,32,768]{3,2,1,0:T(8,128)(2,1)S(1)} collective-permute-done((bf16[4,4,32,768]{3,2,1,0:T(8,128)(2,1)S(1)}, bf16[4,4,32,768]{3,2,1,0:T(8,128)(2,1)S(1)}, u32[]{:S(2)}, u32[]{:S(2)}) %collective-permute-start.13) | collective-permute-done | bytes 786464 | tf_op jit(solution)/shard_map/ppermute | solution.py:482
  88.1 0.2 core_sum.1
  88.3 1.6 %collective-permute-start.16 = (bf16[4,32,768]{2,1,0:T(8,128)(2,1)S(1)}, bf16[4,32,768]{2,1,0:T(8,128)(2,1)S(1)}, u32[]{:S(2)}, u32[]{:S(2)}) collective-permute-start(bf16[4,32,768]{2,1,0:T(8,128)(2,1)S(1)} %get-tuple-element.74), channel_id=1, source_target_pairs={{0,8},{4,12},{8,0},{12,4},{16,24},{20,28},{24,16},{28,20},{1,9},{5... | collective-permute-start | bytes 589832 | tf_op jit(solution)/shard_map/ppermute | solution.py:487
  89.9 0.9 collective-permute-start.17
  90.8 1.4 collective-permute-start.18
  92.2 7.0 %conv_backward.1 = bf16[8,8,64,256]{3,2,1,0:T(8,128)(2,1)} custom-call(bf16[8,512,256]{2,1,0:T(8,128)(2,1)S(1)} %get-tuple-element.69.g_ref, bf16[8,1,64,256]{3,2,1,0:T(8,128)(2,1)S(1)} %collective-permute-done.11.above_ref, bf16[8,1,64,256]{3,2,1,0:T(8,128)(2,1)S(1)} %collective-permute-done.12.below_ref, bf16[8,8,64,256]{3,2,1,0:T(8,128)(2,1)S(1)} %copy-done.2, ...), custom_call_target="tpu_custom_call" | custom-call | flops 4831838208 | bytes 8388608 | tf_op jit(solution)/shard_map/conv_backward/pallas_call | solution.py:20
  99.2 7.4 %collective-permute-done.16.refs_0_ = bf16[4,32,768]{2,1,0:T(8,128)(2,1)S(1)} collective-permute-done((bf16[4,32,768]{2,1,0:T(8,128)(2,1)S(1)}, bf16[4,32,768]{2,1,0:T(8,128)(2,1)S(1)}, u32[]{:S(2)}, u32[]{:S(2)}) %collective-permute-start.16) | collective-permute-done | bytes 196640 | tf_op jit(solution)/shard_map/ppermute | solution.py:487
  106.5 0.1 plane_sum.1
  106.6 0.6 collective-permute-start.19
  107.2 1.3 collective-permute-start.20
  108.6 2.5 %collective-permute-start.21 = (bf16[32,768]{1,0:T(8,128)(2,1)S(1)}, bf16[32,768]{1,0:T(8,128)(2,1)S(1)}, u32[]{:S(2)}, u32[]{:S(2)}) collective-permute-start(bf16[32,768]{1,0:T(8,128)(2,1)S(1)} %get-tuple-element.80), channel_id=1, source_target_pairs={{0,3},{1,2},{2,1},{3,0},{4,7},{5,6},{6,5},{7,4},{8,11},{9,10},{10,... | collective-permute-start | bytes 147464 | tf_op jit(solution)/shard_map/ppermute | solution.py:499
  111.1 2.4 %collective-permute-done.20.refs_1_ = bf16[32,768]{1,0:T(8,128)(2,1)S(1)} collective-permute-done((bf16[32,768]{1,0:T(8,128)(2,1)S(1)}, bf16[32,768]{1,0:T(8,128)(2,1)S(1)}, u32[]{:S(2)}, u32[]{:S(2)}) %collective-permute-start.20) | collective-permute-done | bytes 49184 | tf_op jit(solution)/shard_map/ppermute | solution.py:499
  113.5 1.0 collective-permute-done.21.refs_2_
  114.6 0.7 collective-permute-start.22
  115.2 2.4 %collective-permute-start.23 = (bf16[32,768]{1,0:T(8,128)(2,1)S(1)}, bf16[32,768]{1,0:T(8,128)(2,1)S(1)}, u32[]{:S(2)}, u32[]{:S(2)}) collective-permute-start(bf16[32,768]{1,0:T(8,128)(2,1)S(1)} %line_sum.1.refs_0_), channel_id=1, source_target_pairs={{0,2},{1,3},{2,0},{3,1},{4,6},{5,7},{6,4},{7,5},{8,10},{9,11},{10,... | collective-permute-start | bytes 147464 | tf_op jit(solution)/shard_map/ppermute | solution.py:503
  117.6 1.4 collective-permute-start.24
  119.0 1.2 collective-permute-done.23.refs_2_
  120.2 3.3 %collective-permute-done.24.refs_3_ = bf16[32,768]{1,0:T(8,128)(2,1)S(1)} collective-permute-done((bf16[32,768]{1,0:T(8,128)(2,1)S(1)}, bf16[32,768]{1,0:T(8,128)(2,1)S(1)}, u32[]{:S(2)}, u32[]{:S(2)}) %collective-permute-start.24) | collective-permute-done | bytes 49184 | tf_op jit(solution)/shard_map/ppermute | solution.py:503
  123.6 3.0 %collective-permute-start.25 = (bf16[4,32,768]{2,1,0:T(8,128)(2,1)S(1)}, bf16[4,32,768]{2,1,0:T(8,128)(2,1)S(1)}, u32[]{:S(2)}, u32[]{:S(2)}) collective-permute-start(bf16[4,32,768]{2,1,0:T(8,128)(2,1)S(1)} %line_place.1.refs_0_), channel_id=1, source_target_pairs={{0,8},{4,12},{8,0},{12,4},{16,24},{20,28},{24,16},{28,20},{1,9},{5... | collective-permute-start | bytes 589832 | tf_op jit(solution)/shard_map/ppermute | solution.py:507
  126.5 2.0 %collective-permute-start.26 = (bf16[4,32,768]{2,1,0:T(8,128)(2,1)S(1)}, bf16[4,32,768]{2,1,0:T(8,128)(2,1)S(1)}, u32[]{:S(2)}, u32[]{:S(2)}) collective-permute-start(bf16[4,32,768]{2,1,0:T(8,128)(2,1)S(1)} %line_place.1.refs_0_), channel_id=1, source_target_pairs={{0,16},{4,20},{8,24},{12,28},{16,0},{20,4},{24,8},{28,12},{1,17},{... | collective-permute-start | bytes 589832 | tf_op jit(solution)/shard_map/ppermute | solution.py:507
  128.5 1.4 collective-permute-start.27
  129.9 5.0 %temporal_forward.1 = bf16[8,8,64,256]{3,2,1,0:T(8,128)(2,1)} custom-call(s32[2]{0:T(128)S(1)} %copy-done.5, s32[2]{0:T(128)S(1)} %copy-done.6, bf16[8,512,256]{2,1,0:T(8,128)(2,1)S(1)} %get-tuple-element.61.act_ref.own, bf16[8,512,256]{2,1,0:T(8,128)(2,1)S(1)} %collective-permute-done.15.nxt, bf16[8,512,256]{2,1,0:T(8,128)(2,1)S(1)} %collective-permute-done.14.prv, ...), custom_call_target="tpu_custom_call" | custom-call | flops 1610612736 | bytes 10485760 | tf_op jit(solution)/shard_map/temporal_forward/pallas_call | solution.py:20
  134.9 1.7 %collective-permute-done.27.refs_3_ = bf16[4,32,768]{2,1,0:T(8,128)(2,1)S(1)} collective-permute-done((bf16[4,32,768]{2,1,0:T(8,128)(2,1)S(1)}, bf16[4,32,768]{2,1,0:T(8,128)(2,1)S(1)}, u32[]{:S(2)}, u32[]{:S(2)}) %collective-permute-start.27) | collective-permute-done | bytes 196640 | tf_op jit(solution)/shard_map/ppermute | solution.py:507
  136.6 0.1 plane_place.1.mine_ref
  136.7 0.1 collective-permute-start.28
  136.7 2.3 %collective-permute-done.28.got_ref = bf16[4,4,32,768]{3,2,1,0:T(8,128)(2,1)S(1)} collective-permute-done((bf16[4,4,32,768]{3,2,1,0:T(8,128)(2,1)S(1)}, bf16[4,4,32,768]{3,2,1,0:T(8,128)(2,1)S(1)}, u32[]{:S(2)}, u32[]{:S(2)}) %collective-permute-start.28) | collective-permute-done | bytes 786464 | tf_op jit(solution)/shard_map/ppermute | solution.py:519
  139.0 1.9 %finish.1 = (f32[3,3,256,256]{3,2,1,0:T(8,128)}, f32[3,256,256]{2,1,0:T(8,128)}) custom-call(bf16[4,4,32,768]{3,2,1,0:T(8,128)(2,1)S(1)} %plane_place.1.mine_ref, bf16[4,4,32,768]{3,2,1,0:T(8,128)(2,1)S(1)} %collective-permute-done.28.got_ref), custom_call_target="tpu_custom_call" | custom-call | bytes 4194304 | tf_op jit(solution)/shard_map/finish/pallas_call | solution.py:20
  (34 shorter events, 0.2 us)
Async XLA Ops:
  0.6 35.4 %collective-permute-start.3 = (bf16[8,512,256]{2,1,0:T(8,128)(2,1)}, bf16[8,512,256]{2,1,0:T(8,128)(2,1)S(1)}, u32[]{:S(2)}, u32[]{:S(2)}) collective-permute-start(bf16[8,512,256]{2,1,0:T(8,128)(2,1)} %bitcast.4), channel_id=1, source_target_pairs={{12,28},{16,0},{13,29},{17,1},{14,30},{18,2},{15,31},{19,3}} | collective-permute-start | bytes 6291464 | tf_op jit(solution)/shard_map/ppermute | solution.py:416
  1.9 53.9 %collective-permute-start.5 = (bf16[8,512,256]{2,1,0:T(8,128)(2,1)}, bf16[8,512,256]{2,1,0:T(8,128)(2,1)S(1)}, u32[]{:S(2)}, u32[]{:S(2)}) collective-permute-start(bf16[8,512,256]{2,1,0:T(8,128)(2,1)} %bitcast.5), channel_id=1, source_target_pairs={{4,0},{8,4},{12,8},{20,16},{24,20},{28,24},{5,1},{9,5},{13,9},{21,... | collective-permute-start | bytes 6291464 | tf_op jit(solution)/shard_map/ppermute | solution.py:384
  3.2 52.6 %collective-permute-start.6 = (bf16[8,512,256]{2,1,0:T(8,128)(2,1)}, bf16[8,512,256]{2,1,0:T(8,128)(2,1)S(1)}, u32[]{:S(2)}, u32[]{:S(2)}) collective-permute-start(bf16[8,512,256]{2,1,0:T(8,128)(2,1)} %bitcast.6), channel_id=1, source_target_pairs={{0,4},{4,8},{8,12},{16,20},{20,24},{24,28},{1,5},{5,9},{9,13},{17,... | collective-permute-start | bytes 6291464 | tf_op jit(solution)/shard_map/ppermute | solution.py:384
  7.5 11.1 %collective-permute-start = (bf16[8,1,64,256]{3,2,1,0:T(8,128)(2,1)S(1)}, bf16[8,1,64,256]{3,2,1,0:T(8,128)(2,1)S(1)}, u32[]{:S(2)}, u32[]{:S(2)}) collective-permute-start(bf16[8,1,64,256]{3,2,1,0:T(8,128)(2,1)S(1)} %get-tuple-element.89), channel_id=1, source_target_pairs={{0,1},{1,2},{2,3},{4,5},{5,6},{6,7},{8,9},{9,10},{10,11},{12,13},{... | collective-permute-start | bytes 786440 | tf_op jit(solution)/shard_map/ppermute | solution.py:384
  12.4 10.3 %collective-permute-start.1 = (bf16[8,1,64,256]{3,2,1,0:T(8,128)(2,1)S(1)}, bf16[8,1,64,256]{3,2,1,0:T(8,128)(2,1)S(1)}, u32[]{:S(2)}, u32[]{:S(2)}) collective-permute-start(bf16[8,1,64,256]{3,2,1,0:T(8,128)(2,1)S(1)} %get-tuple-element.88), channel_id=1, source_target_pairs={{1,0},{2,1},{3,2},{5,4},{6,5},{7,6},{9,8},{10,9},{11,10},{13,12},{... | collective-permute-start | bytes 786440 | tf_op jit(solution)/shard_map/ppermute | solution.py:384
  22.7 1.6 %copy-start = (bf16[8,8,64,256]{3,2,1,0:T(8,128)(2,1)S(1)}, bf16[8,8,64,256]{3,2,1,0:T(8,128)(2,1)}, u32[]{:S(2)}) copy-start(bf16[8,8,64,256]{3,2,1,0:T(8,128)(2,1)} %x_ref.5) | copy-start | bytes 6291460
  24.3 1.3 copy-start.4
  25.6 5.6 %copy-start.2 = (bf16[8,8,64,256]{3,2,1,0:T(8,128)(2,1)S(1)}, bf16[8,8,64,256]{3,2,1,0:T(8,128)(2,1)}, u32[]{:S(2)}) copy-start(bf16[8,8,64,256]{3,2,1,0:T(8,128)(2,1)} %cot_ref.1) | copy-start | bytes 6291460
  31.2 13.0 %copy-start.1 = (bf16[8,8,64,256]{3,2,1,0:T(8,128)(2,1)S(1)}, bf16[8,8,64,256]{3,2,1,0:T(8,128)(2,1)}, u32[]{:S(2)}) copy-start(bf16[8,8,64,256]{3,2,1,0:T(8,128)(2,1)} %x_ref.5) | copy-start | bytes 6291460
  31.3 22.7 %collective-permute-start.7 = (bf16[4,512,256]{2,1,0:T(8,128)(2,1)S(1)}, bf16[4,512,256]{2,1,0:T(8,128)(2,1)S(1)}, u32[]{:S(2)}, u32[]{:S(2)}) collective-permute-start(bf16[4,512,256]{2,1,0:T(8,128)(2,1)S(1)} %slice.14), channel_id=1, source_target_pairs={{12,16},{16,12},{13,17},{17,13},{14,18},{18,14},{15,19},{19,15}} | collective-permute-start | bytes 3145736 | tf_op jit(solution)/shard_map/ppermute | solution.py:429
  32.2 3.8 %collective-permute-start.2 = (f32[8,2,256]{2,1,0:T(2,128)S(1)}, f32[8,2,256]{2,1,0:T(2,128)S(1)}, u32[]{:S(2)}, u32[]{:S(2)}) collective-permute-start(f32[8,2,256]{2,1,0:T(2,128)S(1)} %get-tuple-element.47), channel_id=1, source_target_pairs={{0,1},{1,0},{2,3},{3,2},{4,5},{5,4},{6,7},{7,6},{8,9},{9,8},{10,11... | collective-permute-start | bytes 49160 | tf_op jit(solution)/shard_map/ppermute | solution.py:393
  36.1 10.4 %copy-start.5 = (s32[2]{0:T(128)S(1)}, s32[2]{0:T(128)}, u32[]{:S(2)}) copy-start(s32[2]{0:T(128)} %clip_ref.5) | copy-start | bytes 28
  36.1 10.4 %copy-start.7 = (f32[256]{0:T(256)S(1)}, f32[256]{0:T(256)}, u32[]{:S(2)}) copy-start(f32[256]{0:T(256)} %param.12) | copy-start | bytes 3076
  36.1 10.4 %copy-start.8 = (f32[256]{0:T(256)S(1)}, f32[256]{0:T(256)}, u32[]{:S(2)}) copy-start(f32[256]{0:T(256)} %param.13) | copy-start | bytes 3076
  36.1 20.1 %collective-permute-start.8 = (bf16[4,512,256]{2,1,0:T(8,128)(2,1)S(1)}, bf16[4,512,256]{2,1,0:T(8,128)(2,1)S(1)}, u32[]{:S(2)}, u32[]{:S(2)}) collective-permute-start(bf16[4,512,256]{2,1,0:T(8,128)(2,1)S(1)} %slice.15), channel_id=1, source_target_pairs={{28,16},{0,12},{29,17},{1,13},{30,18},{2,14},{31,19},{3,15}} | collective-permute-start | bytes 3145736 | tf_op jit(solution)/shard_map/ppermute | solution.py:433
  41.6 4.8 %collective-permute-start.4 = (f32[8,2,256]{2,1,0:T(2,128)S(1)}, f32[8,2,256]{2,1,0:T(2,128)S(1)}, u32[]{:S(2)}, u32[]{:S(2)}) collective-permute-start(f32[8,2,256]{2,1,0:T(2,128)S(1)} %add.6.refs_0_), channel_id=1, source_target_pairs={{0,2},{1,3},{2,0},{3,1},{4,6},{5,7},{6,4},{7,5},{8,10},{9,11},{10,... | collective-permute-start | bytes 49160 | tf_op jit(solution)/shard_map/ppermute | solution.py:393
  46.5 8.8 %copy-start.3 = (bf16[3,256,256]{2,1,0:T(8,128)(2,1)S(1)}, bf16[3,256,256]{2,1,0:T(8,128)(2,1)}, u32[]{:S(2)}) copy-start(bf16[3,256,256]{2,1,0:T(8,128)(2,1)} %temporal_ref.1) | copy-start | bytes 1179652
  46.5 9.7 %copy-start.6 = (s32[2]{0:T(128)S(1)}, s32[2]{0:T(128)}, u32[]{:S(2)}) copy-start(s32[2]{0:T(128)} %dil_ref.3) | copy-start | bytes 28
  52.6 46.6 %collective-permute-start.14 = (bf16[8,512,256]{2,1,0:T(8,128)(2,1)S(1)}, bf16[8,512,256]{2,1,0:T(8,128)(2,1)S(1)}, u32[]{:S(2)}, u32[]{:S(2)}) collective-permute-start(bf16[8,512,256]{2,1,0:T(8,128)(2,1)S(1)} %get-tuple-element.61.act_ref.own), channel_id=1, source_target_pairs={{0,4},{4,8},{8,12},{12,16},{16,20},{20,24},{24,28},{1,5},{5,9},{9,... | collective-permute-start | bytes 6291464 | tf_op jit(solution)/shard_map/ppermute | solution.py:384
  54.0 45.2 %collective-permute-start.15 = (bf16[8,512,256]{2,1,0:T(8,128)(2,1)S(1)}, bf16[8,512,256]{2,1,0:T(8,128)(2,1)S(1)}, u32[]{:S(2)}, u32[]{:S(2)}) collective-permute-start(bf16[8,512,256]{2,1,0:T(8,128)(2,1)S(1)} %get-tuple-element.61.act_ref.own), channel_id=1, source_target_pairs={{4,0},{8,4},{12,8},{16,12},{20,16},{24,20},{28,24},{5,1},{9,5},{13... | collective-permute-start | bytes 6291464 | tf_op jit(solution)/shard_map/ppermute | solution.py:384
  60.4 3.8 %collective-permute-start.9 = (f32[8,2,256]{2,1,0:T(2,128)S(1)}, f32[8,2,256]{2,1,0:T(2,128)S(1)}, u32[]{:S(2)}, u32[]{:S(2)}) collective-permute-start(f32[8,2,256]{2,1,0:T(2,128)S(1)} %get-tuple-element.59), channel_id=1, source_target_pairs={{0,1},{1,0},{2,3},{3,2},{4,5},{5,4},{6,7},{7,6},{8,9},{9,8},{10,11... | collective-permute-start | bytes 49160 | tf_op jit(solution)/shard_map/ppermute | solution.py:393
  64.2 4.7 %collective-permute-start.10 = (f32[8,2,256]{2,1,0:T(2,128)S(1)}, f32[8,2,256]{2,1,0:T(2,128)S(1)}, u32[]{:S(2)}, u32[]{:S(2)}) collective-permute-start(f32[8,2,256]{2,1,0:T(2,128)S(1)} %add.7.refs_2_), channel_id=1, source_target_pairs={{0,2},{1,3},{2,0},{3,1},{4,6},{5,7},{6,4},{7,5},{8,10},{9,11},{10,... | collective-permute-start | bytes 49160 | tf_op jit(solution)/shard_map/ppermute | solution.py:393
  73.5 10.1 %collective-permute-start.11 = (bf16[8,1,64,256]{3,2,1,0:T(8,128)(2,1)S(1)}, bf16[8,1,64,256]{3,2,1,0:T(8,128)(2,1)S(1)}, u32[]{:S(2)}, u32[]{:S(2)}) collective-permute-start(bf16[8,1,64,256]{3,2,1,0:T(8,128)(2,1)S(1)} %get-tuple-element.63), channel_id=1, source_target_pairs={{0,1},{1,2},{2,3},{4,5},{5,6},{6,7},{8,9},{9,10},{10,11},{12,13},{... | collective-permute-start | bytes 786440 | tf_op jit(solution)/shard_map/ppermute | solution.py:384
  77.2 8.3 %collective-permute-start.12 = (bf16[8,1,64,256]{3,2,1,0:T(8,128)(2,1)S(1)}, bf16[8,1,64,256]{3,2,1,0:T(8,128)(2,1)S(1)}, u32[]{:S(2)}, u32[]{:S(2)}) collective-permute-start(bf16[8,1,64,256]{3,2,1,0:T(8,128)(2,1)S(1)} %get-tuple-element.64), channel_id=1, source_target_pairs={{1,0},{2,1},{3,2},{5,4},{6,5},{7,6},{9,8},{10,9},{11,10},{13,12},{... | collective-permute-start | bytes 786440 | tf_op jit(solution)/shard_map/ppermute | solution.py:384
  85.8 2.4 %collective-permute-start.13 = (bf16[4,4,32,768]{3,2,1,0:T(8,128)(2,1)S(1)}, bf16[4,4,32,768]{3,2,1,0:T(8,128)(2,1)S(1)}, u32[]{:S(2)}, u32[]{:S(2)}) collective-permute-start(bf16[4,4,32,768]{3,2,1,0:T(8,128)(2,1)S(1)} %get-tuple-element.67), channel_id=1, source_target_pairs={{0,4},{4,0},{8,12},{12,8},{16,20},{20,16},{24,28},{28,24},{1,5},{5... | collective-permute-start | bytes 2359304 | tf_op jit(solution)/shard_map/ppermute | solution.py:482
  88.3 18.2 %collective-permute-start.16 = (bf16[4,32,768]{2,1,0:T(8,128)(2,1)S(1)}, bf16[4,32,768]{2,1,0:T(8,128)(2,1)S(1)}, u32[]{:S(2)}, u32[]{:S(2)}) collective-permute-start(bf16[4,32,768]{2,1,0:T(8,128)(2,1)S(1)} %get-tuple-element.74), channel_id=1, source_target_pairs={{0,8},{4,12},{8,0},{12,4},{16,24},{20,28},{24,16},{28,20},{1,9},{5... | collective-permute-start | bytes 589832 | tf_op jit(solution)/shard_map/ppermute | solution.py:487
  89.9 16.7 %collective-permute-start.17 = (bf16[4,32,768]{2,1,0:T(8,128)(2,1)S(1)}, bf16[4,32,768]{2,1,0:T(8,128)(2,1)S(1)}, u32[]{:S(2)}, u32[]{:S(2)}) collective-permute-start(bf16[4,32,768]{2,1,0:T(8,128)(2,1)S(1)} %get-tuple-element.75), channel_id=1, source_target_pairs={{0,16},{4,20},{8,24},{12,28},{16,0},{20,4},{24,8},{28,12},{1,17},{... | collective-permute-start | bytes 589832 | tf_op jit(solution)/shard_map/ppermute | solution.py:487
  90.8 15.7 %collective-permute-start.18 = (bf16[4,32,768]{2,1,0:T(8,128)(2,1)S(1)}, bf16[4,32,768]{2,1,0:T(8,128)(2,1)S(1)}, u32[]{:S(2)}, u32[]{:S(2)}) collective-permute-start(bf16[4,32,768]{2,1,0:T(8,128)(2,1)S(1)} %get-tuple-element.76), channel_id=1, source_target_pairs={{0,24},{4,28},{8,16},{12,20},{16,8},{20,12},{24,0},{28,4},{1,25},{... | collective-permute-start | bytes 589832 | tf_op jit(solution)/shard_map/ppermute | solution.py:487
  106.6 4.5 %collective-permute-start.19 = (bf16[32,768]{1,0:T(8,128)(2,1)S(1)}, bf16[32,768]{1,0:T(8,128)(2,1)S(1)}, u32[]{:S(2)}, u32[]{:S(2)}) collective-permute-start(bf16[32,768]{1,0:T(8,128)(2,1)S(1)} %get-tuple-element.78), channel_id=1, source_target_pairs={{0,1},{1,0},{2,3},{3,2},{4,5},{5,4},{6,7},{7,6},{8,9},{9,8},{10,11... | collective-permute-start | bytes 147464 | tf_op jit(solution)/shard_map/ppermute | solution.py:499
  107.2 6.3 %collective-permute-start.20 = (bf16[32,768]{1,0:T(8,128)(2,1)S(1)}, bf16[32,768]{1,0:T(8,128)(2,1)S(1)}, u32[]{:S(2)}, u32[]{:S(2)}) collective-permute-start(bf16[32,768]{1,0:T(8,128)(2,1)S(1)} %get-tuple-element.79), channel_id=1, source_target_pairs={{0,2},{1,3},{2,0},{3,1},{4,6},{5,7},{6,4},{7,5},{8,10},{9,11},{10,... | collective-permute-start | bytes 147464 | tf_op jit(solution)/shard_map/ppermute | solution.py:499
  108.6 6.0 %collective-permute-start.21 = (bf16[32,768]{1,0:T(8,128)(2,1)S(1)}, bf16[32,768]{1,0:T(8,128)(2,1)S(1)}, u32[]{:S(2)}, u32[]{:S(2)}) collective-permute-start(bf16[32,768]{1,0:T(8,128)(2,1)S(1)} %get-tuple-element.80), channel_id=1, source_target_pairs={{0,3},{1,2},{2,1},{3,0},{4,7},{5,6},{6,5},{7,4},{8,11},{9,10},{10,... | collective-permute-start | bytes 147464 | tf_op jit(solution)/shard_map/ppermute | solution.py:499
  114.6 4.5 %collective-permute-start.22 = (bf16[32,768]{1,0:T(8,128)(2,1)S(1)}, bf16[32,768]{1,0:T(8,128)(2,1)S(1)}, u32[]{:S(2)}, u32[]{:S(2)}) collective-permute-start(bf16[32,768]{1,0:T(8,128)(2,1)S(1)} %line_sum.1.refs_0_), channel_id=1, source_target_pairs={{0,1},{1,0},{2,3},{3,2},{4,5},{5,4},{6,7},{7,6},{8,9},{9,8},{10,11... | collective-permute-start | bytes 147464 | tf_op jit(solution)/shard_map/ppermute | solution.py:503
  115.2 5.0 %collective-permute-start.23 = (bf16[32,768]{1,0:T(8,128)(2,1)S(1)}, bf16[32,768]{1,0:T(8,128)(2,1)S(1)}, u32[]{:S(2)}, u32[]{:S(2)}) collective-permute-start(bf16[32,768]{1,0:T(8,128)(2,1)S(1)} %line_sum.1.refs_0_), channel_id=1, source_target_pairs={{0,2},{1,3},{2,0},{3,1},{4,6},{5,7},{6,4},{7,5},{8,10},{9,11},{10,... | collective-permute-start | bytes 147464 | tf_op jit(solution)/shard_map/ppermute | solution.py:503
  117.6 5.9 %collective-permute-start.24 = (bf16[32,768]{1,0:T(8,128)(2,1)S(1)}, bf16[32,768]{1,0:T(8,128)(2,1)S(1)}, u32[]{:S(2)}, u32[]{:S(2)}) collective-permute-start(bf16[32,768]{1,0:T(8,128)(2,1)S(1)} %line_sum.1.refs_0_), channel_id=1, source_target_pairs={{0,3},{1,2},{2,1},{3,0},{4,7},{5,6},{6,5},{7,4},{8,11},{9,10},{10,... | collective-permute-start | bytes 147464 | tf_op jit(solution)/shard_map/ppermute | solution.py:503
  123.6 11.3 %collective-permute-start.25 = (bf16[4,32,768]{2,1,0:T(8,128)(2,1)S(1)}, bf16[4,32,768]{2,1,0:T(8,128)(2,1)S(1)}, u32[]{:S(2)}, u32[]{:S(2)}) collective-permute-start(bf16[4,32,768]{2,1,0:T(8,128)(2,1)S(1)} %line_place.1.refs_0_), channel_id=1, source_target_pairs={{0,8},{4,12},{8,0},{12,4},{16,24},{20,28},{24,16},{28,20},{1,9},{5... | collective-permute-start | bytes 589832 | tf_op jit(solution)/shard_map/ppermute | solution.py:507
  126.5 8.4 %collective-permute-start.26 = (bf16[4,32,768]{2,1,0:T(8,128)(2,1)S(1)}, bf16[4,32,768]{2,1,0:T(8,128)(2,1)S(1)}, u32[]{:S(2)}, u32[]{:S(2)}) collective-permute-start(bf16[4,32,768]{2,1,0:T(8,128)(2,1)S(1)} %line_place.1.refs_0_), channel_id=1, source_target_pairs={{0,16},{4,20},{8,24},{12,28},{16,0},{20,4},{24,8},{28,12},{1,17},{... | collective-permute-start | bytes 589832 | tf_op jit(solution)/shard_map/ppermute | solution.py:507
  128.5 8.1 %collective-permute-start.27 = (bf16[4,32,768]{2,1,0:T(8,128)(2,1)S(1)}, bf16[4,32,768]{2,1,0:T(8,128)(2,1)S(1)}, u32[]{:S(2)}, u32[]{:S(2)}) collective-permute-start(bf16[4,32,768]{2,1,0:T(8,128)(2,1)S(1)} %line_place.1.refs_0_), channel_id=1, source_target_pairs={{0,24},{4,28},{8,16},{12,20},{16,8},{20,12},{24,0},{28,4},{1,25},{... | collective-permute-start | bytes 589832 | tf_op jit(solution)/shard_map/ppermute | solution.py:507
  136.7 2.4 %collective-permute-start.28 = (bf16[4,4,32,768]{3,2,1,0:T(8,128)(2,1)S(1)}, bf16[4,4,32,768]{3,2,1,0:T(8,128)(2,1)S(1)}, u32[]{:S(2)}, u32[]{:S(2)}) collective-permute-start(bf16[4,4,32,768]{3,2,1,0:T(8,128)(2,1)S(1)} %plane_place.1.mine_ref), channel_id=1, source_target_pairs={{0,4},{4,0},{8,12},{12,8},{16,20},{20,16},{24,28},{28,24},{1,5},{5... | collective-permute-start | bytes 2359304 | tf_op jit(solution)/shard_map/ppermute | solution.py:519
where the time goes:
time: 141 us
  starting transfers between devices  54.1 us (38%)
  Pallas kernels  44.5 us (32%)
  waiting for transfers between devices  37.1 us (26%)
  local copies, waits for them, and re-layouts  4.12 us (3%)
    pallas_call x17, Pallas kernels, call(): pl.pallas_call(kernel, in_specs=[smem if x.dtype == jnp.int32 else vmem f...  44.5 us
    ppermute x8, starting transfers between devices, neighbours(): return (lax.ppermute(high, axis, up), lax.ppermute(low, axis, down))  18.3 us
    ppermute x8, waiting for transfers between devices, neighbours(): return (lax.ppermute(high, axis, up), lax.ppermute(low, axis, down))  10.9 us
    ppermute x4, starting transfers between devices, spread_sums(): got = lax.ppermute(part, axis, [(i, i ^ step) for i in range(size)])  8.84 us
    ppermute x3, waiting for transfers between devices, per_device(): lax.ppermute(x, 'tm', other_chip(s))  7.36 us
    ppermute x3, starting transfers between devices, per_device(): gots = [lax.ppermute(own, 'tm', other_chip(s)) for s in range(1, chips)]  6.36 us
    ppermute x1, starting transfers between devices, per_device(): lax.ppermute(relayed[frames // 2:], 'tm', [(7, 4), (0, 3)])  5.49 us
    ppermute x3, waiting for transfers between devices, per_device(): gots = [lax.ppermute(own, 'space', other_plane(s)) for s in range(1, n)]  4.5 us
  transfers between devices with their start and end apart: 29, of which 14 were waited for; matrix products, arithmetic and copies ran while one was open for 1% of the time, Pallas kernels for 30%

commit v1 on v0

--- a/solution.py
+++ b/solution.py
@@ -422,7 +422,7 @@
     conv_out, sums = call(
         conv_kernel, "conv_forward", [frames_in, above, below, spatial],
         [shape(per_px, F32), shape((frames, 2, channels), F32)],
-        18 * big * channels, 8 * big, [windows], 18,
+        100 * big * channels, 8 * big, [windows], 18,
     )
     if by_corner:
         sums, straight = lax.optimization_barrier((sums, cot))

time: 141 us -> 138 us (0.979)
  waiting for transfers between devices: 37.1 us -> 33 us
    ppermute x1, waiting for transfers between devices: 0.01 us -> 6.51 us  [per_device(): relayed = lax.ppermute(cot, 'tm', [(3, 7), (4, 0)])]
    ppermute x8, waiting for transfers between devices: 10.9 us -> 4.42 us  [neighbours(): return (lax.ppermute(high, axis, up), lax.ppermute(low, axis, down))]
    ppermute x3, waiting for transfers between devices: 7.36 us -> 2.56 us  [per_device(): lax.ppermute(x, 'tm', other_chip(s))]
    ppermute x4, starting transfers between devices: 8.84 us -> 13.3 us  [spread_sums(): got = lax.ppermute(part, axis, [(i, i ^ step) for i in range(size)])]
    ppermute x1, starting transfers between devices: 5.49 us -> 1.49 us  [per_device(): lax.ppermute(relayed[frames // 2:], 'tm', [(7, 4), (0, 3)])]
  transfers between devices with their start and end apart: 29 -> 29, of which waited for: 14 -> 14; matrix products, arithmetic and copies ran while one was open for 1% -> 0% of each run, Pallas kernels for 30% -> 31%
where the time goes in v1:
time: 138 us
  starting transfers between devices  55.1 us (40%)
  Pallas kernels  44.6 us (32%)
  waiting for transfers between devices  33 us (24%)
  local copies, waits for them, and re-layouts  4.12 us (3%)
    pallas_call x17, Pallas kernels, call(): pl.pallas_call(kernel, in_specs=[smem if x.dtype == jnp.int32 else vmem f...  44.6 us
    ppermute x8, starting transfers between devices, neighbours(): return (lax.ppermute(high, axis, up), lax.ppermute(low, axis, down))  18.6 us
    ppermute x4, starting transfers between devices, spread_sums(): got = lax.ppermute(part, axis, [(i, i ^ step) for i in range(size)])  13.3 us
    ppermute x3, starting transfers between devices, per_device(): gots = [lax.ppermute(own, 'tm', other_chip(s)) for s in range(1, chips)]  6.97 us
    ppermute x1, waiting for transfers between devices, per_device(): relayed = lax.ppermute(cot, 'tm', [(3, 7), (4, 0)])  6.51 us
    ppermute x3, starting transfers between devices, per_device(): lax.ppermute(x, 'space', other_plane(s))  4.45 us
    ppermute x3, starting transfers between devices, per_device(): gots = [lax.ppermute(own, 'space', other_plane(s)) for s in range(1, n)]  4.45 us
    ppermute x8, waiting for transfers between devices, neighbours(): return (lax.ppermute(high, axis, up), lax.ppermute(low, axis, down))  4.42 us
  transfers between devices with their start and end apart: 29, of which 14 were waited for; matrix products, arithmetic and copies ran while one was open for 0% of the time, Pallas kernels for 31%

profile of v1, /device:TPU:0, one launch (start us, length us, event | category | flops | bytes accessed | tf_op | source)
XLA Modules:
  0.0 137.8 jit_solution(7030666404091153055)
XLA Ops:
  0.6 1.1 fusion
  1.7 4.9 %collective-permute-start = (bf16[8,1,64,256]{3,2,1,0:T(8,128)(2,1)S(1)}, bf16[8,1,64,256]{3,2,1,0:T(8,128)(2,1)S(1)}, u32[]{:S(2)}, u32[]{:S(2)}) collective-permute-start(bf16[8,1,64,256]{3,2,1,0:T(8,128)(2,1)S(1)} %get-tuple-element.89), channel_id=1, source_target_pairs={{0,1},{1,2},{2,3},{4,5},{5,6},{6,7},{8,9},{9,10},{10,11},{12,13},{... | collective-permute-start | bytes 786440 | tf_op jit(solution)/shard_map/ppermute | solution.py:384
  6.7 1.3 collective-permute-start.1
  8.0 1.3 collective-permute-start.3
  9.3 1.3 collective-permute-start.5
  10.6 3.2 %collective-permute-start.6 = (bf16[8,512,256]{2,1,0:T(8,128)(2,1)}, bf16[8,512,256]{2,1,0:T(8,128)(2,1)S(1)}, u32[]{:S(2)}, u32[]{:S(2)}) collective-permute-start(bf16[8,512,256]{2,1,0:T(8,128)(2,1)} %bitcast.6), channel_id=1, source_target_pairs={{0,4},{4,8},{8,12},{16,20},{20,24},{24,28},{1,5},{5,9},{9,13},{17,... | collective-permute-start | bytes 6291464 | tf_op jit(solution)/shard_map/ppermute | solution.py:384
  13.8 2.6 %collective-permute-done.1.below_ref = bf16[8,1,64,256]{3,2,1,0:T(8,128)(2,1)S(1)} collective-permute-done((bf16[8,1,64,256]{3,2,1,0:T(8,128)(2,1)S(1)}, bf16[8,1,64,256]{3,2,1,0:T(8,128)(2,1)S(1)}, u32[]{:S(2)}, u32[]{:S(2)}) %collective-permute-start.1) | collective-permute-done | bytes 262176 | tf_op jit(solution)/shard_map/ppermute | solution.py:384
  16.3 1.6 %copy-done = bf16[8,8,64,256]{3,2,1,0:T(8,128)(2,1)S(1)} copy-done((bf16[8,8,64,256]{3,2,1,0:T(8,128)(2,1)S(1)}, bf16[8,8,64,256]{3,2,1,0:T(8,128)(2,1)}, u32[]{:S(2)}) %copy-start) | copy-done | bytes 2097176
  17.9 1.3 copy-done.4
  19.2 5.6 %conv_forward.1 = (f32[8,512,256]{2,1,0:T(8,128)S(1)}, f32[8,2,256]{2,1,0:T(2,128)S(1)}) custom-call(bf16[8,8,64,256]{3,2,1,0:T(8,128)(2,1)S(1)} %copy-done, bf16[8,1,64,256]{3,2,1,0:T(8,128)(2,1)S(1)} %collective-permute-done.above_ref, bf16[8,1,64,256]{3,2,1,0:T(8,128)(2,1)S(1)} %collective-permute-done.1.below_ref, bf16[3,3,256,256]{3,2,1,0:T(8,128)(2,1)S(1)} %copy-done.4), custom_call_target="tpu_custom_call" | custom-call | flops 26843545600 | bytes 8388608 | tf_op jit(solution)/shard_map/conv_forward/pallas_call | solution.py:20
  24.8 0.0 copy-start.1
  24.8 0.1 slice.14
  24.9 0.9 collective-permute-start.7
  25.8 1.6 %collective-permute-start.2 = (f32[8,2,256]{2,1,0:T(2,128)S(1)}, f32[8,2,256]{2,1,0:T(2,128)S(1)}, u32[]{:S(2)}, u32[]{:S(2)}) collective-permute-start(f32[8,2,256]{2,1,0:T(2,128)S(1)} %get-tuple-element.47), channel_id=1, source_target_pairs={{0,1},{1,0},{2,3},{3,2},{4,5},{5,4},{6,7},{7,6},{8,9},{9,8},{10,11... | collective-permute-start | bytes 49160 | tf_op jit(solution)/shard_map/ppermute | solution.py:393
  27.4 2.2 %collective-permute-done.2 = f32[8,2,256]{2,1,0:T(2,128)S(1)} collective-permute-done((f32[8,2,256]{2,1,0:T(2,128)S(1)}, f32[8,2,256]{2,1,0:T(2,128)S(1)}, u32[]{:S(2)}, u32[]{:S(2)}) %collective-permute-start.2) | collective-permute-done | bytes 16416 | tf_op jit(solution)/shard_map/ppermute | solution.py:393
  29.6 6.5 %collective-permute-done.3 = bf16[8,512,256]{2,1,0:T(8,128)(2,1)S(1)} collective-permute-done((bf16[8,512,256]{2,1,0:T(8,128)(2,1)}, bf16[8,512,256]{2,1,0:T(8,128)(2,1)S(1)}, u32[]{:S(2)}, u32[]{:S(2)}) %collective-permute-start.3) | collective-permute-done | bytes 2097184 | tf_op jit(solution)/shard_map/ppermute | solution.py:416
  36.1 0.1 slice.15
  36.2 1.5 %collective-permute-start.8 = (bf16[4,512,256]{2,1,0:T(8,128)(2,1)S(1)}, bf16[4,512,256]{2,1,0:T(8,128)(2,1)S(1)}, u32[]{:S(2)}, u32[]{:S(2)}) collective-permute-start(bf16[4,512,256]{2,1,0:T(8,128)(2,1)S(1)} %slice.15), channel_id=1, source_target_pairs={{28,16},{0,12},{29,17},{1,13},{30,18},{2,14},{31,19},{3,15}} | collective-permute-start | bytes 3145736 | tf_op jit(solution)/shard_map/ppermute | solution.py:433
  37.7 3.7 %collective-permute-start.4 = (f32[8,2,256]{2,1,0:T(2,128)S(1)}, f32[8,2,256]{2,1,0:T(2,128)S(1)}, u32[]{:S(2)}, u32[]{:S(2)}) collective-permute-start(f32[8,2,256]{2,1,0:T(2,128)S(1)} %add.6.refs_0_), channel_id=1, source_target_pairs={{0,2},{1,3},{2,0},{3,1},{4,6},{5,7},{6,4},{7,5},{8,10},{9,11},{10,... | collective-permute-start | bytes 49160 | tf_op jit(solution)/shard_map/ppermute | solution.py:393
  41.4 2.2 %turned.1.xt_ref = bf16[768,4096]{1,0:T(8,128)(2,1)S(1)} custom-call(bf16[8,8,64,256]{3,2,1,0:T(8,128)(2,1)S(1)} %copy-done.1, bf16[8,1,64,256]{3,2,1,0:T(8,128)(2,1)S(1)} %collective-permute-done.above_ref, bf16[8,1,64,256]{3,2,1,0:T(8,128)(2,1)S(1)} %collective-permute-done.1.below_ref), custom_call_target="tpu_custom_call" | custom-call | bytes 8388608 | tf_op jit(solution)/shard_map/turned/pallas_call | solution.py:20
  43.7 6.0 %activation.1 = (bf16[8,512,256]{2,1,0:T(8,128)(2,1)S(1)}, bf16[8,512,256]{2,1,0:T(8,128)(2,1)S(1)}, bf16[8,512,256]{2,1,0:T(8,128)(2,1)S(1)}) custom-call(s32[2]{0:T(128)S(1)} %copy-done.5, f32[8,2,256]{2,1,0:T(2,128)S(1)} %add.6.refs_0_, f32[8,2,256]{2,1,0:T(2,128)S(1)} %collective-permute-done.4.refs_1_, f32[8,512,256]{2,1,0:T(8,128)S(1)} %get-tuple-element.52.refs_2_, ...), custom_call_target="tpu_custom_call" | custom-call | flops 10485760 | bytes 10485760 | tf_op jit(solution)/shard_map/activation/pallas_call | solution.py:20
  49.7 1.4 %collective-permute-start.14 = (bf16[8,512,256]{2,1,0:T(8,128)(2,1)S(1)}, bf16[8,512,256]{2,1,0:T(8,128)(2,1)S(1)}, u32[]{:S(2)}, u32[]{:S(2)}) collective-permute-start(bf16[8,512,256]{2,1,0:T(8,128)(2,1)S(1)} %get-tuple-element.61.act_ref.own), channel_id=1, source_target_pairs={{0,4},{4,8},{8,12},{12,16},{16,20},{20,24},{24,28},{1,5},{5,9},{9,... | collective-permute-start | bytes 6291464 | tf_op jit(solution)/shard_map/ppermute | solution.py:384
  51.1 1.3 collective-permute-start.15
  52.5 0.5 turn_weights.1
  52.9 1.5 %collective-permute-done.8.refs_1_ = bf16[4,512,256]{2,1,0:T(8,128)(2,1)S(1)} collective-permute-done((bf16[4,512,256]{2,1,0:T(8,128)(2,1)S(1)}, bf16[4,512,256]{2,1,0:T(8,128)(2,1)S(1)}, u32[]{:S(2)}, u32[]{:S(2)}) %collective-permute-start.8) | collective-permute-done | bytes 1048608 | tf_op jit(solution)/shard_map/ppermute | solution.py:433
  54.4 4.1 %grad_activation.1 = (bf16[8,512,256]{2,1,0:T(8,128)(2,1)S(1)}, bf16[4096,768]{1,0:T(8,128)(2,1)S(1)}, f32[8,2,256]{2,1,0:T(2,128)S(1)}) custom-call(s32[2]{0:T(128)S(1)} %copy-done.5, s32[2]{0:T(128)S(1)} %copy-done.6, bf16[8,512,256]{2,1,0:T(8,128)(2,1)S(1)} %bitcast.8, bf16[8,512,256]{2,1,0:T(8,128)(2,1)S(1)} %collective-permute-done.5.nxt, ...), custom_call_target="tpu_custom_call" | custom-call | flops 1610612736 | bytes 16777216 | tf_op jit(solution)/shard_map/grad_activation/pallas_call | solution.py:20
  58.5 3.9 %collective-permute-start.9 = (f32[8,2,256]{2,1,0:T(2,128)S(1)}, f32[8,2,256]{2,1,0:T(2,128)S(1)}, u32[]{:S(2)}, u32[]{:S(2)}) collective-permute-start(f32[8,2,256]{2,1,0:T(2,128)S(1)} %get-tuple-element.59), channel_id=1, source_target_pairs={{0,1},{1,0},{2,3},{3,2},{4,5},{5,4},{6,7},{7,6},{8,9},{9,8},{10,11... | collective-permute-start | bytes 49160 | tf_op jit(solution)/shard_map/ppermute | solution.py:393
  62.5 1.7 %collective-permute-done.9 = f32[8,2,256]{2,1,0:T(2,128)S(1)} collective-permute-done((f32[8,2,256]{2,1,0:T(2,128)S(1)}, f32[8,2,256]{2,1,0:T(2,128)S(1)}, u32[]{:S(2)}, u32[]{:S(2)}) %collective-permute-start.9) | collective-permute-done | bytes 16416 | tf_op jit(solution)/shard_map/ppermute | solution.py:393
  64.2 4.0 %collective-permute-start.10 = (f32[8,2,256]{2,1,0:T(2,128)S(1)}, f32[8,2,256]{2,1,0:T(2,128)S(1)}, u32[]{:S(2)}, u32[]{:S(2)}) collective-permute-start(f32[8,2,256]{2,1,0:T(2,128)S(1)} %add.7.refs_2_), channel_id=1, source_target_pairs={{0,2},{1,3},{2,0},{3,1},{4,6},{5,7},{6,4},{7,5},{8,10},{9,11},{10,... | collective-permute-start | bytes 49160 | tf_op jit(solution)/shard_map/ppermute | solution.py:393
  68.2 1.9 %temporal_grad.1.temporal_ref = f32[256,768]{1,0:T(8,128)S(1)} custom-call(bf16[8,512,256]{2,1,0:T(8,128)(2,1)S(1)} %get-tuple-element.61.act_ref.own, bf16[4096,768]{1,0:T(8,128)(2,1)S(1)} %get-tuple-element.62.cat_ref), custom_call_target="tpu_custom_call" | custom-call | flops 1610612736 | bytes 8388608 | tf_op jit(solution)/shard_map/temporal_grad/pallas_call | solution.py:20
  70.1 4.6 %norm_backward.1 = (bf16[8,512,256]{2,1,0:T(8,128)(2,1)S(1)}, bf16[8,1,64,256]{3,2,1,0:T(8,128)(2,1)S(1)}, bf16[8,1,64,256]{3,2,1,0:T(8,128)(2,1)S(1)}, bf16[4096,768]{1,0:T(8,128)(2,1)S(1)}) custom-call(bf16[8,512,256]{2,1,0:T(8,128)(2,1)S(1)} %get-tuple-element.53.refs_3_.normed_ref, bf16[8,512,256]{2,1,0:T(8,128)(2,1)S(1)} %get-tuple-element.54.refs_4_.slope_ref, ...), custom_call_target="tpu_custom_call" | custom-call | bytes 12582912 | tf_op jit(solution)/shard_map/norm_backward/pallas_call | solution.py:20
  74.7 3.9 %collective-permute-start.11 = (bf16[8,1,64,256]{3,2,1,0:T(8,128)(2,1)S(1)}, bf16[8,1,64,256]{3,2,1,0:T(8,128)(2,1)S(1)}, u32[]{:S(2)}, u32[]{:S(2)}) collective-permute-start(bf16[8,1,64,256]{3,2,1,0:T(8,128)(2,1)S(1)} %get-tuple-element.63), channel_id=1, source_target_pairs={{0,1},{1,2},{2,3},{4,5},{5,6},{6,7},{8,9},{9,10},{10,11},{12,13},{... | collective-permute-start | bytes 786440 | tf_op jit(solution)/shard_map/ppermute | solution.py:384
  78.7 1.3 collective-permute-start.12
  80.0 5.1 %weight_grad.1.acc_ref = f32[1024,768]{1,0:T(8,128)S(1)} custom-call(bf16[768,4096]{1,0:T(8,128)(2,1)S(1)} %turned.1.xt_ref, bf16[4096,768]{1,0:T(8,128)(2,1)S(1)} %get-tuple-element.60.moved_ref, f32[256,768]{1,0:T(8,128)S(1)} %temporal_grad.1.temporal_ref), custom_call_target="tpu_custom_call" | custom-call | flops 4831838208 | bytes 12582912 | tf_op jit(solution)/shard_map/weight_grad/pallas_call | solution.py:20
  85.1 1.8 %collective-permute-done.12.below_ref = bf16[8,1,64,256]{3,2,1,0:T(8,128)(2,1)S(1)} collective-permute-done((bf16[8,1,64,256]{3,2,1,0:T(8,128)(2,1)S(1)}, bf16[8,1,64,256]{3,2,1,0:T(8,128)(2,1)S(1)}, u32[]{:S(2)}, u32[]{:S(2)}) %collective-permute-start.12) | collective-permute-done | bytes 262176 | tf_op jit(solution)/shard_map/ppermute | solution.py:384
  86.9 0.4 hand_out.1
  87.3 0.1 collective-permute-start.13
  87.4 2.3 %collective-permute-done.13.got_ref = bf16[4,4,32,768]{3,2,1,0:T(8,128)(2,1)S(1)} collective-permute-done((bf16[4,4,32,768]{3,2,1,0:T(8,128)(2,1)S(1)}, bf16[4,4,32,768]{3,2,1,0:T(8,128)(2,1)S(1)}, u32[]{:S(2)}, u32[]{:S(2)}) %collective-permute-start.13) | collective-permute-done | bytes 786464 | tf_op jit(solution)/shard_map/ppermute | solution.py:482
  89.6 0.2 core_sum.1
  89.8 0.1 collective-permute-start.16
  89.9 0.1 collective-permute-start.17
  90.0 3.4 %collective-permute-start.18 = (bf16[4,32,768]{2,1,0:T(8,128)(2,1)S(1)}, bf16[4,32,768]{2,1,0:T(8,128)(2,1)S(1)}, u32[]{:S(2)}, u32[]{:S(2)}) collective-permute-start(bf16[4,32,768]{2,1,0:T(8,128)(2,1)S(1)} %get-tuple-element.76), channel_id=1, source_target_pairs={{0,24},{4,28},{8,16},{12,20},{16,8},{20,12},{24,0},{28,4},{1,25},{... | collective-permute-start | bytes 589832 | tf_op jit(solution)/shard_map/ppermute | solution.py:487
  93.4 7.0 %conv_backward.1 = bf16[8,8,64,256]{3,2,1,0:T(8,128)(2,1)} custom-call(bf16[8,512,256]{2,1,0:T(8,128)(2,1)S(1)} %get-tuple-element.69.g_ref, bf16[8,1,64,256]{3,2,1,0:T(8,128)(2,1)S(1)} %collective-permute-done.11.above_ref, bf16[8,1,64,256]{3,2,1,0:T(8,128)(2,1)S(1)} %collective-permute-done.12.below_ref, bf16[8,8,64,256]{3,2,1,0:T(8,128)(2,1)S(1)} %copy-done.2, ...), custom_call_target="tpu_custom_call" | custom-call | flops 4831838208 | bytes 8388608 | tf_op jit(solution)/shard_map/conv_backward/pallas_call | solution.py:20
  100.4 2.6 %collective-permute-done.16.refs_0_ = bf16[4,32,768]{2,1,0:T(8,128)(2,1)S(1)} collective-permute-done((bf16[4,32,768]{2,1,0:T(8,128)(2,1)S(1)}, bf16[4,32,768]{2,1,0:T(8,128)(2,1)S(1)}, u32[]{:S(2)}, u32[]{:S(2)}) %collective-permute-start.16) | collective-permute-done | bytes 196640 | tf_op jit(solution)/shard_map/ppermute | solution.py:487
  102.9 0.1 plane_sum.1
  103.0 1.7 %collective-permute-start.19 = (bf16[32,768]{1,0:T(8,128)(2,1)S(1)}, bf16[32,768]{1,0:T(8,128)(2,1)S(1)}, u32[]{:S(2)}, u32[]{:S(2)}) collective-permute-start(bf16[32,768]{1,0:T(8,128)(2,1)S(1)} %get-tuple-element.78), channel_id=1, source_target_pairs={{0,1},{1,0},{2,3},{3,2},{4,5},{5,4},{6,7},{7,6},{8,9},{9,8},{10,11... | collective-permute-start | bytes 147464 | tf_op jit(solution)/shard_map/ppermute | solution.py:499
  104.7 1.0 collective-permute-start.20
  105.6 1.8 %collective-permute-start.21 = (bf16[32,768]{1,0:T(8,128)(2,1)S(1)}, bf16[32,768]{1,0:T(8,128)(2,1)S(1)}, u32[]{:S(2)}, u32[]{:S(2)}) collective-permute-start(bf16[32,768]{1,0:T(8,128)(2,1)S(1)} %get-tuple-element.80), channel_id=1, source_target_pairs={{0,3},{1,2},{2,1},{3,0},{4,7},{5,6},{6,5},{7,4},{8,11},{9,10},{10,... | collective-permute-start | bytes 147464 | tf_op jit(solution)/shard_map/ppermute | solution.py:499
  107.5 2.8 %collective-permute-done.20.refs_1_ = bf16[32,768]{1,0:T(8,128)(2,1)S(1)} collective-permute-done((bf16[32,768]{1,0:T(8,128)(2,1)S(1)}, bf16[32,768]{1,0:T(8,128)(2,1)S(1)}, u32[]{:S(2)}, u32[]{:S(2)}) %collective-permute-start.20) | collective-permute-done | bytes 49184 | tf_op jit(solution)/shard_map/ppermute | solution.py:499
  110.3 1.5 %collective-permute-done.21.refs_2_ = bf16[32,768]{1,0:T(8,128)(2,1)S(1)} collective-permute-done((bf16[32,768]{1,0:T(8,128)(2,1)S(1)}, bf16[32,768]{1,0:T(8,128)(2,1)S(1)}, u32[]{:S(2)}, u32[]{:S(2)}) %collective-permute-start.21) | collective-permute-done | bytes 49184 | tf_op jit(solution)/shard_map/ppermute | solution.py:499
  111.8 0.7 collective-permute-start.22
  112.5 1.6 %collective-permute-start.23 = (bf16[32,768]{1,0:T(8,128)(2,1)S(1)}, bf16[32,768]{1,0:T(8,128)(2,1)S(1)}, u32[]{:S(2)}, u32[]{:S(2)}) collective-permute-start(bf16[32,768]{1,0:T(8,128)(2,1)S(1)} %line_sum.1.refs_0_), channel_id=1, source_target_pairs={{0,2},{1,3},{2,0},{3,1},{4,6},{5,7},{6,4},{7,5},{8,10},{9,11},{10,... | collective-permute-start | bytes 147464 | tf_op jit(solution)/shard_map/ppermute | solution.py:503
  114.1 2.2 %collective-permute-start.24 = (bf16[32,768]{1,0:T(8,128)(2,1)S(1)}, bf16[32,768]{1,0:T(8,128)(2,1)S(1)}, u32[]{:S(2)}, u32[]{:S(2)}) collective-permute-start(bf16[32,768]{1,0:T(8,128)(2,1)S(1)} %line_sum.1.refs_0_), channel_id=1, source_target_pairs={{0,3},{1,2},{2,1},{3,0},{4,7},{5,6},{6,5},{7,4},{8,11},{9,10},{10,... | collective-permute-start | bytes 147464 | tf_op jit(solution)/shard_map/ppermute | solution.py:503
  116.2 2.8 %collective-permute-done.23.refs_2_ = bf16[32,768]{1,0:T(8,128)(2,1)S(1)} collective-permute-done((bf16[32,768]{1,0:T(8,128)(2,1)S(1)}, bf16[32,768]{1,0:T(8,128)(2,1)S(1)}, u32[]{:S(2)}, u32[]{:S(2)}) %collective-permute-start.23) | collective-permute-done | bytes 49184 | tf_op jit(solution)/shard_map/ppermute | solution.py:503
  119.1 1.0 collective-permute-done.24.refs_3_
  120.1 5.1 %collective-permute-start.25 = (bf16[4,32,768]{2,1,0:T(8,128)(2,1)S(1)}, bf16[4,32,768]{2,1,0:T(8,128)(2,1)S(1)}, u32[]{:S(2)}, u32[]{:S(2)}) collective-permute-start(bf16[4,32,768]{2,1,0:T(8,128)(2,1)S(1)} %line_place.1.refs_0_), channel_id=1, source_target_pairs={{0,8},{4,12},{8,0},{12,4},{16,24},{20,28},{24,16},{28,20},{1,9},{5... | collective-permute-start | bytes 589832 | tf_op jit(solution)/shard_map/ppermute | solution.py:507
  125.2 0.5 collective-permute-start.26
  125.7 1.4 %collective-permute-start.27 = (bf16[4,32,768]{2,1,0:T(8,128)(2,1)S(1)}, bf16[4,32,768]{2,1,0:T(8,128)(2,1)S(1)}, u32[]{:S(2)}, u32[]{:S(2)}) collective-permute-start(bf16[4,32,768]{2,1,0:T(8,128)(2,1)S(1)} %line_place.1.refs_0_), channel_id=1, source_target_pairs={{0,24},{4,28},{8,16},{12,20},{16,8},{20,12},{24,0},{28,4},{1,25},{... | collective-permute-start | bytes 589832 | tf_op jit(solution)/shard_map/ppermute | solution.py:507
  127.1 5.0 %temporal_forward.1 = bf16[8,8,64,256]{3,2,1,0:T(8,128)(2,1)} custom-call(s32[2]{0:T(128)S(1)} %copy-done.5, s32[2]{0:T(128)S(1)} %copy-done.6, bf16[8,512,256]{2,1,0:T(8,128)(2,1)S(1)} %get-tuple-element.61.act_ref.own, bf16[8,512,256]{2,1,0:T(8,128)(2,1)S(1)} %collective-permute-done.15.nxt, bf16[8,512,256]{2,1,0:T(8,128)(2,1)S(1)} %collective-permute-done.14.prv, ...), custom_call_target="tpu_custom_call" | custom-call | flops 1610612736 | bytes 10485760 | tf_op jit(solution)/shard_map/temporal_forward/pallas_call | solution.py:20
  132.1 1.4 %collective-permute-done.27.refs_3_ = bf16[4,32,768]{2,1,0:T(8,128)(2,1)S(1)} collective-permute-done((bf16[4,32,768]{2,1,0:T(8,128)(2,1)S(1)}, bf16[4,32,768]{2,1,0:T(8,128)(2,1)S(1)}, u32[]{:S(2)}, u32[]{:S(2)}) %collective-permute-start.27) | collective-permute-done | bytes 196640 | tf_op jit(solution)/shard_map/ppermute | solution.py:507
  133.5 0.1 plane_place.1.mine_ref
  133.6 0.1 collective-permute-start.28
  133.7 2.3 %collective-permute-done.28.got_ref = bf16[4,4,32,768]{3,2,1,0:T(8,128)(2,1)S(1)} collective-permute-done((bf16[4,4,32,768]{3,2,1,0:T(8,128)(2,1)S(1)}, bf16[4,4,32,768]{3,2,1,0:T(8,128)(2,1)S(1)}, u32[]{:S(2)}, u32[]{:S(2)}) %collective-permute-start.28) | collective-permute-done | bytes 786464 | tf_op jit(solution)/shard_map/ppermute | solution.py:519
  135.9 1.9 %finish.1 = (f32[3,3,256,256]{3,2,1,0:T(8,128)}, f32[3,256,256]{2,1,0:T(8,128)}) custom-call(bf16[4,4,32,768]{3,2,1,0:T(8,128)(2,1)S(1)} %plane_place.1.mine_ref, bf16[4,4,32,768]{3,2,1,0:T(8,128)(2,1)S(1)} %collective-permute-done.28.got_ref), custom_call_target="tpu_custom_call" | custom-call | bytes 4194304 | tf_op jit(solution)/shard_map/finish/pallas_call | solution.py:20
  (34 shorter events, 0.1 us)
Async XLA Ops:
  1.7 12.0 %collective-permute-start = (bf16[8,1,64,256]{3,2,1,0:T(8,128)(2,1)S(1)}, bf16[8,1,64,256]{3,2,1,0:T(8,128)(2,1)S(1)}, u32[]{:S(2)}, u32[]{:S(2)}) collective-permute-start(bf16[8,1,64,256]{3,2,1,0:T(8,128)(2,1)S(1)} %get-tuple-element.89), channel_id=1, source_target_pairs={{0,1},{1,2},{2,3},{4,5},{5,6},{6,7},{8,9},{9,10},{10,11},{12,13},{... | collective-permute-start | bytes 786440 | tf_op jit(solution)/shard_map/ppermute | solution.py:384
  6.7 9.7 %collective-permute-start.1 = (bf16[8,1,64,256]{3,2,1,0:T(8,128)(2,1)S(1)}, bf16[8,1,64,256]{3,2,1,0:T(8,128)(2,1)S(1)}, u32[]{:S(2)}, u32[]{:S(2)}) collective-permute-start(bf16[8,1,64,256]{3,2,1,0:T(8,128)(2,1)S(1)} %get-tuple-element.88), channel_id=1, source_target_pairs={{1,0},{2,1},{3,2},{5,4},{6,5},{7,6},{9,8},{10,9},{11,10},{13,12},{... | collective-permute-start | bytes 786440 | tf_op jit(solution)/shard_map/ppermute | solution.py:384
  8.0 28.1 %collective-permute-start.3 = (bf16[8,512,256]{2,1,0:T(8,128)(2,1)}, bf16[8,512,256]{2,1,0:T(8,128)(2,1)S(1)}, u32[]{:S(2)}, u32[]{:S(2)}) collective-permute-start(bf16[8,512,256]{2,1,0:T(8,128)(2,1)} %bitcast.4), channel_id=1, source_target_pairs={{12,28},{16,0},{13,29},{17,1},{14,30},{18,2},{15,31},{19,3}} | collective-permute-start | bytes 6291464 | tf_op jit(solution)/shard_map/ppermute | solution.py:416
  9.3 43.7 %collective-permute-start.5 = (bf16[8,512,256]{2,1,0:T(8,128)(2,1)}, bf16[8,512,256]{2,1,0:T(8,128)(2,1)S(1)}, u32[]{:S(2)}, u32[]{:S(2)}) collective-permute-start(bf16[8,512,256]{2,1,0:T(8,128)(2,1)} %bitcast.5), channel_id=1, source_target_pairs={{4,0},{8,4},{12,8},{20,16},{24,20},{28,24},{5,1},{9,5},{13,9},{21,... | collective-permute-start | bytes 6291464 | tf_op jit(solution)/shard_map/ppermute | solution.py:384
  10.6 42.4 %collective-permute-start.6 = (bf16[8,512,256]{2,1,0:T(8,128)(2,1)}, bf16[8,512,256]{2,1,0:T(8,128)(2,1)S(1)}, u32[]{:S(2)}, u32[]{:S(2)}) collective-permute-start(bf16[8,512,256]{2,1,0:T(8,128)(2,1)} %bitcast.6), channel_id=1, source_target_pairs={{0,4},{4,8},{8,12},{16,20},{20,24},{24,28},{1,5},{5,9},{9,13},{17,... | collective-permute-start | bytes 6291464 | tf_op jit(solution)/shard_map/ppermute | solution.py:384
  16.3 1.6 %copy-start = (bf16[8,8,64,256]{3,2,1,0:T(8,128)(2,1)S(1)}, bf16[8,8,64,256]{3,2,1,0:T(8,128)(2,1)}, u32[]{:S(2)}) copy-start(bf16[8,8,64,256]{3,2,1,0:T(8,128)(2,1)} %x_ref.5) | copy-start | bytes 6291460
  17.9 1.3 copy-start.4
  19.2 5.6 %copy-start.2 = (bf16[8,8,64,256]{3,2,1,0:T(8,128)(2,1)S(1)}, bf16[8,8,64,256]{3,2,1,0:T(8,128)(2,1)}, u32[]{:S(2)}) copy-start(bf16[8,8,64,256]{3,2,1,0:T(8,128)(2,1)} %cot_ref.1) | copy-start | bytes 6291460
  24.8 16.6 %copy-start.1 = (bf16[8,8,64,256]{3,2,1,0:T(8,128)(2,1)S(1)}, bf16[8,8,64,256]{3,2,1,0:T(8,128)(2,1)}, u32[]{:S(2)}) copy-start(bf16[8,8,64,256]{3,2,1,0:T(8,128)(2,1)} %x_ref.5) | copy-start | bytes 6291460
  24.9 26.2 %collective-permute-start.7 = (bf16[4,512,256]{2,1,0:T(8,128)(2,1)S(1)}, bf16[4,512,256]{2,1,0:T(8,128)(2,1)S(1)}, u32[]{:S(2)}, u32[]{:S(2)}) collective-permute-start(bf16[4,512,256]{2,1,0:T(8,128)(2,1)S(1)} %slice.14), channel_id=1, source_target_pairs={{12,16},{16,12},{13,17},{17,13},{14,18},{18,14},{15,19},{19,15}} | collective-permute-start | bytes 3145736 | tf_op jit(solution)/shard_map/ppermute | solution.py:429
  25.8 3.8 %collective-permute-start.2 = (f32[8,2,256]{2,1,0:T(2,128)S(1)}, f32[8,2,256]{2,1,0:T(2,128)S(1)}, u32[]{:S(2)}, u32[]{:S(2)}) collective-permute-start(f32[8,2,256]{2,1,0:T(2,128)S(1)} %get-tuple-element.47), channel_id=1, source_target_pairs={{0,1},{1,0},{2,3},{3,2},{4,5},{5,4},{6,7},{7,6},{8,9},{9,8},{10,11... | collective-permute-start | bytes 49160 | tf_op jit(solution)/shard_map/ppermute | solution.py:393
  36.2 7.4 %copy-start.5 = (s32[2]{0:T(128)S(1)}, s32[2]{0:T(128)}, u32[]{:S(2)}) copy-start(s32[2]{0:T(128)} %clip_ref.5) | copy-start | bytes 28
  36.2 7.4 %copy-start.7 = (f32[256]{0:T(256)S(1)}, f32[256]{0:T(256)}, u32[]{:S(2)}) copy-start(f32[256]{0:T(256)} %param.12) | copy-start | bytes 3076
  36.2 7.4 %copy-start.8 = (f32[256]{0:T(256)S(1)}, f32[256]{0:T(256)}, u32[]{:S(2)}) copy-start(f32[256]{0:T(256)} %param.13) | copy-start | bytes 3076
  36.2 18.2 %collective-permute-start.8 = (bf16[4,512,256]{2,1,0:T(8,128)(2,1)S(1)}, bf16[4,512,256]{2,1,0:T(8,128)(2,1)S(1)}, u32[]{:S(2)}, u32[]{:S(2)}) collective-permute-start(bf16[4,512,256]{2,1,0:T(8,128)(2,1)S(1)} %slice.15), channel_id=1, source_target_pairs={{28,16},{0,12},{29,17},{1,13},{30,18},{2,14},{31,19},{3,15}} | collective-permute-start | bytes 3145736 | tf_op jit(solution)/shard_map/ppermute | solution.py:433
  37.7 5.9 %collective-permute-start.4 = (f32[8,2,256]{2,1,0:T(2,128)S(1)}, f32[8,2,256]{2,1,0:T(2,128)S(1)}, u32[]{:S(2)}, u32[]{:S(2)}) collective-permute-start(f32[8,2,256]{2,1,0:T(2,128)S(1)} %add.6.refs_0_), channel_id=1, source_target_pairs={{0,2},{1,3},{2,0},{3,1},{4,6},{5,7},{6,4},{7,5},{8,10},{9,11},{10,... | collective-permute-start | bytes 49160 | tf_op jit(solution)/shard_map/ppermute | solution.py:393
  43.6 8.8 %copy-start.3 = (bf16[3,256,256]{2,1,0:T(8,128)(2,1)S(1)}, bf16[3,256,256]{2,1,0:T(8,128)(2,1)}, u32[]{:S(2)}) copy-start(bf16[3,256,256]{2,1,0:T(8,128)(2,1)} %temporal_ref.1) | copy-start | bytes 1179652
  43.6 10.8 %copy-start.6 = (s32[2]{0:T(128)S(1)}, s32[2]{0:T(128)}, u32[]{:S(2)}) copy-start(s32[2]{0:T(128)} %dil_ref.3) | copy-start | bytes 28
  49.7 50.7 %collective-permute-start.14 = (bf16[8,512,256]{2,1,0:T(8,128)(2,1)S(1)}, bf16[8,512,256]{2,1,0:T(8,128)(2,1)S(1)}, u32[]{:S(2)}, u32[]{:S(2)}) collective-permute-start(bf16[8,512,256]{2,1,0:T(8,128)(2,1)S(1)} %get-tuple-element.61.act_ref.own), channel_id=1, source_target_pairs={{0,4},{4,8},{8,12},{12,16},{16,20},{20,24},{24,28},{1,5},{5,9},{9,... | collective-permute-start | bytes 6291464 | tf_op jit(solution)/shard_map/ppermute | solution.py:384
  51.1 49.2 %collective-permute-start.15 = (bf16[8,512,256]{2,1,0:T(8,128)(2,1)S(1)}, bf16[8,512,256]{2,1,0:T(8,128)(2,1)S(1)}, u32[]{:S(2)}, u32[]{:S(2)}) collective-permute-start(bf16[8,512,256]{2,1,0:T(8,128)(2,1)S(1)} %get-tuple-element.61.act_ref.own), channel_id=1, source_target_pairs={{4,0},{8,4},{12,8},{16,12},{20,16},{24,20},{28,24},{5,1},{9,5},{13... | collective-permute-start | bytes 6291464 | tf_op jit(solution)/shard_map/ppermute | solution.py:384
  58.5 5.7 %collective-permute-start.9 = (f32[8,2,256]{2,1,0:T(2,128)S(1)}, f32[8,2,256]{2,1,0:T(2,128)S(1)}, u32[]{:S(2)}, u32[]{:S(2)}) collective-permute-start(f32[8,2,256]{2,1,0:T(2,128)S(1)} %get-tuple-element.59), channel_id=1, source_target_pairs={{0,1},{1,0},{2,3},{3,2},{4,5},{5,4},{6,7},{7,6},{8,9},{9,8},{10,11... | collective-permute-start | bytes 49160 | tf_op jit(solution)/shard_map/ppermute | solution.py:393
  64.2 5.9 %collective-permute-start.10 = (f32[8,2,256]{2,1,0:T(2,128)S(1)}, f32[8,2,256]{2,1,0:T(2,128)S(1)}, u32[]{:S(2)}, u32[]{:S(2)}) collective-permute-start(f32[8,2,256]{2,1,0:T(2,128)S(1)} %add.7.refs_2_), channel_id=1, source_target_pairs={{0,2},{1,3},{2,0},{3,1},{4,6},{5,7},{6,4},{7,5},{8,10},{9,11},{10,... | collective-permute-start | bytes 49160 | tf_op jit(solution)/shard_map/ppermute | solution.py:393
  74.7 10.4 %collective-permute-start.11 = (bf16[8,1,64,256]{3,2,1,0:T(8,128)(2,1)S(1)}, bf16[8,1,64,256]{3,2,1,0:T(8,128)(2,1)S(1)}, u32[]{:S(2)}, u32[]{:S(2)}) collective-permute-start(bf16[8,1,64,256]{3,2,1,0:T(8,128)(2,1)S(1)} %get-tuple-element.63), channel_id=1, source_target_pairs={{0,1},{1,2},{2,3},{4,5},{5,6},{6,7},{8,9},{9,10},{10,11},{12,13},{... | collective-permute-start | bytes 786440 | tf_op jit(solution)/shard_map/ppermute | solution.py:384
  78.7 8.3 %collective-permute-start.12 = (bf16[8,1,64,256]{3,2,1,0:T(8,128)(2,1)S(1)}, bf16[8,1,64,256]{3,2,1,0:T(8,128)(2,1)S(1)}, u32[]{:S(2)}, u32[]{:S(2)}) collective-permute-start(bf16[8,1,64,256]{3,2,1,0:T(8,128)(2,1)S(1)} %get-tuple-element.64), channel_id=1, source_target_pairs={{1,0},{2,1},{3,2},{5,4},{6,5},{7,6},{9,8},{10,9},{11,10},{13,12},{... | collective-permute-start | bytes 786440 | tf_op jit(solution)/shard_map/ppermute | solution.py:384
  87.3 2.4 %collective-permute-start.13 = (bf16[4,4,32,768]{3,2,1,0:T(8,128)(2,1)S(1)}, bf16[4,4,32,768]{3,2,1,0:T(8,128)(2,1)S(1)}, u32[]{:S(2)}, u32[]{:S(2)}) collective-permute-start(bf16[4,4,32,768]{3,2,1,0:T(8,128)(2,1)S(1)} %get-tuple-element.67), channel_id=1, source_target_pairs={{0,4},{4,0},{8,12},{12,8},{16,20},{20,16},{24,28},{28,24},{1,5},{5... | collective-permute-start | bytes 2359304 | tf_op jit(solution)/shard_map/ppermute | solution.py:482
  89.8 13.1 %collective-permute-start.16 = (bf16[4,32,768]{2,1,0:T(8,128)(2,1)S(1)}, bf16[4,32,768]{2,1,0:T(8,128)(2,1)S(1)}, u32[]{:S(2)}, u32[]{:S(2)}) collective-permute-start(bf16[4,32,768]{2,1,0:T(8,128)(2,1)S(1)} %get-tuple-element.74), channel_id=1, source_target_pairs={{0,8},{4,12},{8,0},{12,4},{16,24},{20,28},{24,16},{28,20},{1,9},{5... | collective-permute-start | bytes 589832 | tf_op jit(solution)/shard_map/ppermute | solution.py:487
  89.9 13.0 %collective-permute-start.17 = (bf16[4,32,768]{2,1,0:T(8,128)(2,1)S(1)}, bf16[4,32,768]{2,1,0:T(8,128)(2,1)S(1)}, u32[]{:S(2)}, u32[]{:S(2)}) collective-permute-start(bf16[4,32,768]{2,1,0:T(8,128)(2,1)S(1)} %get-tuple-element.75), channel_id=1, source_target_pairs={{0,16},{4,20},{8,24},{12,28},{16,0},{20,4},{24,8},{28,12},{1,17},{... | collective-permute-start | bytes 589832 | tf_op jit(solution)/shard_map/ppermute | solution.py:487
  90.0 13.0 %collective-permute-start.18 = (bf16[4,32,768]{2,1,0:T(8,128)(2,1)S(1)}, bf16[4,32,768]{2,1,0:T(8,128)(2,1)S(1)}, u32[]{:S(2)}, u32[]{:S(2)}) collective-permute-start(bf16[4,32,768]{2,1,0:T(8,128)(2,1)S(1)} %get-tuple-element.76), channel_id=1, source_target_pairs={{0,24},{4,28},{8,16},{12,20},{16,8},{20,12},{24,0},{28,4},{1,25},{... | collective-permute-start | bytes 589832 | tf_op jit(solution)/shard_map/ppermute | solution.py:487
  103.0 4.5 %collective-permute-start.19 = (bf16[32,768]{1,0:T(8,128)(2,1)S(1)}, bf16[32,768]{1,0:T(8,128)(2,1)S(1)}, u32[]{:S(2)}, u32[]{:S(2)}) collective-permute-start(bf16[32,768]{1,0:T(8,128)(2,1)S(1)} %get-tuple-element.78), channel_id=1, source_target_pairs={{0,1},{1,0},{2,3},{3,2},{4,5},{5,4},{6,7},{7,6},{8,9},{9,8},{10,11... | collective-permute-start | bytes 147464 | tf_op jit(solution)/shard_map/ppermute | solution.py:499
  104.7 5.6 %collective-permute-start.20 = (bf16[32,768]{1,0:T(8,128)(2,1)S(1)}, bf16[32,768]{1,0:T(8,128)(2,1)S(1)}, u32[]{:S(2)}, u32[]{:S(2)}) collective-permute-start(bf16[32,768]{1,0:T(8,128)(2,1)S(1)} %get-tuple-element.79), channel_id=1, source_target_pairs={{0,2},{1,3},{2,0},{3,1},{4,6},{5,7},{6,4},{7,5},{8,10},{9,11},{10,... | collective-permute-start | bytes 147464 | tf_op jit(solution)/shard_map/ppermute | solution.py:499
  105.6 6.1 %collective-permute-start.21 = (bf16[32,768]{1,0:T(8,128)(2,1)S(1)}, bf16[32,768]{1,0:T(8,128)(2,1)S(1)}, u32[]{:S(2)}, u32[]{:S(2)}) collective-permute-start(bf16[32,768]{1,0:T(8,128)(2,1)S(1)} %get-tuple-element.80), channel_id=1, source_target_pairs={{0,3},{1,2},{2,1},{3,0},{4,7},{5,6},{6,5},{7,4},{8,11},{9,10},{10,... | collective-permute-start | bytes 147464 | tf_op jit(solution)/shard_map/ppermute | solution.py:499
  111.8 4.5 %collective-permute-start.22 = (bf16[32,768]{1,0:T(8,128)(2,1)S(1)}, bf16[32,768]{1,0:T(8,128)(2,1)S(1)}, u32[]{:S(2)}, u32[]{:S(2)}) collective-permute-start(bf16[32,768]{1,0:T(8,128)(2,1)S(1)} %line_sum.1.refs_0_), channel_id=1, source_target_pairs={{0,1},{1,0},{2,3},{3,2},{4,5},{5,4},{6,7},{7,6},{8,9},{9,8},{10,11... | collective-permute-start | bytes 147464 | tf_op jit(solution)/shard_map/ppermute | solution.py:503
  112.5 6.6 %collective-permute-start.23 = (bf16[32,768]{1,0:T(8,128)(2,1)S(1)}, bf16[32,768]{1,0:T(8,128)(2,1)S(1)}, u32[]{:S(2)}, u32[]{:S(2)}) collective-permute-start(bf16[32,768]{1,0:T(8,128)(2,1)S(1)} %line_sum.1.refs_0_), channel_id=1, source_target_pairs={{0,2},{1,3},{2,0},{3,1},{4,6},{5,7},{6,4},{7,5},{8,10},{9,11},{10,... | collective-permute-start | bytes 147464 | tf_op jit(solution)/shard_map/ppermute | solution.py:503
  114.1 6.0 %collective-permute-start.24 = (bf16[32,768]{1,0:T(8,128)(2,1)S(1)}, bf16[32,768]{1,0:T(8,128)(2,1)S(1)}, u32[]{:S(2)}, u32[]{:S(2)}) collective-permute-start(bf16[32,768]{1,0:T(8,128)(2,1)S(1)} %line_sum.1.refs_0_), channel_id=1, source_target_pairs={{0,3},{1,2},{2,1},{3,0},{4,7},{5,6},{6,5},{7,4},{8,11},{9,10},{10,... | collective-permute-start | bytes 147464 | tf_op jit(solution)/shard_map/ppermute | solution.py:503
  120.1 12.0 %collective-permute-start.25 = (bf16[4,32,768]{2,1,0:T(8,128)(2,1)S(1)}, bf16[4,32,768]{2,1,0:T(8,128)(2,1)S(1)}, u32[]{:S(2)}, u32[]{:S(2)}) collective-permute-start(bf16[4,32,768]{2,1,0:T(8,128)(2,1)S(1)} %line_place.1.refs_0_), channel_id=1, source_target_pairs={{0,8},{4,12},{8,0},{12,4},{16,24},{20,28},{24,16},{28,20},{1,9},{5... | collective-permute-start | bytes 589832 | tf_op jit(solution)/shard_map/ppermute | solution.py:507
  125.2 6.9 %collective-permute-start.26 = (bf16[4,32,768]{2,1,0:T(8,128)(2,1)S(1)}, bf16[4,32,768]{2,1,0:T(8,128)(2,1)S(1)}, u32[]{:S(2)}, u32[]{:S(2)}) collective-permute-start(bf16[4,32,768]{2,1,0:T(8,128)(2,1)S(1)} %line_place.1.refs_0_), channel_id=1, source_target_pairs={{0,16},{4,20},{8,24},{12,28},{16,0},{20,4},{24,8},{28,12},{1,17},{... | collective-permute-start | bytes 589832 | tf_op jit(solution)/shard_map/ppermute | solution.py:507
  125.7 7.8 %collective-permute-start.27 = (bf16[4,32,768]{2,1,0:T(8,128)(2,1)S(1)}, bf16[4,32,768]{2,1,0:T(8,128)(2,1)S(1)}, u32[]{:S(2)}, u32[]{:S(2)}) collective-permute-start(bf16[4,32,768]{2,1,0:T(8,128)(2,1)S(1)} %line_place.1.refs_0_), channel_id=1, source_target_pairs={{0,24},{4,28},{8,16},{12,20},{16,8},{20,12},{24,0},{28,4},{1,25},{... | collective-permute-start | bytes 589832 | tf_op jit(solution)/shard_map/ppermute | solution.py:507
  133.6 2.4 %collective-permute-start.28 = (bf16[4,4,32,768]{3,2,1,0:T(8,128)(2,1)S(1)}, bf16[4,4,32,768]{3,2,1,0:T(8,128)(2,1)S(1)}, u32[]{:S(2)}, u32[]{:S(2)}) collective-permute-start(bf16[4,4,32,768]{3,2,1,0:T(8,128)(2,1)S(1)} %plane_place.1.mine_ref), channel_id=1, source_target_pairs={{0,4},{4,0},{8,12},{12,8},{16,20},{20,16},{24,28},{28,24},{1,5},{5... | collective-permute-start | bytes 2359304 | tf_op jit(solution)/shard_map/ppermute | solution.py:519

commit v2 on v1

--- a/solution.py
+++ b/solution.py
@@ -384,6 +384,11 @@
     return lax.ppermute(high, axis, up), lax.ppermute(low, axis, down)
 
 
+def spread_parts(part, axis):
+    size = lax.axis_size(axis)
+    return [part] + [lax.ppermute(part, axis, [(i, i ^ s) for i in range(size)]) for s in range(1, size)]
+
+
 def spread_sums(part, axis):
     size = lax.axis_size(axis)
     step, got = 1, None
@@ -410,11 +415,14 @@
 
     cot = cotangent.reshape(per_px)
     by_corner = tm == 8
-    cot_prev, cot_next = neighbours("tm", cot, cot, 3 if by_corner else None)
+    first, last = frames_in[:, :1], frames_in[:, rows - 1 :]
+    first, last, near = lax.optimization_barrier((first, last, cot))
+    cot_prev, cot_next = neighbours("tm", near, near, 3 if by_corner else None)
     cot_corner = []
     if by_corner:
-        relayed = lax.ppermute(cot, "tm", [(3, 7), (4, 0)])
-    above, below = neighbours("space", frames_in[:, :1], frames_in[:, rows - 1 :])
+        straight, relayed = cot[: frames // 2], cot[frames // 2 :]
+        relayed = lax.ppermute(relayed, "tm", [(3, 7), (4, 0)])
+    above, below = neighbours("space", first, last)
     back_weights, back_taps = call(
         turn_weights_kernel, "turn_weights", [spatial, temporal],
         [shape((3, 3 * channels, channels), BF16), shape((3 * channels, channels), BF16)], 0, big,
@@ -425,12 +433,12 @@
         100 * big * channels, 8 * big, [windows], 18,
     )
     if by_corner:
-        sums, straight = lax.optimization_barrier((sums, cot))
-        cot_corner.append(lax.ppermute(straight[: frames // 2], "tm", [(3, 4), (4, 3)]))
+        sums, straight = lax.optimization_barrier((sums, straight))
+        cot_corner.append(lax.ppermute(straight, "tm", [(3, 4), (4, 3)]))
     parts = spread_sums(sums, "space")
     if by_corner:
         parts[0], relayed = lax.optimization_barrier((parts[0], relayed))
-        cot_corner.append(lax.ppermute(relayed[frames // 2 :], "tm", [(7, 4), (0, 3)]))
+        cot_corner.append(lax.ppermute(relayed, "tm", [(7, 4), (0, 3)]))
     x_turned = call(
         turn_kernel, "turned", [frames_in, above, below], shape((3 * channels, frames * pixels), BF16),
         0, 8 * big, [pltpu.VMEM((pixels, 3 * channels), BF16)],
@@ -448,7 +456,7 @@
         [shape(per_px, BF16), shape((frames * pixels, 3 * channels), BF16), shape((frames, 2, channels), F32)],
         6 * big * channels, 16 * big,
     )
-    grad_parts = spread_sums(grad_sums, "space")
+    grad_parts = spread_parts(grad_sums, "space")
     temporal_part = call(
         temporal_grad_kernel, "temporal_grad", [act, cot_cat],
         shape((channels, 3 * channels), F32), 6 * big * channels, 8 * big,
@@ -497,21 +505,21 @@
         [shape((block, lanes), F32)] + [shape((block, lanes), BF16)] * (n - 1), 0, big,
     )
     gots = [lax.ppermute(x, "space", other_plane(s)) for s, x in enumerate(sends, 1)]
-    own = call(
-        functools.partial(sum_kernel, n - 1), "line_sum", [own, *gots], shape((block, lanes), BF16), 0, big
-    )
-    gots = [lax.ppermute(own, "space", other_plane(s)) for s in range(1, n)]
-    own = call(
-        functools.partial(place_kernel, "space", 0), "line_place", [own, *gots], shape((n, block, lanes), BF16), 0, big
-    )
-    gots = [lax.ppermute(own, "tm", other_chip(s)) for s in range(1, chips)]
-
     out_frames = call(
         out_kernel, "temporal_forward",
         [clip_frames, dilation, act, act_next, act_prev, temporal.reshape(3 * channels, channels), frames_in],
         shape(frames_in.shape, BF16), 6 * big * channels, 10 * big, [windows],
     )
     own, out_frames = lax.optimization_barrier((own, out_frames))
+    own = call(
+        functools.partial(sum_kernel, n - 1), "line_sum", [own, *gots], shape((block, lanes), BF16), 0, big
+    )
+    gots = [lax.ppermute(own, "space", other_plane(s)) for s in range(1, n)]
+    own = call(
+        functools.partial(place_kernel, "space", 0), "line_place", [own, *gots], shape((n, block, lanes), BF16), 0, big
+    )
+    gots = [lax.ppermute(own, "tm", other_chip(s)) for s in range(1, chips)]
+
 
     own = call(
         functools.partial(place_kernel, "tm", 1), "plane_place", [own, *gots], shape((chips, n, block, lanes), BF16), 0, big

time: 138 us -> 138 us (level)
  waiting for transfers between devices: 33 us -> 38 us
  starting transfers between devices: 55.1 us -> 50.8 us
    ppermute x4 -> x2, starting transfers between devices: 13.3 us -> 4.27 us  [spread_sums(): got = lax.ppermute(part, axis, [(i, i ^ step) for i in range(size)])]
    ppermute x3 -> x6, starting transfers between devices: 3.64 us -> 10.9 us  [the longest x1 4.7 us: per_device(): cot_corner.append(lax.ppermute(relayed, 'tm', [(7, 4), (0, 3)]))]
    ppermute x3, waiting for transfers between devices: 2.56 us -> 8.72 us  [per_device(): lax.ppermute(x, 'tm', other_chip(s))]
    ppermute x3, waiting for transfers between devices: 1.45 us -> 6.74 us  [per_device(): gots = [lax.ppermute(own, 'tm', other_chip(s)) for s in range(1, chips)]]
    ppermute x3 -> x6, waiting for transfers between devices: 7.99 us -> 3.31 us  [the longest x3 2.31 us: spread_parts(): lax.ppermute(part, axis, [(i, i ^ s) for i in range(size)])]
    ppermute x8, waiting for transfers between devices: 4.42 us -> 8.96 us  [neighbours(): return (lax.ppermute(high, axis, up), lax.ppermute(low, axis, down))]
    ppermute x3, waiting for transfers between devices: 4.27 us -> 0.01 us  [per_device(): lax.ppermute(x, 'space', other_plane(s))]
    unnamed x18 -> x16, local copies, waits for them, and re-layouts: 2.9 us -> 0.05 us
  transfers between devices with their start and end apart: 29 -> 30, of which waited for: 14 -> 14; matrix products, arithmetic and copies ran while one was open for 0% -> 1% of each run, Pallas kernels for 31% -> 31%
where the time goes in v2:
time: 138 us; the launch traced here: 137 us
  starting transfers between devices  50.8 us (37%)
  Pallas kernels  44.6 us (32%)
  waiting for transfers between devices  38 us (28%)
  local copies, waits for them, and re-layouts  2.8 us (2%)
    pallas_call x17, Pallas kernels, call(): pl.pallas_call(kernel, in_specs=[smem if x.dtype == jnp.int32 else vmem f...  44.6 us
    ppermute x8, starting transfers between devices, neighbours(): return (lax.ppermute(high, axis, up), lax.ppermute(low, axis, down))  16.6 us
    ppermute x8, waiting for transfers between devices, neighbours(): return (lax.ppermute(high, axis, up), lax.ppermute(low, axis, down))  8.96 us
    ppermute x3, waiting for transfers between devices, per_device(): lax.ppermute(x, 'tm', other_chip(s))  8.72 us
    ppermute x3, waiting for transfers between devices, per_device(): gots = [lax.ppermute(own, 'tm', other_chip(s)) for s in range(1, chips)]  6.74 us
    ppermute x3, starting transfers between devices, per_device(): gots = [lax.ppermute(own, 'tm', other_chip(s)) for s in range(1, chips)]  6.48 us
    ppermute x1, starting transfers between devices, per_device(): cot_corner.append(lax.ppermute(relayed, 'tm', [(7, 4), (0, 3)]))  4.7 us
    ppermute x3, starting transfers between devices, per_device(): lax.ppermute(x, 'space', other_plane(s))  4.45 us
  transfers between devices with their start and end apart: 30, of which 14 were waited for; matrix products, arithmetic and copies ran while one was open for 1% of the time, Pallas kernels for 31%

profile of v2, /device:TPU:0, one launch (start us, length us, event | category | flops | bytes accessed | tf_op | source)
XLA Modules:
  0.0 137.3 jit_solution(17202956775929144152)
XLA Ops:
  0.6 1.1 fusion.1
  1.7 0.0 copy-start
  1.7 0.0 copy-start.3
  1.7 1.6 %collective-permute-start.5 = (bf16[8,512,256]{2,1,0:T(8,128)(2,1)}, bf16[8,512,256]{2,1,0:T(8,128)(2,1)S(1)}, u32[]{:S(2)}, u32[]{:S(2)}) collective-permute-start(bf16[8,512,256]{2,1,0:T(8,128)(2,1)} %bitcast.6), channel_id=1, source_target_pairs={{4,0},{8,4},{12,8},{20,16},{24,20},{28,24},{5,1},{9,5},{13,9},{21,... | collective-permute-start | bytes 6291464 | tf_op jit(solution)/shard_map/ppermute | solution.py:384
  3.3 3.2 %collective-permute-start.6 = (bf16[8,512,256]{2,1,0:T(8,128)(2,1)}, bf16[8,512,256]{2,1,0:T(8,128)(2,1)S(1)}, u32[]{:S(2)}, u32[]{:S(2)}) collective-permute-start(bf16[8,512,256]{2,1,0:T(8,128)(2,1)} %bitcast.7), channel_id=1, source_target_pairs={{0,4},{4,8},{8,12},{16,20},{20,24},{24,28},{1,5},{5,9},{9,13},{17,... | collective-permute-start | bytes 6291464 | tf_op jit(solution)/shard_map/ppermute | solution.py:384
  6.5 4.9 %collective-permute-start = (bf16[8,1,64,256]{3,2,1,0:T(8,128)(2,1)S(1)}, bf16[8,1,64,256]{3,2,1,0:T(8,128)(2,1)S(1)}, u32[]{:S(2)}, u32[]{:S(2)}) collective-permute-start(bf16[8,1,64,256]{3,2,1,0:T(8,128)(2,1)S(1)} %get-tuple-element.49), channel_id=1, source_target_pairs={{0,1},{1,2},{2,3},{4,5},{5,6},{6,7},{8,9},{9,10},{10,11},{12,13},{... | collective-permute-start | bytes 786440 | tf_op jit(solution)/shard_map/ppermute | solution.py:384
  11.4 1.3 collective-permute-start.1
  12.7 1.7 %fusion = (bf16[4,8,64,256]{3,2,1,0:T(8,128)(2,1)S(1)}, bf16[4,8,64,256]{3,2,1,0:T(8,128)(2,1)S(1)}) fusion(bf16[8,8,64,256]{3,2,1,0:T(8,128)(2,1)} %cot_ref.1), kind=kLoop, calls=%fused_computation | loop fusion | bytes 4194304 | tf_op jit(solution)/shard_map/slice | solution.py:423
  14.4 1.3 collective-permute-start.3
  15.7 2.4 %collective-permute-done.above_ref = bf16[8,1,64,256]{3,2,1,0:T(8,128)(2,1)S(1)} collective-permute-done((bf16[8,1,64,256]{3,2,1,0:T(8,128)(2,1)S(1)}, bf16[8,1,64,256]{3,2,1,0:T(8,128)(2,1)S(1)}, u32[]{:S(2)}, u32[]{:S(2)}) %collective-permute-start) | collective-permute-done | bytes 262176 | tf_op jit(solution)/shard_map/ppermute | solution.py:384
  18.1 4.1 %collective-permute-done.1.below_ref = bf16[8,1,64,256]{3,2,1,0:T(8,128)(2,1)S(1)} collective-permute-done((bf16[8,1,64,256]{3,2,1,0:T(8,128)(2,1)S(1)}, bf16[8,1,64,256]{3,2,1,0:T(8,128)(2,1)S(1)}, u32[]{:S(2)}, u32[]{:S(2)}) %collective-permute-start.1) | collective-permute-done | bytes 262176 | tf_op jit(solution)/shard_map/ppermute | solution.py:384
  22.2 5.7 %conv_forward.1 = (f32[8,512,256]{2,1,0:T(8,128)S(1)}, f32[8,2,256]{2,1,0:T(2,128)S(1)}) custom-call(bf16[8,8,64,256]{3,2,1,0:T(8,128)(2,1)S(1)} %copy-done, bf16[8,1,64,256]{3,2,1,0:T(8,128)(2,1)S(1)} %collective-permute-done.above_ref, bf16[8,1,64,256]{3,2,1,0:T(8,128)(2,1)S(1)} %collective-permute-done.1.below_ref, bf16[3,3,256,256]{3,2,1,0:T(8,128)(2,1)S(1)} %copy-done.3), custom_call_target="tpu_custom_call" | custom-call | flops 26843545600 | bytes 8388608 | tf_op jit(solution)/shard_map/conv_forward/pallas_call | solution.py:20
  27.9 0.7 collective-permute-start.7
  28.7 1.6 %collective-permute-start.2 = (f32[8,2,256]{2,1,0:T(2,128)S(1)}, f32[8,2,256]{2,1,0:T(2,128)S(1)}, u32[]{:S(2)}, u32[]{:S(2)}) collective-permute-start(f32[8,2,256]{2,1,0:T(2,128)S(1)} %get-tuple-element.52), channel_id=1, source_target_pairs={{0,1},{1,0},{2,3},{3,2},{4,5},{5,4},{6,7},{7,6},{8,9},{9,8},{10,11... | collective-permute-start | bytes 49160 | tf_op jit(solution)/shard_map/ppermute | solution.py:398
  30.3 2.2 %collective-permute-done.2 = f32[8,2,256]{2,1,0:T(2,128)S(1)} collective-permute-done((f32[8,2,256]{2,1,0:T(2,128)S(1)}, f32[8,2,256]{2,1,0:T(2,128)S(1)}, u32[]{:S(2)}, u32[]{:S(2)}) %collective-permute-start.2) | collective-permute-done | bytes 16416 | tf_op jit(solution)/shard_map/ppermute | solution.py:398
  32.5 0.0 copy-start.4
  32.5 4.7 %collective-permute-start.8 = (bf16[4,512,256]{2,1,0:T(8,128)(2,1)S(1)}, bf16[4,512,256]{2,1,0:T(8,128)(2,1)S(1)}, u32[]{:S(2)}, u32[]{:S(2)}) collective-permute-start(bf16[4,512,256]{2,1,0:T(8,128)(2,1)S(1)} %collective-permute-done.3), channel_id=1, source_target_pairs={{28,16},{0,12},{29,17},{1,13},{30,18},{2,14},{31,19},{3,15}} | collective-permute-start | bytes 3145736 | tf_op jit(solution)/shard_map/ppermute | solution.py:441
  37.2 2.6 %collective-permute-start.4 = (f32[8,2,256]{2,1,0:T(2,128)S(1)}, f32[8,2,256]{2,1,0:T(2,128)S(1)}, u32[]{:S(2)}, u32[]{:S(2)}) collective-permute-start(f32[8,2,256]{2,1,0:T(2,128)S(1)} %add.3.refs_0_), channel_id=1, source_target_pairs={{0,2},{1,3},{2,0},{3,1},{4,6},{5,7},{6,4},{7,5},{8,10},{9,11},{10,... | collective-permute-start | bytes 49160 | tf_op jit(solution)/shard_map/ppermute | solution.py:398
  39.9 2.2 %turned.1.xt_ref = bf16[768,4096]{1,0:T(8,128)(2,1)S(1)} custom-call(bf16[8,8,64,256]{3,2,1,0:T(8,128)(2,1)S(1)} %copy-done, bf16[8,1,64,256]{3,2,1,0:T(8,128)(2,1)S(1)} %collective-permute-done.above_ref, bf16[8,1,64,256]{3,2,1,0:T(8,128)(2,1)S(1)} %collective-permute-done.1.below_ref), custom_call_target="tpu_custom_call" | custom-call | bytes 8388608 | tf_op jit(solution)/shard_map/turned/pallas_call | solution.py:20
  42.1 0.0 copy-start.1
  42.1 6.0 %activation.1 = (bf16[8,512,256]{2,1,0:T(8,128)(2,1)S(1)}, bf16[8,512,256]{2,1,0:T(8,128)(2,1)S(1)}, bf16[8,512,256]{2,1,0:T(8,128)(2,1)S(1)}) custom-call(s32[2]{0:T(128)S(1)} %copy-done.4, f32[8,2,256]{2,1,0:T(2,128)S(1)} %add.3.refs_0_, f32[8,2,256]{2,1,0:T(2,128)S(1)} %collective-permute-done.4.refs_1_, f32[8,512,256]{2,1,0:T(8,128)S(1)} %get-tuple-element.57.refs_2_, ...), custom_call_target="tpu_custom_call" | custom-call | flops 10485760 | bytes 10485760 | tf_op jit(solution)/shard_map/activation/pallas_call | solution.py:20
  48.2 1.4 %collective-permute-start.15 = (bf16[8,512,256]{2,1,0:T(8,128)(2,1)S(1)}, bf16[8,512,256]{2,1,0:T(8,128)(2,1)S(1)}, u32[]{:S(2)}, u32[]{:S(2)}) collective-permute-start(bf16[8,512,256]{2,1,0:T(8,128)(2,1)S(1)} %get-tuple-element.67.act_ref.own), channel_id=1, source_target_pairs={{0,4},{4,8},{8,12},{12,16},{16,20},{20,24},{24,28},{1,5},{5,9},{9,... | collective-permute-start | bytes 6291464 | tf_op jit(solution)/shard_map/ppermute | solution.py:384
  49.6 1.3 collective-permute-start.16
  50.9 0.5 turn_weights.1
  51.4 1.0 collective-permute-done.8.refs_1_
  52.4 4.1 %grad_activation.1 = (bf16[8,512,256]{2,1,0:T(8,128)(2,1)S(1)}, bf16[4096,768]{1,0:T(8,128)(2,1)S(1)}, f32[8,2,256]{2,1,0:T(2,128)S(1)}) custom-call(s32[2]{0:T(128)S(1)} %copy-done.4, s32[2]{0:T(128)S(1)} %copy-done.5, bf16[8,512,256]{2,1,0:T(8,128)(2,1)S(1)} %bitcast.8, bf16[8,512,256]{2,1,0:T(8,128)(2,1)S(1)} %collective-permute-done.5.nxt, ...), custom_call_target="tpu_custom_call" | custom-call | flops 1610612736 | bytes 16777216 | tf_op jit(solution)/shard_map/grad_activation/pallas_call | solution.py:20
  56.5 2.8 %collective-permute-start.10 = (f32[8,2,256]{2,1,0:T(2,128)S(1)}, f32[8,2,256]{2,1,0:T(2,128)S(1)}, u32[]{:S(2)}, u32[]{:S(2)}) collective-permute-start(f32[8,2,256]{2,1,0:T(2,128)S(1)} %get-tuple-element.65.refs_2_), channel_id=1, source_target_pairs={{0,2},{1,3},{2,0},{3,1},{4,6},{5,7},{6,4},{7,5},{8,10},{9,11},{10,... | collective-permute-start | bytes 49160 | tf_op jit(solution)/shard_map/ppermute | solution.py:389
  59.3 1.3 collective-permute-start.11
  60.7 1.9 %temporal_grad.1.temporal_ref = f32[256,768]{1,0:T(8,128)S(1)} custom-call(bf16[8,512,256]{2,1,0:T(8,128)(2,1)S(1)} %get-tuple-element.67.act_ref.own, bf16[4096,768]{1,0:T(8,128)(2,1)S(1)} %get-tuple-element.68.cat_ref), custom_call_target="tpu_custom_call" | custom-call | flops 1610612736 | bytes 8388608 | tf_op jit(solution)/shard_map/temporal_grad/pallas_call | solution.py:20
  62.6 2.3 %collective-permute-done.11.refs_5_ = f32[8,2,256]{2,1,0:T(2,128)S(1)} collective-permute-done((f32[8,2,256]{2,1,0:T(2,128)S(1)}, f32[8,2,256]{2,1,0:T(2,128)S(1)}, u32[]{:S(2)}, u32[]{:S(2)}) %collective-permute-start.11) | collective-permute-done | bytes 16416 | tf_op jit(solution)/shard_map/ppermute | solution.py:389
  64.9 4.6 %norm_backward.1 = (bf16[8,512,256]{2,1,0:T(8,128)(2,1)S(1)}, bf16[8,1,64,256]{3,2,1,0:T(8,128)(2,1)S(1)}, bf16[8,1,64,256]{3,2,1,0:T(8,128)(2,1)S(1)}, bf16[4096,768]{1,0:T(8,128)(2,1)S(1)}) custom-call(bf16[8,512,256]{2,1,0:T(8,128)(2,1)S(1)} %get-tuple-element.58.refs_3_.normed_ref, bf16[8,512,256]{2,1,0:T(8,128)(2,1)S(1)} %get-tuple-element.59.refs_4_.slope_ref, ...), custom_call_target="tpu_custom_call" | custom-call | bytes 12582912 | tf_op jit(solution)/shard_map/norm_backward/pallas_call | solution.py:20
  69.5 1.7 %collective-permute-start.12 = (bf16[8,1,64,256]{3,2,1,0:T(8,128)(2,1)S(1)}, bf16[8,1,64,256]{3,2,1,0:T(8,128)(2,1)S(1)}, u32[]{:S(2)}, u32[]{:S(2)}) collective-permute-start(bf16[8,1,64,256]{3,2,1,0:T(8,128)(2,1)S(1)} %get-tuple-element.69), channel_id=1, source_target_pairs={{0,1},{1,2},{2,3},{4,5},{5,6},{6,7},{8,9},{9,10},{10,11},{12,13},{... | collective-permute-start | bytes 786440 | tf_op jit(solution)/shard_map/ppermute | solution.py:384
  71.1 1.3 collective-permute-start.13
  72.4 5.1 %weight_grad.1.acc_ref = f32[1024,768]{1,0:T(8,128)S(1)} custom-call(bf16[768,4096]{1,0:T(8,128)(2,1)S(1)} %turned.1.xt_ref, bf16[4096,768]{1,0:T(8,128)(2,1)S(1)} %get-tuple-element.66.moved_ref, f32[256,768]{1,0:T(8,128)S(1)} %temporal_grad.1.temporal_ref), custom_call_target="tpu_custom_call" | custom-call | flops 4831838208 | bytes 12582912 | tf_op jit(solution)/shard_map/weight_grad/pallas_call | solution.py:20
  77.6 2.4 %collective-permute-done.13.below_ref = bf16[8,1,64,256]{3,2,1,0:T(8,128)(2,1)S(1)} collective-permute-done((bf16[8,1,64,256]{3,2,1,0:T(8,128)(2,1)S(1)}, bf16[8,1,64,256]{3,2,1,0:T(8,128)(2,1)S(1)}, u32[]{:S(2)}, u32[]{:S(2)}) %collective-permute-start.13) | collective-permute-done | bytes 262176 | tf_op jit(solution)/shard_map/ppermute | solution.py:384
  80.0 0.4 hand_out.1
  80.4 0.1 collective-permute-start.14
  80.4 2.3 %collective-permute-done.14.got_ref = bf16[4,4,32,768]{3,2,1,0:T(8,128)(2,1)S(1)} collective-permute-done((bf16[4,4,32,768]{3,2,1,0:T(8,128)(2,1)S(1)}, bf16[4,4,32,768]{3,2,1,0:T(8,128)(2,1)S(1)}, u32[]{:S(2)}, u32[]{:S(2)}) %collective-permute-start.14) | collective-permute-done | bytes 786464 | tf_op jit(solution)/shard_map/ppermute | solution.py:490
  82.7 0.2 core_sum.1
  82.9 0.5 collective-permute-start.17
  83.4 1.1 collective-permute-start.18
  84.5 1.9 %collective-permute-start.19 = (bf16[4,32,768]{2,1,0:T(8,128)(2,1)S(1)}, bf16[4,32,768]{2,1,0:T(8,128)(2,1)S(1)}, u32[]{:S(2)}, u32[]{:S(2)}) collective-permute-start(bf16[4,32,768]{2,1,0:T(8,128)(2,1)S(1)} %get-tuple-element.82), channel_id=1, source_target_pairs={{0,24},{4,28},{8,16},{12,20},{16,8},{20,12},{24,0},{28,4},{1,25},{... | collective-permute-start | bytes 589832 | tf_op jit(solution)/shard_map/ppermute | solution.py:495
  86.4 7.0 %conv_backward.1 = bf16[8,8,64,256]{3,2,1,0:T(8,128)(2,1)} custom-call(bf16[8,512,256]{2,1,0:T(8,128)(2,1)S(1)} %get-tuple-element.75.g_ref, bf16[8,1,64,256]{3,2,1,0:T(8,128)(2,1)S(1)} %collective-permute-done.12.above_ref, bf16[8,1,64,256]{3,2,1,0:T(8,128)(2,1)S(1)} %collective-permute-done.13.below_ref, bf16[8,8,64,256]{3,2,1,0:T(8,128)(2,1)S(1)} %copy-done.1, ...), custom_call_target="tpu_custom_call" | custom-call | flops 4831838208 | bytes 8388608 | tf_op jit(solution)/shard_map/conv_backward/pallas_call | solution.py:20
  93.4 8.7 %collective-permute-done.17.refs_0_ = bf16[4,32,768]{2,1,0:T(8,128)(2,1)S(1)} collective-permute-done((bf16[4,32,768]{2,1,0:T(8,128)(2,1)S(1)}, bf16[4,32,768]{2,1,0:T(8,128)(2,1)S(1)}, u32[]{:S(2)}, u32[]{:S(2)}) %collective-permute-start.17) | collective-permute-done | bytes 196640 | tf_op jit(solution)/shard_map/ppermute | solution.py:495
  102.2 0.1 plane_sum.1
  102.3 0.6 collective-permute-start.20
  102.8 1.5 %collective-permute-start.21 = (bf16[32,768]{1,0:T(8,128)(2,1)S(1)}, bf16[32,768]{1,0:T(8,128)(2,1)S(1)}, u32[]{:S(2)}, u32[]{:S(2)}) collective-permute-start(bf16[32,768]{1,0:T(8,128)(2,1)S(1)} %get-tuple-element.90), channel_id=1, source_target_pairs={{0,2},{1,3},{2,0},{3,1},{4,6},{5,7},{6,4},{7,5},{8,10},{9,11},{10,... | collective-permute-start | bytes 147464 | tf_op jit(solution)/shard_map/ppermute | solution.py:507
  104.4 2.3 %collective-permute-start.22 = (bf16[32,768]{1,0:T(8,128)(2,1)S(1)}, bf16[32,768]{1,0:T(8,128)(2,1)S(1)}, u32[]{:S(2)}, u32[]{:S(2)}) collective-permute-start(bf16[32,768]{1,0:T(8,128)(2,1)S(1)} %get-tuple-element.91), channel_id=1, source_target_pairs={{0,3},{1,2},{2,1},{3,0},{4,7},{5,6},{6,5},{7,4},{8,11},{9,10},{10,... | collective-permute-start | bytes 147464 | tf_op jit(solution)/shard_map/ppermute | solution.py:507
  106.7 5.0 %temporal_forward.1 = bf16[8,8,64,256]{3,2,1,0:T(8,128)(2,1)} custom-call(s32[2]{0:T(128)S(1)} %copy-done.4, s32[2]{0:T(128)S(1)} %copy-done.5, bf16[8,512,256]{2,1,0:T(8,128)(2,1)S(1)} %get-tuple-element.67.act_ref.own, bf16[8,512,256]{2,1,0:T(8,128)(2,1)S(1)} %collective-permute-done.16.nxt, bf16[8,512,256]{2,1,0:T(8,128)(2,1)S(1)} %collective-permute-done.15.prv, ...), custom_call_target="tpu_custom_call" | custom-call | flops 1610612736 | bytes 10485760 | tf_op jit(solution)/shard_map/temporal_forward/pallas_call | solution.py:20
  111.7 0.1 collective-permute-start.23
  111.8 2.0 %collective-permute-start.24 = (bf16[32,768]{1,0:T(8,128)(2,1)S(1)}, bf16[32,768]{1,0:T(8,128)(2,1)S(1)}, u32[]{:S(2)}, u32[]{:S(2)}) collective-permute-start(bf16[32,768]{1,0:T(8,128)(2,1)S(1)} %line_sum.1.refs_0_), channel_id=1, source_target_pairs={{0,2},{1,3},{2,0},{3,1},{4,6},{5,7},{6,4},{7,5},{8,10},{9,11},{10,... | collective-permute-start | bytes 147464 | tf_op jit(solution)/shard_map/ppermute | solution.py:517
  113.8 2.3 %collective-permute-start.25 = (bf16[32,768]{1,0:T(8,128)(2,1)S(1)}, bf16[32,768]{1,0:T(8,128)(2,1)S(1)}, u32[]{:S(2)}, u32[]{:S(2)}) collective-permute-start(bf16[32,768]{1,0:T(8,128)(2,1)S(1)} %line_sum.1.refs_0_), channel_id=1, source_target_pairs={{0,3},{1,2},{2,1},{3,0},{4,7},{5,6},{6,5},{7,4},{8,11},{9,10},{10,... | collective-permute-start | bytes 147464 | tf_op jit(solution)/shard_map/ppermute | solution.py:517
  116.2 1.0 collective-permute-done.24.refs_2_
  117.2 2.5 %collective-permute-done.25.refs_3_ = bf16[32,768]{1,0:T(8,128)(2,1)S(1)} collective-permute-done((bf16[32,768]{1,0:T(8,128)(2,1)S(1)}, bf16[32,768]{1,0:T(8,128)(2,1)S(1)}, u32[]{:S(2)}, u32[]{:S(2)}) %collective-permute-start.25) | collective-permute-done | bytes 49184 | tf_op jit(solution)/shard_map/ppermute | solution.py:517
  119.8 3.1 %collective-permute-start.26 = (bf16[4,32,768]{2,1,0:T(8,128)(2,1)S(1)}, bf16[4,32,768]{2,1,0:T(8,128)(2,1)S(1)}, u32[]{:S(2)}, u32[]{:S(2)}) collective-permute-start(bf16[4,32,768]{2,1,0:T(8,128)(2,1)S(1)} %line_place.1.refs_0_), channel_id=1, source_target_pairs={{0,8},{4,12},{8,0},{12,4},{16,24},{20,28},{24,16},{28,20},{1,9},{5... | collective-permute-start | bytes 589832 | tf_op jit(solution)/shard_map/ppermute | solution.py:521
  122.9 2.0 %collective-permute-start.27 = (bf16[4,32,768]{2,1,0:T(8,128)(2,1)S(1)}, bf16[4,32,768]{2,1,0:T(8,128)(2,1)S(1)}, u32[]{:S(2)}, u32[]{:S(2)}) collective-permute-start(bf16[4,32,768]{2,1,0:T(8,128)(2,1)S(1)} %line_place.1.refs_0_), channel_id=1, source_target_pairs={{0,16},{4,20},{8,24},{12,28},{16,0},{20,4},{24,8},{28,12},{1,17},{... | collective-permute-start | bytes 589832 | tf_op jit(solution)/shard_map/ppermute | solution.py:521
  124.9 1.4 %collective-permute-start.28 = (bf16[4,32,768]{2,1,0:T(8,128)(2,1)S(1)}, bf16[4,32,768]{2,1,0:T(8,128)(2,1)S(1)}, u32[]{:S(2)}, u32[]{:S(2)}) collective-permute-start(bf16[4,32,768]{2,1,0:T(8,128)(2,1)S(1)} %line_place.1.refs_0_), channel_id=1, source_target_pairs={{0,24},{4,28},{8,16},{12,20},{16,8},{20,12},{24,0},{28,4},{1,25},{... | collective-permute-start | bytes 589832 | tf_op jit(solution)/shard_map/ppermute | solution.py:521
  126.2 2.1 %collective-permute-done.26.refs_1_ = bf16[4,32,768]{2,1,0:T(8,128)(2,1)S(1)} collective-permute-done((bf16[4,32,768]{2,1,0:T(8,128)(2,1)S(1)}, bf16[4,32,768]{2,1,0:T(8,128)(2,1)S(1)}, u32[]{:S(2)}, u32[]{:S(2)}) %collective-permute-start.26) | collective-permute-done | bytes 196640 | tf_op jit(solution)/shard_map/ppermute | solution.py:521
  128.3 2.8 %collective-permute-done.27.refs_2_ = bf16[4,32,768]{2,1,0:T(8,128)(2,1)S(1)} collective-permute-done((bf16[4,32,768]{2,1,0:T(8,128)(2,1)S(1)}, bf16[4,32,768]{2,1,0:T(8,128)(2,1)S(1)}, u32[]{:S(2)}, u32[]{:S(2)}) %collective-permute-start.27) | collective-permute-done | bytes 196640 | tf_op jit(solution)/shard_map/ppermute | solution.py:521
  131.1 1.9 %collective-permute-done.28.refs_3_ = bf16[4,32,768]{2,1,0:T(8,128)(2,1)S(1)} collective-permute-done((bf16[4,32,768]{2,1,0:T(8,128)(2,1)S(1)}, bf16[4,32,768]{2,1,0:T(8,128)(2,1)S(1)}, u32[]{:S(2)}, u32[]{:S(2)}) %collective-permute-start.28) | collective-permute-done | bytes 196640 | tf_op jit(solution)/shard_map/ppermute | solution.py:521
  133.0 0.1 plane_place.1.mine_ref
  133.1 0.1 collective-permute-start.29
  133.1 2.3 %collective-permute-done.29.got_ref = bf16[4,4,32,768]{3,2,1,0:T(8,128)(2,1)S(1)} collective-permute-done((bf16[4,4,32,768]{3,2,1,0:T(8,128)(2,1)S(1)}, bf16[4,4,32,768]{3,2,1,0:T(8,128)(2,1)S(1)}, u32[]{:S(2)}, u32[]{:S(2)}) %collective-permute-start.29) | collective-permute-done | bytes 786464 | tf_op jit(solution)/shard_map/ppermute | solution.py:527
  135.4 1.9 %finish.1 = (f32[3,3,256,256]{3,2,1,0:T(8,128)}, f32[3,256,256]{2,1,0:T(8,128)}) custom-call(bf16[4,4,32,768]{3,2,1,0:T(8,128)(2,1)S(1)} %plane_place.1.mine_ref, bf16[4,4,32,768]{3,2,1,0:T(8,128)(2,1)S(1)} %collective-permute-done.29.got_ref), custom_call_target="tpu_custom_call" | custom-call | bytes 4194304 | tf_op jit(solution)/shard_map/finish/pallas_call | solution.py:20
  (32 shorter events, 0.1 us)
Async XLA Ops:
  1.7 20.5 %copy-start = (bf16[8,8,64,256]{3,2,1,0:T(8,128)(2,1)S(1)}, bf16[8,8,64,256]{3,2,1,0:T(8,128)(2,1)}, u32[]{:S(2)}) copy-start(bf16[8,8,64,256]{3,2,1,0:T(8,128)(2,1)} %x_ref.5) | copy-start | bytes 6291460
  1.7 20.5 %copy-start.3 = (bf16[3,3,256,256]{3,2,1,0:T(8,128)(2,1)S(1)}, bf16[3,3,256,256]{3,2,1,0:T(8,128)(2,1)}, u32[]{:S(2)}) copy-start(bf16[3,3,256,256]{3,2,1,0:T(8,128)(2,1)} %spatial_ref.1) | copy-start | bytes 3538948
  1.7 50.7 %collective-permute-start.5 = (bf16[8,512,256]{2,1,0:T(8,128)(2,1)}, bf16[8,512,256]{2,1,0:T(8,128)(2,1)S(1)}, u32[]{:S(2)}, u32[]{:S(2)}) collective-permute-start(bf16[8,512,256]{2,1,0:T(8,128)(2,1)} %bitcast.6), channel_id=1, source_target_pairs={{4,0},{8,4},{12,8},{20,16},{24,20},{28,24},{5,1},{9,5},{13,9},{21,... | collective-permute-start | bytes 6291464 | tf_op jit(solution)/shard_map/ppermute | solution.py:384
  3.3 49.1 %collective-permute-start.6 = (bf16[8,512,256]{2,1,0:T(8,128)(2,1)}, bf16[8,512,256]{2,1,0:T(8,128)(2,1)S(1)}, u32[]{:S(2)}, u32[]{:S(2)}) collective-permute-start(bf16[8,512,256]{2,1,0:T(8,128)(2,1)} %bitcast.7), channel_id=1, source_target_pairs={{0,4},{4,8},{8,12},{16,20},{20,24},{24,28},{1,5},{5,9},{9,13},{17,... | collective-permute-start | bytes 6291464 | tf_op jit(solution)/shard_map/ppermute | solution.py:384
  6.5 11.6 %collective-permute-start = (bf16[8,1,64,256]{3,2,1,0:T(8,128)(2,1)S(1)}, bf16[8,1,64,256]{3,2,1,0:T(8,128)(2,1)S(1)}, u32[]{:S(2)}, u32[]{:S(2)}) collective-permute-start(bf16[8,1,64,256]{3,2,1,0:T(8,128)(2,1)S(1)} %get-tuple-element.49), channel_id=1, source_target_pairs={{0,1},{1,2},{2,3},{4,5},{5,6},{6,7},{8,9},{9,10},{10,11},{12,13},{... | collective-permute-start | bytes 786440 | tf_op jit(solution)/shard_map/ppermute | solution.py:384
  11.4 10.8 %collective-permute-start.1 = (bf16[8,1,64,256]{3,2,1,0:T(8,128)(2,1)S(1)}, bf16[8,1,64,256]{3,2,1,0:T(8,128)(2,1)S(1)}, u32[]{:S(2)}, u32[]{:S(2)}) collective-permute-start(bf16[8,1,64,256]{3,2,1,0:T(8,128)(2,1)S(1)} %get-tuple-element.50), channel_id=1, source_target_pairs={{1,0},{2,1},{3,2},{5,4},{6,5},{7,6},{9,8},{10,9},{11,10},{13,12},{... | collective-permute-start | bytes 786440 | tf_op jit(solution)/shard_map/ppermute | solution.py:384
  14.4 18.1 %collective-permute-start.3 = (bf16[4,512,256]{2,1,0:T(8,128)(2,1)S(1)}, bf16[4,512,256]{2,1,0:T(8,128)(2,1)S(1)}, u32[]{:S(2)}, u32[]{:S(2)}) collective-permute-start(bf16[4,512,256]{2,1,0:T(8,128)(2,1)S(1)} %bitcast.13), channel_id=1, source_target_pairs={{12,28},{16,0},{13,29},{17,1},{14,30},{18,2},{15,31},{19,3}} | collective-permute-start | bytes 3145736 | tf_op jit(solution)/shard_map/ppermute | solution.py:424
  27.9 21.7 %collective-permute-start.7 = (bf16[4,512,256]{2,1,0:T(8,128)(2,1)S(1)}, bf16[4,512,256]{2,1,0:T(8,128)(2,1)S(1)}, u32[]{:S(2)}, u32[]{:S(2)}) collective-permute-start(bf16[4,512,256]{2,1,0:T(8,128)(2,1)S(1)} %bitcast.12), channel_id=1, source_target_pairs={{12,16},{16,12},{13,17},{17,13},{14,18},{18,14},{15,19},{19,15}} | collective-permute-start | bytes 3145736 | tf_op jit(solution)/shard_map/ppermute | solution.py:437
  28.7 3.8 %collective-permute-start.2 = (f32[8,2,256]{2,1,0:T(2,128)S(1)}, f32[8,2,256]{2,1,0:T(2,128)S(1)}, u32[]{:S(2)}, u32[]{:S(2)}) collective-permute-start(f32[8,2,256]{2,1,0:T(2,128)S(1)} %get-tuple-element.52), channel_id=1, source_target_pairs={{0,1},{1,0},{2,3},{3,2},{4,5},{5,4},{6,7},{7,6},{8,9},{9,8},{10,11... | collective-permute-start | bytes 49160 | tf_op jit(solution)/shard_map/ppermute | solution.py:398
  32.5 9.6 %copy-start.4 = (s32[2]{0:T(128)S(1)}, s32[2]{0:T(128)}, u32[]{:S(2)}) copy-start(s32[2]{0:T(128)} %clip_ref.5) | copy-start | bytes 28
  32.5 9.6 %copy-start.6 = (f32[256]{0:T(256)S(1)}, f32[256]{0:T(256)}, u32[]{:S(2)}) copy-start(f32[256]{0:T(256)} %param.12) | copy-start | bytes 3076
  32.5 9.6 %copy-start.7 = (f32[256]{0:T(256)S(1)}, f32[256]{0:T(256)}, u32[]{:S(2)}) copy-start(f32[256]{0:T(256)} %param.13) | copy-start | bytes 3076
  32.5 19.9 %collective-permute-start.8 = (bf16[4,512,256]{2,1,0:T(8,128)(2,1)S(1)}, bf16[4,512,256]{2,1,0:T(8,128)(2,1)S(1)}, u32[]{:S(2)}, u32[]{:S(2)}) collective-permute-start(bf16[4,512,256]{2,1,0:T(8,128)(2,1)S(1)} %collective-permute-done.3), channel_id=1, source_target_pairs={{28,16},{0,12},{29,17},{1,13},{30,18},{2,14},{31,19},{3,15}} | collective-permute-start | bytes 3145736 | tf_op jit(solution)/shard_map/ppermute | solution.py:441
  37.2 4.8 %collective-permute-start.4 = (f32[8,2,256]{2,1,0:T(2,128)S(1)}, f32[8,2,256]{2,1,0:T(2,128)S(1)}, u32[]{:S(2)}, u32[]{:S(2)}) collective-permute-start(f32[8,2,256]{2,1,0:T(2,128)S(1)} %add.3.refs_0_), channel_id=1, source_target_pairs={{0,2},{1,3},{2,0},{3,1},{4,6},{5,7},{6,4},{7,5},{8,10},{9,11},{10,... | collective-permute-start | bytes 49160 | tf_op jit(solution)/shard_map/ppermute | solution.py:398
  42.1 8.8 %copy-start.2 = (bf16[3,256,256]{2,1,0:T(8,128)(2,1)S(1)}, bf16[3,256,256]{2,1,0:T(8,128)(2,1)}, u32[]{:S(2)}) copy-start(bf16[3,256,256]{2,1,0:T(8,128)(2,1)} %temporal_ref.1) | copy-start | bytes 1179652
  42.1 10.3 %copy-start.1 = (bf16[8,8,64,256]{3,2,1,0:T(8,128)(2,1)S(1)}, bf16[8,8,64,256]{3,2,1,0:T(8,128)(2,1)}, u32[]{:S(2)}) copy-start(bf16[8,8,64,256]{3,2,1,0:T(8,128)(2,1)} %cot_ref.1) | copy-start | bytes 6291460
  42.1 10.3 %copy-start.5 = (s32[2]{0:T(128)S(1)}, s32[2]{0:T(128)}, u32[]{:S(2)}) copy-start(s32[2]{0:T(128)} %dil_ref.3) | copy-start | bytes 28
  48.2 45.3 %collective-permute-start.15 = (bf16[8,512,256]{2,1,0:T(8,128)(2,1)S(1)}, bf16[8,512,256]{2,1,0:T(8,128)(2,1)S(1)}, u32[]{:S(2)}, u32[]{:S(2)}) collective-permute-start(bf16[8,512,256]{2,1,0:T(8,128)(2,1)S(1)} %get-tuple-element.67.act_ref.own), channel_id=1, source_target_pairs={{0,4},{4,8},{8,12},{12,16},{16,20},{20,24},{24,28},{1,5},{5,9},{9,... | collective-permute-start | bytes 6291464 | tf_op jit(solution)/shard_map/ppermute | solution.py:384
  49.6 43.8 %collective-permute-start.16 = (bf16[8,512,256]{2,1,0:T(8,128)(2,1)S(1)}, bf16[8,512,256]{2,1,0:T(8,128)(2,1)S(1)}, u32[]{:S(2)}, u32[]{:S(2)}) collective-permute-start(bf16[8,512,256]{2,1,0:T(8,128)(2,1)S(1)} %get-tuple-element.67.act_ref.own), channel_id=1, source_target_pairs={{4,0},{8,4},{12,8},{16,12},{20,16},{24,20},{28,24},{5,1},{9,5},{13... | collective-permute-start | bytes 6291464 | tf_op jit(solution)/shard_map/ppermute | solution.py:384
  56.5 6.0 %collective-permute-start.10 = (f32[8,2,256]{2,1,0:T(2,128)S(1)}, f32[8,2,256]{2,1,0:T(2,128)S(1)}, u32[]{:S(2)}, u32[]{:S(2)}) collective-permute-start(f32[8,2,256]{2,1,0:T(2,128)S(1)} %get-tuple-element.65.refs_2_), channel_id=1, source_target_pairs={{0,2},{1,3},{2,0},{3,1},{4,6},{5,7},{6,4},{7,5},{8,10},{9,11},{10,... | collective-permute-start | bytes 49160 | tf_op jit(solution)/shard_map/ppermute | solution.py:389
  59.3 5.5 %collective-permute-start.11 = (f32[8,2,256]{2,1,0:T(2,128)S(1)}, f32[8,2,256]{2,1,0:T(2,128)S(1)}, u32[]{:S(2)}, u32[]{:S(2)}) collective-permute-start(f32[8,2,256]{2,1,0:T(2,128)S(1)} %get-tuple-element.65.refs_2_), channel_id=1, source_target_pairs={{0,3},{1,2},{2,1},{3,0},{4,7},{5,6},{6,5},{7,4},{8,11},{9,10},{10,... | collective-permute-start | bytes 49160 | tf_op jit(solution)/shard_map/ppermute | solution.py:389
  60.7 4.2 %collective-permute-start.9 = (f32[8,2,256]{2,1,0:T(2,128)S(1)}, f32[8,2,256]{2,1,0:T(2,128)S(1)}, u32[]{:S(2)}, u32[]{:S(2)}) collective-permute-start(f32[8,2,256]{2,1,0:T(2,128)S(1)} %get-tuple-element.65.refs_2_), channel_id=1, source_target_pairs={{0,1},{1,0},{2,3},{3,2},{4,5},{5,4},{6,7},{7,6},{8,9},{9,8},{10,11... | collective-permute-start | bytes 49160 | tf_op jit(solution)/shard_map/ppermute | solution.py:389
  69.5 8.1 %collective-permute-start.12 = (bf16[8,1,64,256]{3,2,1,0:T(8,128)(2,1)S(1)}, bf16[8,1,64,256]{3,2,1,0:T(8,128)(2,1)S(1)}, u32[]{:S(2)}, u32[]{:S(2)}) collective-permute-start(bf16[8,1,64,256]{3,2,1,0:T(8,128)(2,1)S(1)} %get-tuple-element.69), channel_id=1, source_target_pairs={{0,1},{1,2},{2,3},{4,5},{5,6},{6,7},{8,9},{9,10},{10,11},{12,13},{... | collective-permute-start | bytes 786440 | tf_op jit(solution)/shard_map/ppermute | solution.py:384
  71.1 8.9 %collective-permute-start.13 = (bf16[8,1,64,256]{3,2,1,0:T(8,128)(2,1)S(1)}, bf16[8,1,64,256]{3,2,1,0:T(8,128)(2,1)S(1)}, u32[]{:S(2)}, u32[]{:S(2)}) collective-permute-start(bf16[8,1,64,256]{3,2,1,0:T(8,128)(2,1)S(1)} %get-tuple-element.70), channel_id=1, source_target_pairs={{1,0},{2,1},{3,2},{5,4},{6,5},{7,6},{9,8},{10,9},{11,10},{13,12},{... | collective-permute-start | bytes 786440 | tf_op jit(solution)/shard_map/ppermute | solution.py:384
  80.4 2.4 %collective-permute-start.14 = (bf16[4,4,32,768]{3,2,1,0:T(8,128)(2,1)S(1)}, bf16[4,4,32,768]{3,2,1,0:T(8,128)(2,1)S(1)}, u32[]{:S(2)}, u32[]{:S(2)}) collective-permute-start(bf16[4,4,32,768]{3,2,1,0:T(8,128)(2,1)S(1)} %get-tuple-element.73), channel_id=1, source_target_pairs={{0,4},{4,0},{8,12},{12,8},{16,20},{20,16},{24,28},{28,24},{1,5},{5... | collective-permute-start | bytes 2359304 | tf_op jit(solution)/shard_map/ppermute | solution.py:490
  82.9 19.3 %collective-permute-start.17 = (bf16[4,32,768]{2,1,0:T(8,128)(2,1)S(1)}, bf16[4,32,768]{2,1,0:T(8,128)(2,1)S(1)}, u32[]{:S(2)}, u32[]{:S(2)}) collective-permute-start(bf16[4,32,768]{2,1,0:T(8,128)(2,1)S(1)} %get-tuple-element.80), channel_id=1, source_target_pairs={{0,8},{4,12},{8,0},{12,4},{16,24},{20,28},{24,16},{28,20},{1,9},{5... | collective-permute-start | bytes 589832 | tf_op jit(solution)/shard_map/ppermute | solution.py:495
  83.4 18.7 %collective-permute-start.18 = (bf16[4,32,768]{2,1,0:T(8,128)(2,1)S(1)}, bf16[4,32,768]{2,1,0:T(8,128)(2,1)S(1)}, u32[]{:S(2)}, u32[]{:S(2)}) collective-permute-start(bf16[4,32,768]{2,1,0:T(8,128)(2,1)S(1)} %get-tuple-element.81), channel_id=1, source_target_pairs={{0,16},{4,20},{8,24},{12,28},{16,0},{20,4},{24,8},{28,12},{1,17},{... | collective-permute-start | bytes 589832 | tf_op jit(solution)/shard_map/ppermute | solution.py:495
  84.5 17.6 %collective-permute-start.19 = (bf16[4,32,768]{2,1,0:T(8,128)(2,1)S(1)}, bf16[4,32,768]{2,1,0:T(8,128)(2,1)S(1)}, u32[]{:S(2)}, u32[]{:S(2)}) collective-permute-start(bf16[4,32,768]{2,1,0:T(8,128)(2,1)S(1)} %get-tuple-element.82), channel_id=1, source_target_pairs={{0,24},{4,28},{8,16},{12,20},{16,8},{20,12},{24,0},{28,4},{1,25},{... | collective-permute-start | bytes 589832 | tf_op jit(solution)/shard_map/ppermute | solution.py:495
  102.3 9.4 %collective-permute-start.20 = (bf16[32,768]{1,0:T(8,128)(2,1)S(1)}, bf16[32,768]{1,0:T(8,128)(2,1)S(1)}, u32[]{:S(2)}, u32[]{:S(2)}) collective-permute-start(bf16[32,768]{1,0:T(8,128)(2,1)S(1)} %get-tuple-element.89), channel_id=1, source_target_pairs={{0,1},{1,0},{2,3},{3,2},{4,5},{5,4},{6,7},{7,6},{8,9},{9,8},{10,11... | collective-permute-start | bytes 147464 | tf_op jit(solution)/shard_map/ppermute | solution.py:507
  102.8 8.8 %collective-permute-start.21 = (bf16[32,768]{1,0:T(8,128)(2,1)S(1)}, bf16[32,768]{1,0:T(8,128)(2,1)S(1)}, u32[]{:S(2)}, u32[]{:S(2)}) collective-permute-start(bf16[32,768]{1,0:T(8,128)(2,1)S(1)} %get-tuple-element.90), channel_id=1, source_target_pairs={{0,2},{1,3},{2,0},{3,1},{4,6},{5,7},{6,4},{7,5},{8,10},{9,11},{10,... | collective-permute-start | bytes 147464 | tf_op jit(solution)/shard_map/ppermute | solution.py:507
  104.4 7.3 %collective-permute-start.22 = (bf16[32,768]{1,0:T(8,128)(2,1)S(1)}, bf16[32,768]{1,0:T(8,128)(2,1)S(1)}, u32[]{:S(2)}, u32[]{:S(2)}) collective-permute-start(bf16[32,768]{1,0:T(8,128)(2,1)S(1)} %get-tuple-element.91), channel_id=1, source_target_pairs={{0,3},{1,2},{2,1},{3,0},{4,7},{5,6},{6,5},{7,4},{8,11},{9,10},{10,... | collective-permute-start | bytes 147464 | tf_op jit(solution)/shard_map/ppermute | solution.py:507
  111.7 4.5 %collective-permute-start.23 = (bf16[32,768]{1,0:T(8,128)(2,1)S(1)}, bf16[32,768]{1,0:T(8,128)(2,1)S(1)}, u32[]{:S(2)}, u32[]{:S(2)}) collective-permute-start(bf16[32,768]{1,0:T(8,128)(2,1)S(1)} %line_sum.1.refs_0_), channel_id=1, source_target_pairs={{0,1},{1,0},{2,3},{3,2},{4,5},{5,4},{6,7},{7,6},{8,9},{9,8},{10,11... | collective-permute-start | bytes 147464 | tf_op jit(solution)/shard_map/ppermute | solution.py:517
  111.8 5.4 %collective-permute-start.24 = (bf16[32,768]{1,0:T(8,128)(2,1)S(1)}, bf16[32,768]{1,0:T(8,128)(2,1)S(1)}, u32[]{:S(2)}, u32[]{:S(2)}) collective-permute-start(bf16[32,768]{1,0:T(8,128)(2,1)S(1)} %line_sum.1.refs_0_), channel_id=1, source_target_pairs={{0,2},{1,3},{2,0},{3,1},{4,6},{5,7},{6,4},{7,5},{8,10},{9,11},{10,... | collective-permute-start | bytes 147464 | tf_op jit(solution)/shard_map/ppermute | solution.py:517
  113.8 5.9 %collective-permute-start.25 = (bf16[32,768]{1,0:T(8,128)(2,1)S(1)}, bf16[32,768]{1,0:T(8,128)(2,1)S(1)}, u32[]{:S(2)}, u32[]{:S(2)}) collective-permute-start(bf16[32,768]{1,0:T(8,128)(2,1)S(1)} %line_sum.1.refs_0_), channel_id=1, source_target_pairs={{0,3},{1,2},{2,1},{3,0},{4,7},{5,6},{6,5},{7,4},{8,11},{9,10},{10,... | collective-permute-start | bytes 147464 | tf_op jit(solution)/shard_map/ppermute | solution.py:517
  119.8 8.5 %collective-permute-start.26 = (bf16[4,32,768]{2,1,0:T(8,128)(2,1)S(1)}, bf16[4,32,768]{2,1,0:T(8,128)(2,1)S(1)}, u32[]{:S(2)}, u32[]{:S(2)}) collective-permute-start(bf16[4,32,768]{2,1,0:T(8,128)(2,1)S(1)} %line_place.1.refs_0_), channel_id=1, source_target_pairs={{0,8},{4,12},{8,0},{12,4},{16,24},{20,28},{24,16},{28,20},{1,9},{5... | collective-permute-start | bytes 589832 | tf_op jit(solution)/shard_map/ppermute | solution.py:521
  122.9 8.3 %collective-permute-start.27 = (bf16[4,32,768]{2,1,0:T(8,128)(2,1)S(1)}, bf16[4,32,768]{2,1,0:T(8,128)(2,1)S(1)}, u32[]{:S(2)}, u32[]{:S(2)}) collective-permute-start(bf16[4,32,768]{2,1,0:T(8,128)(2,1)S(1)} %line_place.1.refs_0_), channel_id=1, source_target_pairs={{0,16},{4,20},{8,24},{12,28},{16,0},{20,4},{24,8},{28,12},{1,17},{... | collective-permute-start | bytes 589832 | tf_op jit(solution)/shard_map/ppermute | solution.py:521
  124.9 8.1 %collective-permute-start.28 = (bf16[4,32,768]{2,1,0:T(8,128)(2,1)S(1)}, bf16[4,32,768]{2,1,0:T(8,128)(2,1)S(1)}, u32[]{:S(2)}, u32[]{:S(2)}) collective-permute-start(bf16[4,32,768]{2,1,0:T(8,128)(2,1)S(1)} %line_place.1.refs_0_), channel_id=1, source_target_pairs={{0,24},{4,28},{8,16},{12,20},{16,8},{20,12},{24,0},{28,4},{1,25},{... | collective-permute-start | bytes 589832 | tf_op jit(solution)/shard_map/ppermute | solution.py:521
  133.1 2.4 %collective-permute-start.29 = (bf16[4,4,32,768]{3,2,1,0:T(8,128)(2,1)S(1)}, bf16[4,4,32,768]{3,2,1,0:T(8,128)(2,1)S(1)}, u32[]{:S(2)}, u32[]{:S(2)}) collective-permute-start(bf16[4,4,32,768]{3,2,1,0:T(8,128)(2,1)S(1)} %plane_place.1.mine_ref), channel_id=1, source_target_pairs={{0,4},{4,0},{8,12},{12,8},{16,20},{20,16},{24,28},{28,24},{1,5},{5... | collective-permute-start | bytes 2359304 | tf_op jit(solution)/shard_map/ppermute | solution.py:527

commit v3 on v2

--- a/solution.py
+++ b/solution.py
@@ -109,29 +109,34 @@
 def gather_taps(clip_ref, dil_ref, local, own, nxt, prv, corner, cat_ref, at, up_slot):
     frames, pixels, channels = own.shape
     later, earlier, used = slot_sources(clip_ref, dil_ref, local, frames)
-    me, half = lax.axis_index("tm"), frames // 2
+    me = lax.axis_index("tm")
 
     def put(slot, ref, index):
         cat_ref[pl.ds(at, pixels), slot * channels : (slot + 1) * channels] = ref[index]
 
     def clear(slot):
         cat_ref[pl.ds(at, pixels), slot * channels : (slot + 1) * channels] = jnp.zeros((pixels, channels), BF16)
+
+    def put_from(slot, pieces, wanted, index):
+        start = 0
+        for ref in pieces:
+            count = ref.shape[0]
+            here = wanted & (index >= start) & (index < start + count)
+            pl.when(here)(functools.partial(put, slot, ref, jnp.clip(index - start, 0, count - 1)))
+            start += count
 
     for slot, (index, which), other, shift, turn in (
         (up_slot, later, nxt, -frames, 3),
         (2 - up_slot, earlier, prv, frames, 4),
     ):
-        beyond = which == 2
-        there = jnp.clip(index + shift, 0, frames - 1)
         pl.when(which == 0)(functools.partial(clear, slot))
         pl.when(which == 1)(functools.partial(put, slot, own, jnp.clip(index, 0, frames - 1)))
+        there = jnp.clip(index + shift, 0, frames - 1)
+        beyond = which == 2
         if corner:
-            by_corner = beyond & (me == turn)
-            low, high = by_corner & (there < half), by_corner & (there >= half)
-            pl.when(low)(functools.partial(put, slot, corner[0], jnp.minimum(there, half - 1)))
-            pl.when(high)(functools.partial(put, slot, corner[1], jnp.maximum(there - half, 0)))
+            put_from(slot, corner, beyond & (me == turn), there)
             beyond = beyond & (me != turn)
-        pl.when(beyond)(functools.partial(put, slot, other, there))
+        put_from(slot, other, beyond, there)
     pl.when(used)(functools.partial(put, 1, own, local))
     pl.when(jnp.logical_not(used))(functools.partial(clear, 1))
 
@@ -173,8 +178,8 @@
 
 def act_kernel(n, entries, group_size, clip_ref, *refs):
     parts, refs = refs[:n], refs[n:]
-    conv_ref, gain_ref, shift_ref, act_ref, normed_ref, slope_ref = refs
-    frames = conv_ref.shape[0]
+    conv_ref, gain_ref, shift_ref, act_ref, early_ref, late_ref, normed_ref, slope_ref = refs
+    frames, ahead = conv_ref.shape[0], early_ref.shape[0]
     first = lax.axis_index("tm") * frames
     filled = clip_ref[0] + clip_ref[1]
     half_gain, half_shift = 0.5 * gain_ref[...], 0.5 * shift_ref[...]
@@ -183,7 +188,17 @@
         mean, inv = mean_and_inv(parts, f, entries, group_size)
         normed = (conv_ref[f] - mean) * inv
         h, rise, slope = silu_parts(normed, half_gain, half_shift)
-        act_ref[f] = jnp.where(first + f < filled, h * rise, 0.0).astype(BF16)
+        act = jnp.where(first + f < filled, h * rise, 0.0).astype(BF16)
+        act_ref[f] = act
+
+        @pl.when(f < ahead)
+        def _():
+            early_ref[jnp.minimum(f, ahead - 1)] = act
+
+        @pl.when(f >= ahead)
+        def _():
+            late_ref[jnp.maximum(f - ahead, 0)] = act
+
         normed_ref[f] = normed.astype(BF16)
         slope_ref[f] = slope.astype(BF16)
 
@@ -222,7 +237,7 @@
         rows = pl.ds(pl.multiple_of(2 * pair * pixels, 2 * pixels), 2 * pixels)
         for b in range(2):
             at = pl.multiple_of((2 * pair + b) * pixels, pixels)
-            gather_taps(clip_ref, dil_ref, 2 * pair + b, own, nxt, prv, corner, cat_ref, at, 0)
+            gather_taps(clip_ref, dil_ref, 2 * pair + b, own, (nxt,), (prv,), corner, cat_ref, at, 0)
         grad_act = dot(cat_ref[rows], tw_ref[...]).astype(BF16)
         for b in range(2):
             f = 2 * pair + b
@@ -304,13 +319,13 @@
     loop(frames // 2, body)
 
 
-def out_kernel(clip_ref, dil_ref, own, nxt, prv, tw_ref, x_ref, out_ref, cat_ref):
+def out_kernel(clip_ref, dil_ref, own, nxt_a, nxt_b, prv_a, prv_b, tw_ref, x_ref, out_ref, cat_ref):
     frames, rows, width, channels = x_ref.shape
     pixels = rows * width
 
     def body(pair):
         for b in range(2):
-            gather_taps(clip_ref, dil_ref, 2 * pair + b, own, nxt, prv, (), cat_ref, b * pixels, 2)
+            gather_taps(clip_ref, dil_ref, 2 * pair + b, own, (nxt_a, nxt_b), (prv_a, prv_b), (), cat_ref, b * pixels, 2)
         temporal_out = dot(cat_ref[...], tw_ref[...]).astype(BF16).astype(F32)
         for b in range(2):
             one = temporal_out[b * pixels : (b + 1) * pixels].reshape(rows, width, channels)
@@ -444,11 +459,12 @@
         0, 8 * big, [pltpu.VMEM((pixels, 3 * channels), BF16)],
     )
     x_turned, *parts = lax.optimization_barrier((x_turned, *parts))
-    act, normed, slope = call(
+    ahead = (3 * frames) // 4
+    act, act_early, act_late, normed, slope = call(
         functools.partial(act_kernel, len(parts), entries, group_size), "activation",
-        [clip_frames, *parts, conv_out, gain, shift], [shape(per_px, BF16)] * 3, 10 * big, 10 * big,
-    )
-    act_prev, act_next = neighbours("tm", act, act)
+        [clip_frames, *parts, conv_out, gain, shift], [shape((k, pixels, channels), BF16) for k in (frames, ahead, frames - ahead, frames, frames)], 10 * big, 10 * big,
+    )
+    act_prev, act_next = neighbours("tm", act_early, act_early)
 
     grad_act, cot_cat, grad_sums = call(
         functools.partial(grad_act_kernel, len(cot_corner)), "grad_activation",
@@ -505,12 +521,8 @@
         [shape((block, lanes), F32)] + [shape((block, lanes), BF16)] * (n - 1), 0, big,
     )
     gots = [lax.ppermute(x, "space", other_plane(s)) for s, x in enumerate(sends, 1)]
-    out_frames = call(
-        out_kernel, "temporal_forward",
-        [clip_frames, dilation, act, act_next, act_prev, temporal.reshape(3 * channels, channels), frames_in],
-        shape(frames_in.shape, BF16), 6 * big * channels, 10 * big, [windows],
-    )
-    own, out_frames = lax.optimization_barrier((own, out_frames))
+    gots[0], act_late = lax.optimization_barrier((gots[0], act_late))
+    late_prev, late_next = neighbours("tm", act_late, act_late)
     own = call(
         functools.partial(sum_kernel, n - 1), "line_sum", [own, *gots], shape((block, lanes), BF16), 0, big
     )
@@ -521,6 +533,12 @@
     gots = [lax.ppermute(own, "tm", other_chip(s)) for s in range(1, chips)]
 
 
+    out_frames = call(
+        out_kernel, "temporal_forward",
+        [clip_frames, dilation, act, act_next, late_next, act_prev, late_prev, temporal.reshape(3 * channels, channels), frames_in],
+        shape(frames_in.shape, BF16), 6 * big * channels, 10 * big, [windows],
+    )
+    own, out_frames = lax.optimization_barrier((own, out_frames))
     own = call(
         functools.partial(place_kernel, "tm", 1), "plane_place", [own, *gots], shape((chips, n, block, lanes), BF16), 0, big
     )

time: 138 us -> 134 us (0.971)
  waiting for transfers between devices: 38 us -> 33.4 us
    ppermute x3, waiting for transfers between devices: 0.01 us -> 8.13 us  [per_device(): lax.ppermute(x, 'space', other_plane(s))]
    ppermute x3, waiting for transfers between devices: 8.72 us -> 1.62 us  [per_device(): lax.ppermute(x, 'tm', other_chip(s))]
    ppermute x8 -> x10, starting transfers between devices: 16.6 us -> 21.7 us  [neighbours(): return (lax.ppermute(high, axis, up), lax.ppermute(low, axis, down))]
    ppermute x3, waiting for transfers between devices: 6.74 us -> 2.01 us  [per_device(): gots = [lax.ppermute(own, 'tm', other_chip(s)) for s in range(1, chips)]]
    ppermute x3, starting transfers between devices: 6.48 us -> 3.55 us  [per_device(): gots = [lax.ppermute(own, 'tm', other_chip(s)) for s in range(1, chips)]]
    ppermute x2, starting transfers between devices: 4.27 us -> 2.73 us  [spread_sums(): got = lax.ppermute(part, axis, [(i, i ^ step) for i in range(size)])]
    ppermute x8 -> x10, waiting for transfers between devices: 8.96 us -> 9.15 us  [neighbours(): return (lax.ppermute(high, axis, up), lax.ppermute(low, axis, down))]
  transfers between devices with their start and end apart: 30 -> 32, of which waited for: 14 -> 17; matrix products, arithmetic and copies ran while one was open for 1% -> 1% of each run, Pallas kernels for 31% -> 32%
where the time goes in v3:
time: 134 us; the launch traced here: 133 us
  starting transfers between devices  51.1 us (38%)
  Pallas kernels  45.1 us (34%)
  waiting for transfers between devices  33.4 us (25%)
  local copies, waits for them, and re-layouts  2.8 us (2%)
    pallas_call x17, Pallas kernels, call(): pl.pallas_call(kernel, in_specs=[smem if x.dtype == jnp.int32 else vmem f...  45.1 us
    ppermute x10, starting transfers between devices, neighbours(): return (lax.ppermute(high, axis, up), lax.ppermute(low, axis, down))  21.7 us
    ppermute x10, waiting for transfers between devices, neighbours(): return (lax.ppermute(high, axis, up), lax.ppermute(low, axis, down))  9.15 us
    ppermute x3, waiting for transfers between devices, per_device(): lax.ppermute(x, 'space', other_plane(s))  8.13 us
    ppermute x3, starting transfers between devices, per_device(): gots = [lax.ppermute(own, 'space', other_plane(s)) for s in range(1, n)]  4.45 us
    ppermute x1, starting transfers between devices, per_device(): cot_corner.append(lax.ppermute(relayed, 'tm', [(7, 4), (0, 3)]))  4.41 us
    ppermute x3, starting transfers between devices, spread_parts(): lax.ppermute(part, axis, [(i, i ^ s) for i in range(size)])  4.21 us
    ppermute x3, starting transfers between devices, per_device(): lax.ppermute(x, 'space', other_plane(s))  4.17 us
  transfers between devices with their start and end apart: 32, of which 17 were waited for; matrix products, arithmetic and copies ran while one was open for 1% of the time, Pallas kernels for 32%

profile of v3, /device:TPU:0, one launch (start us, length us, event | category | flops | bytes accessed | tf_op | source)
XLA Modules:
  0.0 133.3 jit_solution(6410757574767316571)
XLA Ops:
  0.6 1.1 fusion.1
  1.7 1.6 %collective-permute-start.5 = (bf16[8,512,256]{2,1,0:T(8,128)(2,1)}, bf16[8,512,256]{2,1,0:T(8,128)(2,1)S(1)}, u32[]{:S(2)}, u32[]{:S(2)}) collective-permute-start(bf16[8,512,256]{2,1,0:T(8,128)(2,1)} %bitcast.6), channel_id=1, source_target_pairs={{4,0},{8,4},{12,8},{20,16},{24,20},{28,24},{5,1},{9,5},{13,9},{21,... | collective-permute-start | bytes 6291464 | tf_op jit(solution)/shard_map/ppermute | solution.py:399
  3.3 3.2 %collective-permute-start.6 = (bf16[8,512,256]{2,1,0:T(8,128)(2,1)}, bf16[8,512,256]{2,1,0:T(8,128)(2,1)S(1)}, u32[]{:S(2)}, u32[]{:S(2)}) collective-permute-start(bf16[8,512,256]{2,1,0:T(8,128)(2,1)} %bitcast.7), channel_id=1, source_target_pairs={{0,4},{4,8},{8,12},{16,20},{20,24},{24,28},{1,5},{5,9},{9,13},{17,... | collective-permute-start | bytes 6291464 | tf_op jit(solution)/shard_map/ppermute | solution.py:399
  6.5 4.9 %collective-permute-start = (bf16[8,1,64,256]{3,2,1,0:T(8,128)(2,1)S(1)}, bf16[8,1,64,256]{3,2,1,0:T(8,128)(2,1)S(1)}, u32[]{:S(2)}, u32[]{:S(2)}) collective-permute-start(bf16[8,1,64,256]{3,2,1,0:T(8,128)(2,1)S(1)} %get-tuple-element.53), channel_id=1, source_target_pairs={{0,1},{1,2},{2,3},{4,5},{5,6},{6,7},{8,9},{9,10},{10,11},{12,13},{... | collective-permute-start | bytes 786440 | tf_op jit(solution)/shard_map/ppermute | solution.py:399
  11.4 1.3 collective-permute-start.1
  12.7 1.7 %fusion = (bf16[4,8,64,256]{3,2,1,0:T(8,128)(2,1)S(1)}, bf16[4,8,64,256]{3,2,1,0:T(8,128)(2,1)S(1)}) fusion(bf16[8,8,64,256]{3,2,1,0:T(8,128)(2,1)} %cot_ref.1), kind=kLoop, calls=%fused_computation | loop fusion | bytes 4194304 | tf_op jit(solution)/shard_map/slice | solution.py:438
  14.4 1.4 %collective-permute-start.3 = (bf16[4,512,256]{2,1,0:T(8,128)(2,1)S(1)}, bf16[4,512,256]{2,1,0:T(8,128)(2,1)S(1)}, u32[]{:S(2)}, u32[]{:S(2)}) collective-permute-start(bf16[4,512,256]{2,1,0:T(8,128)(2,1)S(1)} %bitcast.13), channel_id=1, source_target_pairs={{12,28},{16,0},{13,29},{17,1},{14,30},{18,2},{15,31},{19,3}} | collective-permute-start | bytes 3145736 | tf_op jit(solution)/shard_map/ppermute | solution.py:439
  15.8 2.2 %collective-permute-done.above_ref = bf16[8,1,64,256]{3,2,1,0:T(8,128)(2,1)S(1)} collective-permute-done((bf16[8,1,64,256]{3,2,1,0:T(8,128)(2,1)S(1)}, bf16[8,1,64,256]{3,2,1,0:T(8,128)(2,1)S(1)}, u32[]{:S(2)}, u32[]{:S(2)}) %collective-permute-start) | collective-permute-done | bytes 262176 | tf_op jit(solution)/shard_map/ppermute | solution.py:399
  18.1 4.1 %collective-permute-done.1.below_ref = bf16[8,1,64,256]{3,2,1,0:T(8,128)(2,1)S(1)} collective-permute-done((bf16[8,1,64,256]{3,2,1,0:T(8,128)(2,1)S(1)}, bf16[8,1,64,256]{3,2,1,0:T(8,128)(2,1)S(1)}, u32[]{:S(2)}, u32[]{:S(2)}) %collective-permute-start.1) | collective-permute-done | bytes 262176 | tf_op jit(solution)/shard_map/ppermute | solution.py:399
  22.2 5.7 %conv_forward.1 = (f32[8,512,256]{2,1,0:T(8,128)S(1)}, f32[8,2,256]{2,1,0:T(2,128)S(1)}) custom-call(bf16[8,8,64,256]{3,2,1,0:T(8,128)(2,1)S(1)} %copy-done, bf16[8,1,64,256]{3,2,1,0:T(8,128)(2,1)S(1)} %collective-permute-done.above_ref, bf16[8,1,64,256]{3,2,1,0:T(8,128)(2,1)S(1)} %collective-permute-done.1.below_ref, bf16[3,3,256,256]{3,2,1,0:T(8,128)(2,1)S(1)} %copy-done.3), custom_call_target="tpu_custom_call" | custom-call | flops 26843545600 | bytes 8388608 | tf_op jit(solution)/shard_map/conv_forward/pallas_call | solution.py:20
  27.9 1.6 %collective-permute-start.2 = (f32[8,2,256]{2,1,0:T(2,128)S(1)}, f32[8,2,256]{2,1,0:T(2,128)S(1)}, u32[]{:S(2)}, u32[]{:S(2)}) collective-permute-start(f32[8,2,256]{2,1,0:T(2,128)S(1)} %get-tuple-element.56), channel_id=1, source_target_pairs={{0,1},{1,0},{2,3},{3,2},{4,5},{5,4},{6,7},{7,6},{8,9},{9,8},{10,11... | collective-permute-start | bytes 49160 | tf_op jit(solution)/shard_map/ppermute | solution.py:413
  29.6 0.7 collective-permute-start.7
  30.3 1.5 %collective-permute-done.2 = f32[8,2,256]{2,1,0:T(2,128)S(1)} collective-permute-done((f32[8,2,256]{2,1,0:T(2,128)S(1)}, f32[8,2,256]{2,1,0:T(2,128)S(1)}, u32[]{:S(2)}, u32[]{:S(2)}) %collective-permute-start.2) | collective-permute-done | bytes 16416 | tf_op jit(solution)/shard_map/ppermute | solution.py:413
  31.8 4.4 %collective-permute-start.8 = (bf16[4,512,256]{2,1,0:T(8,128)(2,1)S(1)}, bf16[4,512,256]{2,1,0:T(8,128)(2,1)S(1)}, u32[]{:S(2)}, u32[]{:S(2)}) collective-permute-start(bf16[4,512,256]{2,1,0:T(8,128)(2,1)S(1)} %collective-permute-done.3), channel_id=1, source_target_pairs={{28,16},{0,12},{29,17},{1,13},{30,18},{2,14},{31,19},{3,15}} | collective-permute-start | bytes 3145736 | tf_op jit(solution)/shard_map/ppermute | solution.py:456
  36.2 1.1 collective-permute-start.4
  37.3 0.5 turn_weights.1
  37.8 2.2 %turned.1.xt_ref = bf16[768,4096]{1,0:T(8,128)(2,1)S(1)} custom-call(bf16[8,8,64,256]{3,2,1,0:T(8,128)(2,1)S(1)} %copy-done, bf16[8,1,64,256]{3,2,1,0:T(8,128)(2,1)S(1)} %collective-permute-done.above_ref, bf16[8,1,64,256]{3,2,1,0:T(8,128)(2,1)S(1)} %collective-permute-done.1.below_ref), custom_call_target="tpu_custom_call" | custom-call | bytes 8388608 | tf_op jit(solution)/shard_map/turned/pallas_call | solution.py:20
  40.0 1.0 collective-permute-done.4.refs_1_
  41.0 6.2 %activation.1 = (bf16[8,512,256]{2,1,0:T(8,128)(2,1)S(1)}, bf16[6,512,256]{2,1,0:T(8,128)(2,1)S(1)}, bf16[2,512,256]{2,1,0:T(8,128)(2,1)S(1)}, bf16[8,512,256]{2,1,0:T(8,128)(2,1)S(1)}, bf16[8,512,256]{2,1,0:T(8,128)(2,1)S(1)}) custom-call(s32[2]{0:T(128)S(1)} %copy-done.4, f32[8,2,256]{2,1,0:T(2,128)S(1)} %add.3.refs_0_, ...), custom_call_target="tpu_custom_call" | custom-call | flops 10485760 | bytes 10485760 | tf_op jit(solution)/shard_map/activation/pallas_call | solution.py:20
  47.2 1.4 %collective-permute-start.15 = (bf16[6,512,256]{2,1,0:T(8,128)(2,1)S(1)}, bf16[6,512,256]{2,1,0:T(8,128)(2,1)S(1)}, u32[]{:S(2)}, u32[]{:S(2)}) collective-permute-start(bf16[6,512,256]{2,1,0:T(8,128)(2,1)S(1)} %get-tuple-element.83), channel_id=1, source_target_pairs={{0,4},{4,8},{8,12},{12,16},{16,20},{20,24},{24,28},{1,5},{5,9},{9,... | collective-permute-start | bytes 4718600 | tf_op jit(solution)/shard_map/ppermute | solution.py:399
  48.7 1.3 collective-permute-start.16
  50.0 0.4 collective-permute-done.8.refs_1_
  50.4 4.2 %grad_activation.1 = (bf16[8,512,256]{2,1,0:T(8,128)(2,1)S(1)}, bf16[4096,768]{1,0:T(8,128)(2,1)S(1)}, f32[8,2,256]{2,1,0:T(2,128)S(1)}) custom-call(s32[2]{0:T(128)S(1)} %copy-done.4, s32[2]{0:T(128)S(1)} %copy-done.5, bf16[8,512,256]{2,1,0:T(8,128)(2,1)S(1)} %bitcast.8, bf16[8,512,256]{2,1,0:T(8,128)(2,1)S(1)} %collective-permute-done.5.nxt, ...), custom_call_target="tpu_custom_call" | custom-call | flops 1610612736 | bytes 16777216 | tf_op jit(solution)/shard_map/grad_activation/pallas_call | solution.py:20
  54.6 0.7 collective-permute-start.10
  55.3 3.1 %collective-permute-start.11 = (f32[8,2,256]{2,1,0:T(2,128)S(1)}, f32[8,2,256]{2,1,0:T(2,128)S(1)}, u32[]{:S(2)}, u32[]{:S(2)}) collective-permute-start(f32[8,2,256]{2,1,0:T(2,128)S(1)} %get-tuple-element.69.refs_2_), channel_id=1, source_target_pairs={{0,3},{1,2},{2,1},{3,0},{4,7},{5,6},{6,5},{7,4},{8,11},{9,10},{10,... | collective-permute-start | bytes 49160 | tf_op jit(solution)/shard_map/ppermute | solution.py:404
  58.3 0.5 collective-permute-start.9
  58.8 1.9 %temporal_grad.1.temporal_ref = f32[256,768]{1,0:T(8,128)S(1)} custom-call(bf16[8,512,256]{2,1,0:T(8,128)(2,1)S(1)} %get-tuple-element.71.act_ref.own, bf16[4096,768]{1,0:T(8,128)(2,1)S(1)} %get-tuple-element.72.cat_ref), custom_call_target="tpu_custom_call" | custom-call | flops 1610612736 | bytes 8388608 | tf_op jit(solution)/shard_map/temporal_grad/pallas_call | solution.py:20
  60.7 0.1 collective-permute-done.11.refs_5_
  60.8 1.2 collective-permute-done.9.refs_3_
  62.1 4.6 %norm_backward.1 = (bf16[8,512,256]{2,1,0:T(8,128)(2,1)S(1)}, bf16[8,1,64,256]{3,2,1,0:T(8,128)(2,1)S(1)}, bf16[8,1,64,256]{3,2,1,0:T(8,128)(2,1)S(1)}, bf16[4096,768]{1,0:T(8,128)(2,1)S(1)}) custom-call(bf16[8,512,256]{2,1,0:T(8,128)(2,1)S(1)} %get-tuple-element.62.refs_3_.normed_ref, bf16[8,512,256]{2,1,0:T(8,128)(2,1)S(1)} %get-tuple-element.63.refs_4_.slope_ref, ...), custom_call_target="tpu_custom_call" | custom-call | bytes 12582912 | tf_op jit(solution)/shard_map/norm_backward/pallas_call | solution.py:20
  66.6 2.4 %collective-permute-start.12 = (bf16[8,1,64,256]{3,2,1,0:T(8,128)(2,1)S(1)}, bf16[8,1,64,256]{3,2,1,0:T(8,128)(2,1)S(1)}, u32[]{:S(2)}, u32[]{:S(2)}) collective-permute-start(bf16[8,1,64,256]{3,2,1,0:T(8,128)(2,1)S(1)} %get-tuple-element.73), channel_id=1, source_target_pairs={{0,1},{1,2},{2,3},{4,5},{5,6},{6,7},{8,9},{9,10},{10,11},{12,13},{... | collective-permute-start | bytes 786440 | tf_op jit(solution)/shard_map/ppermute | solution.py:399
  69.1 1.3 collective-permute-start.13
  70.4 5.1 %weight_grad.1.acc_ref = f32[1024,768]{1,0:T(8,128)S(1)} custom-call(bf16[768,4096]{1,0:T(8,128)(2,1)S(1)} %turned.1.xt_ref, bf16[4096,768]{1,0:T(8,128)(2,1)S(1)} %get-tuple-element.70.moved_ref, f32[256,768]{1,0:T(8,128)S(1)} %temporal_grad.1.temporal_ref), custom_call_target="tpu_custom_call" | custom-call | flops 4831838208 | bytes 12582912 | tf_op jit(solution)/shard_map/weight_grad/pallas_call | solution.py:20
  75.5 2.8 %collective-permute-done.13.below_ref = bf16[8,1,64,256]{3,2,1,0:T(8,128)(2,1)S(1)} collective-permute-done((bf16[8,1,64,256]{3,2,1,0:T(8,128)(2,1)S(1)}, bf16[8,1,64,256]{3,2,1,0:T(8,128)(2,1)S(1)}, u32[]{:S(2)}, u32[]{:S(2)}) %collective-permute-start.13) | collective-permute-done | bytes 262176 | tf_op jit(solution)/shard_map/ppermute | solution.py:399
  78.3 0.4 hand_out.1
  78.7 2.3 %collective-permute-done.14.got_ref = bf16[4,4,32,768]{3,2,1,0:T(8,128)(2,1)S(1)} collective-permute-done((bf16[4,4,32,768]{3,2,1,0:T(8,128)(2,1)S(1)}, bf16[4,4,32,768]{3,2,1,0:T(8,128)(2,1)S(1)}, u32[]{:S(2)}, u32[]{:S(2)}) %collective-permute-start.14) | collective-permute-done | bytes 786464 | tf_op jit(solution)/shard_map/ppermute | solution.py:506
  81.0 0.2 core_sum.1
  81.2 1.1 collective-permute-start.17
  82.2 0.6 collective-permute-start.18
  82.8 1.9 %collective-permute-start.19 = (bf16[4,32,768]{2,1,0:T(8,128)(2,1)S(1)}, bf16[4,32,768]{2,1,0:T(8,128)(2,1)S(1)}, u32[]{:S(2)}, u32[]{:S(2)}) collective-permute-start(bf16[4,32,768]{2,1,0:T(8,128)(2,1)S(1)} %get-tuple-element.87), channel_id=1, source_target_pairs={{0,24},{4,28},{8,16},{12,20},{16,8},{20,12},{24,0},{28,4},{1,25},{... | collective-permute-start | bytes 589832 | tf_op jit(solution)/shard_map/ppermute | solution.py:511
  84.7 7.0 %conv_backward.1 = bf16[8,8,64,256]{3,2,1,0:T(8,128)(2,1)} custom-call(bf16[8,512,256]{2,1,0:T(8,128)(2,1)S(1)} %get-tuple-element.79.g_ref, bf16[8,1,64,256]{3,2,1,0:T(8,128)(2,1)S(1)} %collective-permute-done.12.above_ref, bf16[8,1,64,256]{3,2,1,0:T(8,128)(2,1)S(1)} %collective-permute-done.13.below_ref, bf16[8,8,64,256]{3,2,1,0:T(8,128)(2,1)S(1)} %copy-done.1, ...), custom_call_target="tpu_custom_call" | custom-call | flops 4831838208 | bytes 8388608 | tf_op jit(solution)/shard_map/conv_backward/pallas_call | solution.py:20
  91.7 1.6 %collective-permute-done.18.refs_1_ = bf16[4,32,768]{2,1,0:T(8,128)(2,1)S(1)} collective-permute-done((bf16[4,32,768]{2,1,0:T(8,128)(2,1)S(1)}, bf16[4,32,768]{2,1,0:T(8,128)(2,1)S(1)}, u32[]{:S(2)}, u32[]{:S(2)}) %collective-permute-start.18) | collective-permute-done | bytes 196640 | tf_op jit(solution)/shard_map/ppermute | solution.py:511
  93.3 0.1 plane_sum.1
  93.4 0.9 collective-permute-start.20
  94.3 3.3 %collective-permute-done.20.refs_0_ = bf16[32,768]{1,0:T(8,128)(2,1)S(1)} collective-permute-done((bf16[32,768]{1,0:T(8,128)(2,1)S(1)}, bf16[32,768]{1,0:T(8,128)(2,1)S(1)}, u32[]{:S(2)}, u32[]{:S(2)}) %collective-permute-start.20) | collective-permute-done | bytes 49184 | tf_op jit(solution)/shard_map/ppermute | solution.py:523
  97.6 1.3 collective-permute-start.26
  98.9 3.1 %collective-permute-start.27 = (bf16[2,512,256]{2,1,0:T(8,128)(2,1)S(1)}, bf16[2,512,256]{2,1,0:T(8,128)(2,1)S(1)}, u32[]{:S(2)}, u32[]{:S(2)}) collective-permute-start(bf16[2,512,256]{2,1,0:T(8,128)(2,1)S(1)} %get-tuple-element.95), channel_id=1, source_target_pairs={{0,4},{4,8},{8,12},{12,16},{16,20},{20,24},{24,28},{1,5},{5,9},{9,... | collective-permute-start | bytes 1572872 | tf_op jit(solution)/shard_map/ppermute | solution.py:399
  101.9 2.2 %collective-permute-start.21 = (bf16[32,768]{1,0:T(8,128)(2,1)S(1)}, bf16[32,768]{1,0:T(8,128)(2,1)S(1)}, u32[]{:S(2)}, u32[]{:S(2)}) collective-permute-start(bf16[32,768]{1,0:T(8,128)(2,1)S(1)} %get-tuple-element.92), channel_id=1, source_target_pairs={{0,2},{1,3},{2,0},{3,1},{4,6},{5,7},{6,4},{7,5},{8,10},{9,11},{10,... | collective-permute-start | bytes 147464 | tf_op jit(solution)/shard_map/ppermute | solution.py:523
  104.2 1.1 collective-permute-start.22
  105.2 3.8 %collective-permute-done.21.refs_1_ = bf16[32,768]{1,0:T(8,128)(2,1)S(1)} collective-permute-done((bf16[32,768]{1,0:T(8,128)(2,1)S(1)}, bf16[32,768]{1,0:T(8,128)(2,1)S(1)}, u32[]{:S(2)}, u32[]{:S(2)}) %collective-permute-start.21) | collective-permute-done | bytes 49184 | tf_op jit(solution)/shard_map/ppermute | solution.py:523
  109.0 1.1 collective-permute-done.22.refs_2_
  110.1 0.1 collective-permute-start.23
  110.2 2.2 %collective-permute-start.24 = (bf16[32,768]{1,0:T(8,128)(2,1)S(1)}, bf16[32,768]{1,0:T(8,128)(2,1)S(1)}, u32[]{:S(2)}, u32[]{:S(2)}) collective-permute-start(bf16[32,768]{1,0:T(8,128)(2,1)S(1)} %line_sum.1.refs_0_), channel_id=1, source_target_pairs={{0,2},{1,3},{2,0},{3,1},{4,6},{5,7},{6,4},{7,5},{8,10},{9,11},{10,... | collective-permute-start | bytes 147464 | tf_op jit(solution)/shard_map/ppermute | solution.py:529
  112.4 2.2 %collective-permute-start.25 = (bf16[32,768]{1,0:T(8,128)(2,1)S(1)}, bf16[32,768]{1,0:T(8,128)(2,1)S(1)}, u32[]{:S(2)}, u32[]{:S(2)}) collective-permute-start(bf16[32,768]{1,0:T(8,128)(2,1)S(1)} %line_sum.1.refs_0_), channel_id=1, source_target_pairs={{0,3},{1,2},{2,1},{3,0},{4,7},{5,6},{6,5},{7,4},{8,11},{9,10},{10,... | collective-permute-start | bytes 147464 | tf_op jit(solution)/shard_map/ppermute | solution.py:529
  114.6 1.2 collective-permute-done.24.refs_2_
  115.8 2.5 %collective-permute-done.25.refs_3_ = bf16[32,768]{1,0:T(8,128)(2,1)S(1)} collective-permute-done((bf16[32,768]{1,0:T(8,128)(2,1)S(1)}, bf16[32,768]{1,0:T(8,128)(2,1)S(1)}, u32[]{:S(2)}, u32[]{:S(2)}) %collective-permute-start.25) | collective-permute-done | bytes 49184 | tf_op jit(solution)/shard_map/ppermute | solution.py:529
  118.3 1.0 collective-permute-start.28
  119.3 0.8 collective-permute-start.29
  120.2 1.7 %collective-permute-start.30 = (bf16[4,32,768]{2,1,0:T(8,128)(2,1)S(1)}, bf16[4,32,768]{2,1,0:T(8,128)(2,1)S(1)}, u32[]{:S(2)}, u32[]{:S(2)}) collective-permute-start(bf16[4,32,768]{2,1,0:T(8,128)(2,1)S(1)} %line_place.1.refs_0_), channel_id=1, source_target_pairs={{0,24},{4,28},{8,16},{12,20},{16,8},{20,12},{24,0},{28,4},{1,25},{... | collective-permute-start | bytes 589832 | tf_op jit(solution)/shard_map/ppermute | solution.py:533
  121.9 5.2 %temporal_forward.1 = bf16[8,8,64,256]{3,2,1,0:T(8,128)(2,1)} custom-call(s32[2]{0:T(128)S(1)} %copy-done.4, s32[2]{0:T(128)S(1)} %copy-done.5, bf16[8,512,256]{2,1,0:T(8,128)(2,1)S(1)} %get-tuple-element.71.act_ref.own, bf16[6,512,256]{2,1,0:T(8,128)(2,1)S(1)} %collective-permute-done.16.nxt_a, bf16[2,512,256]{2,1,0:T(8,128)(2,1)S(1)} %collective-permute-done.26.nxt_b, ...), custom_call_target="tpu_custom_call" | custom-call | flops 1610612736 | bytes 10485760 | tf_op jit(solution)/shard_map/temporal_forward/pallas_call | solution.py:20
  127.0 2.0 %collective-permute-done.29.refs_2_ = bf16[4,32,768]{2,1,0:T(8,128)(2,1)S(1)} collective-permute-done((bf16[4,32,768]{2,1,0:T(8,128)(2,1)S(1)}, bf16[4,32,768]{2,1,0:T(8,128)(2,1)S(1)}, u32[]{:S(2)}, u32[]{:S(2)}) %collective-permute-start.29) | collective-permute-done | bytes 196640 | tf_op jit(solution)/shard_map/ppermute | solution.py:533
  129.1 0.1 collective-permute-start.31
  129.2 2.3 %collective-permute-done.31.got_ref = bf16[4,4,32,768]{3,2,1,0:T(8,128)(2,1)S(1)} collective-permute-done((bf16[4,4,32,768]{3,2,1,0:T(8,128)(2,1)S(1)}, bf16[4,4,32,768]{3,2,1,0:T(8,128)(2,1)S(1)}, u32[]{:S(2)}, u32[]{:S(2)}) %collective-permute-start.31) | collective-permute-done | bytes 786464 | tf_op jit(solution)/shard_map/ppermute | solution.py:545
  131.5 1.9 %finish.1 = (f32[3,3,256,256]{3,2,1,0:T(8,128)}, f32[3,256,256]{2,1,0:T(8,128)}) custom-call(bf16[4,4,32,768]{3,2,1,0:T(8,128)(2,1)S(1)} %plane_place.1.mine_ref, bf16[4,4,32,768]{3,2,1,0:T(8,128)(2,1)S(1)} %collective-permute-done.31.got_ref), custom_call_target="tpu_custom_call" | custom-call | bytes 4194304 | tf_op jit(solution)/shard_map/finish/pallas_call | solution.py:20
  (36 shorter events, 0.3 us)
Async XLA Ops:
  1.7 20.5 %copy-start = (bf16[8,8,64,256]{3,2,1,0:T(8,128)(2,1)S(1)}, bf16[8,8,64,256]{3,2,1,0:T(8,128)(2,1)}, u32[]{:S(2)}) copy-start(bf16[8,8,64,256]{3,2,1,0:T(8,128)(2,1)} %x_ref.5) | copy-start | bytes 6291460
  1.7 20.5 %copy-start.3 = (bf16[3,3,256,256]{3,2,1,0:T(8,128)(2,1)S(1)}, bf16[3,3,256,256]{3,2,1,0:T(8,128)(2,1)}, u32[]{:S(2)}) copy-start(bf16[3,3,256,256]{3,2,1,0:T(8,128)(2,1)} %spatial_ref.1) | copy-start | bytes 3538948
  1.7 48.6 %collective-permute-start.5 = (bf16[8,512,256]{2,1,0:T(8,128)(2,1)}, bf16[8,512,256]{2,1,0:T(8,128)(2,1)S(1)}, u32[]{:S(2)}, u32[]{:S(2)}) collective-permute-start(bf16[8,512,256]{2,1,0:T(8,128)(2,1)} %bitcast.6), channel_id=1, source_target_pairs={{4,0},{8,4},{12,8},{20,16},{24,20},{28,24},{5,1},{9,5},{13,9},{21,... | collective-permute-start | bytes 6291464 | tf_op jit(solution)/shard_map/ppermute | solution.py:399
  3.3 47.1 %collective-permute-start.6 = (bf16[8,512,256]{2,1,0:T(8,128)(2,1)}, bf16[8,512,256]{2,1,0:T(8,128)(2,1)S(1)}, u32[]{:S(2)}, u32[]{:S(2)}) collective-permute-start(bf16[8,512,256]{2,1,0:T(8,128)(2,1)} %bitcast.7), channel_id=1, source_target_pairs={{0,4},{4,8},{8,12},{16,20},{20,24},{24,28},{1,5},{5,9},{9,13},{17,... | collective-permute-start | bytes 6291464 | tf_op jit(solution)/shard_map/ppermute | solution.py:399
  6.5 11.6 %collective-permute-start = (bf16[8,1,64,256]{3,2,1,0:T(8,128)(2,1)S(1)}, bf16[8,1,64,256]{3,2,1,0:T(8,128)(2,1)S(1)}, u32[]{:S(2)}, u32[]{:S(2)}) collective-permute-start(bf16[8,1,64,256]{3,2,1,0:T(8,128)(2,1)S(1)} %get-tuple-element.53), channel_id=1, source_target_pairs={{0,1},{1,2},{2,3},{4,5},{5,6},{6,7},{8,9},{9,10},{10,11},{12,13},{... | collective-permute-start | bytes 786440 | tf_op jit(solution)/shard_map/ppermute | solution.py:399
  11.4 10.8 %collective-permute-start.1 = (bf16[8,1,64,256]{3,2,1,0:T(8,128)(2,1)S(1)}, bf16[8,1,64,256]{3,2,1,0:T(8,128)(2,1)S(1)}, u32[]{:S(2)}, u32[]{:S(2)}) collective-permute-start(bf16[8,1,64,256]{3,2,1,0:T(8,128)(2,1)S(1)} %get-tuple-element.54), channel_id=1, source_target_pairs={{1,0},{2,1},{3,2},{5,4},{6,5},{7,6},{9,8},{10,9},{11,10},{13,12},{... | collective-permute-start | bytes 786440 | tf_op jit(solution)/shard_map/ppermute | solution.py:399
  14.4 22.9 %copy-start.2 = (bf16[3,256,256]{2,1,0:T(8,128)(2,1)S(1)}, bf16[3,256,256]{2,1,0:T(8,128)(2,1)}, u32[]{:S(2)}) copy-start(bf16[3,256,256]{2,1,0:T(8,128)(2,1)} %temporal_ref.1) | copy-start | bytes 1179652
  14.4 17.3 %collective-permute-start.3 = (bf16[4,512,256]{2,1,0:T(8,128)(2,1)S(1)}, bf16[4,512,256]{2,1,0:T(8,128)(2,1)S(1)}, u32[]{:S(2)}, u32[]{:S(2)}) collective-permute-start(bf16[4,512,256]{2,1,0:T(8,128)(2,1)S(1)} %bitcast.13), channel_id=1, source_target_pairs={{12,28},{16,0},{13,29},{17,1},{14,30},{18,2},{15,31},{19,3}} | collective-permute-start | bytes 3145736 | tf_op jit(solution)/shard_map/ppermute | solution.py:439
  27.9 3.8 %collective-permute-start.2 = (f32[8,2,256]{2,1,0:T(2,128)S(1)}, f32[8,2,256]{2,1,0:T(2,128)S(1)}, u32[]{:S(2)}, u32[]{:S(2)}) collective-permute-start(f32[8,2,256]{2,1,0:T(2,128)S(1)} %get-tuple-element.56), channel_id=1, source_target_pairs={{0,1},{1,0},{2,3},{3,2},{4,5},{5,4},{6,7},{7,6},{8,9},{9,8},{10,11... | collective-permute-start | bytes 49160 | tf_op jit(solution)/shard_map/ppermute | solution.py:413
  29.6 19.1 %collective-permute-start.7 = (bf16[4,512,256]{2,1,0:T(8,128)(2,1)S(1)}, bf16[4,512,256]{2,1,0:T(8,128)(2,1)S(1)}, u32[]{:S(2)}, u32[]{:S(2)}) collective-permute-start(bf16[4,512,256]{2,1,0:T(8,128)(2,1)S(1)} %bitcast.12), channel_id=1, source_target_pairs={{12,16},{16,12},{13,17},{17,13},{14,18},{18,14},{15,19},{19,15}} | collective-permute-start | bytes 3145736 | tf_op jit(solution)/shard_map/ppermute | solution.py:452
  31.8 18.6 %collective-permute-start.8 = (bf16[4,512,256]{2,1,0:T(8,128)(2,1)S(1)}, bf16[4,512,256]{2,1,0:T(8,128)(2,1)S(1)}, u32[]{:S(2)}, u32[]{:S(2)}) collective-permute-start(bf16[4,512,256]{2,1,0:T(8,128)(2,1)S(1)} %collective-permute-done.3), channel_id=1, source_target_pairs={{28,16},{0,12},{29,17},{1,13},{30,18},{2,14},{31,19},{3,15}} | collective-permute-start | bytes 3145736 | tf_op jit(solution)/shard_map/ppermute | solution.py:456
  36.2 4.8 %collective-permute-start.4 = (f32[8,2,256]{2,1,0:T(2,128)S(1)}, f32[8,2,256]{2,1,0:T(2,128)S(1)}, u32[]{:S(2)}, u32[]{:S(2)}) collective-permute-start(f32[8,2,256]{2,1,0:T(2,128)S(1)} %add.3.refs_0_), channel_id=1, source_target_pairs={{0,2},{1,3},{2,0},{3,1},{4,6},{5,7},{6,4},{7,5},{8,10},{9,11},{10,... | collective-permute-start | bytes 49160 | tf_op jit(solution)/shard_map/ppermute | solution.py:413
  37.8 3.2 %copy-start.4 = (s32[2]{0:T(128)S(1)}, s32[2]{0:T(128)}, u32[]{:S(2)}) copy-start(s32[2]{0:T(128)} %clip_ref.5) | copy-start | bytes 28
  37.8 3.2 %copy-start.6 = (f32[256]{0:T(256)S(1)}, f32[256]{0:T(256)}, u32[]{:S(2)}) copy-start(f32[256]{0:T(256)} %param.12) | copy-start | bytes 3076
  37.8 3.2 %copy-start.7 = (f32[256]{0:T(256)S(1)}, f32[256]{0:T(256)}, u32[]{:S(2)}) copy-start(f32[256]{0:T(256)} %param.13) | copy-start | bytes 3076
  41.0 9.4 %copy-start.1 = (bf16[8,8,64,256]{3,2,1,0:T(8,128)(2,1)S(1)}, bf16[8,8,64,256]{3,2,1,0:T(8,128)(2,1)}, u32[]{:S(2)}) copy-start(bf16[8,8,64,256]{3,2,1,0:T(8,128)(2,1)} %cot_ref.1) | copy-start | bytes 6291460
  41.0 9.4 %copy-start.5 = (s32[2]{0:T(128)S(1)}, s32[2]{0:T(128)}, u32[]{:S(2)}) copy-start(s32[2]{0:T(128)} %dil_ref.3) | copy-start | bytes 28
  47.2 44.5 %collective-permute-start.15 = (bf16[6,512,256]{2,1,0:T(8,128)(2,1)S(1)}, bf16[6,512,256]{2,1,0:T(8,128)(2,1)S(1)}, u32[]{:S(2)}, u32[]{:S(2)}) collective-permute-start(bf16[6,512,256]{2,1,0:T(8,128)(2,1)S(1)} %get-tuple-element.83), channel_id=1, source_target_pairs={{0,4},{4,8},{8,12},{12,16},{16,20},{20,24},{24,28},{1,5},{5,9},{9,... | collective-permute-start | bytes 4718600 | tf_op jit(solution)/shard_map/ppermute | solution.py:399
  48.7 43.1 %collective-permute-start.16 = (bf16[6,512,256]{2,1,0:T(8,128)(2,1)S(1)}, bf16[6,512,256]{2,1,0:T(8,128)(2,1)S(1)}, u32[]{:S(2)}, u32[]{:S(2)}) collective-permute-start(bf16[6,512,256]{2,1,0:T(8,128)(2,1)S(1)} %get-tuple-element.83), channel_id=1, source_target_pairs={{4,0},{8,4},{12,8},{16,12},{20,16},{24,20},{28,24},{5,1},{9,5},{13... | collective-permute-start | bytes 4718600 | tf_op jit(solution)/shard_map/ppermute | solution.py:399
  54.6 6.1 %collective-permute-start.10 = (f32[8,2,256]{2,1,0:T(2,128)S(1)}, f32[8,2,256]{2,1,0:T(2,128)S(1)}, u32[]{:S(2)}, u32[]{:S(2)}) collective-permute-start(f32[8,2,256]{2,1,0:T(2,128)S(1)} %get-tuple-element.69.refs_2_), channel_id=1, source_target_pairs={{0,2},{1,3},{2,0},{3,1},{4,6},{5,7},{6,4},{7,5},{8,10},{9,11},{10,... | collective-permute-start | bytes 49160 | tf_op jit(solution)/shard_map/ppermute | solution.py:404
  55.3 5.6 %collective-permute-start.11 = (f32[8,2,256]{2,1,0:T(2,128)S(1)}, f32[8,2,256]{2,1,0:T(2,128)S(1)}, u32[]{:S(2)}, u32[]{:S(2)}) collective-permute-start(f32[8,2,256]{2,1,0:T(2,128)S(1)} %get-tuple-element.69.refs_2_), channel_id=1, source_target_pairs={{0,3},{1,2},{2,1},{3,0},{4,7},{5,6},{6,5},{7,4},{8,11},{9,10},{10,... | collective-permute-start | bytes 49160 | tf_op jit(solution)/shard_map/ppermute | solution.py:404
  58.3 3.7 %collective-permute-start.9 = (f32[8,2,256]{2,1,0:T(2,128)S(1)}, f32[8,2,256]{2,1,0:T(2,128)S(1)}, u32[]{:S(2)}, u32[]{:S(2)}) collective-permute-start(f32[8,2,256]{2,1,0:T(2,128)S(1)} %get-tuple-element.69.refs_2_), channel_id=1, source_target_pairs={{0,1},{1,0},{2,3},{3,2},{4,5},{5,4},{6,7},{7,6},{8,9},{9,8},{10,11... | collective-permute-start | bytes 49160 | tf_op jit(solution)/shard_map/ppermute | solution.py:404
  66.6 8.8 %collective-permute-start.12 = (bf16[8,1,64,256]{3,2,1,0:T(8,128)(2,1)S(1)}, bf16[8,1,64,256]{3,2,1,0:T(8,128)(2,1)S(1)}, u32[]{:S(2)}, u32[]{:S(2)}) collective-permute-start(bf16[8,1,64,256]{3,2,1,0:T(8,128)(2,1)S(1)} %get-tuple-element.73), channel_id=1, source_target_pairs={{0,1},{1,2},{2,3},{4,5},{5,6},{6,7},{8,9},{9,10},{10,11},{12,13},{... | collective-permute-start | bytes 786440 | tf_op jit(solution)/shard_map/ppermute | solution.py:399
  69.1 9.2 %collective-permute-start.13 = (bf16[8,1,64,256]{3,2,1,0:T(8,128)(2,1)S(1)}, bf16[8,1,64,256]{3,2,1,0:T(8,128)(2,1)S(1)}, u32[]{:S(2)}, u32[]{:S(2)}) collective-permute-start(bf16[8,1,64,256]{3,2,1,0:T(8,128)(2,1)S(1)} %get-tuple-element.74), channel_id=1, source_target_pairs={{1,0},{2,1},{3,2},{5,4},{6,5},{7,6},{9,8},{10,9},{11,10},{13,12},{... | collective-permute-start | bytes 786440 | tf_op jit(solution)/shard_map/ppermute | solution.py:399
  78.6 2.4 %collective-permute-start.14 = (bf16[4,4,32,768]{3,2,1,0:T(8,128)(2,1)S(1)}, bf16[4,4,32,768]{3,2,1,0:T(8,128)(2,1)S(1)}, u32[]{:S(2)}, u32[]{:S(2)}) collective-permute-start(bf16[4,4,32,768]{3,2,1,0:T(8,128)(2,1)S(1)} %get-tuple-element.77), channel_id=1, source_target_pairs={{0,4},{4,0},{8,12},{12,8},{16,20},{20,16},{24,28},{28,24},{1,5},{5... | collective-permute-start | bytes 2359304 | tf_op jit(solution)/shard_map/ppermute | solution.py:506
  81.2 10.6 %collective-permute-start.17 = (bf16[4,32,768]{2,1,0:T(8,128)(2,1)S(1)}, bf16[4,32,768]{2,1,0:T(8,128)(2,1)S(1)}, u32[]{:S(2)}, u32[]{:S(2)}) collective-permute-start(bf16[4,32,768]{2,1,0:T(8,128)(2,1)S(1)} %get-tuple-element.85), channel_id=1, source_target_pairs={{0,8},{4,12},{8,0},{12,4},{16,24},{20,28},{24,16},{28,20},{1,9},{5... | collective-permute-start | bytes 589832 | tf_op jit(solution)/shard_map/ppermute | solution.py:511
  82.2 11.1 %collective-permute-start.18 = (bf16[4,32,768]{2,1,0:T(8,128)(2,1)S(1)}, bf16[4,32,768]{2,1,0:T(8,128)(2,1)S(1)}, u32[]{:S(2)}, u32[]{:S(2)}) collective-permute-start(bf16[4,32,768]{2,1,0:T(8,128)(2,1)S(1)} %get-tuple-element.86), channel_id=1, source_target_pairs={{0,16},{4,20},{8,24},{12,28},{16,0},{20,4},{24,8},{28,12},{1,17},{... | collective-permute-start | bytes 589832 | tf_op jit(solution)/shard_map/ppermute | solution.py:511
  82.8 10.5 %collective-permute-start.19 = (bf16[4,32,768]{2,1,0:T(8,128)(2,1)S(1)}, bf16[4,32,768]{2,1,0:T(8,128)(2,1)S(1)}, u32[]{:S(2)}, u32[]{:S(2)}) collective-permute-start(bf16[4,32,768]{2,1,0:T(8,128)(2,1)S(1)} %get-tuple-element.87), channel_id=1, source_target_pairs={{0,24},{4,28},{8,16},{12,20},{16,8},{20,12},{24,0},{28,4},{1,25},{... | collective-permute-start | bytes 589832 | tf_op jit(solution)/shard_map/ppermute | solution.py:511
  93.4 4.2 %collective-permute-start.20 = (bf16[32,768]{1,0:T(8,128)(2,1)S(1)}, bf16[32,768]{1,0:T(8,128)(2,1)S(1)}, u32[]{:S(2)}, u32[]{:S(2)}) collective-permute-start(bf16[32,768]{1,0:T(8,128)(2,1)S(1)} %get-tuple-element.89), channel_id=1, source_target_pairs={{0,1},{1,0},{2,3},{3,2},{4,5},{5,4},{6,7},{7,6},{8,9},{9,8},{10,11... | collective-permute-start | bytes 147464 | tf_op jit(solution)/shard_map/ppermute | solution.py:523
  97.6 24.3 %collective-permute-start.26 = (bf16[2,512,256]{2,1,0:T(8,128)(2,1)S(1)}, bf16[2,512,256]{2,1,0:T(8,128)(2,1)S(1)}, u32[]{:S(2)}, u32[]{:S(2)}) collective-permute-start(bf16[2,512,256]{2,1,0:T(8,128)(2,1)S(1)} %get-tuple-element.95), channel_id=1, source_target_pairs={{4,0},{8,4},{12,8},{16,12},{20,16},{24,20},{28,24},{5,1},{9,5},{13... | collective-permute-start | bytes 1572872 | tf_op jit(solution)/shard_map/ppermute | solution.py:399
  98.9 23.0 %collective-permute-start.27 = (bf16[2,512,256]{2,1,0:T(8,128)(2,1)S(1)}, bf16[2,512,256]{2,1,0:T(8,128)(2,1)S(1)}, u32[]{:S(2)}, u32[]{:S(2)}) collective-permute-start(bf16[2,512,256]{2,1,0:T(8,128)(2,1)S(1)} %get-tuple-element.95), channel_id=1, source_target_pairs={{0,4},{4,8},{8,12},{12,16},{16,20},{20,24},{24,28},{1,5},{5,9},{9,... | collective-permute-start | bytes 1572872 | tf_op jit(solution)/shard_map/ppermute | solution.py:399
  101.9 7.1 %collective-permute-start.21 = (bf16[32,768]{1,0:T(8,128)(2,1)S(1)}, bf16[32,768]{1,0:T(8,128)(2,1)S(1)}, u32[]{:S(2)}, u32[]{:S(2)}) collective-permute-start(bf16[32,768]{1,0:T(8,128)(2,1)S(1)} %get-tuple-element.92), channel_id=1, source_target_pairs={{0,2},{1,3},{2,0},{3,1},{4,6},{5,7},{6,4},{7,5},{8,10},{9,11},{10,... | collective-permute-start | bytes 147464 | tf_op jit(solution)/shard_map/ppermute | solution.py:523
  104.2 5.9 %collective-permute-start.22 = (bf16[32,768]{1,0:T(8,128)(2,1)S(1)}, bf16[32,768]{1,0:T(8,128)(2,1)S(1)}, u32[]{:S(2)}, u32[]{:S(2)}) collective-permute-start(bf16[32,768]{1,0:T(8,128)(2,1)S(1)} %get-tuple-element.93), channel_id=1, source_target_pairs={{0,3},{1,2},{2,1},{3,0},{4,7},{5,6},{6,5},{7,4},{8,11},{9,10},{10,... | collective-permute-start | bytes 147464 | tf_op jit(solution)/shard_map/ppermute | solution.py:523
  110.1 4.5 %collective-permute-start.23 = (bf16[32,768]{1,0:T(8,128)(2,1)S(1)}, bf16[32,768]{1,0:T(8,128)(2,1)S(1)}, u32[]{:S(2)}, u32[]{:S(2)}) collective-permute-start(bf16[32,768]{1,0:T(8,128)(2,1)S(1)} %line_sum.1.refs_0_), channel_id=1, source_target_pairs={{0,1},{1,0},{2,3},{3,2},{4,5},{5,4},{6,7},{7,6},{8,9},{9,8},{10,11... | collective-permute-start | bytes 147464 | tf_op jit(solution)/shard_map/ppermute | solution.py:529
  110.2 5.5 %collective-permute-start.24 = (bf16[32,768]{1,0:T(8,128)(2,1)S(1)}, bf16[32,768]{1,0:T(8,128)(2,1)S(1)}, u32[]{:S(2)}, u32[]{:S(2)}) collective-permute-start(bf16[32,768]{1,0:T(8,128)(2,1)S(1)} %line_sum.1.refs_0_), channel_id=1, source_target_pairs={{0,2},{1,3},{2,0},{3,1},{4,6},{5,7},{6,4},{7,5},{8,10},{9,11},{10,... | collective-permute-start | bytes 147464 | tf_op jit(solution)/shard_map/ppermute | solution.py:529
  112.4 5.9 %collective-permute-start.25 = (bf16[32,768]{1,0:T(8,128)(2,1)S(1)}, bf16[32,768]{1,0:T(8,128)(2,1)S(1)}, u32[]{:S(2)}, u32[]{:S(2)}) collective-permute-start(bf16[32,768]{1,0:T(8,128)(2,1)S(1)} %line_sum.1.refs_0_), channel_id=1, source_target_pairs={{0,3},{1,2},{2,1},{3,0},{4,7},{5,6},{6,5},{7,4},{8,11},{9,10},{10,... | collective-permute-start | bytes 147464 | tf_op jit(solution)/shard_map/ppermute | solution.py:529
  118.3 8.7 %collective-permute-start.28 = (bf16[4,32,768]{2,1,0:T(8,128)(2,1)S(1)}, bf16[4,32,768]{2,1,0:T(8,128)(2,1)S(1)}, u32[]{:S(2)}, u32[]{:S(2)}) collective-permute-start(bf16[4,32,768]{2,1,0:T(8,128)(2,1)S(1)} %line_place.1.refs_0_), channel_id=1, source_target_pairs={{0,8},{4,12},{8,0},{12,4},{16,24},{20,28},{24,16},{28,20},{1,9},{5... | collective-permute-start | bytes 589832 | tf_op jit(solution)/shard_map/ppermute | solution.py:533
  119.3 9.7 %collective-permute-start.29 = (bf16[4,32,768]{2,1,0:T(8,128)(2,1)S(1)}, bf16[4,32,768]{2,1,0:T(8,128)(2,1)S(1)}, u32[]{:S(2)}, u32[]{:S(2)}) collective-permute-start(bf16[4,32,768]{2,1,0:T(8,128)(2,1)S(1)} %line_place.1.refs_0_), channel_id=1, source_target_pairs={{0,16},{4,20},{8,24},{12,28},{16,0},{20,4},{24,8},{28,12},{1,17},{... | collective-permute-start | bytes 589832 | tf_op jit(solution)/shard_map/ppermute | solution.py:533
  120.2 8.9 %collective-permute-start.30 = (bf16[4,32,768]{2,1,0:T(8,128)(2,1)S(1)}, bf16[4,32,768]{2,1,0:T(8,128)(2,1)S(1)}, u32[]{:S(2)}, u32[]{:S(2)}) collective-permute-start(bf16[4,32,768]{2,1,0:T(8,128)(2,1)S(1)} %line_place.1.refs_0_), channel_id=1, source_target_pairs={{0,24},{4,28},{8,16},{12,20},{16,8},{20,12},{24,0},{28,4},{1,25},{... | collective-permute-start | bytes 589832 | tf_op jit(solution)/shard_map/ppermute | solution.py:533
  129.1 2.4 %collective-permute-start.31 = (bf16[4,4,32,768]{3,2,1,0:T(8,128)(2,1)S(1)}, bf16[4,4,32,768]{3,2,1,0:T(8,128)(2,1)S(1)}, u32[]{:S(2)}, u32[]{:S(2)}) collective-permute-start(bf16[4,4,32,768]{3,2,1,0:T(8,128)(2,1)S(1)} %plane_place.1.mine_ref), channel_id=1, source_target_pairs={{0,4},{4,0},{8,12},{12,8},{16,20},{20,16},{24,28},{28,24},{1,5},{5... | collective-permute-start | bytes 2359304 | tf_op jit(solution)/shard_map/ppermute | solution.py:545

commit v4 on v3

--- a/solution.py
+++ b/solution.py
@@ -521,7 +521,7 @@
         [shape((block, lanes), F32)] + [shape((block, lanes), BF16)] * (n - 1), 0, big,
     )
     gots = [lax.ppermute(x, "space", other_plane(s)) for s, x in enumerate(sends, 1)]
-    gots[0], act_late = lax.optimization_barrier((gots[0], act_late))
+    own, act_late = lax.optimization_barrier((own, act_late))
     late_prev, late_next = neighbours("tm", act_late, act_late)
     own = call(
         functools.partial(sum_kernel, n - 1), "line_sum", [own, *gots], shape((block, lanes), BF16), 0, big

time: 134 us -> 130 us (0.970)
  waiting for transfers between devices: 33.4 us -> 29.6 us
    ppermute x3, waiting for transfers between devices: 8.13 us -> 4.48 us  [per_device(): lax.ppermute(x, 'space', other_plane(s))]
  transfers between devices with their start and end apart: 32 -> 32, of which waited for: 17 -> 16; matrix products, arithmetic and copies ran while one was open for 1% -> 1% of each run, Pallas kernels for 32% -> 33%
where the time goes in v4:
time: 130 us
  starting transfers between devices  51.4 us (40%)
  Pallas kernels  45.1 us (35%)
  waiting for transfers between devices  29.6 us (23%)
  local copies, waits for them, and re-layouts  2.8 us (2%)
    pallas_call x17, Pallas kernels, call(): pl.pallas_call(kernel, in_specs=[smem if x.dtype == jnp.int32 else vmem f...  45.1 us
    ppermute x10, starting transfers between devices, neighbours(): return (lax.ppermute(high, axis, up), lax.ppermute(low, axis, down))  21.7 us
    ppermute x10, waiting for transfers between devices, neighbours(): return (lax.ppermute(high, axis, up), lax.ppermute(low, axis, down))  9.14 us
    ppermute x3, starting transfers between devices, per_device(): lax.ppermute(x, 'space', other_plane(s))  4.48 us
    ppermute x3, waiting for transfers between devices, per_device(): lax.ppermute(x, 'space', other_plane(s))  4.48 us
    ppermute x3, starting transfers between devices, per_device(): gots = [lax.ppermute(own, 'space', other_plane(s)) for s in range(1, n)]  4.45 us
    ppermute x1, starting transfers between devices, per_device(): cot_corner.append(lax.ppermute(relayed, 'tm', [(7, 4), (0, 3)]))  4.41 us
    ppermute x3, starting transfers between devices, spread_parts(): lax.ppermute(part, axis, [(i, i ^ s) for i in range(size)])  4.21 us
  transfers between devices with their start and end apart: 32, of which 16 were waited for; matrix products, arithmetic and copies ran while one was open for 1% of the time, Pallas kernels for 33%

profile of v4, /device:TPU:0, one launch (start us, length us, event | category | flops | bytes accessed | tf_op | source)
XLA Modules:
  0.0 129.9 jit_solution(2816865403712851122)
XLA Ops:
  0.6 1.1 fusion.1
  1.7 1.6 %collective-permute-start.5 = (bf16[8,512,256]{2,1,0:T(8,128)(2,1)}, bf16[8,512,256]{2,1,0:T(8,128)(2,1)S(1)}, u32[]{:S(2)}, u32[]{:S(2)}) collective-permute-start(bf16[8,512,256]{2,1,0:T(8,128)(2,1)} %bitcast.6), channel_id=1, source_target_pairs={{4,0},{8,4},{12,8},{20,16},{24,20},{28,24},{5,1},{9,5},{13,9},{21,... | collective-permute-start | bytes 6291464 | tf_op jit(solution)/shard_map/ppermute | solution.py:399
  3.3 3.2 %collective-permute-start.6 = (bf16[8,512,256]{2,1,0:T(8,128)(2,1)}, bf16[8,512,256]{2,1,0:T(8,128)(2,1)S(1)}, u32[]{:S(2)}, u32[]{:S(2)}) collective-permute-start(bf16[8,512,256]{2,1,0:T(8,128)(2,1)} %bitcast.7), channel_id=1, source_target_pairs={{0,4},{4,8},{8,12},{16,20},{20,24},{24,28},{1,5},{5,9},{9,13},{17,... | collective-permute-start | bytes 6291464 | tf_op jit(solution)/shard_map/ppermute | solution.py:399
  6.5 4.9 %collective-permute-start = (bf16[8,1,64,256]{3,2,1,0:T(8,128)(2,1)S(1)}, bf16[8,1,64,256]{3,2,1,0:T(8,128)(2,1)S(1)}, u32[]{:S(2)}, u32[]{:S(2)}) collective-permute-start(bf16[8,1,64,256]{3,2,1,0:T(8,128)(2,1)S(1)} %get-tuple-element.53), channel_id=1, source_target_pairs={{0,1},{1,2},{2,3},{4,5},{5,6},{6,7},{8,9},{9,10},{10,11},{12,13},{... | collective-permute-start | bytes 786440 | tf_op jit(solution)/shard_map/ppermute | solution.py:399
  11.4 1.3 collective-permute-start.1
  12.7 1.7 %fusion = (bf16[4,8,64,256]{3,2,1,0:T(8,128)(2,1)S(1)}, bf16[4,8,64,256]{3,2,1,0:T(8,128)(2,1)S(1)}) fusion(bf16[8,8,64,256]{3,2,1,0:T(8,128)(2,1)} %cot_ref.1), kind=kLoop, calls=%fused_computation | loop fusion | bytes 4194304 | tf_op jit(solution)/shard_map/slice | solution.py:438
  14.4 1.4 %collective-permute-start.3 = (bf16[4,512,256]{2,1,0:T(8,128)(2,1)S(1)}, bf16[4,512,256]{2,1,0:T(8,128)(2,1)S(1)}, u32[]{:S(2)}, u32[]{:S(2)}) collective-permute-start(bf16[4,512,256]{2,1,0:T(8,128)(2,1)S(1)} %bitcast.13), channel_id=1, source_target_pairs={{12,28},{16,0},{13,29},{17,1},{14,30},{18,2},{15,31},{19,3}} | collective-permute-start | bytes 3145736 | tf_op jit(solution)/shard_map/ppermute | solution.py:439
  15.8 2.2 %collective-permute-done.above_ref = bf16[8,1,64,256]{3,2,1,0:T(8,128)(2,1)S(1)} collective-permute-done((bf16[8,1,64,256]{3,2,1,0:T(8,128)(2,1)S(1)}, bf16[8,1,64,256]{3,2,1,0:T(8,128)(2,1)S(1)}, u32[]{:S(2)}, u32[]{:S(2)}) %collective-permute-start) | collective-permute-done | bytes 262176 | tf_op jit(solution)/shard_map/ppermute | solution.py:399
  18.1 4.1 %collective-permute-done.1.below_ref = bf16[8,1,64,256]{3,2,1,0:T(8,128)(2,1)S(1)} collective-permute-done((bf16[8,1,64,256]{3,2,1,0:T(8,128)(2,1)S(1)}, bf16[8,1,64,256]{3,2,1,0:T(8,128)(2,1)S(1)}, u32[]{:S(2)}, u32[]{:S(2)}) %collective-permute-start.1) | collective-permute-done | bytes 262176 | tf_op jit(solution)/shard_map/ppermute | solution.py:399
  22.2 5.7 %conv_forward.1 = (f32[8,512,256]{2,1,0:T(8,128)S(1)}, f32[8,2,256]{2,1,0:T(2,128)S(1)}) custom-call(bf16[8,8,64,256]{3,2,1,0:T(8,128)(2,1)S(1)} %copy-done, bf16[8,1,64,256]{3,2,1,0:T(8,128)(2,1)S(1)} %collective-permute-done.above_ref, bf16[8,1,64,256]{3,2,1,0:T(8,128)(2,1)S(1)} %collective-permute-done.1.below_ref, bf16[3,3,256,256]{3,2,1,0:T(8,128)(2,1)S(1)} %copy-done.3), custom_call_target="tpu_custom_call" | custom-call | flops 26843545600 | bytes 8388608 | tf_op jit(solution)/shard_map/conv_forward/pallas_call | solution.py:20
  27.9 1.6 %collective-permute-start.2 = (f32[8,2,256]{2,1,0:T(2,128)S(1)}, f32[8,2,256]{2,1,0:T(2,128)S(1)}, u32[]{:S(2)}, u32[]{:S(2)}) collective-permute-start(f32[8,2,256]{2,1,0:T(2,128)S(1)} %get-tuple-element.56), channel_id=1, source_target_pairs={{0,1},{1,0},{2,3},{3,2},{4,5},{5,4},{6,7},{7,6},{8,9},{9,8},{10,11... | collective-permute-start | bytes 49160 | tf_op jit(solution)/shard_map/ppermute | solution.py:413
  29.6 0.7 collective-permute-start.7
  30.3 1.5 %collective-permute-done.2 = f32[8,2,256]{2,1,0:T(2,128)S(1)} collective-permute-done((f32[8,2,256]{2,1,0:T(2,128)S(1)}, f32[8,2,256]{2,1,0:T(2,128)S(1)}, u32[]{:S(2)}, u32[]{:S(2)}) %collective-permute-start.2) | collective-permute-done | bytes 16416 | tf_op jit(solution)/shard_map/ppermute | solution.py:413
  31.8 4.4 %collective-permute-start.8 = (bf16[4,512,256]{2,1,0:T(8,128)(2,1)S(1)}, bf16[4,512,256]{2,1,0:T(8,128)(2,1)S(1)}, u32[]{:S(2)}, u32[]{:S(2)}) collective-permute-start(bf16[4,512,256]{2,1,0:T(8,128)(2,1)S(1)} %collective-permute-done.3), channel_id=1, source_target_pairs={{28,16},{0,12},{29,17},{1,13},{30,18},{2,14},{31,19},{3,15}} | collective-permute-start | bytes 3145736 | tf_op jit(solution)/shard_map/ppermute | solution.py:456
  36.2 1.1 collective-permute-start.4
  37.3 0.5 turn_weights.1
  37.8 2.2 %turned.1.xt_ref = bf16[768,4096]{1,0:T(8,128)(2,1)S(1)} custom-call(bf16[8,8,64,256]{3,2,1,0:T(8,128)(2,1)S(1)} %copy-done, bf16[8,1,64,256]{3,2,1,0:T(8,128)(2,1)S(1)} %collective-permute-done.above_ref, bf16[8,1,64,256]{3,2,1,0:T(8,128)(2,1)S(1)} %collective-permute-done.1.below_ref), custom_call_target="tpu_custom_call" | custom-call | bytes 8388608 | tf_op jit(solution)/shard_map/turned/pallas_call | solution.py:20
  40.0 1.0 collective-permute-done.4.refs_1_
  41.0 6.2 %activation.1 = (bf16[8,512,256]{2,1,0:T(8,128)(2,1)S(1)}, bf16[6,512,256]{2,1,0:T(8,128)(2,1)S(1)}, bf16[2,512,256]{2,1,0:T(8,128)(2,1)S(1)}, bf16[8,512,256]{2,1,0:T(8,128)(2,1)S(1)}, bf16[8,512,256]{2,1,0:T(8,128)(2,1)S(1)}) custom-call(s32[2]{0:T(128)S(1)} %copy-done.4, f32[8,2,256]{2,1,0:T(2,128)S(1)} %add.3.refs_0_, ...), custom_call_target="tpu_custom_call" | custom-call | flops 10485760 | bytes 10485760 | tf_op jit(solution)/shard_map/activation/pallas_call | solution.py:20
  47.2 1.4 %collective-permute-start.15 = (bf16[6,512,256]{2,1,0:T(8,128)(2,1)S(1)}, bf16[6,512,256]{2,1,0:T(8,128)(2,1)S(1)}, u32[]{:S(2)}, u32[]{:S(2)}) collective-permute-start(bf16[6,512,256]{2,1,0:T(8,128)(2,1)S(1)} %get-tuple-element.83), channel_id=1, source_target_pairs={{0,4},{4,8},{8,12},{12,16},{16,20},{20,24},{24,28},{1,5},{5,9},{9,... | collective-permute-start | bytes 4718600 | tf_op jit(solution)/shard_map/ppermute | solution.py:399
  48.7 1.3 collective-permute-start.16
  50.0 0.4 collective-permute-done.8.refs_1_
  50.4 4.2 %grad_activation.1 = (bf16[8,512,256]{2,1,0:T(8,128)(2,1)S(1)}, bf16[4096,768]{1,0:T(8,128)(2,1)S(1)}, f32[8,2,256]{2,1,0:T(2,128)S(1)}) custom-call(s32[2]{0:T(128)S(1)} %copy-done.4, s32[2]{0:T(128)S(1)} %copy-done.5, bf16[8,512,256]{2,1,0:T(8,128)(2,1)S(1)} %bitcast.8, bf16[8,512,256]{2,1,0:T(8,128)(2,1)S(1)} %collective-permute-done.5.nxt, ...), custom_call_target="tpu_custom_call" | custom-call | flops 1610612736 | bytes 16777216 | tf_op jit(solution)/shard_map/grad_activation/pallas_call | solution.py:20
  54.6 0.7 collective-permute-start.10
  55.3 3.1 %collective-permute-start.11 = (f32[8,2,256]{2,1,0:T(2,128)S(1)}, f32[8,2,256]{2,1,0:T(2,128)S(1)}, u32[]{:S(2)}, u32[]{:S(2)}) collective-permute-start(f32[8,2,256]{2,1,0:T(2,128)S(1)} %get-tuple-element.69.refs_2_), channel_id=1, source_target_pairs={{0,3},{1,2},{2,1},{3,0},{4,7},{5,6},{6,5},{7,4},{8,11},{9,10},{10,... | collective-permute-start | bytes 49160 | tf_op jit(solution)/shard_map/ppermute | solution.py:404
  58.3 0.5 collective-permute-start.9
  58.8 1.9 %temporal_grad.1.temporal_ref = f32[256,768]{1,0:T(8,128)S(1)} custom-call(bf16[8,512,256]{2,1,0:T(8,128)(2,1)S(1)} %get-tuple-element.71.act_ref.own, bf16[4096,768]{1,0:T(8,128)(2,1)S(1)} %get-tuple-element.72.cat_ref), custom_call_target="tpu_custom_call" | custom-call | flops 1610612736 | bytes 8388608 | tf_op jit(solution)/shard_map/temporal_grad/pallas_call | solution.py:20
  60.7 0.1 collective-permute-done.11.refs_5_
  60.8 1.2 collective-permute-done.9.refs_3_
  62.1 4.6 %norm_backward.1 = (bf16[8,512,256]{2,1,0:T(8,128)(2,1)S(1)}, bf16[8,1,64,256]{3,2,1,0:T(8,128)(2,1)S(1)}, bf16[8,1,64,256]{3,2,1,0:T(8,128)(2,1)S(1)}, bf16[4096,768]{1,0:T(8,128)(2,1)S(1)}) custom-call(bf16[8,512,256]{2,1,0:T(8,128)(2,1)S(1)} %get-tuple-element.62.refs_3_.normed_ref, bf16[8,512,256]{2,1,0:T(8,128)(2,1)S(1)} %get-tuple-element.63.refs_4_.slope_ref, ...), custom_call_target="tpu_custom_call" | custom-call | bytes 12582912 | tf_op jit(solution)/shard_map/norm_backward/pallas_call | solution.py:20
  66.7 2.4 %collective-permute-start.12 = (bf16[8,1,64,256]{3,2,1,0:T(8,128)(2,1)S(1)}, bf16[8,1,64,256]{3,2,1,0:T(8,128)(2,1)S(1)}, u32[]{:S(2)}, u32[]{:S(2)}) collective-permute-start(bf16[8,1,64,256]{3,2,1,0:T(8,128)(2,1)S(1)} %get-tuple-element.73), channel_id=1, source_target_pairs={{0,1},{1,2},{2,3},{4,5},{5,6},{6,7},{8,9},{9,10},{10,11},{12,13},{... | collective-permute-start | bytes 786440 | tf_op jit(solution)/shard_map/ppermute | solution.py:399
  69.1 1.3 collective-permute-start.13
  70.4 5.1 %weight_grad.1.acc_ref = f32[1024,768]{1,0:T(8,128)S(1)} custom-call(bf16[768,4096]{1,0:T(8,128)(2,1)S(1)} %turned.1.xt_ref, bf16[4096,768]{1,0:T(8,128)(2,1)S(1)} %get-tuple-element.70.moved_ref, f32[256,768]{1,0:T(8,128)S(1)} %temporal_grad.1.temporal_ref), custom_call_target="tpu_custom_call" | custom-call | flops 4831838208 | bytes 12582912 | tf_op jit(solution)/shard_map/weight_grad/pallas_call | solution.py:20
  75.5 2.8 %collective-permute-done.13.below_ref = bf16[8,1,64,256]{3,2,1,0:T(8,128)(2,1)S(1)} collective-permute-done((bf16[8,1,64,256]{3,2,1,0:T(8,128)(2,1)S(1)}, bf16[8,1,64,256]{3,2,1,0:T(8,128)(2,1)S(1)}, u32[]{:S(2)}, u32[]{:S(2)}) %collective-permute-start.13) | collective-permute-done | bytes 262176 | tf_op jit(solution)/shard_map/ppermute | solution.py:399
  78.3 0.4 hand_out.1
  78.6 0.1 collective-permute-start.14
  78.7 2.3 %collective-permute-done.14.got_ref = bf16[4,4,32,768]{3,2,1,0:T(8,128)(2,1)S(1)} collective-permute-done((bf16[4,4,32,768]{3,2,1,0:T(8,128)(2,1)S(1)}, bf16[4,4,32,768]{3,2,1,0:T(8,128)(2,1)S(1)}, u32[]{:S(2)}, u32[]{:S(2)}) %collective-permute-start.14) | collective-permute-done | bytes 786464 | tf_op jit(solution)/shard_map/ppermute | solution.py:506
  81.0 0.2 core_sum.1
  81.2 1.1 collective-permute-start.17
  82.2 0.6 collective-permute-start.18
  82.8 1.9 %collective-permute-start.19 = (bf16[4,32,768]{2,1,0:T(8,128)(2,1)S(1)}, bf16[4,32,768]{2,1,0:T(8,128)(2,1)S(1)}, u32[]{:S(2)}, u32[]{:S(2)}) collective-permute-start(bf16[4,32,768]{2,1,0:T(8,128)(2,1)S(1)} %get-tuple-element.87), channel_id=1, source_target_pairs={{0,24},{4,28},{8,16},{12,20},{16,8},{20,12},{24,0},{28,4},{1,25},{... | collective-permute-start | bytes 589832 | tf_op jit(solution)/shard_map/ppermute | solution.py:511
  84.7 7.0 %conv_backward.1 = bf16[8,8,64,256]{3,2,1,0:T(8,128)(2,1)} custom-call(bf16[8,512,256]{2,1,0:T(8,128)(2,1)S(1)} %get-tuple-element.79.g_ref, bf16[8,1,64,256]{3,2,1,0:T(8,128)(2,1)S(1)} %collective-permute-done.12.above_ref, bf16[8,1,64,256]{3,2,1,0:T(8,128)(2,1)S(1)} %collective-permute-done.13.below_ref, bf16[8,8,64,256]{3,2,1,0:T(8,128)(2,1)S(1)} %copy-done.1, ...), custom_call_target="tpu_custom_call" | custom-call | flops 4831838208 | bytes 8388608 | tf_op jit(solution)/shard_map/conv_backward/pallas_call | solution.py:20
  91.7 1.6 %collective-permute-done.18.refs_1_ = bf16[4,32,768]{2,1,0:T(8,128)(2,1)S(1)} collective-permute-done((bf16[4,32,768]{2,1,0:T(8,128)(2,1)S(1)}, bf16[4,32,768]{2,1,0:T(8,128)(2,1)S(1)}, u32[]{:S(2)}, u32[]{:S(2)}) %collective-permute-start.18) | collective-permute-done | bytes 196640 | tf_op jit(solution)/shard_map/ppermute | solution.py:511
  93.3 0.1 plane_sum.1
  93.4 1.3 collective-permute-start.26
  94.7 3.1 %collective-permute-start.27 = (bf16[2,512,256]{2,1,0:T(8,128)(2,1)S(1)}, bf16[2,512,256]{2,1,0:T(8,128)(2,1)S(1)}, u32[]{:S(2)}, u32[]{:S(2)}) collective-permute-start(bf16[2,512,256]{2,1,0:T(8,128)(2,1)S(1)} %get-tuple-element.95), channel_id=1, source_target_pairs={{0,4},{4,8},{8,12},{12,16},{16,20},{20,24},{24,28},{1,5},{5,9},{9,... | collective-permute-start | bytes 1572872 | tf_op jit(solution)/shard_map/ppermute | solution.py:399
  97.8 0.9 collective-permute-start.20
  98.7 2.1 %collective-permute-start.21 = (bf16[32,768]{1,0:T(8,128)(2,1)S(1)}, bf16[32,768]{1,0:T(8,128)(2,1)S(1)}, u32[]{:S(2)}, u32[]{:S(2)}) collective-permute-start(bf16[32,768]{1,0:T(8,128)(2,1)S(1)} %get-tuple-element.92), channel_id=1, source_target_pairs={{0,2},{1,3},{2,0},{3,1},{4,6},{5,7},{6,4},{7,5},{8,10},{9,11},{10,... | collective-permute-start | bytes 147464 | tf_op jit(solution)/shard_map/ppermute | solution.py:523
  100.8 1.5 %collective-permute-start.22 = (bf16[32,768]{1,0:T(8,128)(2,1)S(1)}, bf16[32,768]{1,0:T(8,128)(2,1)S(1)}, u32[]{:S(2)}, u32[]{:S(2)}) collective-permute-start(bf16[32,768]{1,0:T(8,128)(2,1)S(1)} %get-tuple-element.93), channel_id=1, source_target_pairs={{0,3},{1,2},{2,1},{3,0},{4,7},{5,6},{6,5},{7,4},{8,11},{9,10},{10,... | collective-permute-start | bytes 147464 | tf_op jit(solution)/shard_map/ppermute | solution.py:523
  102.3 2.6 %collective-permute-done.21.refs_1_ = bf16[32,768]{1,0:T(8,128)(2,1)S(1)} collective-permute-done((bf16[32,768]{1,0:T(8,128)(2,1)S(1)}, bf16[32,768]{1,0:T(8,128)(2,1)S(1)}, u32[]{:S(2)}, u32[]{:S(2)}) %collective-permute-start.21) | collective-permute-done | bytes 49184 | tf_op jit(solution)/shard_map/ppermute | solution.py:523
  104.9 1.9 %collective-permute-done.22.refs_2_ = bf16[32,768]{1,0:T(8,128)(2,1)S(1)} collective-permute-done((bf16[32,768]{1,0:T(8,128)(2,1)S(1)}, bf16[32,768]{1,0:T(8,128)(2,1)S(1)}, u32[]{:S(2)}, u32[]{:S(2)}) %collective-permute-start.22) | collective-permute-done | bytes 49184 | tf_op jit(solution)/shard_map/ppermute | solution.py:523
  106.8 0.7 collective-permute-start.23
  107.5 1.8 %collective-permute-start.24 = (bf16[32,768]{1,0:T(8,128)(2,1)S(1)}, bf16[32,768]{1,0:T(8,128)(2,1)S(1)}, u32[]{:S(2)}, u32[]{:S(2)}) collective-permute-start(bf16[32,768]{1,0:T(8,128)(2,1)S(1)} %line_sum.1.refs_0_), channel_id=1, source_target_pairs={{0,2},{1,3},{2,0},{3,1},{4,6},{5,7},{6,4},{7,5},{8,10},{9,11},{10,... | collective-permute-start | bytes 147464 | tf_op jit(solution)/shard_map/ppermute | solution.py:529
  109.3 1.9 %collective-permute-start.25 = (bf16[32,768]{1,0:T(8,128)(2,1)S(1)}, bf16[32,768]{1,0:T(8,128)(2,1)S(1)}, u32[]{:S(2)}, u32[]{:S(2)}) collective-permute-start(bf16[32,768]{1,0:T(8,128)(2,1)S(1)} %line_sum.1.refs_0_), channel_id=1, source_target_pairs={{0,3},{1,2},{2,1},{3,0},{4,7},{5,6},{6,5},{7,4},{8,11},{9,10},{10,... | collective-permute-start | bytes 147464 | tf_op jit(solution)/shard_map/ppermute | solution.py:529
  111.2 2.7 %collective-permute-done.24.refs_2_ = bf16[32,768]{1,0:T(8,128)(2,1)S(1)} collective-permute-done((bf16[32,768]{1,0:T(8,128)(2,1)S(1)}, bf16[32,768]{1,0:T(8,128)(2,1)S(1)}, u32[]{:S(2)}, u32[]{:S(2)}) %collective-permute-start.24) | collective-permute-done | bytes 49184 | tf_op jit(solution)/shard_map/ppermute | solution.py:529
  113.9 1.3 collective-permute-done.25.refs_3_
  115.2 0.9 collective-permute-start.28
  116.2 0.5 collective-permute-start.29
  116.7 2.1 %collective-permute-start.30 = (bf16[4,32,768]{2,1,0:T(8,128)(2,1)S(1)}, bf16[4,32,768]{2,1,0:T(8,128)(2,1)S(1)}, u32[]{:S(2)}, u32[]{:S(2)}) collective-permute-start(bf16[4,32,768]{2,1,0:T(8,128)(2,1)S(1)} %line_place.1.refs_0_), channel_id=1, source_target_pairs={{0,24},{4,28},{8,16},{12,20},{16,8},{20,12},{24,0},{28,4},{1,25},{... | collective-permute-start | bytes 589832 | tf_op jit(solution)/shard_map/ppermute | solution.py:533
  118.8 5.2 %temporal_forward.1 = bf16[8,8,64,256]{3,2,1,0:T(8,128)(2,1)} custom-call(s32[2]{0:T(128)S(1)} %copy-done.4, s32[2]{0:T(128)S(1)} %copy-done.5, bf16[8,512,256]{2,1,0:T(8,128)(2,1)S(1)} %get-tuple-element.71.act_ref.own, bf16[6,512,256]{2,1,0:T(8,128)(2,1)S(1)} %collective-permute-done.16.nxt_a, bf16[2,512,256]{2,1,0:T(8,128)(2,1)S(1)} %collective-permute-done.26.nxt_b, ...), custom_call_target="tpu_custom_call" | custom-call | flops 1610612736 | bytes 10485760 | tf_op jit(solution)/shard_map/temporal_forward/pallas_call | solution.py:20
  124.0 1.6 %collective-permute-done.29.refs_2_ = bf16[4,32,768]{2,1,0:T(8,128)(2,1)S(1)} collective-permute-done((bf16[4,32,768]{2,1,0:T(8,128)(2,1)S(1)}, bf16[4,32,768]{2,1,0:T(8,128)(2,1)S(1)}, u32[]{:S(2)}, u32[]{:S(2)}) %collective-permute-start.29) | collective-permute-done | bytes 196640 | tf_op jit(solution)/shard_map/ppermute | solution.py:533
  125.7 0.1 collective-permute-start.31
  125.7 2.3 %collective-permute-done.31.got_ref = bf16[4,4,32,768]{3,2,1,0:T(8,128)(2,1)S(1)} collective-permute-done((bf16[4,4,32,768]{3,2,1,0:T(8,128)(2,1)S(1)}, bf16[4,4,32,768]{3,2,1,0:T(8,128)(2,1)S(1)}, u32[]{:S(2)}, u32[]{:S(2)}) %collective-permute-start.31) | collective-permute-done | bytes 786464 | tf_op jit(solution)/shard_map/ppermute | solution.py:545
  128.0 1.9 %finish.1 = (f32[3,3,256,256]{3,2,1,0:T(8,128)}, f32[3,256,256]{2,1,0:T(8,128)}) custom-call(bf16[4,4,32,768]{3,2,1,0:T(8,128)(2,1)S(1)} %plane_place.1.mine_ref, bf16[4,4,32,768]{3,2,1,0:T(8,128)(2,1)S(1)} %collective-permute-done.31.got_ref), custom_call_target="tpu_custom_call" | custom-call | bytes 4194304 | tf_op jit(solution)/shard_map/finish/pallas_call | solution.py:20
  (36 shorter events, 0.2 us)
Async XLA Ops:
  1.7 20.5 %copy-start = (bf16[8,8,64,256]{3,2,1,0:T(8,128)(2,1)S(1)}, bf16[8,8,64,256]{3,2,1,0:T(8,128)(2,1)}, u32[]{:S(2)}) copy-start(bf16[8,8,64,256]{3,2,1,0:T(8,128)(2,1)} %x_ref.5) | copy-start | bytes 6291460
  1.7 20.5 %copy-start.3 = (bf16[3,3,256,256]{3,2,1,0:T(8,128)(2,1)S(1)}, bf16[3,3,256,256]{3,2,1,0:T(8,128)(2,1)}, u32[]{:S(2)}) copy-start(bf16[3,3,256,256]{3,2,1,0:T(8,128)(2,1)} %spatial_ref.1) | copy-start | bytes 3538948
  1.7 48.6 %collective-permute-start.5 = (bf16[8,512,256]{2,1,0:T(8,128)(2,1)}, bf16[8,512,256]{2,1,0:T(8,128)(2,1)S(1)}, u32[]{:S(2)}, u32[]{:S(2)}) collective-permute-start(bf16[8,512,256]{2,1,0:T(8,128)(2,1)} %bitcast.6), channel_id=1, source_target_pairs={{4,0},{8,4},{12,8},{20,16},{24,20},{28,24},{5,1},{9,5},{13,9},{21,... | collective-permute-start | bytes 6291464 | tf_op jit(solution)/shard_map/ppermute | solution.py:399
  3.3 47.1 %collective-permute-start.6 = (bf16[8,512,256]{2,1,0:T(8,128)(2,1)}, bf16[8,512,256]{2,1,0:T(8,128)(2,1)S(1)}, u32[]{:S(2)}, u32[]{:S(2)}) collective-permute-start(bf16[8,512,256]{2,1,0:T(8,128)(2,1)} %bitcast.7), channel_id=1, source_target_pairs={{0,4},{4,8},{8,12},{16,20},{20,24},{24,28},{1,5},{5,9},{9,13},{17,... | collective-permute-start | bytes 6291464 | tf_op jit(solution)/shard_map/ppermute | solution.py:399
  6.5 11.6 %collective-permute-start = (bf16[8,1,64,256]{3,2,1,0:T(8,128)(2,1)S(1)}, bf16[8,1,64,256]{3,2,1,0:T(8,128)(2,1)S(1)}, u32[]{:S(2)}, u32[]{:S(2)}) collective-permute-start(bf16[8,1,64,256]{3,2,1,0:T(8,128)(2,1)S(1)} %get-tuple-element.53), channel_id=1, source_target_pairs={{0,1},{1,2},{2,3},{4,5},{5,6},{6,7},{8,9},{9,10},{10,11},{12,13},{... | collective-permute-start | bytes 786440 | tf_op jit(solution)/shard_map/ppermute | solution.py:399
  11.4 10.8 %collective-permute-start.1 = (bf16[8,1,64,256]{3,2,1,0:T(8,128)(2,1)S(1)}, bf16[8,1,64,256]{3,2,1,0:T(8,128)(2,1)S(1)}, u32[]{:S(2)}, u32[]{:S(2)}) collective-permute-start(bf16[8,1,64,256]{3,2,1,0:T(8,128)(2,1)S(1)} %get-tuple-element.54), channel_id=1, source_target_pairs={{1,0},{2,1},{3,2},{5,4},{6,5},{7,6},{9,8},{10,9},{11,10},{13,12},{... | collective-permute-start | bytes 786440 | tf_op jit(solution)/shard_map/ppermute | solution.py:399
  14.4 22.9 %copy-start.2 = (bf16[3,256,256]{2,1,0:T(8,128)(2,1)S(1)}, bf16[3,256,256]{2,1,0:T(8,128)(2,1)}, u32[]{:S(2)}) copy-start(bf16[3,256,256]{2,1,0:T(8,128)(2,1)} %temporal_ref.1) | copy-start | bytes 1179652
  14.4 17.3 %collective-permute-start.3 = (bf16[4,512,256]{2,1,0:T(8,128)(2,1)S(1)}, bf16[4,512,256]{2,1,0:T(8,128)(2,1)S(1)}, u32[]{:S(2)}, u32[]{:S(2)}) collective-permute-start(bf16[4,512,256]{2,1,0:T(8,128)(2,1)S(1)} %bitcast.13), channel_id=1, source_target_pairs={{12,28},{16,0},{13,29},{17,1},{14,30},{18,2},{15,31},{19,3}} | collective-permute-start | bytes 3145736 | tf_op jit(solution)/shard_map/ppermute | solution.py:439
  27.9 3.8 %collective-permute-start.2 = (f32[8,2,256]{2,1,0:T(2,128)S(1)}, f32[8,2,256]{2,1,0:T(2,128)S(1)}, u32[]{:S(2)}, u32[]{:S(2)}) collective-permute-start(f32[8,2,256]{2,1,0:T(2,128)S(1)} %get-tuple-element.56), channel_id=1, source_target_pairs={{0,1},{1,0},{2,3},{3,2},{4,5},{5,4},{6,7},{7,6},{8,9},{9,8},{10,11... | collective-permute-start | bytes 49160 | tf_op jit(solution)/shard_map/ppermute | solution.py:413
  29.6 19.1 %collective-permute-start.7 = (bf16[4,512,256]{2,1,0:T(8,128)(2,1)S(1)}, bf16[4,512,256]{2,1,0:T(8,128)(2,1)S(1)}, u32[]{:S(2)}, u32[]{:S(2)}) collective-permute-start(bf16[4,512,256]{2,1,0:T(8,128)(2,1)S(1)} %bitcast.12), channel_id=1, source_target_pairs={{12,16},{16,12},{13,17},{17,13},{14,18},{18,14},{15,19},{19,15}} | collective-permute-start | bytes 3145736 | tf_op jit(solution)/shard_map/ppermute | solution.py:452
  31.8 18.6 %collective-permute-start.8 = (bf16[4,512,256]{2,1,0:T(8,128)(2,1)S(1)}, bf16[4,512,256]{2,1,0:T(8,128)(2,1)S(1)}, u32[]{:S(2)}, u32[]{:S(2)}) collective-permute-start(bf16[4,512,256]{2,1,0:T(8,128)(2,1)S(1)} %collective-permute-done.3), channel_id=1, source_target_pairs={{28,16},{0,12},{29,17},{1,13},{30,18},{2,14},{31,19},{3,15}} | collective-permute-start | bytes 3145736 | tf_op jit(solution)/shard_map/ppermute | solution.py:456
  36.2 4.8 %collective-permute-start.4 = (f32[8,2,256]{2,1,0:T(2,128)S(1)}, f32[8,2,256]{2,1,0:T(2,128)S(1)}, u32[]{:S(2)}, u32[]{:S(2)}) collective-permute-start(f32[8,2,256]{2,1,0:T(2,128)S(1)} %add.3.refs_0_), channel_id=1, source_target_pairs={{0,2},{1,3},{2,0},{3,1},{4,6},{5,7},{6,4},{7,5},{8,10},{9,11},{10,... | collective-permute-start | bytes 49160 | tf_op jit(solution)/shard_map/ppermute | solution.py:413
  37.8 3.2 %copy-start.4 = (s32[2]{0:T(128)S(1)}, s32[2]{0:T(128)}, u32[]{:S(2)}) copy-start(s32[2]{0:T(128)} %clip_ref.5) | copy-start | bytes 28
  37.8 3.2 %copy-start.6 = (f32[256]{0:T(256)S(1)}, f32[256]{0:T(256)}, u32[]{:S(2)}) copy-start(f32[256]{0:T(256)} %param.12) | copy-start | bytes 3076
  37.8 3.2 %copy-start.7 = (f32[256]{0:T(256)S(1)}, f32[256]{0:T(256)}, u32[]{:S(2)}) copy-start(f32[256]{0:T(256)} %param.13) | copy-start | bytes 3076
  41.0 9.4 %copy-start.1 = (bf16[8,8,64,256]{3,2,1,0:T(8,128)(2,1)S(1)}, bf16[8,8,64,256]{3,2,1,0:T(8,128)(2,1)}, u32[]{:S(2)}) copy-start(bf16[8,8,64,256]{3,2,1,0:T(8,128)(2,1)} %cot_ref.1) | copy-start | bytes 6291460
  41.0 9.4 %copy-start.5 = (s32[2]{0:T(128)S(1)}, s32[2]{0:T(128)}, u32[]{:S(2)}) copy-start(s32[2]{0:T(128)} %dil_ref.3) | copy-start | bytes 28
  47.2 44.5 %collective-permute-start.15 = (bf16[6,512,256]{2,1,0:T(8,128)(2,1)S(1)}, bf16[6,512,256]{2,1,0:T(8,128)(2,1)S(1)}, u32[]{:S(2)}, u32[]{:S(2)}) collective-permute-start(bf16[6,512,256]{2,1,0:T(8,128)(2,1)S(1)} %get-tuple-element.83), channel_id=1, source_target_pairs={{0,4},{4,8},{8,12},{12,16},{16,20},{20,24},{24,28},{1,5},{5,9},{9,... | collective-permute-start | bytes 4718600 | tf_op jit(solution)/shard_map/ppermute | solution.py:399
  48.7 43.1 %collective-permute-start.16 = (bf16[6,512,256]{2,1,0:T(8,128)(2,1)S(1)}, bf16[6,512,256]{2,1,0:T(8,128)(2,1)S(1)}, u32[]{:S(2)}, u32[]{:S(2)}) collective-permute-start(bf16[6,512,256]{2,1,0:T(8,128)(2,1)S(1)} %get-tuple-element.83), channel_id=1, source_target_pairs={{4,0},{8,4},{12,8},{16,12},{20,16},{24,20},{28,24},{5,1},{9,5},{13... | collective-permute-start | bytes 4718600 | tf_op jit(solution)/shard_map/ppermute | solution.py:399
  54.6 6.1 %collective-permute-start.10 = (f32[8,2,256]{2,1,0:T(2,128)S(1)}, f32[8,2,256]{2,1,0:T(2,128)S(1)}, u32[]{:S(2)}, u32[]{:S(2)}) collective-permute-start(f32[8,2,256]{2,1,0:T(2,128)S(1)} %get-tuple-element.69.refs_2_), channel_id=1, source_target_pairs={{0,2},{1,3},{2,0},{3,1},{4,6},{5,7},{6,4},{7,5},{8,10},{9,11},{10,... | collective-permute-start | bytes 49160 | tf_op jit(solution)/shard_map/ppermute | solution.py:404
  55.3 5.6 %collective-permute-start.11 = (f32[8,2,256]{2,1,0:T(2,128)S(1)}, f32[8,2,256]{2,1,0:T(2,128)S(1)}, u32[]{:S(2)}, u32[]{:S(2)}) collective-permute-start(f32[8,2,256]{2,1,0:T(2,128)S(1)} %get-tuple-element.69.refs_2_), channel_id=1, source_target_pairs={{0,3},{1,2},{2,1},{3,0},{4,7},{5,6},{6,5},{7,4},{8,11},{9,10},{10,... | collective-permute-start | bytes 49160 | tf_op jit(solution)/shard_map/ppermute | solution.py:404
  58.3 3.7 %collective-permute-start.9 = (f32[8,2,256]{2,1,0:T(2,128)S(1)}, f32[8,2,256]{2,1,0:T(2,128)S(1)}, u32[]{:S(2)}, u32[]{:S(2)}) collective-permute-start(f32[8,2,256]{2,1,0:T(2,128)S(1)} %get-tuple-element.69.refs_2_), channel_id=1, source_target_pairs={{0,1},{1,0},{2,3},{3,2},{4,5},{5,4},{6,7},{7,6},{8,9},{9,8},{10,11... | collective-permute-start | bytes 49160 | tf_op jit(solution)/shard_map/ppermute | solution.py:404
  66.7 8.8 %collective-permute-start.12 = (bf16[8,1,64,256]{3,2,1,0:T(8,128)(2,1)S(1)}, bf16[8,1,64,256]{3,2,1,0:T(8,128)(2,1)S(1)}, u32[]{:S(2)}, u32[]{:S(2)}) collective-permute-start(bf16[8,1,64,256]{3,2,1,0:T(8,128)(2,1)S(1)} %get-tuple-element.73), channel_id=1, source_target_pairs={{0,1},{1,2},{2,3},{4,5},{5,6},{6,7},{8,9},{9,10},{10,11},{12,13},{... | collective-permute-start | bytes 786440 | tf_op jit(solution)/shard_map/ppermute | solution.py:399
  69.1 9.2 %collective-permute-start.13 = (bf16[8,1,64,256]{3,2,1,0:T(8,128)(2,1)S(1)}, bf16[8,1,64,256]{3,2,1,0:T(8,128)(2,1)S(1)}, u32[]{:S(2)}, u32[]{:S(2)}) collective-permute-start(bf16[8,1,64,256]{3,2,1,0:T(8,128)(2,1)S(1)} %get-tuple-element.74), channel_id=1, source_target_pairs={{1,0},{2,1},{3,2},{5,4},{6,5},{7,6},{9,8},{10,9},{11,10},{13,12},{... | collective-permute-start | bytes 786440 | tf_op jit(solution)/shard_map/ppermute | solution.py:399
  78.6 2.4 %collective-permute-start.14 = (bf16[4,4,32,768]{3,2,1,0:T(8,128)(2,1)S(1)}, bf16[4,4,32,768]{3,2,1,0:T(8,128)(2,1)S(1)}, u32[]{:S(2)}, u32[]{:S(2)}) collective-permute-start(bf16[4,4,32,768]{3,2,1,0:T(8,128)(2,1)S(1)} %get-tuple-element.77), channel_id=1, source_target_pairs={{0,4},{4,0},{8,12},{12,8},{16,20},{20,16},{24,28},{28,24},{1,5},{5... | collective-permute-start | bytes 2359304 | tf_op jit(solution)/shard_map/ppermute | solution.py:506
  81.2 10.6 %collective-permute-start.17 = (bf16[4,32,768]{2,1,0:T(8,128)(2,1)S(1)}, bf16[4,32,768]{2,1,0:T(8,128)(2,1)S(1)}, u32[]{:S(2)}, u32[]{:S(2)}) collective-permute-start(bf16[4,32,768]{2,1,0:T(8,128)(2,1)S(1)} %get-tuple-element.85), channel_id=1, source_target_pairs={{0,8},{4,12},{8,0},{12,4},{16,24},{20,28},{24,16},{28,20},{1,9},{5... | collective-permute-start | bytes 589832 | tf_op jit(solution)/shard_map/ppermute | solution.py:511
  82.2 11.1 %collective-permute-start.18 = (bf16[4,32,768]{2,1,0:T(8,128)(2,1)S(1)}, bf16[4,32,768]{2,1,0:T(8,128)(2,1)S(1)}, u32[]{:S(2)}, u32[]{:S(2)}) collective-permute-start(bf16[4,32,768]{2,1,0:T(8,128)(2,1)S(1)} %get-tuple-element.86), channel_id=1, source_target_pairs={{0,16},{4,20},{8,24},{12,28},{16,0},{20,4},{24,8},{28,12},{1,17},{... | collective-permute-start | bytes 589832 | tf_op jit(solution)/shard_map/ppermute | solution.py:511
  82.8 10.5 %collective-permute-start.19 = (bf16[4,32,768]{2,1,0:T(8,128)(2,1)S(1)}, bf16[4,32,768]{2,1,0:T(8,128)(2,1)S(1)}, u32[]{:S(2)}, u32[]{:S(2)}) collective-permute-start(bf16[4,32,768]{2,1,0:T(8,128)(2,1)S(1)} %get-tuple-element.87), channel_id=1, source_target_pairs={{0,24},{4,28},{8,16},{12,20},{16,8},{20,12},{24,0},{28,4},{1,25},{... | collective-permute-start | bytes 589832 | tf_op jit(solution)/shard_map/ppermute | solution.py:511
  93.4 25.4 %collective-permute-start.26 = (bf16[2,512,256]{2,1,0:T(8,128)(2,1)S(1)}, bf16[2,512,256]{2,1,0:T(8,128)(2,1)S(1)}, u32[]{:S(2)}, u32[]{:S(2)}) collective-permute-start(bf16[2,512,256]{2,1,0:T(8,128)(2,1)S(1)} %get-tuple-element.95), channel_id=1, source_target_pairs={{4,0},{8,4},{12,8},{16,12},{20,16},{24,20},{28,24},{5,1},{9,5},{13... | collective-permute-start | bytes 1572872 | tf_op jit(solution)/shard_map/ppermute | solution.py:399
  94.7 24.1 %collective-permute-start.27 = (bf16[2,512,256]{2,1,0:T(8,128)(2,1)S(1)}, bf16[2,512,256]{2,1,0:T(8,128)(2,1)S(1)}, u32[]{:S(2)}, u32[]{:S(2)}) collective-permute-start(bf16[2,512,256]{2,1,0:T(8,128)(2,1)S(1)} %get-tuple-element.95), channel_id=1, source_target_pairs={{0,4},{4,8},{8,12},{12,16},{16,20},{20,24},{24,28},{1,5},{5,9},{9,... | collective-permute-start | bytes 1572872 | tf_op jit(solution)/shard_map/ppermute | solution.py:399
  97.8 4.5 %collective-permute-start.20 = (bf16[32,768]{1,0:T(8,128)(2,1)S(1)}, bf16[32,768]{1,0:T(8,128)(2,1)S(1)}, u32[]{:S(2)}, u32[]{:S(2)}) collective-permute-start(bf16[32,768]{1,0:T(8,128)(2,1)S(1)} %get-tuple-element.91), channel_id=1, source_target_pairs={{0,1},{1,0},{2,3},{3,2},{4,5},{5,4},{6,7},{7,6},{8,9},{9,8},{10,11... | collective-permute-start | bytes 147464 | tf_op jit(solution)/shard_map/ppermute | solution.py:523
  98.7 6.2 %collective-permute-start.21 = (bf16[32,768]{1,0:T(8,128)(2,1)S(1)}, bf16[32,768]{1,0:T(8,128)(2,1)S(1)}, u32[]{:S(2)}, u32[]{:S(2)}) collective-permute-start(bf16[32,768]{1,0:T(8,128)(2,1)S(1)} %get-tuple-element.92), channel_id=1, source_target_pairs={{0,2},{1,3},{2,0},{3,1},{4,6},{5,7},{6,4},{7,5},{8,10},{9,11},{10,... | collective-permute-start | bytes 147464 | tf_op jit(solution)/shard_map/ppermute | solution.py:523
  100.8 5.9 %collective-permute-start.22 = (bf16[32,768]{1,0:T(8,128)(2,1)S(1)}, bf16[32,768]{1,0:T(8,128)(2,1)S(1)}, u32[]{:S(2)}, u32[]{:S(2)}) collective-permute-start(bf16[32,768]{1,0:T(8,128)(2,1)S(1)} %get-tuple-element.93), channel_id=1, source_target_pairs={{0,3},{1,2},{2,1},{3,0},{4,7},{5,6},{6,5},{7,4},{8,11},{9,10},{10,... | collective-permute-start | bytes 147464 | tf_op jit(solution)/shard_map/ppermute | solution.py:523
  106.8 4.5 %collective-permute-start.23 = (bf16[32,768]{1,0:T(8,128)(2,1)S(1)}, bf16[32,768]{1,0:T(8,128)(2,1)S(1)}, u32[]{:S(2)}, u32[]{:S(2)}) collective-permute-start(bf16[32,768]{1,0:T(8,128)(2,1)S(1)} %line_sum.1.refs_0_), channel_id=1, source_target_pairs={{0,1},{1,0},{2,3},{3,2},{4,5},{5,4},{6,7},{7,6},{8,9},{9,8},{10,11... | collective-permute-start | bytes 147464 | tf_op jit(solution)/shard_map/ppermute | solution.py:529
  107.5 6.4 %collective-permute-start.24 = (bf16[32,768]{1,0:T(8,128)(2,1)S(1)}, bf16[32,768]{1,0:T(8,128)(2,1)S(1)}, u32[]{:S(2)}, u32[]{:S(2)}) collective-permute-start(bf16[32,768]{1,0:T(8,128)(2,1)S(1)} %line_sum.1.refs_0_), channel_id=1, source_target_pairs={{0,2},{1,3},{2,0},{3,1},{4,6},{5,7},{6,4},{7,5},{8,10},{9,11},{10,... | collective-permute-start | bytes 147464 | tf_op jit(solution)/shard_map/ppermute | solution.py:529
  109.3 5.9 %collective-permute-start.25 = (bf16[32,768]{1,0:T(8,128)(2,1)S(1)}, bf16[32,768]{1,0:T(8,128)(2,1)S(1)}, u32[]{:S(2)}, u32[]{:S(2)}) collective-permute-start(bf16[32,768]{1,0:T(8,128)(2,1)S(1)} %line_sum.1.refs_0_), channel_id=1, source_target_pairs={{0,3},{1,2},{2,1},{3,0},{4,7},{5,6},{6,5},{7,4},{8,11},{9,10},{10,... | collective-permute-start | bytes 147464 | tf_op jit(solution)/shard_map/ppermute | solution.py:529
  115.2 8.7 %collective-permute-start.28 = (bf16[4,32,768]{2,1,0:T(8,128)(2,1)S(1)}, bf16[4,32,768]{2,1,0:T(8,128)(2,1)S(1)}, u32[]{:S(2)}, u32[]{:S(2)}) collective-permute-start(bf16[4,32,768]{2,1,0:T(8,128)(2,1)S(1)} %line_place.1.refs_0_), channel_id=1, source_target_pairs={{0,8},{4,12},{8,0},{12,4},{16,24},{20,28},{24,16},{28,20},{1,9},{5... | collective-permute-start | bytes 589832 | tf_op jit(solution)/shard_map/ppermute | solution.py:533
  116.2 9.4 %collective-permute-start.29 = (bf16[4,32,768]{2,1,0:T(8,128)(2,1)S(1)}, bf16[4,32,768]{2,1,0:T(8,128)(2,1)S(1)}, u32[]{:S(2)}, u32[]{:S(2)}) collective-permute-start(bf16[4,32,768]{2,1,0:T(8,128)(2,1)S(1)} %line_place.1.refs_0_), channel_id=1, source_target_pairs={{0,16},{4,20},{8,24},{12,28},{16,0},{20,4},{24,8},{28,12},{1,17},{... | collective-permute-start | bytes 589832 | tf_op jit(solution)/shard_map/ppermute | solution.py:533
  116.7 8.9 %collective-permute-start.30 = (bf16[4,32,768]{2,1,0:T(8,128)(2,1)S(1)}, bf16[4,32,768]{2,1,0:T(8,128)(2,1)S(1)}, u32[]{:S(2)}, u32[]{:S(2)}) collective-permute-start(bf16[4,32,768]{2,1,0:T(8,128)(2,1)S(1)} %line_place.1.refs_0_), channel_id=1, source_target_pairs={{0,24},{4,28},{8,16},{12,20},{16,8},{20,12},{24,0},{28,4},{1,25},{... | collective-permute-start | bytes 589832 | tf_op jit(solution)/shard_map/ppermute | solution.py:533
  125.7 2.4 %collective-permute-start.31 = (bf16[4,4,32,768]{3,2,1,0:T(8,128)(2,1)S(1)}, bf16[4,4,32,768]{3,2,1,0:T(8,128)(2,1)S(1)}, u32[]{:S(2)}, u32[]{:S(2)}) collective-permute-start(bf16[4,4,32,768]{3,2,1,0:T(8,128)(2,1)S(1)} %plane_place.1.mine_ref), channel_id=1, source_target_pairs={{0,4},{4,0},{8,12},{12,8},{16,20},{20,16},{24,28},{28,24},{1,5},{5... | collective-permute-start | bytes 2359304 | tf_op jit(solution)/shard_map/ppermute | solution.py:545

commit v5 on v4

--- a/solution.py
+++ b/solution.py
@@ -433,11 +433,12 @@
     first, last = frames_in[:, :1], frames_in[:, rows - 1 :]
     first, last, near = lax.optimization_barrier((first, last, cot))
     cot_prev, cot_next = neighbours("tm", near, near, 3 if by_corner else None)
+    above, below = neighbours("space", first, last)
     cot_corner = []
     if by_corner:
-        straight, relayed = cot[: frames // 2], cot[frames // 2 :]
+        above, below, late = lax.optimization_barrier((above, below, cot))
+        straight, relayed = late[: frames // 2], late[frames // 2 :]
         relayed = lax.ppermute(relayed, "tm", [(3, 7), (4, 0)])
-    above, below = neighbours("space", first, last)
     back_weights, back_taps = call(
         turn_weights_kernel, "turn_weights", [spatial, temporal],
         [shape((3, 3 * channels, channels), BF16), shape((3 * channels, channels), BF16)], 0, big,
@@ -451,13 +452,13 @@
         sums, straight = lax.optimization_barrier((sums, straight))
         cot_corner.append(lax.ppermute(straight, "tm", [(3, 4), (4, 3)]))
     parts = spread_sums(sums, "space")
-    if by_corner:
-        parts[0], relayed = lax.optimization_barrier((parts[0], relayed))
-        cot_corner.append(lax.ppermute(relayed, "tm", [(7, 4), (0, 3)]))
     x_turned = call(
         turn_kernel, "turned", [frames_in, above, below], shape((3 * channels, frames * pixels), BF16),
         0, 8 * big, [pltpu.VMEM((pixels, 3 * channels), BF16)],
     )
+    if by_corner:
+        parts[1], relayed = lax.optimization_barrier((parts[1], relayed))
+        cot_corner.append(lax.ppermute(relayed, "tm", [(7, 4), (0, 3)]))
     x_turned, *parts = lax.optimization_barrier((x_turned, *parts))
     ahead = (3 * frames) // 4
     act, act_early, act_late, normed, slope = call(

time: 130 us -> 136 us (1.046)
  starting transfers between devices: 51.4 us -> 54.5 us
  waiting for transfers between devices: 29.6 us -> 32.4 us
    ppermute x1, waiting for transfers between devices: 0.4 us -> 5.36 us  [per_device(): cot_corner.append(lax.ppermute(relayed, 'tm', [(7, 4), (0, 3)]))]
    ppermute x10, waiting for transfers between devices: 9.14 us -> 5.73 us  [neighbours(): return (lax.ppermute(high, axis, up), lax.ppermute(low, axis, down))]
    ppermute x2, starting transfers between devices: 2.73 us -> 4.41 us  [spread_sums(): got = lax.ppermute(part, axis, [(i, i ^ step) for i in range(size)])]
  transfers between devices with their start and end apart: 32 -> 32, of which waited for: 16 -> 15; matrix products, arithmetic and copies ran while one was open for 1% -> 1% of each run, Pallas kernels for 33% -> 32%
where the time goes in v5:
time: 136 us
  starting transfers between devices  54.5 us (40%)
  Pallas kernels  45.1 us (33%)
  waiting for transfers between devices  32.4 us (24%)
  local copies, waits for them, and re-layouts  2.8 us (2%)
    pallas_call x17, Pallas kernels, call(): pl.pallas_call(kernel, in_specs=[smem if x.dtype == jnp.int32 else vmem f...  45.1 us
    ppermute x10, starting transfers between devices, neighbours(): return (lax.ppermute(high, axis, up), lax.ppermute(low, axis, down))  22.8 us
    ppermute x10, waiting for transfers between devices, neighbours(): return (lax.ppermute(high, axis, up), lax.ppermute(low, axis, down))  5.73 us
    ppermute x1, waiting for transfers between devices, per_device(): cot_corner.append(lax.ppermute(relayed, 'tm', [(7, 4), (0, 3)]))  5.36 us
    ppermute x3, waiting for transfers between devices, per_device(): lax.ppermute(x, 'space', other_plane(s))  4.68 us
    ppermute x1, starting transfers between devices, per_device(): cot_corner.append(lax.ppermute(relayed, 'tm', [(7, 4), (0, 3)]))  4.57 us
    ppermute x3, starting transfers between devices, per_device(): lax.ppermute(x, 'space', other_plane(s))  4.52 us
    ppermute x3, starting transfers between devices, per_device(): gots = [lax.ppermute(own, 'space', other_plane(s)) for s in range(1, n)]  4.45 us
  transfers between devices with their start and end apart: 32, of which 15 were waited for; matrix products, arithmetic and copies ran while one was open for 1% of the time, Pallas kernels for 32%

profile of v5, /device:TPU:0, one launch (start us, length us, event | category | flops | bytes accessed | tf_op | source)
XLA Modules:
  0.0 135.8 jit_solution(12456186244988107880)
XLA Ops:
  0.6 1.1 fusion.1
  1.7 5.2 %collective-permute-start = (bf16[8,1,64,256]{3,2,1,0:T(8,128)(2,1)S(1)}, bf16[8,1,64,256]{3,2,1,0:T(8,128)(2,1)S(1)}, u32[]{:S(2)}, u32[]{:S(2)}) collective-permute-start(bf16[8,1,64,256]{3,2,1,0:T(8,128)(2,1)S(1)} %get-tuple-element.56), channel_id=1, source_target_pairs={{0,1},{1,2},{2,3},{4,5},{5,6},{6,7},{8,9},{9,10},{10,11},{12,13},{... | collective-permute-start | bytes 786440 | tf_op jit(solution)/shard_map/ppermute | solution.py:399
  6.9 1.3 collective-permute-start.1
  8.2 1.3 collective-permute-start.5
  9.5 3.2 %collective-permute-start.6 = (bf16[8,512,256]{2,1,0:T(8,128)(2,1)}, bf16[8,512,256]{2,1,0:T(8,128)(2,1)S(1)}, u32[]{:S(2)}, u32[]{:S(2)}) collective-permute-start(bf16[8,512,256]{2,1,0:T(8,128)(2,1)} %bitcast.5), channel_id=1, source_target_pairs={{0,4},{4,8},{8,12},{16,20},{20,24},{24,28},{1,5},{5,9},{9,13},{17,... | collective-permute-start | bytes 6291464 | tf_op jit(solution)/shard_map/ppermute | solution.py:399
  12.7 3.9 %collective-permute-done.1.below_ref = bf16[8,1,64,256]{3,2,1,0:T(8,128)(2,1)S(1)} collective-permute-done((bf16[8,1,64,256]{3,2,1,0:T(8,128)(2,1)S(1)}, bf16[8,1,64,256]{3,2,1,0:T(8,128)(2,1)S(1)}, u32[]{:S(2)}, u32[]{:S(2)}) %collective-permute-start.1) | collective-permute-done | bytes 262176 | tf_op jit(solution)/shard_map/ppermute | solution.py:399
  16.6 1.7 %fusion = (bf16[4,512,256]{2,1,0:T(8,128)(2,1)S(1)}, bf16[4,512,256]{2,1,0:T(8,128)(2,1)S(1)}) fusion(bf16[8,512,256]{2,1,0:T(8,128)(2,1)} %bitcast.6), kind=kLoop, calls=%fused_computation | loop fusion | bytes 4194304 | tf_op jit(solution)/shard_map/slice | solution.py:440
  18.3 1.4 %collective-permute-start.4 = (bf16[4,512,256]{2,1,0:T(8,128)(2,1)S(1)}, bf16[4,512,256]{2,1,0:T(8,128)(2,1)S(1)}, u32[]{:S(2)}, u32[]{:S(2)}) collective-permute-start(bf16[4,512,256]{2,1,0:T(8,128)(2,1)S(1)} %get-tuple-element.108), channel_id=1, source_target_pairs={{12,28},{16,0},{13,29},{17,1},{14,30},{18,2},{15,31},{19,3}} | collective-permute-start | bytes 3145736 | tf_op jit(solution)/shard_map/ppermute | solution.py:441
  19.7 5.7 %conv_forward.1 = (f32[8,512,256]{2,1,0:T(8,128)S(1)}, f32[8,2,256]{2,1,0:T(2,128)S(1)}) custom-call(bf16[8,8,64,256]{3,2,1,0:T(8,128)(2,1)S(1)} %copy-done, bf16[8,1,64,256]{3,2,1,0:T(8,128)(2,1)S(1)} %collective-permute-done.above_ref, bf16[8,1,64,256]{3,2,1,0:T(8,128)(2,1)S(1)} %collective-permute-done.1.below_ref, bf16[3,3,256,256]{3,2,1,0:T(8,128)(2,1)S(1)} %copy-done.3), custom_call_target="tpu_custom_call" | custom-call | flops 26843545600 | bytes 8388608 | tf_op jit(solution)/shard_map/conv_forward/pallas_call | solution.py:20
  25.5 1.6 %collective-permute-start.2 = (f32[8,2,256]{2,1,0:T(2,128)S(1)}, f32[8,2,256]{2,1,0:T(2,128)S(1)}, u32[]{:S(2)}, u32[]{:S(2)}) collective-permute-start(f32[8,2,256]{2,1,0:T(2,128)S(1)} %get-tuple-element.62), channel_id=1, source_target_pairs={{0,1},{1,0},{2,3},{3,2},{4,5},{5,4},{6,7},{7,6},{8,9},{9,8},{10,11... | collective-permute-start | bytes 49160 | tf_op jit(solution)/shard_map/ppermute | solution.py:413
  27.1 2.2 %collective-permute-done.2 = f32[8,2,256]{2,1,0:T(2,128)S(1)} collective-permute-done((f32[8,2,256]{2,1,0:T(2,128)S(1)}, f32[8,2,256]{2,1,0:T(2,128)S(1)}, u32[]{:S(2)}, u32[]{:S(2)}) %collective-permute-start.2) | collective-permute-done | bytes 16416 | tf_op jit(solution)/shard_map/ppermute | solution.py:413
  29.3 2.8 %collective-permute-start.3 = (f32[8,2,256]{2,1,0:T(2,128)S(1)}, f32[8,2,256]{2,1,0:T(2,128)S(1)}, u32[]{:S(2)}, u32[]{:S(2)}) collective-permute-start(f32[8,2,256]{2,1,0:T(2,128)S(1)} %add.3.refs_0_), channel_id=1, source_target_pairs={{0,2},{1,3},{2,0},{3,1},{4,6},{5,7},{6,4},{7,5},{8,10},{9,11},{10,... | collective-permute-start | bytes 49160 | tf_op jit(solution)/shard_map/ppermute | solution.py:413
  32.0 0.7 collective-permute-start.7
  32.8 1.2 collective-permute-done.3.refs_1_
  34.0 1.1 collective-permute-done.4
  35.1 4.6 %collective-permute-start.8 = (bf16[4,512,256]{2,1,0:T(8,128)(2,1)S(1)}, bf16[4,512,256]{2,1,0:T(8,128)(2,1)S(1)}, u32[]{:S(2)}, u32[]{:S(2)}) collective-permute-start(bf16[4,512,256]{2,1,0:T(8,128)(2,1)S(1)} %collective-permute-done.4), channel_id=1, source_target_pairs={{28,16},{0,12},{29,17},{1,13},{30,18},{2,14},{31,19},{3,15}} | collective-permute-start | bytes 3145736 | tf_op jit(solution)/shard_map/ppermute | solution.py:461
  39.7 0.5 turn_weights.1
  40.2 2.2 %turned.1.xt_ref = bf16[768,4096]{1,0:T(8,128)(2,1)S(1)} custom-call(bf16[8,8,64,256]{3,2,1,0:T(8,128)(2,1)S(1)} %copy-done, bf16[8,1,64,256]{3,2,1,0:T(8,128)(2,1)S(1)} %collective-permute-done.above_ref, bf16[8,1,64,256]{3,2,1,0:T(8,128)(2,1)S(1)} %collective-permute-done.1.below_ref), custom_call_target="tpu_custom_call" | custom-call | bytes 8388608 | tf_op jit(solution)/shard_map/turned/pallas_call | solution.py:20
  42.4 6.2 %activation.1 = (bf16[8,512,256]{2,1,0:T(8,128)(2,1)S(1)}, bf16[6,512,256]{2,1,0:T(8,128)(2,1)S(1)}, bf16[2,512,256]{2,1,0:T(8,128)(2,1)S(1)}, bf16[8,512,256]{2,1,0:T(8,128)(2,1)S(1)}, bf16[8,512,256]{2,1,0:T(8,128)(2,1)S(1)}) custom-call(s32[2]{0:T(128)S(1)} %copy-done.4, f32[8,2,256]{2,1,0:T(2,128)S(1)} %add.3.refs_0_, ...), custom_call_target="tpu_custom_call" | custom-call | flops 10485760 | bytes 10485760 | tf_op jit(solution)/shard_map/activation/pallas_call | solution.py:20
  48.7 1.4 %collective-permute-start.15 = (bf16[6,512,256]{2,1,0:T(8,128)(2,1)S(1)}, bf16[6,512,256]{2,1,0:T(8,128)(2,1)S(1)}, u32[]{:S(2)}, u32[]{:S(2)}) collective-permute-start(bf16[6,512,256]{2,1,0:T(8,128)(2,1)S(1)} %get-tuple-element.89), channel_id=1, source_target_pairs={{0,4},{4,8},{8,12},{12,16},{16,20},{20,24},{24,28},{1,5},{5,9},{9,... | collective-permute-start | bytes 4718600 | tf_op jit(solution)/shard_map/ppermute | solution.py:399
  50.1 1.3 collective-permute-start.16
  51.4 5.4 %collective-permute-done.8.refs_1_ = bf16[4,512,256]{2,1,0:T(8,128)(2,1)S(1)} collective-permute-done((bf16[4,512,256]{2,1,0:T(8,128)(2,1)S(1)}, bf16[4,512,256]{2,1,0:T(8,128)(2,1)S(1)}, u32[]{:S(2)}, u32[]{:S(2)}) %collective-permute-start.8) | collective-permute-done | bytes 1048608 | tf_op jit(solution)/shard_map/ppermute | solution.py:461
  56.8 4.2 %grad_activation.1 = (bf16[8,512,256]{2,1,0:T(8,128)(2,1)S(1)}, bf16[4096,768]{1,0:T(8,128)(2,1)S(1)}, f32[8,2,256]{2,1,0:T(2,128)S(1)}) custom-call(s32[2]{0:T(128)S(1)} %copy-done.4, s32[2]{0:T(128)S(1)} %copy-done.5, bf16[8,512,256]{2,1,0:T(8,128)(2,1)S(1)} %bitcast.7, bf16[8,512,256]{2,1,0:T(8,128)(2,1)S(1)} %collective-permute-done.5.nxt, ...), custom_call_target="tpu_custom_call" | custom-call | flops 1610612736 | bytes 16777216 | tf_op jit(solution)/shard_map/grad_activation/pallas_call | solution.py:20
  61.0 0.1 collective-permute-start.10
  61.1 0.8 collective-permute-start.11
  61.9 2.7 %collective-permute-start.9 = (f32[8,2,256]{2,1,0:T(2,128)S(1)}, f32[8,2,256]{2,1,0:T(2,128)S(1)}, u32[]{:S(2)}, u32[]{:S(2)}) collective-permute-start(f32[8,2,256]{2,1,0:T(2,128)S(1)} %get-tuple-element.75.refs_2_), channel_id=1, source_target_pairs={{0,1},{1,0},{2,3},{3,2},{4,5},{5,4},{6,7},{7,6},{8,9},{9,8},{10,11... | collective-permute-start | bytes 49160 | tf_op jit(solution)/shard_map/ppermute | solution.py:404
  64.6 1.9 %temporal_grad.1.temporal_ref = f32[256,768]{1,0:T(8,128)S(1)} custom-call(bf16[8,512,256]{2,1,0:T(8,128)(2,1)S(1)} %get-tuple-element.77.act_ref.own, bf16[4096,768]{1,0:T(8,128)(2,1)S(1)} %get-tuple-element.78.cat_ref), custom_call_target="tpu_custom_call" | custom-call | flops 1610612736 | bytes 8388608 | tf_op jit(solution)/shard_map/temporal_grad/pallas_call | solution.py:20
  66.4 0.2 collective-permute-done.11.refs_5_
  66.7 4.6 %norm_backward.1 = (bf16[8,512,256]{2,1,0:T(8,128)(2,1)S(1)}, bf16[8,1,64,256]{3,2,1,0:T(8,128)(2,1)S(1)}, bf16[8,1,64,256]{3,2,1,0:T(8,128)(2,1)S(1)}, bf16[4096,768]{1,0:T(8,128)(2,1)S(1)}) custom-call(bf16[8,512,256]{2,1,0:T(8,128)(2,1)S(1)} %get-tuple-element.68.refs_3_.normed_ref, bf16[8,512,256]{2,1,0:T(8,128)(2,1)S(1)} %get-tuple-element.69.refs_4_.slope_ref, ...), custom_call_target="tpu_custom_call" | custom-call | bytes 12582912 | tf_op jit(solution)/shard_map/norm_backward/pallas_call | solution.py:20
  71.3 3.5 %collective-permute-start.12 = (bf16[8,1,64,256]{3,2,1,0:T(8,128)(2,1)S(1)}, bf16[8,1,64,256]{3,2,1,0:T(8,128)(2,1)S(1)}, u32[]{:S(2)}, u32[]{:S(2)}) collective-permute-start(bf16[8,1,64,256]{3,2,1,0:T(8,128)(2,1)S(1)} %get-tuple-element.79), channel_id=1, source_target_pairs={{0,1},{1,2},{2,3},{4,5},{5,6},{6,7},{8,9},{9,10},{10,11},{12,13},{... | collective-permute-start | bytes 786440 | tf_op jit(solution)/shard_map/ppermute | solution.py:399
  74.8 1.3 collective-permute-start.13
  76.1 5.1 %weight_grad.1.acc_ref = f32[1024,768]{1,0:T(8,128)S(1)} custom-call(bf16[768,4096]{1,0:T(8,128)(2,1)S(1)} %turned.1.xt_ref, bf16[4096,768]{1,0:T(8,128)(2,1)S(1)} %get-tuple-element.76.moved_ref, f32[256,768]{1,0:T(8,128)S(1)} %temporal_grad.1.temporal_ref), custom_call_target="tpu_custom_call" | custom-call | flops 4831838208 | bytes 12582912 | tf_op jit(solution)/shard_map/weight_grad/pallas_call | solution.py:20
  81.2 1.8 %collective-permute-done.13.below_ref = bf16[8,1,64,256]{3,2,1,0:T(8,128)(2,1)S(1)} collective-permute-done((bf16[8,1,64,256]{3,2,1,0:T(8,128)(2,1)S(1)}, bf16[8,1,64,256]{3,2,1,0:T(8,128)(2,1)S(1)}, u32[]{:S(2)}, u32[]{:S(2)}) %collective-permute-start.13) | collective-permute-done | bytes 262176 | tf_op jit(solution)/shard_map/ppermute | solution.py:399
  83.1 0.4 hand_out.1
  83.4 0.1 collective-permute-start.14
  83.5 2.3 %collective-permute-done.14.got_ref = bf16[4,4,32,768]{3,2,1,0:T(8,128)(2,1)S(1)} collective-permute-done((bf16[4,4,32,768]{3,2,1,0:T(8,128)(2,1)S(1)}, bf16[4,4,32,768]{3,2,1,0:T(8,128)(2,1)S(1)}, u32[]{:S(2)}, u32[]{:S(2)}) %collective-permute-start.14) | collective-permute-done | bytes 786464 | tf_op jit(solution)/shard_map/ppermute | solution.py:507
  85.8 0.2 core_sum.1
  86.0 0.1 collective-permute-start.17
  86.1 2.9 %collective-permute-start.18 = (bf16[4,32,768]{2,1,0:T(8,128)(2,1)S(1)}, bf16[4,32,768]{2,1,0:T(8,128)(2,1)S(1)}, u32[]{:S(2)}, u32[]{:S(2)}) collective-permute-start(bf16[4,32,768]{2,1,0:T(8,128)(2,1)S(1)} %get-tuple-element.92), channel_id=1, source_target_pairs={{0,16},{4,20},{8,24},{12,28},{16,0},{20,4},{24,8},{28,12},{1,17},{... | collective-permute-start | bytes 589832 | tf_op jit(solution)/shard_map/ppermute | solution.py:512
  88.9 1.4 %collective-permute-start.19 = (bf16[4,32,768]{2,1,0:T(8,128)(2,1)S(1)}, bf16[4,32,768]{2,1,0:T(8,128)(2,1)S(1)}, u32[]{:S(2)}, u32[]{:S(2)}) collective-permute-start(bf16[4,32,768]{2,1,0:T(8,128)(2,1)S(1)} %get-tuple-element.93), channel_id=1, source_target_pairs={{0,24},{4,28},{8,16},{12,20},{16,8},{20,12},{24,0},{28,4},{1,25},{... | collective-permute-start | bytes 589832 | tf_op jit(solution)/shard_map/ppermute | solution.py:512
  90.3 7.0 %conv_backward.1 = bf16[8,8,64,256]{3,2,1,0:T(8,128)(2,1)} custom-call(bf16[8,512,256]{2,1,0:T(8,128)(2,1)S(1)} %get-tuple-element.85.g_ref, bf16[8,1,64,256]{3,2,1,0:T(8,128)(2,1)S(1)} %collective-permute-done.12.above_ref, bf16[8,1,64,256]{3,2,1,0:T(8,128)(2,1)S(1)} %collective-permute-done.13.below_ref, bf16[8,8,64,256]{3,2,1,0:T(8,128)(2,1)S(1)} %copy-done.1, ...), custom_call_target="tpu_custom_call" | custom-call | flops 4831838208 | bytes 8388608 | tf_op jit(solution)/shard_map/conv_backward/pallas_call | solution.py:20
  97.3 0.3 collective-permute-done.18.refs_1_
  97.6 1.8 %collective-permute-done.19.refs_2_ = bf16[4,32,768]{2,1,0:T(8,128)(2,1)S(1)} collective-permute-done((bf16[4,32,768]{2,1,0:T(8,128)(2,1)S(1)}, bf16[4,32,768]{2,1,0:T(8,128)(2,1)S(1)}, u32[]{:S(2)}, u32[]{:S(2)}) %collective-permute-start.19) | collective-permute-done | bytes 196640 | tf_op jit(solution)/shard_map/ppermute | solution.py:512
  99.4 0.1 plane_sum.1
  99.5 1.3 collective-permute-start.26
  100.8 3.1 %collective-permute-start.27 = (bf16[2,512,256]{2,1,0:T(8,128)(2,1)S(1)}, bf16[2,512,256]{2,1,0:T(8,128)(2,1)S(1)}, u32[]{:S(2)}, u32[]{:S(2)}) collective-permute-start(bf16[2,512,256]{2,1,0:T(8,128)(2,1)S(1)} %get-tuple-element.101), channel_id=1, source_target_pairs={{0,4},{4,8},{8,12},{12,16},{16,20},{20,24},{24,28},{1,5},{5,9},{9,... | collective-permute-start | bytes 1572872 | tf_op jit(solution)/shard_map/ppermute | solution.py:399
  103.9 2.1 %collective-permute-start.20 = (bf16[32,768]{1,0:T(8,128)(2,1)S(1)}, bf16[32,768]{1,0:T(8,128)(2,1)S(1)}, u32[]{:S(2)}, u32[]{:S(2)}) collective-permute-start(bf16[32,768]{1,0:T(8,128)(2,1)S(1)} %get-tuple-element.97), channel_id=1, source_target_pairs={{0,1},{1,0},{2,3},{3,2},{4,5},{5,4},{6,7},{7,6},{8,9},{9,8},{10,11... | collective-permute-start | bytes 147464 | tf_op jit(solution)/shard_map/ppermute | solution.py:524
  106.0 0.7 collective-permute-start.21
  106.7 1.7 %collective-permute-start.22 = (bf16[32,768]{1,0:T(8,128)(2,1)S(1)}, bf16[32,768]{1,0:T(8,128)(2,1)S(1)}, u32[]{:S(2)}, u32[]{:S(2)}) collective-permute-start(bf16[32,768]{1,0:T(8,128)(2,1)S(1)} %get-tuple-element.99), channel_id=1, source_target_pairs={{0,3},{1,2},{2,1},{3,0},{4,7},{5,6},{6,5},{7,4},{8,11},{9,10},{10,... | collective-permute-start | bytes 147464 | tf_op jit(solution)/shard_map/ppermute | solution.py:524
  108.4 4.7 %collective-permute-done.21.refs_1_ = bf16[32,768]{1,0:T(8,128)(2,1)S(1)} collective-permute-done((bf16[32,768]{1,0:T(8,128)(2,1)S(1)}, bf16[32,768]{1,0:T(8,128)(2,1)S(1)}, u32[]{:S(2)}, u32[]{:S(2)}) %collective-permute-start.21) | collective-permute-done | bytes 49184 | tf_op jit(solution)/shard_map/ppermute | solution.py:524
  113.1 1.3 collective-permute-start.23
  114.5 1.2 collective-permute-start.24
  115.6 1.9 %collective-permute-start.25 = (bf16[32,768]{1,0:T(8,128)(2,1)S(1)}, bf16[32,768]{1,0:T(8,128)(2,1)S(1)}, u32[]{:S(2)}, u32[]{:S(2)}) collective-permute-start(bf16[32,768]{1,0:T(8,128)(2,1)S(1)} %line_sum.1.refs_0_), channel_id=1, source_target_pairs={{0,3},{1,2},{2,1},{3,0},{4,7},{5,6},{6,5},{7,4},{8,11},{9,10},{10,... | collective-permute-start | bytes 147464 | tf_op jit(solution)/shard_map/ppermute | solution.py:530
  117.6 2.8 %collective-permute-done.24.refs_2_ = bf16[32,768]{1,0:T(8,128)(2,1)S(1)} collective-permute-done((bf16[32,768]{1,0:T(8,128)(2,1)S(1)}, bf16[32,768]{1,0:T(8,128)(2,1)S(1)}, u32[]{:S(2)}, u32[]{:S(2)}) %collective-permute-start.24) | collective-permute-done | bytes 49184 | tf_op jit(solution)/shard_map/ppermute | solution.py:530
  120.4 1.1 collective-permute-done.25.refs_3_
  121.6 0.9 collective-permute-start.28
  122.4 0.9 collective-permute-start.29
  123.4 1.8 %collective-permute-start.30 = (bf16[4,32,768]{2,1,0:T(8,128)(2,1)S(1)}, bf16[4,32,768]{2,1,0:T(8,128)(2,1)S(1)}, u32[]{:S(2)}, u32[]{:S(2)}) collective-permute-start(bf16[4,32,768]{2,1,0:T(8,128)(2,1)S(1)} %line_place.1.refs_0_), channel_id=1, source_target_pairs={{0,24},{4,28},{8,16},{12,20},{16,8},{20,12},{24,0},{28,4},{1,25},{... | collective-permute-start | bytes 589832 | tf_op jit(solution)/shard_map/ppermute | solution.py:534
  125.1 5.2 %temporal_forward.1 = bf16[8,8,64,256]{3,2,1,0:T(8,128)(2,1)} custom-call(s32[2]{0:T(128)S(1)} %copy-done.4, s32[2]{0:T(128)S(1)} %copy-done.5, bf16[8,512,256]{2,1,0:T(8,128)(2,1)S(1)} %get-tuple-element.77.act_ref.own, bf16[6,512,256]{2,1,0:T(8,128)(2,1)S(1)} %collective-permute-done.16.nxt_a, bf16[2,512,256]{2,1,0:T(8,128)(2,1)S(1)} %collective-permute-done.26.nxt_b, ...), custom_call_target="tpu_custom_call" | custom-call | flops 1610612736 | bytes 10485760 | tf_op jit(solution)/shard_map/temporal_forward/pallas_call | solution.py:20
  130.3 1.3 collective-permute-done.29.refs_2_
  131.6 0.1 plane_place.1.mine_ref
  131.6 0.1 collective-permute-start.31
  131.7 2.3 %collective-permute-done.31.got_ref = bf16[4,4,32,768]{3,2,1,0:T(8,128)(2,1)S(1)} collective-permute-done((bf16[4,4,32,768]{3,2,1,0:T(8,128)(2,1)S(1)}, bf16[4,4,32,768]{3,2,1,0:T(8,128)(2,1)S(1)}, u32[]{:S(2)}, u32[]{:S(2)}) %collective-permute-start.31) | collective-permute-done | bytes 786464 | tf_op jit(solution)/shard_map/ppermute | solution.py:546
  134.0 1.9 %finish.1 = (f32[3,3,256,256]{3,2,1,0:T(8,128)}, f32[3,256,256]{2,1,0:T(8,128)}) custom-call(bf16[4,4,32,768]{3,2,1,0:T(8,128)(2,1)S(1)} %plane_place.1.mine_ref, bf16[4,4,32,768]{3,2,1,0:T(8,128)(2,1)S(1)} %collective-permute-done.31.got_ref), custom_call_target="tpu_custom_call" | custom-call | bytes 4194304 | tf_op jit(solution)/shard_map/finish/pallas_call | solution.py:20
  (36 shorter events, 0.2 us)
Async XLA Ops:
  1.7 18.0 %copy-start = (bf16[8,8,64,256]{3,2,1,0:T(8,128)(2,1)S(1)}, bf16[8,8,64,256]{3,2,1,0:T(8,128)(2,1)}, u32[]{:S(2)}) copy-start(bf16[8,8,64,256]{3,2,1,0:T(8,128)(2,1)} %x_ref.5) | copy-start | bytes 6291460
  1.7 18.0 %copy-start.3 = (bf16[3,3,256,256]{3,2,1,0:T(8,128)(2,1)S(1)}, bf16[3,3,256,256]{3,2,1,0:T(8,128)(2,1)}, u32[]{:S(2)}) copy-start(bf16[3,3,256,256]{3,2,1,0:T(8,128)(2,1)} %spatial_ref.1) | copy-start | bytes 3538948
  1.7 11.0 %collective-permute-start = (bf16[8,1,64,256]{3,2,1,0:T(8,128)(2,1)S(1)}, bf16[8,1,64,256]{3,2,1,0:T(8,128)(2,1)S(1)}, u32[]{:S(2)}, u32[]{:S(2)}) collective-permute-start(bf16[8,1,64,256]{3,2,1,0:T(8,128)(2,1)S(1)} %get-tuple-element.56), channel_id=1, source_target_pairs={{0,1},{1,2},{2,3},{4,5},{5,6},{6,7},{8,9},{9,10},{10,11},{12,13},{... | collective-permute-start | bytes 786440 | tf_op jit(solution)/shard_map/ppermute | solution.py:399
  6.9 9.7 %collective-permute-start.1 = (bf16[8,1,64,256]{3,2,1,0:T(8,128)(2,1)S(1)}, bf16[8,1,64,256]{3,2,1,0:T(8,128)(2,1)S(1)}, u32[]{:S(2)}, u32[]{:S(2)}) collective-permute-start(bf16[8,1,64,256]{3,2,1,0:T(8,128)(2,1)S(1)} %get-tuple-element.57), channel_id=1, source_target_pairs={{1,0},{2,1},{3,2},{5,4},{6,5},{7,6},{9,8},{10,9},{11,10},{13,12},{... | collective-permute-start | bytes 786440 | tf_op jit(solution)/shard_map/ppermute | solution.py:399
  8.2 43.2 %collective-permute-start.5 = (bf16[8,512,256]{2,1,0:T(8,128)(2,1)}, bf16[8,512,256]{2,1,0:T(8,128)(2,1)S(1)}, u32[]{:S(2)}, u32[]{:S(2)}) collective-permute-start(bf16[8,512,256]{2,1,0:T(8,128)(2,1)} %bitcast.4), channel_id=1, source_target_pairs={{4,0},{8,4},{12,8},{20,16},{24,20},{28,24},{5,1},{9,5},{13,9},{21,... | collective-permute-start | bytes 6291464 | tf_op jit(solution)/shard_map/ppermute | solution.py:399
  9.5 41.9 %collective-permute-start.6 = (bf16[8,512,256]{2,1,0:T(8,128)(2,1)}, bf16[8,512,256]{2,1,0:T(8,128)(2,1)S(1)}, u32[]{:S(2)}, u32[]{:S(2)}) collective-permute-start(bf16[8,512,256]{2,1,0:T(8,128)(2,1)} %bitcast.5), channel_id=1, source_target_pairs={{0,4},{4,8},{8,12},{16,20},{20,24},{24,28},{1,5},{5,9},{9,13},{17,... | collective-permute-start | bytes 6291464 | tf_op jit(solution)/shard_map/ppermute | solution.py:399
  18.3 21.4 %copy-start.2 = (bf16[3,256,256]{2,1,0:T(8,128)(2,1)S(1)}, bf16[3,256,256]{2,1,0:T(8,128)(2,1)}, u32[]{:S(2)}) copy-start(bf16[3,256,256]{2,1,0:T(8,128)(2,1)} %temporal_ref.1) | copy-start | bytes 1179652
  18.3 16.8 %collective-permute-start.4 = (bf16[4,512,256]{2,1,0:T(8,128)(2,1)S(1)}, bf16[4,512,256]{2,1,0:T(8,128)(2,1)S(1)}, u32[]{:S(2)}, u32[]{:S(2)}) collective-permute-start(bf16[4,512,256]{2,1,0:T(8,128)(2,1)S(1)} %get-tuple-element.108), channel_id=1, source_target_pairs={{12,28},{16,0},{13,29},{17,1},{14,30},{18,2},{15,31},{19,3}} | collective-permute-start | bytes 3145736 | tf_op jit(solution)/shard_map/ppermute | solution.py:441
  25.5 3.8 %collective-permute-start.2 = (f32[8,2,256]{2,1,0:T(2,128)S(1)}, f32[8,2,256]{2,1,0:T(2,128)S(1)}, u32[]{:S(2)}, u32[]{:S(2)}) collective-permute-start(f32[8,2,256]{2,1,0:T(2,128)S(1)} %get-tuple-element.62), channel_id=1, source_target_pairs={{0,1},{1,0},{2,3},{3,2},{4,5},{5,4},{6,7},{7,6},{8,9},{9,8},{10,11... | collective-permute-start | bytes 49160 | tf_op jit(solution)/shard_map/ppermute | solution.py:413
  29.3 4.7 %collective-permute-start.3 = (f32[8,2,256]{2,1,0:T(2,128)S(1)}, f32[8,2,256]{2,1,0:T(2,128)S(1)}, u32[]{:S(2)}, u32[]{:S(2)}) collective-permute-start(f32[8,2,256]{2,1,0:T(2,128)S(1)} %add.3.refs_0_), channel_id=1, source_target_pairs={{0,2},{1,3},{2,0},{3,1},{4,6},{5,7},{6,4},{7,5},{8,10},{9,11},{10,... | collective-permute-start | bytes 49160 | tf_op jit(solution)/shard_map/ppermute | solution.py:413
  32.0 18.0 %collective-permute-start.7 = (bf16[4,512,256]{2,1,0:T(8,128)(2,1)S(1)}, bf16[4,512,256]{2,1,0:T(8,128)(2,1)S(1)}, u32[]{:S(2)}, u32[]{:S(2)}) collective-permute-start(bf16[4,512,256]{2,1,0:T(8,128)(2,1)S(1)} %get-tuple-element.71), channel_id=1, source_target_pairs={{12,16},{16,12},{13,17},{17,13},{14,18},{18,14},{15,19},{19,15}} | collective-permute-start | bytes 3145736 | tf_op jit(solution)/shard_map/ppermute | solution.py:453
  35.1 21.7 %collective-permute-start.8 = (bf16[4,512,256]{2,1,0:T(8,128)(2,1)S(1)}, bf16[4,512,256]{2,1,0:T(8,128)(2,1)S(1)}, u32[]{:S(2)}, u32[]{:S(2)}) collective-permute-start(bf16[4,512,256]{2,1,0:T(8,128)(2,1)S(1)} %collective-permute-done.4), channel_id=1, source_target_pairs={{28,16},{0,12},{29,17},{1,13},{30,18},{2,14},{31,19},{3,15}} | collective-permute-start | bytes 3145736 | tf_op jit(solution)/shard_map/ppermute | solution.py:461
  40.2 2.2 %copy-start.4 = (s32[2]{0:T(128)S(1)}, s32[2]{0:T(128)}, u32[]{:S(2)}) copy-start(s32[2]{0:T(128)} %clip_ref.5) | copy-start | bytes 28
  40.2 2.2 %copy-start.6 = (f32[256]{0:T(256)S(1)}, f32[256]{0:T(256)}, u32[]{:S(2)}) copy-start(f32[256]{0:T(256)} %param.12) | copy-start | bytes 3076
  40.2 2.2 %copy-start.7 = (f32[256]{0:T(256)S(1)}, f32[256]{0:T(256)}, u32[]{:S(2)}) copy-start(f32[256]{0:T(256)} %param.13) | copy-start | bytes 3076
  42.4 14.4 %copy-start.1 = (bf16[8,8,64,256]{3,2,1,0:T(8,128)(2,1)S(1)}, bf16[8,8,64,256]{3,2,1,0:T(8,128)(2,1)}, u32[]{:S(2)}) copy-start(bf16[8,8,64,256]{3,2,1,0:T(8,128)(2,1)} %cot_ref.1) | copy-start | bytes 6291460
  42.4 14.4 %copy-start.5 = (s32[2]{0:T(128)S(1)}, s32[2]{0:T(128)}, u32[]{:S(2)}) copy-start(s32[2]{0:T(128)} %dil_ref.3) | copy-start | bytes 28
  48.7 48.6 %collective-permute-start.15 = (bf16[6,512,256]{2,1,0:T(8,128)(2,1)S(1)}, bf16[6,512,256]{2,1,0:T(8,128)(2,1)S(1)}, u32[]{:S(2)}, u32[]{:S(2)}) collective-permute-start(bf16[6,512,256]{2,1,0:T(8,128)(2,1)S(1)} %get-tuple-element.89), channel_id=1, source_target_pairs={{0,4},{4,8},{8,12},{12,16},{16,20},{20,24},{24,28},{1,5},{5,9},{9,... | collective-permute-start | bytes 4718600 | tf_op jit(solution)/shard_map/ppermute | solution.py:399
  50.1 47.2 %collective-permute-start.16 = (bf16[6,512,256]{2,1,0:T(8,128)(2,1)S(1)}, bf16[6,512,256]{2,1,0:T(8,128)(2,1)S(1)}, u32[]{:S(2)}, u32[]{:S(2)}) collective-permute-start(bf16[6,512,256]{2,1,0:T(8,128)(2,1)S(1)} %get-tuple-element.89), channel_id=1, source_target_pairs={{4,0},{8,4},{12,8},{16,12},{20,16},{24,20},{28,24},{5,1},{9,5},{13... | collective-permute-start | bytes 4718600 | tf_op jit(solution)/shard_map/ppermute | solution.py:399
  61.0 5.4 %collective-permute-start.10 = (f32[8,2,256]{2,1,0:T(2,128)S(1)}, f32[8,2,256]{2,1,0:T(2,128)S(1)}, u32[]{:S(2)}, u32[]{:S(2)}) collective-permute-start(f32[8,2,256]{2,1,0:T(2,128)S(1)} %get-tuple-element.75.refs_2_), channel_id=1, source_target_pairs={{0,2},{1,3},{2,0},{3,1},{4,6},{5,7},{6,4},{7,5},{8,10},{9,11},{10,... | collective-permute-start | bytes 49160 | tf_op jit(solution)/shard_map/ppermute | solution.py:404
  61.1 5.6 %collective-permute-start.11 = (f32[8,2,256]{2,1,0:T(2,128)S(1)}, f32[8,2,256]{2,1,0:T(2,128)S(1)}, u32[]{:S(2)}, u32[]{:S(2)}) collective-permute-start(f32[8,2,256]{2,1,0:T(2,128)S(1)} %get-tuple-element.75.refs_2_), channel_id=1, source_target_pairs={{0,3},{1,2},{2,1},{3,0},{4,7},{5,6},{6,5},{7,4},{8,11},{9,10},{10,... | collective-permute-start | bytes 49160 | tf_op jit(solution)/shard_map/ppermute | solution.py:404
  61.9 4.8 %collective-permute-start.9 = (f32[8,2,256]{2,1,0:T(2,128)S(1)}, f32[8,2,256]{2,1,0:T(2,128)S(1)}, u32[]{:S(2)}, u32[]{:S(2)}) collective-permute-start(f32[8,2,256]{2,1,0:T(2,128)S(1)} %get-tuple-element.75.refs_2_), channel_id=1, source_target_pairs={{0,1},{1,0},{2,3},{3,2},{4,5},{5,4},{6,7},{7,6},{8,9},{9,8},{10,11... | collective-permute-start | bytes 49160 | tf_op jit(solution)/shard_map/ppermute | solution.py:404
  71.3 10.0 %collective-permute-start.12 = (bf16[8,1,64,256]{3,2,1,0:T(8,128)(2,1)S(1)}, bf16[8,1,64,256]{3,2,1,0:T(8,128)(2,1)S(1)}, u32[]{:S(2)}, u32[]{:S(2)}) collective-permute-start(bf16[8,1,64,256]{3,2,1,0:T(8,128)(2,1)S(1)} %get-tuple-element.79), channel_id=1, source_target_pairs={{0,1},{1,2},{2,3},{4,5},{5,6},{6,7},{8,9},{9,10},{10,11},{12,13},{... | collective-permute-start | bytes 786440 | tf_op jit(solution)/shard_map/ppermute | solution.py:399
  74.8 8.3 %collective-permute-start.13 = (bf16[8,1,64,256]{3,2,1,0:T(8,128)(2,1)S(1)}, bf16[8,1,64,256]{3,2,1,0:T(8,128)(2,1)S(1)}, u32[]{:S(2)}, u32[]{:S(2)}) collective-permute-start(bf16[8,1,64,256]{3,2,1,0:T(8,128)(2,1)S(1)} %get-tuple-element.80), channel_id=1, source_target_pairs={{1,0},{2,1},{3,2},{5,4},{6,5},{7,6},{9,8},{10,9},{11,10},{13,12},{... | collective-permute-start | bytes 786440 | tf_op jit(solution)/shard_map/ppermute | solution.py:399
  83.4 2.4 %collective-permute-start.14 = (bf16[4,4,32,768]{3,2,1,0:T(8,128)(2,1)S(1)}, bf16[4,4,32,768]{3,2,1,0:T(8,128)(2,1)S(1)}, u32[]{:S(2)}, u32[]{:S(2)}) collective-permute-start(bf16[4,4,32,768]{3,2,1,0:T(8,128)(2,1)S(1)} %get-tuple-element.83), channel_id=1, source_target_pairs={{0,4},{4,0},{8,12},{12,8},{16,20},{20,16},{24,28},{28,24},{1,5},{5... | collective-permute-start | bytes 2359304 | tf_op jit(solution)/shard_map/ppermute | solution.py:507
  86.0 11.3 %collective-permute-start.17 = (bf16[4,32,768]{2,1,0:T(8,128)(2,1)S(1)}, bf16[4,32,768]{2,1,0:T(8,128)(2,1)S(1)}, u32[]{:S(2)}, u32[]{:S(2)}) collective-permute-start(bf16[4,32,768]{2,1,0:T(8,128)(2,1)S(1)} %get-tuple-element.91), channel_id=1, source_target_pairs={{0,8},{4,12},{8,0},{12,4},{16,24},{20,28},{24,16},{28,20},{1,9},{5... | collective-permute-start | bytes 589832 | tf_op jit(solution)/shard_map/ppermute | solution.py:512
  86.1 11.5 %collective-permute-start.18 = (bf16[4,32,768]{2,1,0:T(8,128)(2,1)S(1)}, bf16[4,32,768]{2,1,0:T(8,128)(2,1)S(1)}, u32[]{:S(2)}, u32[]{:S(2)}) collective-permute-start(bf16[4,32,768]{2,1,0:T(8,128)(2,1)S(1)} %get-tuple-element.92), channel_id=1, source_target_pairs={{0,16},{4,20},{8,24},{12,28},{16,0},{20,4},{24,8},{28,12},{1,17},{... | collective-permute-start | bytes 589832 | tf_op jit(solution)/shard_map/ppermute | solution.py:512
  88.9 10.5 %collective-permute-start.19 = (bf16[4,32,768]{2,1,0:T(8,128)(2,1)S(1)}, bf16[4,32,768]{2,1,0:T(8,128)(2,1)S(1)}, u32[]{:S(2)}, u32[]{:S(2)}) collective-permute-start(bf16[4,32,768]{2,1,0:T(8,128)(2,1)S(1)} %get-tuple-element.93), channel_id=1, source_target_pairs={{0,24},{4,28},{8,16},{12,20},{16,8},{20,12},{24,0},{28,4},{1,25},{... | collective-permute-start | bytes 589832 | tf_op jit(solution)/shard_map/ppermute | solution.py:512
  99.5 25.6 %collective-permute-start.26 = (bf16[2,512,256]{2,1,0:T(8,128)(2,1)S(1)}, bf16[2,512,256]{2,1,0:T(8,128)(2,1)S(1)}, u32[]{:S(2)}, u32[]{:S(2)}) collective-permute-start(bf16[2,512,256]{2,1,0:T(8,128)(2,1)S(1)} %get-tuple-element.101), channel_id=1, source_target_pairs={{4,0},{8,4},{12,8},{16,12},{20,16},{24,20},{28,24},{5,1},{9,5},{13... | collective-permute-start | bytes 1572872 | tf_op jit(solution)/shard_map/ppermute | solution.py:399
  100.8 24.3 %collective-permute-start.27 = (bf16[2,512,256]{2,1,0:T(8,128)(2,1)S(1)}, bf16[2,512,256]{2,1,0:T(8,128)(2,1)S(1)}, u32[]{:S(2)}, u32[]{:S(2)}) collective-permute-start(bf16[2,512,256]{2,1,0:T(8,128)(2,1)S(1)} %get-tuple-element.101), channel_id=1, source_target_pairs={{0,4},{4,8},{8,12},{12,16},{16,20},{20,24},{24,28},{1,5},{5,9},{9,... | collective-permute-start | bytes 1572872 | tf_op jit(solution)/shard_map/ppermute | solution.py:399
  103.9 4.5 %collective-permute-start.20 = (bf16[32,768]{1,0:T(8,128)(2,1)S(1)}, bf16[32,768]{1,0:T(8,128)(2,1)S(1)}, u32[]{:S(2)}, u32[]{:S(2)}) collective-permute-start(bf16[32,768]{1,0:T(8,128)(2,1)S(1)} %get-tuple-element.97), channel_id=1, source_target_pairs={{0,1},{1,0},{2,3},{3,2},{4,5},{5,4},{6,7},{7,6},{8,9},{9,8},{10,11... | collective-permute-start | bytes 147464 | tf_op jit(solution)/shard_map/ppermute | solution.py:524
  106.0 7.1 %collective-permute-start.21 = (bf16[32,768]{1,0:T(8,128)(2,1)S(1)}, bf16[32,768]{1,0:T(8,128)(2,1)S(1)}, u32[]{:S(2)}, u32[]{:S(2)}) collective-permute-start(bf16[32,768]{1,0:T(8,128)(2,1)S(1)} %get-tuple-element.98), channel_id=1, source_target_pairs={{0,2},{1,3},{2,0},{3,1},{4,6},{5,7},{6,4},{7,5},{8,10},{9,11},{10,... | collective-permute-start | bytes 147464 | tf_op jit(solution)/shard_map/ppermute | solution.py:524
  106.7 6.4 %collective-permute-start.22 = (bf16[32,768]{1,0:T(8,128)(2,1)S(1)}, bf16[32,768]{1,0:T(8,128)(2,1)S(1)}, u32[]{:S(2)}, u32[]{:S(2)}) collective-permute-start(bf16[32,768]{1,0:T(8,128)(2,1)S(1)} %get-tuple-element.99), channel_id=1, source_target_pairs={{0,3},{1,2},{2,1},{3,0},{4,7},{5,6},{6,5},{7,4},{8,11},{9,10},{10,... | collective-permute-start | bytes 147464 | tf_op jit(solution)/shard_map/ppermute | solution.py:524
  113.1 4.5 %collective-permute-start.23 = (bf16[32,768]{1,0:T(8,128)(2,1)S(1)}, bf16[32,768]{1,0:T(8,128)(2,1)S(1)}, u32[]{:S(2)}, u32[]{:S(2)}) collective-permute-start(bf16[32,768]{1,0:T(8,128)(2,1)S(1)} %line_sum.1.refs_0_), channel_id=1, source_target_pairs={{0,1},{1,0},{2,3},{3,2},{4,5},{5,4},{6,7},{7,6},{8,9},{9,8},{10,11... | collective-permute-start | bytes 147464 | tf_op jit(solution)/shard_map/ppermute | solution.py:530
  114.5 5.9 %collective-permute-start.24 = (bf16[32,768]{1,0:T(8,128)(2,1)S(1)}, bf16[32,768]{1,0:T(8,128)(2,1)S(1)}, u32[]{:S(2)}, u32[]{:S(2)}) collective-permute-start(bf16[32,768]{1,0:T(8,128)(2,1)S(1)} %line_sum.1.refs_0_), channel_id=1, source_target_pairs={{0,2},{1,3},{2,0},{3,1},{4,6},{5,7},{6,4},{7,5},{8,10},{9,11},{10,... | collective-permute-start | bytes 147464 | tf_op jit(solution)/shard_map/ppermute | solution.py:530
  115.6 5.9 %collective-permute-start.25 = (bf16[32,768]{1,0:T(8,128)(2,1)S(1)}, bf16[32,768]{1,0:T(8,128)(2,1)S(1)}, u32[]{:S(2)}, u32[]{:S(2)}) collective-permute-start(bf16[32,768]{1,0:T(8,128)(2,1)S(1)} %line_sum.1.refs_0_), channel_id=1, source_target_pairs={{0,3},{1,2},{2,1},{3,0},{4,7},{5,6},{6,5},{7,4},{8,11},{9,10},{10,... | collective-permute-start | bytes 147464 | tf_op jit(solution)/shard_map/ppermute | solution.py:530
  121.6 8.7 %collective-permute-start.28 = (bf16[4,32,768]{2,1,0:T(8,128)(2,1)S(1)}, bf16[4,32,768]{2,1,0:T(8,128)(2,1)S(1)}, u32[]{:S(2)}, u32[]{:S(2)}) collective-permute-start(bf16[4,32,768]{2,1,0:T(8,128)(2,1)S(1)} %line_place.1.refs_0_), channel_id=1, source_target_pairs={{0,8},{4,12},{8,0},{12,4},{16,24},{20,28},{24,16},{28,20},{1,9},{5... | collective-permute-start | bytes 589832 | tf_op jit(solution)/shard_map/ppermute | solution.py:534
  122.4 9.1 %collective-permute-start.29 = (bf16[4,32,768]{2,1,0:T(8,128)(2,1)S(1)}, bf16[4,32,768]{2,1,0:T(8,128)(2,1)S(1)}, u32[]{:S(2)}, u32[]{:S(2)}) collective-permute-start(bf16[4,32,768]{2,1,0:T(8,128)(2,1)S(1)} %line_place.1.refs_0_), channel_id=1, source_target_pairs={{0,16},{4,20},{8,24},{12,28},{16,0},{20,4},{24,8},{28,12},{1,17},{... | collective-permute-start | bytes 589832 | tf_op jit(solution)/shard_map/ppermute | solution.py:534
  123.4 8.2 %collective-permute-start.30 = (bf16[4,32,768]{2,1,0:T(8,128)(2,1)S(1)}, bf16[4,32,768]{2,1,0:T(8,128)(2,1)S(1)}, u32[]{:S(2)}, u32[]{:S(2)}) collective-permute-start(bf16[4,32,768]{2,1,0:T(8,128)(2,1)S(1)} %line_place.1.refs_0_), channel_id=1, source_target_pairs={{0,24},{4,28},{8,16},{12,20},{16,8},{20,12},{24,0},{28,4},{1,25},{... | collective-permute-start | bytes 589832 | tf_op jit(solution)/shard_map/ppermute | solution.py:534
  131.6 2.4 %collective-permute-start.31 = (bf16[4,4,32,768]{3,2,1,0:T(8,128)(2,1)S(1)}, bf16[4,4,32,768]{3,2,1,0:T(8,128)(2,1)S(1)}, u32[]{:S(2)}, u32[]{:S(2)}) collective-permute-start(bf16[4,4,32,768]{3,2,1,0:T(8,128)(2,1)S(1)} %plane_place.1.mine_ref), channel_id=1, source_target_pairs={{0,4},{4,0},{8,12},{12,8},{16,20},{20,16},{24,28},{28,24},{1,5},{5... | collective-permute-start | bytes 2359304 | tf_op jit(solution)/shard_map/ppermute | solution.py:546

commit v6 on v4

--- a/solution.py
+++ b/solution.py
@@ -49,18 +49,19 @@
     return row
 
 
-def frame_stats(part_refs, f, entries, group_size):
-    total = part_refs[0][f]
+def group_means(part_refs, entries, group_size):
+    total = part_refs[0][...]
     for ref in part_refs[1:]:
-        total = total + ref[f]
-    return group_total(total, group_size) / entries
-
-
-def mean_and_inv(part_refs, f, entries, group_size):
-    both = frame_stats(part_refs, f, entries, group_size)
-    mean = both[0:1]
-    inv = lax.rsqrt(both[1:2] - mean * mean + NORM_EPS)
-    return mean, inv
+        total = total + ref[...]
+    frames, _, channels = total.shape
+    means = group_total(total.reshape(2 * frames, channels), group_size) / entries
+    means = means.reshape(frames, 2, channels)
+    return means[:, 0], means[:, 1]
+
+
+def mean_and_inv(part_refs, entries, group_size):
+    mean, square = group_means(part_refs, entries, group_size)
+    return mean, lax.rsqrt(square - mean * mean + NORM_EPS)
 
 
 def column_sums(first, second):
@@ -178,15 +179,15 @@
 
 def act_kernel(n, entries, group_size, clip_ref, *refs):
     parts, refs = refs[:n], refs[n:]
-    conv_ref, gain_ref, shift_ref, act_ref, early_ref, late_ref, normed_ref, slope_ref = refs
+    conv_ref, gain_ref, shift_ref, act_ref, early_ref, late_ref, normed_ref, slope_ref, mean_ref, inv_ref = refs
     frames, ahead = conv_ref.shape[0], early_ref.shape[0]
     first = lax.axis_index("tm") * frames
     filled = clip_ref[0] + clip_ref[1]
     half_gain, half_shift = 0.5 * gain_ref[...], 0.5 * shift_ref[...]
+    mean_ref[...], inv_ref[...] = mean_and_inv(parts, entries, group_size)
 
     def body(f):
-        mean, inv = mean_and_inv(parts, f, entries, group_size)
-        normed = (conv_ref[f] - mean) * inv
+        normed = (conv_ref[f] - mean_ref[pl.ds(f, 1)]) * inv_ref[pl.ds(f, 1)]
         h, rise, slope = silu_parts(normed, half_gain, half_shift)
         act = jnp.where(first + f < filled, h * rise, 0.0).astype(BF16)
         act_ref[f] = act
@@ -256,15 +257,17 @@
 
 def norm_back_kernel(n, m, entries, group_size, normed_ref, slope_ref, ga_ref, *refs):
     parts, grad_parts = refs[:n], refs[n : n + m]
-    g_ref, first_ref, last_ref, moved_ref = refs[n + m :]
+    g_ref, first_ref, last_ref, moved_ref, inv_ref, first_mean_ref, second_mean_ref = refs[n + m :]
     _, pixels, channels = normed_ref.shape
     width = first_ref.shape[2]
 
+    _, inv_ref[...] = mean_and_inv(parts, entries, group_size)
+    first_mean_ref[...], second_mean_ref[...] = group_means(grad_parts, entries, group_size)
+
     def body(f):
-        _, inv = mean_and_inv(parts, f, entries, group_size)
-        means = frame_stats(grad_parts, f, entries, group_size)
+        row = pl.ds(f, 1)
         gn = ga_ref[f].astype(F32) * slope_ref[f].astype(F32)
-        wide = inv * (gn - means[0:1] - normed_ref[f].astype(F32) * means[1:2])
+        wide = inv_ref[row] * (gn - first_mean_ref[row] - normed_ref[f].astype(F32) * second_mean_ref[row])
         grad = wide.astype(BF16)
         g_ref[f] = grad
         first_ref[f, 0] = grad[:width]
@@ -460,9 +463,10 @@
     )
     x_turned, *parts = lax.optimization_barrier((x_turned, *parts))
     ahead = (3 * frames) // 4
+    row = pltpu.VMEM((frames, channels), F32)
     act, act_early, act_late, normed, slope = call(
         functools.partial(act_kernel, len(parts), entries, group_size), "activation",
-        [clip_frames, *parts, conv_out, gain, shift], [shape((k, pixels, channels), BF16) for k in (frames, ahead, frames - ahead, frames, frames)], 10 * big, 10 * big,
+        [clip_frames, *parts, conv_out, gain, shift], [shape((k, pixels, channels), BF16) for k in (frames, ahead, frames - ahead, frames, frames)], 10 * big, 10 * big, [row] * 2,
     )
     act_prev, act_next = neighbours("tm", act_early, act_early)
 
@@ -483,7 +487,7 @@
         [normed, slope, grad_act, *parts, *grad_parts],
         [shape(per_px, BF16)] + [shape((frames, 1, width, channels), BF16)] * 2
         + [shape((frames * pixels, lanes), BF16)],
-        0, 12 * big,
+        0, 12 * big, [row] * 3,
     )
     grad_above, grad_below = neighbours("space", first_rows, last_rows)
     sums = call(

time: 130 us -> 130 us (level)
  Pallas kernels: 45.1 us -> 39.8 us
  waiting for transfers between devices: 29.6 us -> 34.6 us
    ppermute x1, waiting for transfers between devices: 0.4 us -> 6.16 us  [per_device(): cot_corner.append(lax.ppermute(relayed, 'tm', [(7, 4), (0, 3)]))]
    pallas_call x17, Pallas kernels: 45.1 us -> 39.8 us  [call(): pl.pallas_call(kernel, in_specs=[smem if x.dtype == jnp.int32 else vmem f...]
  transfers between devices with their start and end apart: 32 -> 32, of which waited for: 16 -> 14; matrix products, arithmetic and copies ran while one was open for 1% -> 1% of each run, Pallas kernels for 33% -> 29%
where the time goes in v6:
time: 130 us
  starting transfers between devices  51.4 us (40%)
  Pallas kernels  39.8 us (31%)
  waiting for transfers between devices  34.6 us (27%)
  local copies, waits for them, and re-layouts  2.8 us (2%)
    pallas_call x17, Pallas kernels, call(): pl.pallas_call(kernel, in_specs=[smem if x.dtype == jnp.int32 else vmem f...  39.8 us
    ppermute x10, starting transfers between devices, neighbours(): return (lax.ppermute(high, axis, up), lax.ppermute(low, axis, down))  21.7 us
    ppermute x10, waiting for transfers between devices, neighbours(): return (lax.ppermute(high, axis, up), lax.ppermute(low, axis, down))  8.23 us
    ppermute x1, waiting for transfers between devices, per_device(): cot_corner.append(lax.ppermute(relayed, 'tm', [(7, 4), (0, 3)]))  6.16 us
    ppermute x3, waiting for transfers between devices, per_device(): lax.ppermute(x, 'space', other_plane(s))  5.09 us
    ppermute x3, starting transfers between devices, per_device(): lax.ppermute(x, 'space', other_plane(s))  4.52 us
    ppermute x3, starting transfers between devices, per_device(): gots = [lax.ppermute(own, 'space', other_plane(s)) for s in range(1, n)]  4.45 us
    ppermute x1, starting transfers between devices, per_device(): cot_corner.append(lax.ppermute(relayed, 'tm', [(7, 4), (0, 3)]))  4.41 us
  transfers between devices with their start and end apart: 32, of which 14 were waited for; matrix products, arithmetic and copies ran while one was open for 1% of the time, Pallas kernels for 29%

profile of v6, /device:TPU:0, one launch (start us, length us, event | category | flops | bytes accessed | tf_op | source)
XLA Modules:
  0.0 129.7 jit_solution(576428290289935306)
XLA Ops:
  0.6 1.1 fusion.1
  1.7 1.6 %collective-permute-start.5 = (bf16[8,512,256]{2,1,0:T(8,128)(2,1)}, bf16[8,512,256]{2,1,0:T(8,128)(2,1)S(1)}, u32[]{:S(2)}, u32[]{:S(2)}) collective-permute-start(bf16[8,512,256]{2,1,0:T(8,128)(2,1)} %bitcast.6), channel_id=1, source_target_pairs={{4,0},{8,4},{12,8},{20,16},{24,20},{28,24},{5,1},{9,5},{13,9},{21,... | collective-permute-start | bytes 6291464 | tf_op jit(solution)/shard_map/ppermute | solution.py:402
  3.3 3.2 %collective-permute-start.6 = (bf16[8,512,256]{2,1,0:T(8,128)(2,1)}, bf16[8,512,256]{2,1,0:T(8,128)(2,1)S(1)}, u32[]{:S(2)}, u32[]{:S(2)}) collective-permute-start(bf16[8,512,256]{2,1,0:T(8,128)(2,1)} %bitcast.7), channel_id=1, source_target_pairs={{0,4},{4,8},{8,12},{16,20},{20,24},{24,28},{1,5},{5,9},{9,13},{17,... | collective-permute-start | bytes 6291464 | tf_op jit(solution)/shard_map/ppermute | solution.py:402
  6.5 4.9 %collective-permute-start = (bf16[8,1,64,256]{3,2,1,0:T(8,128)(2,1)S(1)}, bf16[8,1,64,256]{3,2,1,0:T(8,128)(2,1)S(1)}, u32[]{:S(2)}, u32[]{:S(2)}) collective-permute-start(bf16[8,1,64,256]{3,2,1,0:T(8,128)(2,1)S(1)} %get-tuple-element.53), channel_id=1, source_target_pairs={{0,1},{1,2},{2,3},{4,5},{5,6},{6,7},{8,9},{9,10},{10,11},{12,13},{... | collective-permute-start | bytes 786440 | tf_op jit(solution)/shard_map/ppermute | solution.py:402
  11.4 1.3 collective-permute-start.1
  12.7 1.7 %fusion = (bf16[4,8,64,256]{3,2,1,0:T(8,128)(2,1)S(1)}, bf16[4,8,64,256]{3,2,1,0:T(8,128)(2,1)S(1)}) fusion(bf16[8,8,64,256]{3,2,1,0:T(8,128)(2,1)} %cot_ref.1), kind=kLoop, calls=%fused_computation | loop fusion | bytes 4194304 | tf_op jit(solution)/shard_map/slice | solution.py:441
  14.4 0.0 copy-start.2
  14.4 1.4 %collective-permute-start.3 = (bf16[4,512,256]{2,1,0:T(8,128)(2,1)S(1)}, bf16[4,512,256]{2,1,0:T(8,128)(2,1)S(1)}, u32[]{:S(2)}, u32[]{:S(2)}) collective-permute-start(bf16[4,512,256]{2,1,0:T(8,128)(2,1)S(1)} %bitcast.13), channel_id=1, source_target_pairs={{12,28},{16,0},{13,29},{17,1},{14,30},{18,2},{15,31},{19,3}} | collective-permute-start | bytes 3145736 | tf_op jit(solution)/shard_map/ppermute | solution.py:442
  15.8 2.2 %collective-permute-done.above_ref = bf16[8,1,64,256]{3,2,1,0:T(8,128)(2,1)S(1)} collective-permute-done((bf16[8,1,64,256]{3,2,1,0:T(8,128)(2,1)S(1)}, bf16[8,1,64,256]{3,2,1,0:T(8,128)(2,1)S(1)}, u32[]{:S(2)}, u32[]{:S(2)}) %collective-permute-start) | collective-permute-done | bytes 262176 | tf_op jit(solution)/shard_map/ppermute | solution.py:402
  18.1 4.1 %collective-permute-done.1.below_ref = bf16[8,1,64,256]{3,2,1,0:T(8,128)(2,1)S(1)} collective-permute-done((bf16[8,1,64,256]{3,2,1,0:T(8,128)(2,1)S(1)}, bf16[8,1,64,256]{3,2,1,0:T(8,128)(2,1)S(1)}, u32[]{:S(2)}, u32[]{:S(2)}) %collective-permute-start.1) | collective-permute-done | bytes 262176 | tf_op jit(solution)/shard_map/ppermute | solution.py:402
  22.2 5.7 %conv_forward.1 = (f32[8,512,256]{2,1,0:T(8,128)S(1)}, f32[8,2,256]{2,1,0:T(2,128)S(1)}) custom-call(bf16[8,8,64,256]{3,2,1,0:T(8,128)(2,1)S(1)} %copy-done, bf16[8,1,64,256]{3,2,1,0:T(8,128)(2,1)S(1)} %collective-permute-done.above_ref, bf16[8,1,64,256]{3,2,1,0:T(8,128)(2,1)S(1)} %collective-permute-done.1.below_ref, bf16[3,3,256,256]{3,2,1,0:T(8,128)(2,1)S(1)} %copy-done.3), custom_call_target="tpu_custom_call" | custom-call | flops 26843545600 | bytes 8388608 | tf_op jit(solution)/shard_map/conv_forward/pallas_call | solution.py:20
  27.9 1.6 %collective-permute-start.2 = (f32[8,2,256]{2,1,0:T(2,128)S(1)}, f32[8,2,256]{2,1,0:T(2,128)S(1)}, u32[]{:S(2)}, u32[]{:S(2)}) collective-permute-start(f32[8,2,256]{2,1,0:T(2,128)S(1)} %get-tuple-element.56), channel_id=1, source_target_pairs={{0,1},{1,0},{2,3},{3,2},{4,5},{5,4},{6,7},{7,6},{8,9},{9,8},{10,11... | collective-permute-start | bytes 49160 | tf_op jit(solution)/shard_map/ppermute | solution.py:416
  29.6 0.7 collective-permute-start.7
  30.3 1.5 %collective-permute-done.2 = f32[8,2,256]{2,1,0:T(2,128)S(1)} collective-permute-done((f32[8,2,256]{2,1,0:T(2,128)S(1)}, f32[8,2,256]{2,1,0:T(2,128)S(1)}, u32[]{:S(2)}, u32[]{:S(2)}) %collective-permute-start.2) | collective-permute-done | bytes 16416 | tf_op jit(solution)/shard_map/ppermute | solution.py:416
  31.8 4.4 %collective-permute-start.8 = (bf16[4,512,256]{2,1,0:T(8,128)(2,1)S(1)}, bf16[4,512,256]{2,1,0:T(8,128)(2,1)S(1)}, u32[]{:S(2)}, u32[]{:S(2)}) collective-permute-start(bf16[4,512,256]{2,1,0:T(8,128)(2,1)S(1)} %collective-permute-done.3), channel_id=1, source_target_pairs={{28,16},{0,12},{29,17},{1,13},{30,18},{2,14},{31,19},{3,15}} | collective-permute-start | bytes 3145736 | tf_op jit(solution)/shard_map/ppermute | solution.py:459
  36.2 1.1 collective-permute-start.4
  37.3 0.5 turn_weights.1
  37.8 0.0 copy-start.4
  37.8 2.2 %turned.1.xt_ref = bf16[768,4096]{1,0:T(8,128)(2,1)S(1)} custom-call(bf16[8,8,64,256]{3,2,1,0:T(8,128)(2,1)S(1)} %copy-done, bf16[8,1,64,256]{3,2,1,0:T(8,128)(2,1)S(1)} %collective-permute-done.above_ref, bf16[8,1,64,256]{3,2,1,0:T(8,128)(2,1)S(1)} %collective-permute-done.1.below_ref), custom_call_target="tpu_custom_call" | custom-call | bytes 8388608 | tf_op jit(solution)/shard_map/turned/pallas_call | solution.py:20
  40.0 1.0 collective-permute-done.4.refs_1_
  41.0 3.4 %activation.1 = (bf16[8,512,256]{2,1,0:T(8,128)(2,1)S(1)}, bf16[6,512,256]{2,1,0:T(8,128)(2,1)S(1)}, bf16[2,512,256]{2,1,0:T(8,128)(2,1)S(1)}, bf16[8,512,256]{2,1,0:T(8,128)(2,1)S(1)}, bf16[8,512,256]{2,1,0:T(8,128)(2,1)S(1)}) custom-call(s32[2]{0:T(128)S(1)} %copy-done.4, f32[8,2,256]{2,1,0:T(2,128)S(1)} %add.3.refs_0_, ...), custom_call_target="tpu_custom_call" | custom-call | flops 10485760 | bytes 10485760 | tf_op jit(solution)/shard_map/activation/pallas_call | solution.py:20
  44.4 1.4 %collective-permute-start.15 = (bf16[6,512,256]{2,1,0:T(8,128)(2,1)S(1)}, bf16[6,512,256]{2,1,0:T(8,128)(2,1)S(1)}, u32[]{:S(2)}, u32[]{:S(2)}) collective-permute-start(bf16[6,512,256]{2,1,0:T(8,128)(2,1)S(1)} %get-tuple-element.83), channel_id=1, source_target_pairs={{0,4},{4,8},{8,12},{12,16},{16,20},{20,24},{24,28},{1,5},{5,9},{9,... | collective-permute-start | bytes 4718600 | tf_op jit(solution)/shard_map/ppermute | solution.py:402
  45.8 1.3 collective-permute-start.16
  47.1 6.2 %collective-permute-done.8.refs_1_ = bf16[4,512,256]{2,1,0:T(8,128)(2,1)S(1)} collective-permute-done((bf16[4,512,256]{2,1,0:T(8,128)(2,1)S(1)}, bf16[4,512,256]{2,1,0:T(8,128)(2,1)S(1)}, u32[]{:S(2)}, u32[]{:S(2)}) %collective-permute-start.8) | collective-permute-done | bytes 1048608 | tf_op jit(solution)/shard_map/ppermute | solution.py:459
  53.3 4.2 %grad_activation.1 = (bf16[8,512,256]{2,1,0:T(8,128)(2,1)S(1)}, bf16[4096,768]{1,0:T(8,128)(2,1)S(1)}, f32[8,2,256]{2,1,0:T(2,128)S(1)}) custom-call(s32[2]{0:T(128)S(1)} %copy-done.4, s32[2]{0:T(128)S(1)} %copy-done.5, bf16[8,512,256]{2,1,0:T(8,128)(2,1)S(1)} %bitcast.8, bf16[8,512,256]{2,1,0:T(8,128)(2,1)S(1)} %collective-permute-done.5.nxt, ...), custom_call_target="tpu_custom_call" | custom-call | flops 1610612736 | bytes 16777216 | tf_op jit(solution)/shard_map/grad_activation/pallas_call | solution.py:20
  57.5 0.2 collective-permute-start.10
  57.7 3.5 %collective-permute-start.11 = (f32[8,2,256]{2,1,0:T(2,128)S(1)}, f32[8,2,256]{2,1,0:T(2,128)S(1)}, u32[]{:S(2)}, u32[]{:S(2)}) collective-permute-start(f32[8,2,256]{2,1,0:T(2,128)S(1)} %get-tuple-element.69.refs_2_), channel_id=1, source_target_pairs={{0,3},{1,2},{2,1},{3,0},{4,7},{5,6},{6,5},{7,4},{8,11},{9,10},{10,... | collective-permute-start | bytes 49160 | tf_op jit(solution)/shard_map/ppermute | solution.py:407
  61.2 0.5 collective-permute-start.9
  61.7 1.9 %temporal_grad.1.temporal_ref = f32[256,768]{1,0:T(8,128)S(1)} custom-call(bf16[8,512,256]{2,1,0:T(8,128)(2,1)S(1)} %get-tuple-element.71.act_ref.own, bf16[4096,768]{1,0:T(8,128)(2,1)S(1)} %get-tuple-element.72.cat_ref), custom_call_target="tpu_custom_call" | custom-call | flops 1610612736 | bytes 8388608 | tf_op jit(solution)/shard_map/temporal_grad/pallas_call | solution.py:20
  63.6 1.3 %collective-permute-done.9.refs_3_ = f32[8,2,256]{2,1,0:T(2,128)S(1)} collective-permute-done((f32[8,2,256]{2,1,0:T(2,128)S(1)}, f32[8,2,256]{2,1,0:T(2,128)S(1)}, u32[]{:S(2)}, u32[]{:S(2)}) %collective-permute-start.9) | collective-permute-done | bytes 16416 | tf_op jit(solution)/shard_map/ppermute | solution.py:407
  64.9 2.2 %norm_backward.1 = (bf16[8,512,256]{2,1,0:T(8,128)(2,1)S(1)}, bf16[8,1,64,256]{3,2,1,0:T(8,128)(2,1)S(1)}, bf16[8,1,64,256]{3,2,1,0:T(8,128)(2,1)S(1)}, bf16[4096,768]{1,0:T(8,128)(2,1)S(1)}) custom-call(bf16[8,512,256]{2,1,0:T(8,128)(2,1)S(1)} %get-tuple-element.62.refs_3_.normed_ref, bf16[8,512,256]{2,1,0:T(8,128)(2,1)S(1)} %get-tuple-element.63.refs_4_.slope_ref, ...), custom_call_target="tpu_custom_call" | custom-call | bytes 12582912 | tf_op jit(solution)/shard_map/norm_backward/pallas_call | solution.py:20
  67.2 2.4 %collective-permute-start.12 = (bf16[8,1,64,256]{3,2,1,0:T(8,128)(2,1)S(1)}, bf16[8,1,64,256]{3,2,1,0:T(8,128)(2,1)S(1)}, u32[]{:S(2)}, u32[]{:S(2)}) collective-permute-start(bf16[8,1,64,256]{3,2,1,0:T(8,128)(2,1)S(1)} %get-tuple-element.73), channel_id=1, source_target_pairs={{0,1},{1,2},{2,3},{4,5},{5,6},{6,7},{8,9},{9,10},{10,11},{12,13},{... | collective-permute-start | bytes 786440 | tf_op jit(solution)/shard_map/ppermute | solution.py:402
  69.6 1.3 collective-permute-start.13
  70.9 5.1 %weight_grad.1.acc_ref = f32[1024,768]{1,0:T(8,128)S(1)} custom-call(bf16[768,4096]{1,0:T(8,128)(2,1)S(1)} %turned.1.xt_ref, bf16[4096,768]{1,0:T(8,128)(2,1)S(1)} %get-tuple-element.70.moved_ref, f32[256,768]{1,0:T(8,128)S(1)} %temporal_grad.1.temporal_ref), custom_call_target="tpu_custom_call" | custom-call | flops 4831838208 | bytes 12582912 | tf_op jit(solution)/shard_map/weight_grad/pallas_call | solution.py:20
  76.0 1.8 %collective-permute-done.13.below_ref = bf16[8,1,64,256]{3,2,1,0:T(8,128)(2,1)S(1)} collective-permute-done((bf16[8,1,64,256]{3,2,1,0:T(8,128)(2,1)S(1)}, bf16[8,1,64,256]{3,2,1,0:T(8,128)(2,1)S(1)}, u32[]{:S(2)}, u32[]{:S(2)}) %collective-permute-start.13) | collective-permute-done | bytes 262176 | tf_op jit(solution)/shard_map/ppermute | solution.py:402
  77.8 0.4 hand_out.1
  78.2 0.1 collective-permute-start.14
  78.3 2.3 %collective-permute-done.14.got_ref = bf16[4,4,32,768]{3,2,1,0:T(8,128)(2,1)S(1)} collective-permute-done((bf16[4,4,32,768]{3,2,1,0:T(8,128)(2,1)S(1)}, bf16[4,4,32,768]{3,2,1,0:T(8,128)(2,1)S(1)}, u32[]{:S(2)}, u32[]{:S(2)}) %collective-permute-start.14) | collective-permute-done | bytes 786464 | tf_op jit(solution)/shard_map/ppermute | solution.py:510
  80.6 0.2 core_sum.1
  80.8 0.1 collective-permute-start.17
  80.8 0.1 collective-permute-start.18
  80.9 3.4 %collective-permute-start.19 = (bf16[4,32,768]{2,1,0:T(8,128)(2,1)S(1)}, bf16[4,32,768]{2,1,0:T(8,128)(2,1)S(1)}, u32[]{:S(2)}, u32[]{:S(2)}) collective-permute-start(bf16[4,32,768]{2,1,0:T(8,128)(2,1)S(1)} %get-tuple-element.87), channel_id=1, source_target_pairs={{0,24},{4,28},{8,16},{12,20},{16,8},{20,12},{24,0},{28,4},{1,25},{... | collective-permute-start | bytes 589832 | tf_op jit(solution)/shard_map/ppermute | solution.py:515
  84.3 7.0 %conv_backward.1 = bf16[8,8,64,256]{3,2,1,0:T(8,128)(2,1)} custom-call(bf16[8,512,256]{2,1,0:T(8,128)(2,1)S(1)} %get-tuple-element.79.g_ref, bf16[8,1,64,256]{3,2,1,0:T(8,128)(2,1)S(1)} %collective-permute-done.12.above_ref, bf16[8,1,64,256]{3,2,1,0:T(8,128)(2,1)S(1)} %collective-permute-done.13.below_ref, bf16[8,8,64,256]{3,2,1,0:T(8,128)(2,1)S(1)} %copy-done.1, ...), custom_call_target="tpu_custom_call" | custom-call | flops 4831838208 | bytes 8388608 | tf_op jit(solution)/shard_map/conv_backward/pallas_call | solution.py:20
  91.3 0.7 collective-permute-done.18.refs_1_
  92.1 0.1 plane_sum.1
  92.1 1.3 collective-permute-start.26
  93.4 3.1 %collective-permute-start.27 = (bf16[2,512,256]{2,1,0:T(8,128)(2,1)S(1)}, bf16[2,512,256]{2,1,0:T(8,128)(2,1)S(1)}, u32[]{:S(2)}, u32[]{:S(2)}) collective-permute-start(bf16[2,512,256]{2,1,0:T(8,128)(2,1)S(1)} %get-tuple-element.95), channel_id=1, source_target_pairs={{0,4},{4,8},{8,12},{12,16},{16,20},{20,24},{24,28},{1,5},{5,9},{9,... | collective-permute-start | bytes 1572872 | tf_op jit(solution)/shard_map/ppermute | solution.py:402
  96.5 2.1 %collective-permute-start.20 = (bf16[32,768]{1,0:T(8,128)(2,1)S(1)}, bf16[32,768]{1,0:T(8,128)(2,1)S(1)}, u32[]{:S(2)}, u32[]{:S(2)}) collective-permute-start(bf16[32,768]{1,0:T(8,128)(2,1)S(1)} %get-tuple-element.91), channel_id=1, source_target_pairs={{0,1},{1,0},{2,3},{3,2},{4,5},{5,4},{6,7},{7,6},{8,9},{9,8},{10,11... | collective-permute-start | bytes 147464 | tf_op jit(solution)/shard_map/ppermute | solution.py:527
  98.6 1.2 collective-permute-start.21
  99.8 1.2 collective-permute-start.22
  101.0 5.1 %collective-permute-done.21.refs_1_ = bf16[32,768]{1,0:T(8,128)(2,1)S(1)} collective-permute-done((bf16[32,768]{1,0:T(8,128)(2,1)S(1)}, bf16[32,768]{1,0:T(8,128)(2,1)S(1)}, u32[]{:S(2)}, u32[]{:S(2)}) %collective-permute-start.21) | collective-permute-done | bytes 49184 | tf_op jit(solution)/shard_map/ppermute | solution.py:527
  106.2 1.7 %collective-permute-start.23 = (bf16[32,768]{1,0:T(8,128)(2,1)S(1)}, bf16[32,768]{1,0:T(8,128)(2,1)S(1)}, u32[]{:S(2)}, u32[]{:S(2)}) collective-permute-start(bf16[32,768]{1,0:T(8,128)(2,1)S(1)} %line_sum.1.refs_0_), channel_id=1, source_target_pairs={{0,1},{1,0},{2,3},{3,2},{4,5},{5,4},{6,7},{7,6},{8,9},{9,8},{10,11... | collective-permute-start | bytes 147464 | tf_op jit(solution)/shard_map/ppermute | solution.py:533
  107.8 0.9 collective-permute-start.24
  108.7 1.9 %collective-permute-start.25 = (bf16[32,768]{1,0:T(8,128)(2,1)S(1)}, bf16[32,768]{1,0:T(8,128)(2,1)S(1)}, u32[]{:S(2)}, u32[]{:S(2)}) collective-permute-start(bf16[32,768]{1,0:T(8,128)(2,1)S(1)} %line_sum.1.refs_0_), channel_id=1, source_target_pairs={{0,3},{1,2},{2,1},{3,0},{4,7},{5,6},{6,5},{7,4},{8,11},{9,10},{10,... | collective-permute-start | bytes 147464 | tf_op jit(solution)/shard_map/ppermute | solution.py:533
  110.6 3.6 %collective-permute-done.24.refs_2_ = bf16[32,768]{1,0:T(8,128)(2,1)S(1)} collective-permute-done((bf16[32,768]{1,0:T(8,128)(2,1)S(1)}, bf16[32,768]{1,0:T(8,128)(2,1)S(1)}, u32[]{:S(2)}, u32[]{:S(2)}) %collective-permute-start.24) | collective-permute-done | bytes 49184 | tf_op jit(solution)/shard_map/ppermute | solution.py:533
  114.2 0.5 collective-permute-done.25.refs_3_
  114.8 1.6 %collective-permute-start.28 = (bf16[4,32,768]{2,1,0:T(8,128)(2,1)S(1)}, bf16[4,32,768]{2,1,0:T(8,128)(2,1)S(1)}, u32[]{:S(2)}, u32[]{:S(2)}) collective-permute-start(bf16[4,32,768]{2,1,0:T(8,128)(2,1)S(1)} %line_place.1.refs_0_), channel_id=1, source_target_pairs={{0,8},{4,12},{8,0},{12,4},{16,24},{20,28},{24,16},{28,20},{1,9},{5... | collective-permute-start | bytes 589832 | tf_op jit(solution)/shard_map/ppermute | solution.py:537
  116.3 2.0 %collective-permute-start.30 = (bf16[4,32,768]{2,1,0:T(8,128)(2,1)S(1)}, bf16[4,32,768]{2,1,0:T(8,128)(2,1)S(1)}, u32[]{:S(2)}, u32[]{:S(2)}) collective-permute-start(bf16[4,32,768]{2,1,0:T(8,128)(2,1)S(1)} %line_place.1.refs_0_), channel_id=1, source_target_pairs={{0,24},{4,28},{8,16},{12,20},{16,8},{20,12},{24,0},{28,4},{1,25},{... | collective-permute-start | bytes 589832 | tf_op jit(solution)/shard_map/ppermute | solution.py:537
  118.3 5.2 %temporal_forward.1 = bf16[8,8,64,256]{3,2,1,0:T(8,128)(2,1)} custom-call(s32[2]{0:T(128)S(1)} %copy-done.4, s32[2]{0:T(128)S(1)} %copy-done.5, bf16[8,512,256]{2,1,0:T(8,128)(2,1)S(1)} %get-tuple-element.71.act_ref.own, bf16[6,512,256]{2,1,0:T(8,128)(2,1)S(1)} %collective-permute-done.16.nxt_a, bf16[2,512,256]{2,1,0:T(8,128)(2,1)S(1)} %collective-permute-done.26.nxt_b, ...), custom_call_target="tpu_custom_call" | custom-call | flops 1610612736 | bytes 10485760 | tf_op jit(solution)/shard_map/temporal_forward/pallas_call | solution.py:20
  123.5 1.9 %collective-permute-done.29.refs_2_ = bf16[4,32,768]{2,1,0:T(8,128)(2,1)S(1)} collective-permute-done((bf16[4,32,768]{2,1,0:T(8,128)(2,1)S(1)}, bf16[4,32,768]{2,1,0:T(8,128)(2,1)S(1)}, u32[]{:S(2)}, u32[]{:S(2)}) %collective-permute-start.29) | collective-permute-done | bytes 196640 | tf_op jit(solution)/shard_map/ppermute | solution.py:537
  125.4 0.1 plane_place.1.mine_ref
  125.5 0.1 collective-permute-start.31
  125.5 2.3 %collective-permute-done.31.got_ref = bf16[4,4,32,768]{3,2,1,0:T(8,128)(2,1)S(1)} collective-permute-done((bf16[4,4,32,768]{3,2,1,0:T(8,128)(2,1)S(1)}, bf16[4,4,32,768]{3,2,1,0:T(8,128)(2,1)S(1)}, u32[]{:S(2)}, u32[]{:S(2)}) %collective-permute-start.31) | collective-permute-done | bytes 786464 | tf_op jit(solution)/shard_map/ppermute | solution.py:549
  127.8 1.9 %finish.1 = (f32[3,3,256,256]{3,2,1,0:T(8,128)}, f32[3,256,256]{2,1,0:T(8,128)}) custom-call(bf16[4,4,32,768]{3,2,1,0:T(8,128)(2,1)S(1)} %plane_place.1.mine_ref, bf16[4,4,32,768]{3,2,1,0:T(8,128)(2,1)S(1)} %collective-permute-done.31.got_ref), custom_call_target="tpu_custom_call" | custom-call | bytes 4194304 | tf_op jit(solution)/shard_map/finish/pallas_call | solution.py:20
  (36 shorter events, 0.1 us)
Async XLA Ops:
  1.7 20.5 %copy-start = (bf16[8,8,64,256]{3,2,1,0:T(8,128)(2,1)S(1)}, bf16[8,8,64,256]{3,2,1,0:T(8,128)(2,1)}, u32[]{:S(2)}) copy-start(bf16[8,8,64,256]{3,2,1,0:T(8,128)(2,1)} %x_ref.5) | copy-start | bytes 6291460
  1.7 20.5 %copy-start.3 = (bf16[3,3,256,256]{3,2,1,0:T(8,128)(2,1)S(1)}, bf16[3,3,256,256]{3,2,1,0:T(8,128)(2,1)}, u32[]{:S(2)}) copy-start(bf16[3,3,256,256]{3,2,1,0:T(8,128)(2,1)} %spatial_ref.1) | copy-start | bytes 3538948
  1.7 51.5 %collective-permute-start.5 = (bf16[8,512,256]{2,1,0:T(8,128)(2,1)}, bf16[8,512,256]{2,1,0:T(8,128)(2,1)S(1)}, u32[]{:S(2)}, u32[]{:S(2)}) collective-permute-start(bf16[8,512,256]{2,1,0:T(8,128)(2,1)} %bitcast.6), channel_id=1, source_target_pairs={{4,0},{8,4},{12,8},{20,16},{24,20},{28,24},{5,1},{9,5},{13,9},{21,... | collective-permute-start | bytes 6291464 | tf_op jit(solution)/shard_map/ppermute | solution.py:402
  3.3 49.9 %collective-permute-start.6 = (bf16[8,512,256]{2,1,0:T(8,128)(2,1)}, bf16[8,512,256]{2,1,0:T(8,128)(2,1)S(1)}, u32[]{:S(2)}, u32[]{:S(2)}) collective-permute-start(bf16[8,512,256]{2,1,0:T(8,128)(2,1)} %bitcast.7), channel_id=1, source_target_pairs={{0,4},{4,8},{8,12},{16,20},{20,24},{24,28},{1,5},{5,9},{9,13},{17,... | collective-permute-start | bytes 6291464 | tf_op jit(solution)/shard_map/ppermute | solution.py:402
  6.5 11.6 %collective-permute-start = (bf16[8,1,64,256]{3,2,1,0:T(8,128)(2,1)S(1)}, bf16[8,1,64,256]{3,2,1,0:T(8,128)(2,1)S(1)}, u32[]{:S(2)}, u32[]{:S(2)}) collective-permute-start(bf16[8,1,64,256]{3,2,1,0:T(8,128)(2,1)S(1)} %get-tuple-element.53), channel_id=1, source_target_pairs={{0,1},{1,2},{2,3},{4,5},{5,6},{6,7},{8,9},{9,10},{10,11},{12,13},{... | collective-permute-start | bytes 786440 | tf_op jit(solution)/shard_map/ppermute | solution.py:402
  11.4 10.8 %collective-permute-start.1 = (bf16[8,1,64,256]{3,2,1,0:T(8,128)(2,1)S(1)}, bf16[8,1,64,256]{3,2,1,0:T(8,128)(2,1)S(1)}, u32[]{:S(2)}, u32[]{:S(2)}) collective-permute-start(bf16[8,1,64,256]{3,2,1,0:T(8,128)(2,1)S(1)} %get-tuple-element.54), channel_id=1, source_target_pairs={{1,0},{2,1},{3,2},{5,4},{6,5},{7,6},{9,8},{10,9},{11,10},{13,12},{... | collective-permute-start | bytes 786440 | tf_op jit(solution)/shard_map/ppermute | solution.py:402
  14.4 22.9 %copy-start.2 = (bf16[3,256,256]{2,1,0:T(8,128)(2,1)S(1)}, bf16[3,256,256]{2,1,0:T(8,128)(2,1)}, u32[]{:S(2)}) copy-start(bf16[3,256,256]{2,1,0:T(8,128)(2,1)} %temporal_ref.1) | copy-start | bytes 1179652
  14.4 17.3 %collective-permute-start.3 = (bf16[4,512,256]{2,1,0:T(8,128)(2,1)S(1)}, bf16[4,512,256]{2,1,0:T(8,128)(2,1)S(1)}, u32[]{:S(2)}, u32[]{:S(2)}) collective-permute-start(bf16[4,512,256]{2,1,0:T(8,128)(2,1)S(1)} %bitcast.13), channel_id=1, source_target_pairs={{12,28},{16,0},{13,29},{17,1},{14,30},{18,2},{15,31},{19,3}} | collective-permute-start | bytes 3145736 | tf_op jit(solution)/shard_map/ppermute | solution.py:442
  27.9 3.8 %collective-permute-start.2 = (f32[8,2,256]{2,1,0:T(2,128)S(1)}, f32[8,2,256]{2,1,0:T(2,128)S(1)}, u32[]{:S(2)}, u32[]{:S(2)}) collective-permute-start(f32[8,2,256]{2,1,0:T(2,128)S(1)} %get-tuple-element.56), channel_id=1, source_target_pairs={{0,1},{1,0},{2,3},{3,2},{4,5},{5,4},{6,7},{7,6},{8,9},{9,8},{10,11... | collective-permute-start | bytes 49160 | tf_op jit(solution)/shard_map/ppermute | solution.py:416
  29.6 16.2 %collective-permute-start.7 = (bf16[4,512,256]{2,1,0:T(8,128)(2,1)S(1)}, bf16[4,512,256]{2,1,0:T(8,128)(2,1)S(1)}, u32[]{:S(2)}, u32[]{:S(2)}) collective-permute-start(bf16[4,512,256]{2,1,0:T(8,128)(2,1)S(1)} %bitcast.12), channel_id=1, source_target_pairs={{12,16},{16,12},{13,17},{17,13},{14,18},{18,14},{15,19},{19,15}} | collective-permute-start | bytes 3145736 | tf_op jit(solution)/shard_map/ppermute | solution.py:455
  31.8 21.5 %collective-permute-start.8 = (bf16[4,512,256]{2,1,0:T(8,128)(2,1)S(1)}, bf16[4,512,256]{2,1,0:T(8,128)(2,1)S(1)}, u32[]{:S(2)}, u32[]{:S(2)}) collective-permute-start(bf16[4,512,256]{2,1,0:T(8,128)(2,1)S(1)} %collective-permute-done.3), channel_id=1, source_target_pairs={{28,16},{0,12},{29,17},{1,13},{30,18},{2,14},{31,19},{3,15}} | collective-permute-start | bytes 3145736 | tf_op jit(solution)/shard_map/ppermute | solution.py:459
  36.2 4.8 %collective-permute-start.4 = (f32[8,2,256]{2,1,0:T(2,128)S(1)}, f32[8,2,256]{2,1,0:T(2,128)S(1)}, u32[]{:S(2)}, u32[]{:S(2)}) collective-permute-start(f32[8,2,256]{2,1,0:T(2,128)S(1)} %add.3.refs_0_), channel_id=1, source_target_pairs={{0,2},{1,3},{2,0},{3,1},{4,6},{5,7},{6,4},{7,5},{8,10},{9,11},{10,... | collective-permute-start | bytes 49160 | tf_op jit(solution)/shard_map/ppermute | solution.py:416
  37.8 3.2 %copy-start.4 = (s32[2]{0:T(128)S(1)}, s32[2]{0:T(128)}, u32[]{:S(2)}) copy-start(s32[2]{0:T(128)} %clip_ref.5) | copy-start | bytes 28
  37.8 3.2 %copy-start.6 = (f32[256]{0:T(256)S(1)}, f32[256]{0:T(256)}, u32[]{:S(2)}) copy-start(f32[256]{0:T(256)} %param.12) | copy-start | bytes 3076
  37.8 3.2 %copy-start.7 = (f32[256]{0:T(256)S(1)}, f32[256]{0:T(256)}, u32[]{:S(2)}) copy-start(f32[256]{0:T(256)} %param.13) | copy-start | bytes 3076
  41.0 12.3 %copy-start.1 = (bf16[8,8,64,256]{3,2,1,0:T(8,128)(2,1)S(1)}, bf16[8,8,64,256]{3,2,1,0:T(8,128)(2,1)}, u32[]{:S(2)}) copy-start(bf16[8,8,64,256]{3,2,1,0:T(8,128)(2,1)} %cot_ref.1) | copy-start | bytes 6291460
  41.0 12.3 %copy-start.5 = (s32[2]{0:T(128)S(1)}, s32[2]{0:T(128)}, u32[]{:S(2)}) copy-start(s32[2]{0:T(128)} %dil_ref.3) | copy-start | bytes 28
  44.4 46.9 %collective-permute-start.15 = (bf16[6,512,256]{2,1,0:T(8,128)(2,1)S(1)}, bf16[6,512,256]{2,1,0:T(8,128)(2,1)S(1)}, u32[]{:S(2)}, u32[]{:S(2)}) collective-permute-start(bf16[6,512,256]{2,1,0:T(8,128)(2,1)S(1)} %get-tuple-element.83), channel_id=1, source_target_pairs={{0,4},{4,8},{8,12},{12,16},{16,20},{20,24},{24,28},{1,5},{5,9},{9,... | collective-permute-start | bytes 4718600 | tf_op jit(solution)/shard_map/ppermute | solution.py:402
  45.8 45.5 %collective-permute-start.16 = (bf16[6,512,256]{2,1,0:T(8,128)(2,1)S(1)}, bf16[6,512,256]{2,1,0:T(8,128)(2,1)S(1)}, u32[]{:S(2)}, u32[]{:S(2)}) collective-permute-start(bf16[6,512,256]{2,1,0:T(8,128)(2,1)S(1)} %get-tuple-element.83), channel_id=1, source_target_pairs={{4,0},{8,4},{12,8},{16,12},{20,16},{24,20},{28,24},{5,1},{9,5},{13... | collective-permute-start | bytes 4718600 | tf_op jit(solution)/shard_map/ppermute | solution.py:402
  57.5 6.1 %collective-permute-start.10 = (f32[8,2,256]{2,1,0:T(2,128)S(1)}, f32[8,2,256]{2,1,0:T(2,128)S(1)}, u32[]{:S(2)}, u32[]{:S(2)}) collective-permute-start(f32[8,2,256]{2,1,0:T(2,128)S(1)} %get-tuple-element.69.refs_2_), channel_id=1, source_target_pairs={{0,2},{1,3},{2,0},{3,1},{4,6},{5,7},{6,4},{7,5},{8,10},{9,11},{10,... | collective-permute-start | bytes 49160 | tf_op jit(solution)/shard_map/ppermute | solution.py:407
  57.7 5.9 %collective-permute-start.11 = (f32[8,2,256]{2,1,0:T(2,128)S(1)}, f32[8,2,256]{2,1,0:T(2,128)S(1)}, u32[]{:S(2)}, u32[]{:S(2)}) collective-permute-start(f32[8,2,256]{2,1,0:T(2,128)S(1)} %get-tuple-element.69.refs_2_), channel_id=1, source_target_pairs={{0,3},{1,2},{2,1},{3,0},{4,7},{5,6},{6,5},{7,4},{8,11},{9,10},{10,... | collective-permute-start | bytes 49160 | tf_op jit(solution)/shard_map/ppermute | solution.py:407
  61.2 3.7 %collective-permute-start.9 = (f32[8,2,256]{2,1,0:T(2,128)S(1)}, f32[8,2,256]{2,1,0:T(2,128)S(1)}, u32[]{:S(2)}, u32[]{:S(2)}) collective-permute-start(f32[8,2,256]{2,1,0:T(2,128)S(1)} %get-tuple-element.69.refs_2_), channel_id=1, source_target_pairs={{0,1},{1,0},{2,3},{3,2},{4,5},{5,4},{6,7},{7,6},{8,9},{9,8},{10,11... | collective-permute-start | bytes 49160 | tf_op jit(solution)/shard_map/ppermute | solution.py:407
  67.2 8.8 %collective-permute-start.12 = (bf16[8,1,64,256]{3,2,1,0:T(8,128)(2,1)S(1)}, bf16[8,1,64,256]{3,2,1,0:T(8,128)(2,1)S(1)}, u32[]{:S(2)}, u32[]{:S(2)}) collective-permute-start(bf16[8,1,64,256]{3,2,1,0:T(8,128)(2,1)S(1)} %get-tuple-element.73), channel_id=1, source_target_pairs={{0,1},{1,2},{2,3},{4,5},{5,6},{6,7},{8,9},{9,10},{10,11},{12,13},{... | collective-permute-start | bytes 786440 | tf_op jit(solution)/shard_map/ppermute | solution.py:402
  69.6 8.3 %collective-permute-start.13 = (bf16[8,1,64,256]{3,2,1,0:T(8,128)(2,1)S(1)}, bf16[8,1,64,256]{3,2,1,0:T(8,128)(2,1)S(1)}, u32[]{:S(2)}, u32[]{:S(2)}) collective-permute-start(bf16[8,1,64,256]{3,2,1,0:T(8,128)(2,1)S(1)} %get-tuple-element.74), channel_id=1, source_target_pairs={{1,0},{2,1},{3,2},{5,4},{6,5},{7,6},{9,8},{10,9},{11,10},{13,12},{... | collective-permute-start | bytes 786440 | tf_op jit(solution)/shard_map/ppermute | solution.py:402
  78.2 2.4 %collective-permute-start.14 = (bf16[4,4,32,768]{3,2,1,0:T(8,128)(2,1)S(1)}, bf16[4,4,32,768]{3,2,1,0:T(8,128)(2,1)S(1)}, u32[]{:S(2)}, u32[]{:S(2)}) collective-permute-start(bf16[4,4,32,768]{3,2,1,0:T(8,128)(2,1)S(1)} %get-tuple-element.77), channel_id=1, source_target_pairs={{0,4},{4,0},{8,12},{12,8},{16,20},{20,16},{24,28},{28,24},{1,5},{5... | collective-permute-start | bytes 2359304 | tf_op jit(solution)/shard_map/ppermute | solution.py:510
  80.8 10.6 %collective-permute-start.17 = (bf16[4,32,768]{2,1,0:T(8,128)(2,1)S(1)}, bf16[4,32,768]{2,1,0:T(8,128)(2,1)S(1)}, u32[]{:S(2)}, u32[]{:S(2)}) collective-permute-start(bf16[4,32,768]{2,1,0:T(8,128)(2,1)S(1)} %get-tuple-element.85), channel_id=1, source_target_pairs={{0,8},{4,12},{8,0},{12,4},{16,24},{20,28},{24,16},{28,20},{1,9},{5... | collective-permute-start | bytes 589832 | tf_op jit(solution)/shard_map/ppermute | solution.py:515
  80.8 11.2 %collective-permute-start.18 = (bf16[4,32,768]{2,1,0:T(8,128)(2,1)S(1)}, bf16[4,32,768]{2,1,0:T(8,128)(2,1)S(1)}, u32[]{:S(2)}, u32[]{:S(2)}) collective-permute-start(bf16[4,32,768]{2,1,0:T(8,128)(2,1)S(1)} %get-tuple-element.86), channel_id=1, source_target_pairs={{0,16},{4,20},{8,24},{12,28},{16,0},{20,4},{24,8},{28,12},{1,17},{... | collective-permute-start | bytes 589832 | tf_op jit(solution)/shard_map/ppermute | solution.py:515
  80.9 11.1 %collective-permute-start.19 = (bf16[4,32,768]{2,1,0:T(8,128)(2,1)S(1)}, bf16[4,32,768]{2,1,0:T(8,128)(2,1)S(1)}, u32[]{:S(2)}, u32[]{:S(2)}) collective-permute-start(bf16[4,32,768]{2,1,0:T(8,128)(2,1)S(1)} %get-tuple-element.87), channel_id=1, source_target_pairs={{0,24},{4,28},{8,16},{12,20},{16,8},{20,12},{24,0},{28,4},{1,25},{... | collective-permute-start | bytes 589832 | tf_op jit(solution)/shard_map/ppermute | solution.py:515
  92.1 26.2 %collective-permute-start.26 = (bf16[2,512,256]{2,1,0:T(8,128)(2,1)S(1)}, bf16[2,512,256]{2,1,0:T(8,128)(2,1)S(1)}, u32[]{:S(2)}, u32[]{:S(2)}) collective-permute-start(bf16[2,512,256]{2,1,0:T(8,128)(2,1)S(1)} %get-tuple-element.95), channel_id=1, source_target_pairs={{4,0},{8,4},{12,8},{16,12},{20,16},{24,20},{28,24},{5,1},{9,5},{13... | collective-permute-start | bytes 1572872 | tf_op jit(solution)/shard_map/ppermute | solution.py:402
  93.4 24.9 %collective-permute-start.27 = (bf16[2,512,256]{2,1,0:T(8,128)(2,1)S(1)}, bf16[2,512,256]{2,1,0:T(8,128)(2,1)S(1)}, u32[]{:S(2)}, u32[]{:S(2)}) collective-permute-start(bf16[2,512,256]{2,1,0:T(8,128)(2,1)S(1)} %get-tuple-element.95), channel_id=1, source_target_pairs={{0,4},{4,8},{8,12},{12,16},{16,20},{20,24},{24,28},{1,5},{5,9},{9,... | collective-permute-start | bytes 1572872 | tf_op jit(solution)/shard_map/ppermute | solution.py:402
  96.5 4.5 %collective-permute-start.20 = (bf16[32,768]{1,0:T(8,128)(2,1)S(1)}, bf16[32,768]{1,0:T(8,128)(2,1)S(1)}, u32[]{:S(2)}, u32[]{:S(2)}) collective-permute-start(bf16[32,768]{1,0:T(8,128)(2,1)S(1)} %get-tuple-element.91), channel_id=1, source_target_pairs={{0,1},{1,0},{2,3},{3,2},{4,5},{5,4},{6,7},{7,6},{8,9},{9,8},{10,11... | collective-permute-start | bytes 147464 | tf_op jit(solution)/shard_map/ppermute | solution.py:527
  98.6 7.5 %collective-permute-start.21 = (bf16[32,768]{1,0:T(8,128)(2,1)S(1)}, bf16[32,768]{1,0:T(8,128)(2,1)S(1)}, u32[]{:S(2)}, u32[]{:S(2)}) collective-permute-start(bf16[32,768]{1,0:T(8,128)(2,1)S(1)} %get-tuple-element.92), channel_id=1, source_target_pairs={{0,2},{1,3},{2,0},{3,1},{4,6},{5,7},{6,4},{7,5},{8,10},{9,11},{10,... | collective-permute-start | bytes 147464 | tf_op jit(solution)/shard_map/ppermute | solution.py:527
  99.8 6.3 %collective-permute-start.22 = (bf16[32,768]{1,0:T(8,128)(2,1)S(1)}, bf16[32,768]{1,0:T(8,128)(2,1)S(1)}, u32[]{:S(2)}, u32[]{:S(2)}) collective-permute-start(bf16[32,768]{1,0:T(8,128)(2,1)S(1)} %get-tuple-element.93), channel_id=1, source_target_pairs={{0,3},{1,2},{2,1},{3,0},{4,7},{5,6},{6,5},{7,4},{8,11},{9,10},{10,... | collective-permute-start | bytes 147464 | tf_op jit(solution)/shard_map/ppermute | solution.py:527
  106.2 4.5 %collective-permute-start.23 = (bf16[32,768]{1,0:T(8,128)(2,1)S(1)}, bf16[32,768]{1,0:T(8,128)(2,1)S(1)}, u32[]{:S(2)}, u32[]{:S(2)}) collective-permute-start(bf16[32,768]{1,0:T(8,128)(2,1)S(1)} %line_sum.1.refs_0_), channel_id=1, source_target_pairs={{0,1},{1,0},{2,3},{3,2},{4,5},{5,4},{6,7},{7,6},{8,9},{9,8},{10,11... | collective-permute-start | bytes 147464 | tf_op jit(solution)/shard_map/ppermute | solution.py:533
  107.8 6.3 %collective-permute-start.24 = (bf16[32,768]{1,0:T(8,128)(2,1)S(1)}, bf16[32,768]{1,0:T(8,128)(2,1)S(1)}, u32[]{:S(2)}, u32[]{:S(2)}) collective-permute-start(bf16[32,768]{1,0:T(8,128)(2,1)S(1)} %line_sum.1.refs_0_), channel_id=1, source_target_pairs={{0,2},{1,3},{2,0},{3,1},{4,6},{5,7},{6,4},{7,5},{8,10},{9,11},{10,... | collective-permute-start | bytes 147464 | tf_op jit(solution)/shard_map/ppermute | solution.py:533
  108.7 6.0 %collective-permute-start.25 = (bf16[32,768]{1,0:T(8,128)(2,1)S(1)}, bf16[32,768]{1,0:T(8,128)(2,1)S(1)}, u32[]{:S(2)}, u32[]{:S(2)}) collective-permute-start(bf16[32,768]{1,0:T(8,128)(2,1)S(1)} %line_sum.1.refs_0_), channel_id=1, source_target_pairs={{0,3},{1,2},{2,1},{3,0},{4,7},{5,6},{6,5},{7,4},{8,11},{9,10},{10,... | collective-permute-start | bytes 147464 | tf_op jit(solution)/shard_map/ppermute | solution.py:533
  114.8 8.7 %collective-permute-start.28 = (bf16[4,32,768]{2,1,0:T(8,128)(2,1)S(1)}, bf16[4,32,768]{2,1,0:T(8,128)(2,1)S(1)}, u32[]{:S(2)}, u32[]{:S(2)}) collective-permute-start(bf16[4,32,768]{2,1,0:T(8,128)(2,1)S(1)} %line_place.1.refs_0_), channel_id=1, source_target_pairs={{0,8},{4,12},{8,0},{12,4},{16,24},{20,28},{24,16},{28,20},{1,9},{5... | collective-permute-start | bytes 589832 | tf_op jit(solution)/shard_map/ppermute | solution.py:537
  116.3 9.1 %collective-permute-start.29 = (bf16[4,32,768]{2,1,0:T(8,128)(2,1)S(1)}, bf16[4,32,768]{2,1,0:T(8,128)(2,1)S(1)}, u32[]{:S(2)}, u32[]{:S(2)}) collective-permute-start(bf16[4,32,768]{2,1,0:T(8,128)(2,1)S(1)} %line_place.1.refs_0_), channel_id=1, source_target_pairs={{0,16},{4,20},{8,24},{12,28},{16,0},{20,4},{24,8},{28,12},{1,17},{... | collective-permute-start | bytes 589832 | tf_op jit(solution)/shard_map/ppermute | solution.py:537
  116.3 9.1 %collective-permute-start.30 = (bf16[4,32,768]{2,1,0:T(8,128)(2,1)S(1)}, bf16[4,32,768]{2,1,0:T(8,128)(2,1)S(1)}, u32[]{:S(2)}, u32[]{:S(2)}) collective-permute-start(bf16[4,32,768]{2,1,0:T(8,128)(2,1)S(1)} %line_place.1.refs_0_), channel_id=1, source_target_pairs={{0,24},{4,28},{8,16},{12,20},{16,8},{20,12},{24,0},{28,4},{1,25},{... | collective-permute-start | bytes 589832 | tf_op jit(solution)/shard_map/ppermute | solution.py:537
  125.5 2.4 %collective-permute-start.31 = (bf16[4,4,32,768]{3,2,1,0:T(8,128)(2,1)S(1)}, bf16[4,4,32,768]{3,2,1,0:T(8,128)(2,1)S(1)}, u32[]{:S(2)}, u32[]{:S(2)}) collective-permute-start(bf16[4,4,32,768]{3,2,1,0:T(8,128)(2,1)S(1)} %plane_place.1.mine_ref), channel_id=1, source_target_pairs={{0,4},{4,0},{8,12},{12,8},{16,20},{20,16},{24,28},{28,24},{1,5},{5... | collective-permute-start | bytes 2359304 | tf_op jit(solution)/shard_map/ppermute | solution.py:549

commit v7 on v6

--- a/solution.py
+++ b/solution.py
@@ -468,6 +468,7 @@
         functools.partial(act_kernel, len(parts), entries, group_size), "activation",
         [clip_frames, *parts, conv_out, gain, shift], [shape((k, pixels, channels), BF16) for k in (frames, ahead, frames - ahead, frames, frames)], 10 * big, 10 * big, [row] * 2,
     )
+    act_early, *cot_corner = lax.optimization_barrier((act_early, *cot_corner))
     act_prev, act_next = neighbours("tm", act_early, act_early)
 
     grad_act, cot_cat, grad_sums = call(

time: 130 us -> 142 us (1.092)
  waiting for transfers between devices: 34.6 us -> 41.8 us
  starting transfers between devices: 51.4 us -> 56.1 us
    ppermute x3, waiting for transfers between devices: 0.75 us -> 9.12 us  [per_device(): lax.ppermute(x, 'tm', other_chip(s))]
    ppermute x3, starting transfers between devices: 3.55 us -> 6.9 us  [per_device(): gots = [lax.ppermute(own, 'tm', other_chip(s)) for s in range(1, chips)]]
    ppermute x10, waiting for transfers between devices: 8.23 us -> 10.9 us  [neighbours(): return (lax.ppermute(high, axis, up), lax.ppermute(low, axis, down))]
    ppermute x1, waiting for transfers between devices: 6.16 us -> 4.04 us  [per_device(): cot_corner.append(lax.ppermute(relayed, 'tm', [(7, 4), (0, 3)]))]
  transfers between devices with their start and end apart: 32 -> 32, of which waited for: 14 -> 17; matrix products, arithmetic and copies ran while one was open for 1% -> 1% of each run, Pallas kernels for 29% -> 24%
where the time goes in v7:
time: 142 us; the launch traced here: 141 us
  starting transfers between devices  56.1 us (40%)
  waiting for transfers between devices  41.8 us (29%)
  Pallas kernels  39.8 us (28%)
  local copies, waits for them, and re-layouts  2.8 us (2%)
    pallas_call x17, Pallas kernels, call(): pl.pallas_call(kernel, in_specs=[smem if x.dtype == jnp.int32 else vmem f...  39.8 us
    ppermute x10, starting transfers between devices, neighbours(): return (lax.ppermute(high, axis, up), lax.ppermute(low, axis, down))  22.6 us
    ppermute x10, waiting for transfers between devices, neighbours(): return (lax.ppermute(high, axis, up), lax.ppermute(low, axis, down))  10.9 us
    ppermute x3, waiting for transfers between devices, per_device(): lax.ppermute(x, 'tm', other_chip(s))  9.12 us
    ppermute x3, starting transfers between devices, per_device(): gots = [lax.ppermute(own, 'tm', other_chip(s)) for s in range(1, chips)]  6.9 us
    ppermute x3, starting transfers between devices, per_device(): lax.ppermute(x, 'tm', other_chip(s))  4.71 us
    ppermute x3, waiting for transfers between devices, per_device(): lax.ppermute(x, 'space', other_plane(s))  4.61 us
    ppermute x3, starting transfers between devices, per_device(): gots = [lax.ppermute(own, 'space', other_plane(s)) for s in range(1, n)]  4.47 us
  transfers between devices with their start and end apart: 32, of which 17 were waited for; matrix products, arithmetic and copies ran while one was open for 1% of the time, Pallas kernels for 24%

profile of v7, /device:TPU:0, one launch (start us, length us, event | category | flops | bytes accessed | tf_op | source)
XLA Modules:
  0.0 141.5 jit_solution(2236443681608456013)
XLA Ops:
  0.6 1.1 fusion.1
  1.7 1.6 %collective-permute-start.5 = (bf16[8,512,256]{2,1,0:T(8,128)(2,1)}, bf16[8,512,256]{2,1,0:T(8,128)(2,1)S(1)}, u32[]{:S(2)}, u32[]{:S(2)}) collective-permute-start(bf16[8,512,256]{2,1,0:T(8,128)(2,1)} %bitcast.6), channel_id=1, source_target_pairs={{4,0},{8,4},{12,8},{20,16},{24,20},{28,24},{5,1},{9,5},{13,9},{21,... | collective-permute-start | bytes 6291464 | tf_op jit(solution)/shard_map/ppermute | solution.py:402
  3.3 3.2 %collective-permute-start.6 = (bf16[8,512,256]{2,1,0:T(8,128)(2,1)}, bf16[8,512,256]{2,1,0:T(8,128)(2,1)S(1)}, u32[]{:S(2)}, u32[]{:S(2)}) collective-permute-start(bf16[8,512,256]{2,1,0:T(8,128)(2,1)} %bitcast.7), channel_id=1, source_target_pairs={{0,4},{4,8},{8,12},{16,20},{20,24},{24,28},{1,5},{5,9},{9,13},{17,... | collective-permute-start | bytes 6291464 | tf_op jit(solution)/shard_map/ppermute | solution.py:402
  6.5 4.9 %collective-permute-start = (bf16[8,1,64,256]{3,2,1,0:T(8,128)(2,1)S(1)}, bf16[8,1,64,256]{3,2,1,0:T(8,128)(2,1)S(1)}, u32[]{:S(2)}, u32[]{:S(2)}) collective-permute-start(bf16[8,1,64,256]{3,2,1,0:T(8,128)(2,1)S(1)} %get-tuple-element.56), channel_id=1, source_target_pairs={{0,1},{1,2},{2,3},{4,5},{5,6},{6,7},{8,9},{9,10},{10,11},{12,13},{... | collective-permute-start | bytes 786440 | tf_op jit(solution)/shard_map/ppermute | solution.py:402
  11.4 1.3 collective-permute-start.1
  12.7 1.7 %fusion = (bf16[4,8,64,256]{3,2,1,0:T(8,128)(2,1)S(1)}, bf16[4,8,64,256]{3,2,1,0:T(8,128)(2,1)S(1)}) fusion(bf16[8,8,64,256]{3,2,1,0:T(8,128)(2,1)} %cot_ref.1), kind=kLoop, calls=%fused_computation | loop fusion | bytes 4194304 | tf_op jit(solution)/shard_map/slice | solution.py:441
  14.4 1.4 %collective-permute-start.3 = (bf16[4,512,256]{2,1,0:T(8,128)(2,1)S(1)}, bf16[4,512,256]{2,1,0:T(8,128)(2,1)S(1)}, u32[]{:S(2)}, u32[]{:S(2)}) collective-permute-start(bf16[4,512,256]{2,1,0:T(8,128)(2,1)S(1)} %bitcast.13), channel_id=1, source_target_pairs={{12,28},{16,0},{13,29},{17,1},{14,30},{18,2},{15,31},{19,3}} | collective-permute-start | bytes 3145736 | tf_op jit(solution)/shard_map/ppermute | solution.py:442
  15.8 2.2 %collective-permute-done.above_ref = bf16[8,1,64,256]{3,2,1,0:T(8,128)(2,1)S(1)} collective-permute-done((bf16[8,1,64,256]{3,2,1,0:T(8,128)(2,1)S(1)}, bf16[8,1,64,256]{3,2,1,0:T(8,128)(2,1)S(1)}, u32[]{:S(2)}, u32[]{:S(2)}) %collective-permute-start) | collective-permute-done | bytes 262176 | tf_op jit(solution)/shard_map/ppermute | solution.py:402
  18.1 4.1 %collective-permute-done.1.below_ref = bf16[8,1,64,256]{3,2,1,0:T(8,128)(2,1)S(1)} collective-permute-done((bf16[8,1,64,256]{3,2,1,0:T(8,128)(2,1)S(1)}, bf16[8,1,64,256]{3,2,1,0:T(8,128)(2,1)S(1)}, u32[]{:S(2)}, u32[]{:S(2)}) %collective-permute-start.1) | collective-permute-done | bytes 262176 | tf_op jit(solution)/shard_map/ppermute | solution.py:402
  22.2 5.7 %conv_forward.1 = (f32[8,512,256]{2,1,0:T(8,128)S(1)}, f32[8,2,256]{2,1,0:T(2,128)S(1)}) custom-call(bf16[8,8,64,256]{3,2,1,0:T(8,128)(2,1)S(1)} %copy-done, bf16[8,1,64,256]{3,2,1,0:T(8,128)(2,1)S(1)} %collective-permute-done.above_ref, bf16[8,1,64,256]{3,2,1,0:T(8,128)(2,1)S(1)} %collective-permute-done.1.below_ref, bf16[3,3,256,256]{3,2,1,0:T(8,128)(2,1)S(1)} %copy-done.3), custom_call_target="tpu_custom_call" | custom-call | flops 26843545600 | bytes 8388608 | tf_op jit(solution)/shard_map/conv_forward/pallas_call | solution.py:20
  27.9 1.6 %collective-permute-start.2 = (f32[8,2,256]{2,1,0:T(2,128)S(1)}, f32[8,2,256]{2,1,0:T(2,128)S(1)}, u32[]{:S(2)}, u32[]{:S(2)}) collective-permute-start(f32[8,2,256]{2,1,0:T(2,128)S(1)} %get-tuple-element.59), channel_id=1, source_target_pairs={{0,1},{1,0},{2,3},{3,2},{4,5},{5,4},{6,7},{7,6},{8,9},{9,8},{10,11... | collective-permute-start | bytes 49160 | tf_op jit(solution)/shard_map/ppermute | solution.py:416
  29.6 0.7 collective-permute-start.7
  30.3 1.5 %collective-permute-done.2 = f32[8,2,256]{2,1,0:T(2,128)S(1)} collective-permute-done((f32[8,2,256]{2,1,0:T(2,128)S(1)}, f32[8,2,256]{2,1,0:T(2,128)S(1)}, u32[]{:S(2)}, u32[]{:S(2)}) %collective-permute-start.2) | collective-permute-done | bytes 16416 | tf_op jit(solution)/shard_map/ppermute | solution.py:416
  31.8 4.4 %collective-permute-start.8 = (bf16[4,512,256]{2,1,0:T(8,128)(2,1)S(1)}, bf16[4,512,256]{2,1,0:T(8,128)(2,1)S(1)}, u32[]{:S(2)}, u32[]{:S(2)}) collective-permute-start(bf16[4,512,256]{2,1,0:T(8,128)(2,1)S(1)} %collective-permute-done.3), channel_id=1, source_target_pairs={{28,16},{0,12},{29,17},{1,13},{30,18},{2,14},{31,19},{3,15}} | collective-permute-start | bytes 3145736 | tf_op jit(solution)/shard_map/ppermute | solution.py:459
  36.2 1.1 collective-permute-start.4
  37.3 0.5 turn_weights.1
  37.8 2.2 %turned.1.xt_ref = bf16[768,4096]{1,0:T(8,128)(2,1)S(1)} custom-call(bf16[8,8,64,256]{3,2,1,0:T(8,128)(2,1)S(1)} %copy-done, bf16[8,1,64,256]{3,2,1,0:T(8,128)(2,1)S(1)} %collective-permute-done.above_ref, bf16[8,1,64,256]{3,2,1,0:T(8,128)(2,1)S(1)} %collective-permute-done.1.below_ref), custom_call_target="tpu_custom_call" | custom-call | bytes 8388608 | tf_op jit(solution)/shard_map/turned/pallas_call | solution.py:20
  40.0 1.0 collective-permute-done.4.refs_1_
  41.0 3.4 %activation.1 = (bf16[8,512,256]{2,1,0:T(8,128)(2,1)S(1)}, bf16[6,512,256]{2,1,0:T(8,128)(2,1)S(1)}, bf16[2,512,256]{2,1,0:T(8,128)(2,1)S(1)}, bf16[8,512,256]{2,1,0:T(8,128)(2,1)S(1)}, bf16[8,512,256]{2,1,0:T(8,128)(2,1)S(1)}) custom-call(s32[2]{0:T(128)S(1)} %copy-done.4, f32[8,2,256]{2,1,0:T(2,128)S(1)} %add.3.refs_0_, ...), custom_call_target="tpu_custom_call" | custom-call | flops 10485760 | bytes 10485760 | tf_op jit(solution)/shard_map/activation/pallas_call | solution.py:20
  44.4 4.0 %collective-permute-done.8.refs_1_ = bf16[4,512,256]{2,1,0:T(8,128)(2,1)S(1)} collective-permute-done((bf16[4,512,256]{2,1,0:T(8,128)(2,1)S(1)}, bf16[4,512,256]{2,1,0:T(8,128)(2,1)S(1)}, u32[]{:S(2)}, u32[]{:S(2)}) %collective-permute-start.8) | collective-permute-done | bytes 1048608 | tf_op jit(solution)/shard_map/ppermute | solution.py:459
  48.4 4.2 %grad_activation.1 = (bf16[8,512,256]{2,1,0:T(8,128)(2,1)S(1)}, bf16[4096,768]{1,0:T(8,128)(2,1)S(1)}, f32[8,2,256]{2,1,0:T(2,128)S(1)}) custom-call(s32[2]{0:T(128)S(1)} %copy-done.4, s32[2]{0:T(128)S(1)} %copy-done.5, bf16[8,512,256]{2,1,0:T(8,128)(2,1)S(1)} %bitcast.8, bf16[8,512,256]{2,1,0:T(8,128)(2,1)S(1)} %collective-permute-done.5.nxt, ...), custom_call_target="tpu_custom_call" | custom-call | flops 1610612736 | bytes 16777216 | tf_op jit(solution)/shard_map/grad_activation/pallas_call | solution.py:20
  52.7 1.1 collective-permute-start.10
  53.8 1.8 %collective-permute-start.11 = (f32[8,2,256]{2,1,0:T(2,128)S(1)}, f32[8,2,256]{2,1,0:T(2,128)S(1)}, u32[]{:S(2)}, u32[]{:S(2)}) collective-permute-start(f32[8,2,256]{2,1,0:T(2,128)S(1)} %get-tuple-element.75.refs_2_), channel_id=1, source_target_pairs={{0,3},{1,2},{2,1},{3,0},{4,7},{5,6},{6,5},{7,4},{8,11},{9,10},{10,... | collective-permute-start | bytes 49160 | tf_op jit(solution)/shard_map/ppermute | solution.py:407
  55.6 0.7 collective-permute-start.9
  56.2 1.4 collective-permute-start.15
  57.6 1.3 collective-permute-start.16
  58.9 1.9 %temporal_grad.1.temporal_ref = f32[256,768]{1,0:T(8,128)S(1)} custom-call(bf16[8,512,256]{2,1,0:T(8,128)(2,1)S(1)} %get-tuple-element.77.act_ref.own, bf16[4096,768]{1,0:T(8,128)(2,1)S(1)} %get-tuple-element.78.cat_ref), custom_call_target="tpu_custom_call" | custom-call | flops 1610612736 | bytes 8388608 | tf_op jit(solution)/shard_map/temporal_grad/pallas_call | solution.py:20
  60.8 2.2 %norm_backward.1 = (bf16[8,512,256]{2,1,0:T(8,128)(2,1)S(1)}, bf16[8,1,64,256]{3,2,1,0:T(8,128)(2,1)S(1)}, bf16[8,1,64,256]{3,2,1,0:T(8,128)(2,1)S(1)}, bf16[4096,768]{1,0:T(8,128)(2,1)S(1)}) custom-call(bf16[8,512,256]{2,1,0:T(8,128)(2,1)S(1)} %get-tuple-element.65.refs_3_.normed_ref, bf16[8,512,256]{2,1,0:T(8,128)(2,1)S(1)} %get-tuple-element.66.refs_4_.slope_ref, ...), custom_call_target="tpu_custom_call" | custom-call | bytes 12582912 | tf_op jit(solution)/shard_map/norm_backward/pallas_call | solution.py:20
  63.0 3.3 %collective-permute-start.12 = (bf16[8,1,64,256]{3,2,1,0:T(8,128)(2,1)S(1)}, bf16[8,1,64,256]{3,2,1,0:T(8,128)(2,1)S(1)}, u32[]{:S(2)}, u32[]{:S(2)}) collective-permute-start(bf16[8,1,64,256]{3,2,1,0:T(8,128)(2,1)S(1)} %get-tuple-element.79), channel_id=1, source_target_pairs={{0,1},{1,2},{2,3},{4,5},{5,6},{6,7},{8,9},{9,10},{10,11},{12,13},{... | collective-permute-start | bytes 786440 | tf_op jit(solution)/shard_map/ppermute | solution.py:402
  66.3 1.3 collective-permute-start.13
  67.6 5.1 %weight_grad.1.acc_ref = f32[1024,768]{1,0:T(8,128)S(1)} custom-call(bf16[768,4096]{1,0:T(8,128)(2,1)S(1)} %turned.1.xt_ref, bf16[4096,768]{1,0:T(8,128)(2,1)S(1)} %get-tuple-element.76.moved_ref, f32[256,768]{1,0:T(8,128)S(1)} %temporal_grad.1.temporal_ref), custom_call_target="tpu_custom_call" | custom-call | flops 4831838208 | bytes 12582912 | tf_op jit(solution)/shard_map/weight_grad/pallas_call | solution.py:20
  72.8 0.1 collective-permute-done.12.above_ref
  72.8 4.4 %collective-permute-done.13.below_ref = bf16[8,1,64,256]{3,2,1,0:T(8,128)(2,1)S(1)} collective-permute-done((bf16[8,1,64,256]{3,2,1,0:T(8,128)(2,1)S(1)}, bf16[8,1,64,256]{3,2,1,0:T(8,128)(2,1)S(1)}, u32[]{:S(2)}, u32[]{:S(2)}) %collective-permute-start.13) | collective-permute-done | bytes 262176 | tf_op jit(solution)/shard_map/ppermute | solution.py:402
  77.3 0.4 hand_out.1
  77.7 2.3 %collective-permute-done.14.got_ref = bf16[4,4,32,768]{3,2,1,0:T(8,128)(2,1)S(1)} collective-permute-done((bf16[4,4,32,768]{3,2,1,0:T(8,128)(2,1)S(1)}, bf16[4,4,32,768]{3,2,1,0:T(8,128)(2,1)S(1)}, u32[]{:S(2)}, u32[]{:S(2)}) %collective-permute-start.14) | collective-permute-done | bytes 786464 | tf_op jit(solution)/shard_map/ppermute | solution.py:511
  80.0 0.2 core_sum.1
  80.2 2.4 %collective-permute-start.17 = (bf16[4,32,768]{2,1,0:T(8,128)(2,1)S(1)}, bf16[4,32,768]{2,1,0:T(8,128)(2,1)S(1)}, u32[]{:S(2)}, u32[]{:S(2)}) collective-permute-start(bf16[4,32,768]{2,1,0:T(8,128)(2,1)S(1)} %get-tuple-element.91), channel_id=1, source_target_pairs={{0,8},{4,12},{8,0},{12,4},{16,24},{20,28},{24,16},{28,20},{1,9},{5... | collective-permute-start | bytes 589832 | tf_op jit(solution)/shard_map/ppermute | solution.py:516
  82.6 0.9 collective-permute-start.18
  83.5 1.4 collective-permute-start.19
  84.9 6.9 %conv_backward.1 = bf16[8,8,64,256]{3,2,1,0:T(8,128)(2,1)} custom-call(bf16[8,512,256]{2,1,0:T(8,128)(2,1)S(1)} %get-tuple-element.85.g_ref, bf16[8,1,64,256]{3,2,1,0:T(8,128)(2,1)S(1)} %collective-permute-done.12.above_ref, bf16[8,1,64,256]{3,2,1,0:T(8,128)(2,1)S(1)} %collective-permute-done.13.below_ref, bf16[8,8,64,256]{3,2,1,0:T(8,128)(2,1)S(1)} %copy-done.1, ...), custom_call_target="tpu_custom_call" | custom-call | flops 4831838208 | bytes 8388608 | tf_op jit(solution)/shard_map/conv_backward/pallas_call | solution.py:20
  91.8 9.1 %collective-permute-done.17.refs_0_ = bf16[4,32,768]{2,1,0:T(8,128)(2,1)S(1)} collective-permute-done((bf16[4,32,768]{2,1,0:T(8,128)(2,1)S(1)}, bf16[4,32,768]{2,1,0:T(8,128)(2,1)S(1)}, u32[]{:S(2)}, u32[]{:S(2)}) %collective-permute-start.17) | collective-permute-done | bytes 196640 | tf_op jit(solution)/shard_map/ppermute | solution.py:516
  101.0 0.1 plane_sum.1
  101.1 1.3 collective-permute-start.26
  102.4 3.1 %collective-permute-start.27 = (bf16[2,512,256]{2,1,0:T(8,128)(2,1)S(1)}, bf16[2,512,256]{2,1,0:T(8,128)(2,1)S(1)}, u32[]{:S(2)}, u32[]{:S(2)}) collective-permute-start(bf16[2,512,256]{2,1,0:T(8,128)(2,1)S(1)} %get-tuple-element.101), channel_id=1, source_target_pairs={{0,4},{4,8},{8,12},{12,16},{16,20},{20,24},{24,28},{1,5},{5,9},{9,... | collective-permute-start | bytes 1572872 | tf_op jit(solution)/shard_map/ppermute | solution.py:402
  105.4 1.5 %collective-permute-start.20 = (bf16[32,768]{1,0:T(8,128)(2,1)S(1)}, bf16[32,768]{1,0:T(8,128)(2,1)S(1)}, u32[]{:S(2)}, u32[]{:S(2)}) collective-permute-start(bf16[32,768]{1,0:T(8,128)(2,1)S(1)} %get-tuple-element.97), channel_id=1, source_target_pairs={{0,1},{1,0},{2,3},{3,2},{4,5},{5,4},{6,7},{7,6},{8,9},{9,8},{10,11... | collective-permute-start | bytes 147464 | tf_op jit(solution)/shard_map/ppermute | solution.py:528
  106.9 1.6 %collective-permute-start.21 = (bf16[32,768]{1,0:T(8,128)(2,1)S(1)}, bf16[32,768]{1,0:T(8,128)(2,1)S(1)}, u32[]{:S(2)}, u32[]{:S(2)}) collective-permute-start(bf16[32,768]{1,0:T(8,128)(2,1)S(1)} %get-tuple-element.98), channel_id=1, source_target_pairs={{0,2},{1,3},{2,0},{3,1},{4,6},{5,7},{6,4},{7,5},{8,10},{9,11},{10,... | collective-permute-start | bytes 147464 | tf_op jit(solution)/shard_map/ppermute | solution.py:528
  108.5 1.3 collective-permute-start.22
  109.9 2.6 %collective-permute-done.21.refs_1_ = bf16[32,768]{1,0:T(8,128)(2,1)S(1)} collective-permute-done((bf16[32,768]{1,0:T(8,128)(2,1)S(1)}, bf16[32,768]{1,0:T(8,128)(2,1)S(1)}, u32[]{:S(2)}, u32[]{:S(2)}) %collective-permute-start.21) | collective-permute-done | bytes 49184 | tf_op jit(solution)/shard_map/ppermute | solution.py:528
  112.5 2.0 %collective-permute-done.22.refs_2_ = bf16[32,768]{1,0:T(8,128)(2,1)S(1)} collective-permute-done((bf16[32,768]{1,0:T(8,128)(2,1)S(1)}, bf16[32,768]{1,0:T(8,128)(2,1)S(1)}, u32[]{:S(2)}, u32[]{:S(2)}) %collective-permute-start.22) | collective-permute-done | bytes 49184 | tf_op jit(solution)/shard_map/ppermute | solution.py:528
  114.5 0.7 collective-permute-start.23
  115.3 1.8 %collective-permute-start.24 = (bf16[32,768]{1,0:T(8,128)(2,1)S(1)}, bf16[32,768]{1,0:T(8,128)(2,1)S(1)}, u32[]{:S(2)}, u32[]{:S(2)}) collective-permute-start(bf16[32,768]{1,0:T(8,128)(2,1)S(1)} %line_sum.1.refs_0_), channel_id=1, source_target_pairs={{0,2},{1,3},{2,0},{3,1},{4,6},{5,7},{6,4},{7,5},{8,10},{9,11},{10,... | collective-permute-start | bytes 147464 | tf_op jit(solution)/shard_map/ppermute | solution.py:534
  117.0 1.9 %collective-permute-start.25 = (bf16[32,768]{1,0:T(8,128)(2,1)S(1)}, bf16[32,768]{1,0:T(8,128)(2,1)S(1)}, u32[]{:S(2)}, u32[]{:S(2)}) collective-permute-start(bf16[32,768]{1,0:T(8,128)(2,1)S(1)} %line_sum.1.refs_0_), channel_id=1, source_target_pairs={{0,3},{1,2},{2,1},{3,0},{4,7},{5,6},{6,5},{7,4},{8,11},{9,10},{10,... | collective-permute-start | bytes 147464 | tf_op jit(solution)/shard_map/ppermute | solution.py:534
  119.0 0.2 collective-permute-done.23.refs_1_
  119.2 3.2 %collective-permute-done.24.refs_2_ = bf16[32,768]{1,0:T(8,128)(2,1)S(1)} collective-permute-done((bf16[32,768]{1,0:T(8,128)(2,1)S(1)}, bf16[32,768]{1,0:T(8,128)(2,1)S(1)}, u32[]{:S(2)}, u32[]{:S(2)}) %collective-permute-start.24) | collective-permute-done | bytes 49184 | tf_op jit(solution)/shard_map/ppermute | solution.py:534
  122.4 0.6 collective-permute-done.25.refs_3_
  123.0 3.5 %collective-permute-start.28 = (bf16[4,32,768]{2,1,0:T(8,128)(2,1)S(1)}, bf16[4,32,768]{2,1,0:T(8,128)(2,1)S(1)}, u32[]{:S(2)}, u32[]{:S(2)}) collective-permute-start(bf16[4,32,768]{2,1,0:T(8,128)(2,1)S(1)} %line_place.1.refs_0_), channel_id=1, source_target_pairs={{0,8},{4,12},{8,0},{12,4},{16,24},{20,28},{24,16},{28,20},{1,9},{5... | collective-permute-start | bytes 589832 | tf_op jit(solution)/shard_map/ppermute | solution.py:538
  126.5 2.0 %collective-permute-start.29 = (bf16[4,32,768]{2,1,0:T(8,128)(2,1)S(1)}, bf16[4,32,768]{2,1,0:T(8,128)(2,1)S(1)}, u32[]{:S(2)}, u32[]{:S(2)}) collective-permute-start(bf16[4,32,768]{2,1,0:T(8,128)(2,1)S(1)} %line_place.1.refs_0_), channel_id=1, source_target_pairs={{0,16},{4,20},{8,24},{12,28},{16,0},{20,4},{24,8},{28,12},{1,17},{... | collective-permute-start | bytes 589832 | tf_op jit(solution)/shard_map/ppermute | solution.py:538
  128.5 1.4 collective-permute-start.30
  129.9 5.2 %temporal_forward.1 = bf16[8,8,64,256]{3,2,1,0:T(8,128)(2,1)} custom-call(s32[2]{0:T(128)S(1)} %copy-done.4, s32[2]{0:T(128)S(1)} %copy-done.5, bf16[8,512,256]{2,1,0:T(8,128)(2,1)S(1)} %get-tuple-element.77.act_ref.own, bf16[6,512,256]{2,1,0:T(8,128)(2,1)S(1)} %collective-permute-done.16.nxt_a, bf16[2,512,256]{2,1,0:T(8,128)(2,1)S(1)} %collective-permute-done.26.nxt_b, ...), custom_call_target="tpu_custom_call" | custom-call | flops 1610612736 | bytes 10485760 | tf_op jit(solution)/shard_map/temporal_forward/pallas_call | solution.py:20
  135.1 0.7 collective-permute-done.29.refs_2_
  135.8 1.4 collective-permute-done.30.refs_3_
  137.2 0.1 collective-permute-start.31
  137.3 2.3 %collective-permute-done.31.got_ref = bf16[4,4,32,768]{3,2,1,0:T(8,128)(2,1)S(1)} collective-permute-done((bf16[4,4,32,768]{3,2,1,0:T(8,128)(2,1)S(1)}, bf16[4,4,32,768]{3,2,1,0:T(8,128)(2,1)S(1)}, u32[]{:S(2)}, u32[]{:S(2)}) %collective-permute-start.31) | collective-permute-done | bytes 786464 | tf_op jit(solution)/shard_map/ppermute | solution.py:550
  139.6 1.9 %finish.1 = (f32[3,3,256,256]{3,2,1,0:T(8,128)}, f32[3,256,256]{2,1,0:T(8,128)}) custom-call(bf16[4,4,32,768]{3,2,1,0:T(8,128)(2,1)S(1)} %plane_place.1.mine_ref, bf16[4,4,32,768]{3,2,1,0:T(8,128)(2,1)S(1)} %collective-permute-done.31.got_ref), custom_call_target="tpu_custom_call" | custom-call | bytes 4194304 | tf_op jit(solution)/shard_map/finish/pallas_call | solution.py:20
  (36 shorter events, 0.3 us)
Async XLA Ops:
  1.7 20.5 %copy-start = (bf16[8,8,64,256]{3,2,1,0:T(8,128)(2,1)S(1)}, bf16[8,8,64,256]{3,2,1,0:T(8,128)(2,1)}, u32[]{:S(2)}) copy-start(bf16[8,8,64,256]{3,2,1,0:T(8,128)(2,1)} %x_ref.5) | copy-start | bytes 6291460
  1.7 20.5 %copy-start.3 = (bf16[3,3,256,256]{3,2,1,0:T(8,128)(2,1)S(1)}, bf16[3,3,256,256]{3,2,1,0:T(8,128)(2,1)}, u32[]{:S(2)}) copy-start(bf16[3,3,256,256]{3,2,1,0:T(8,128)(2,1)} %spatial_ref.1) | copy-start | bytes 3538948
  1.7 46.7 %collective-permute-start.5 = (bf16[8,512,256]{2,1,0:T(8,128)(2,1)}, bf16[8,512,256]{2,1,0:T(8,128)(2,1)S(1)}, u32[]{:S(2)}, u32[]{:S(2)}) collective-permute-start(bf16[8,512,256]{2,1,0:T(8,128)(2,1)} %bitcast.6), channel_id=1, source_target_pairs={{4,0},{8,4},{12,8},{20,16},{24,20},{28,24},{5,1},{9,5},{13,9},{21,... | collective-permute-start | bytes 6291464 | tf_op jit(solution)/shard_map/ppermute | solution.py:402
  3.3 45.1 %collective-permute-start.6 = (bf16[8,512,256]{2,1,0:T(8,128)(2,1)}, bf16[8,512,256]{2,1,0:T(8,128)(2,1)S(1)}, u32[]{:S(2)}, u32[]{:S(2)}) collective-permute-start(bf16[8,512,256]{2,1,0:T(8,128)(2,1)} %bitcast.7), channel_id=1, source_target_pairs={{0,4},{4,8},{8,12},{16,20},{20,24},{24,28},{1,5},{5,9},{9,13},{17,... | collective-permute-start | bytes 6291464 | tf_op jit(solution)/shard_map/ppermute | solution.py:402
  6.5 11.6 %collective-permute-start = (bf16[8,1,64,256]{3,2,1,0:T(8,128)(2,1)S(1)}, bf16[8,1,64,256]{3,2,1,0:T(8,128)(2,1)S(1)}, u32[]{:S(2)}, u32[]{:S(2)}) collective-permute-start(bf16[8,1,64,256]{3,2,1,0:T(8,128)(2,1)S(1)} %get-tuple-element.56), channel_id=1, source_target_pairs={{0,1},{1,2},{2,3},{4,5},{5,6},{6,7},{8,9},{9,10},{10,11},{12,13},{... | collective-permute-start | bytes 786440 | tf_op jit(solution)/shard_map/ppermute | solution.py:402
  11.4 10.8 %collective-permute-start.1 = (bf16[8,1,64,256]{3,2,1,0:T(8,128)(2,1)S(1)}, bf16[8,1,64,256]{3,2,1,0:T(8,128)(2,1)S(1)}, u32[]{:S(2)}, u32[]{:S(2)}) collective-permute-start(bf16[8,1,64,256]{3,2,1,0:T(8,128)(2,1)S(1)} %get-tuple-element.57), channel_id=1, source_target_pairs={{1,0},{2,1},{3,2},{5,4},{6,5},{7,6},{9,8},{10,9},{11,10},{13,12},{... | collective-permute-start | bytes 786440 | tf_op jit(solution)/shard_map/ppermute | solution.py:402
  14.4 22.9 %copy-start.2 = (bf16[3,256,256]{2,1,0:T(8,128)(2,1)S(1)}, bf16[3,256,256]{2,1,0:T(8,128)(2,1)}, u32[]{:S(2)}) copy-start(bf16[3,256,256]{2,1,0:T(8,128)(2,1)} %temporal_ref.1) | copy-start | bytes 1179652
  14.4 17.3 %collective-permute-start.3 = (bf16[4,512,256]{2,1,0:T(8,128)(2,1)S(1)}, bf16[4,512,256]{2,1,0:T(8,128)(2,1)S(1)}, u32[]{:S(2)}, u32[]{:S(2)}) collective-permute-start(bf16[4,512,256]{2,1,0:T(8,128)(2,1)S(1)} %bitcast.13), channel_id=1, source_target_pairs={{12,28},{16,0},{13,29},{17,1},{14,30},{18,2},{15,31},{19,3}} | collective-permute-start | bytes 3145736 | tf_op jit(solution)/shard_map/ppermute | solution.py:442
  27.9 3.8 %collective-permute-start.2 = (f32[8,2,256]{2,1,0:T(2,128)S(1)}, f32[8,2,256]{2,1,0:T(2,128)S(1)}, u32[]{:S(2)}, u32[]{:S(2)}) collective-permute-start(f32[8,2,256]{2,1,0:T(2,128)S(1)} %get-tuple-element.59), channel_id=1, source_target_pairs={{0,1},{1,0},{2,3},{3,2},{4,5},{5,4},{6,7},{7,6},{8,9},{9,8},{10,11... | collective-permute-start | bytes 49160 | tf_op jit(solution)/shard_map/ppermute | solution.py:416
  29.6 14.8 %collective-permute-start.7 = (bf16[4,512,256]{2,1,0:T(8,128)(2,1)S(1)}, bf16[4,512,256]{2,1,0:T(8,128)(2,1)S(1)}, u32[]{:S(2)}, u32[]{:S(2)}) collective-permute-start(bf16[4,512,256]{2,1,0:T(8,128)(2,1)S(1)} %bitcast.12), channel_id=1, source_target_pairs={{12,16},{16,12},{13,17},{17,13},{14,18},{18,14},{15,19},{19,15}} | collective-permute-start | bytes 3145736 | tf_op jit(solution)/shard_map/ppermute | solution.py:455
  31.8 16.7 %collective-permute-start.8 = (bf16[4,512,256]{2,1,0:T(8,128)(2,1)S(1)}, bf16[4,512,256]{2,1,0:T(8,128)(2,1)S(1)}, u32[]{:S(2)}, u32[]{:S(2)}) collective-permute-start(bf16[4,512,256]{2,1,0:T(8,128)(2,1)S(1)} %collective-permute-done.3), channel_id=1, source_target_pairs={{28,16},{0,12},{29,17},{1,13},{30,18},{2,14},{31,19},{3,15}} | collective-permute-start | bytes 3145736 | tf_op jit(solution)/shard_map/ppermute | solution.py:459
  36.2 4.8 %collective-permute-start.4 = (f32[8,2,256]{2,1,0:T(2,128)S(1)}, f32[8,2,256]{2,1,0:T(2,128)S(1)}, u32[]{:S(2)}, u32[]{:S(2)}) collective-permute-start(f32[8,2,256]{2,1,0:T(2,128)S(1)} %add.3.refs_0_), channel_id=1, source_target_pairs={{0,2},{1,3},{2,0},{3,1},{4,6},{5,7},{6,4},{7,5},{8,10},{9,11},{10,... | collective-permute-start | bytes 49160 | tf_op jit(solution)/shard_map/ppermute | solution.py:416
  37.8 3.2 %copy-start.4 = (s32[2]{0:T(128)S(1)}, s32[2]{0:T(128)}, u32[]{:S(2)}) copy-start(s32[2]{0:T(128)} %clip_ref.5) | copy-start | bytes 28
  37.8 3.2 %copy-start.6 = (f32[256]{0:T(256)S(1)}, f32[256]{0:T(256)}, u32[]{:S(2)}) copy-start(f32[256]{0:T(256)} %param.12) | copy-start | bytes 3076
  37.8 3.2 %copy-start.7 = (f32[256]{0:T(256)S(1)}, f32[256]{0:T(256)}, u32[]{:S(2)}) copy-start(f32[256]{0:T(256)} %param.13) | copy-start | bytes 3076
  41.0 7.5 %copy-start.1 = (bf16[8,8,64,256]{3,2,1,0:T(8,128)(2,1)S(1)}, bf16[8,8,64,256]{3,2,1,0:T(8,128)(2,1)}, u32[]{:S(2)}) copy-start(bf16[8,8,64,256]{3,2,1,0:T(8,128)(2,1)} %cot_ref.1) | copy-start | bytes 6291460
  41.0 7.4 %copy-start.5 = (s32[2]{0:T(128)S(1)}, s32[2]{0:T(128)}, u32[]{:S(2)}) copy-start(s32[2]{0:T(128)} %dil_ref.3) | copy-start | bytes 28
  52.7 8.1 %collective-permute-start.10 = (f32[8,2,256]{2,1,0:T(2,128)S(1)}, f32[8,2,256]{2,1,0:T(2,128)S(1)}, u32[]{:S(2)}, u32[]{:S(2)}) collective-permute-start(f32[8,2,256]{2,1,0:T(2,128)S(1)} %get-tuple-element.75.refs_2_), channel_id=1, source_target_pairs={{0,2},{1,3},{2,0},{3,1},{4,6},{5,7},{6,4},{7,5},{8,10},{9,11},{10,... | collective-permute-start | bytes 49160 | tf_op jit(solution)/shard_map/ppermute | solution.py:407
  53.8 7.0 %collective-permute-start.11 = (f32[8,2,256]{2,1,0:T(2,128)S(1)}, f32[8,2,256]{2,1,0:T(2,128)S(1)}, u32[]{:S(2)}, u32[]{:S(2)}) collective-permute-start(f32[8,2,256]{2,1,0:T(2,128)S(1)} %get-tuple-element.75.refs_2_), channel_id=1, source_target_pairs={{0,3},{1,2},{2,1},{3,0},{4,7},{5,6},{6,5},{7,4},{8,11},{9,10},{10,... | collective-permute-start | bytes 49160 | tf_op jit(solution)/shard_map/ppermute | solution.py:407
  55.6 5.3 %collective-permute-start.9 = (f32[8,2,256]{2,1,0:T(2,128)S(1)}, f32[8,2,256]{2,1,0:T(2,128)S(1)}, u32[]{:S(2)}, u32[]{:S(2)}) collective-permute-start(f32[8,2,256]{2,1,0:T(2,128)S(1)} %get-tuple-element.75.refs_2_), channel_id=1, source_target_pairs={{0,1},{1,0},{2,3},{3,2},{4,5},{5,4},{6,7},{7,6},{8,9},{9,8},{10,11... | collective-permute-start | bytes 49160 | tf_op jit(solution)/shard_map/ppermute | solution.py:407
  56.2 35.6 %collective-permute-start.15 = (bf16[6,512,256]{2,1,0:T(8,128)(2,1)S(1)}, bf16[6,512,256]{2,1,0:T(8,128)(2,1)S(1)}, u32[]{:S(2)}, u32[]{:S(2)}) collective-permute-start(bf16[6,512,256]{2,1,0:T(8,128)(2,1)S(1)} %get-tuple-element.89), channel_id=1, source_target_pairs={{0,4},{4,8},{8,12},{12,16},{16,20},{20,24},{24,28},{1,5},{5,9},{9,... | collective-permute-start | bytes 4718600 | tf_op jit(solution)/shard_map/ppermute | solution.py:402
  57.6 34.2 %collective-permute-start.16 = (bf16[6,512,256]{2,1,0:T(8,128)(2,1)S(1)}, bf16[6,512,256]{2,1,0:T(8,128)(2,1)S(1)}, u32[]{:S(2)}, u32[]{:S(2)}) collective-permute-start(bf16[6,512,256]{2,1,0:T(8,128)(2,1)S(1)} %get-tuple-element.89), channel_id=1, source_target_pairs={{4,0},{8,4},{12,8},{16,12},{20,16},{24,20},{28,24},{5,1},{9,5},{13... | collective-permute-start | bytes 4718600 | tf_op jit(solution)/shard_map/ppermute | solution.py:402
  63.0 9.8 %collective-permute-start.12 = (bf16[8,1,64,256]{3,2,1,0:T(8,128)(2,1)S(1)}, bf16[8,1,64,256]{3,2,1,0:T(8,128)(2,1)S(1)}, u32[]{:S(2)}, u32[]{:S(2)}) collective-permute-start(bf16[8,1,64,256]{3,2,1,0:T(8,128)(2,1)S(1)} %get-tuple-element.79), channel_id=1, source_target_pairs={{0,1},{1,2},{2,3},{4,5},{5,6},{6,7},{8,9},{9,10},{10,11},{12,13},{... | collective-permute-start | bytes 786440 | tf_op jit(solution)/shard_map/ppermute | solution.py:402
  66.3 10.9 %collective-permute-start.13 = (bf16[8,1,64,256]{3,2,1,0:T(8,128)(2,1)S(1)}, bf16[8,1,64,256]{3,2,1,0:T(8,128)(2,1)S(1)}, u32[]{:S(2)}, u32[]{:S(2)}) collective-permute-start(bf16[8,1,64,256]{3,2,1,0:T(8,128)(2,1)S(1)} %get-tuple-element.80), channel_id=1, source_target_pairs={{1,0},{2,1},{3,2},{5,4},{6,5},{7,6},{9,8},{10,9},{11,10},{13,12},{... | collective-permute-start | bytes 786440 | tf_op jit(solution)/shard_map/ppermute | solution.py:402
  77.7 2.4 %collective-permute-start.14 = (bf16[4,4,32,768]{3,2,1,0:T(8,128)(2,1)S(1)}, bf16[4,4,32,768]{3,2,1,0:T(8,128)(2,1)S(1)}, u32[]{:S(2)}, u32[]{:S(2)}) collective-permute-start(bf16[4,4,32,768]{3,2,1,0:T(8,128)(2,1)S(1)} %get-tuple-element.83), channel_id=1, source_target_pairs={{0,4},{4,0},{8,12},{12,8},{16,20},{20,16},{24,28},{28,24},{1,5},{5... | collective-permute-start | bytes 2359304 | tf_op jit(solution)/shard_map/ppermute | solution.py:511
  80.2 20.8 %collective-permute-start.17 = (bf16[4,32,768]{2,1,0:T(8,128)(2,1)S(1)}, bf16[4,32,768]{2,1,0:T(8,128)(2,1)S(1)}, u32[]{:S(2)}, u32[]{:S(2)}) collective-permute-start(bf16[4,32,768]{2,1,0:T(8,128)(2,1)S(1)} %get-tuple-element.91), channel_id=1, source_target_pairs={{0,8},{4,12},{8,0},{12,4},{16,24},{20,28},{24,16},{28,20},{1,9},{5... | collective-permute-start | bytes 589832 | tf_op jit(solution)/shard_map/ppermute | solution.py:516
  82.6 18.4 %collective-permute-start.18 = (bf16[4,32,768]{2,1,0:T(8,128)(2,1)S(1)}, bf16[4,32,768]{2,1,0:T(8,128)(2,1)S(1)}, u32[]{:S(2)}, u32[]{:S(2)}) collective-permute-start(bf16[4,32,768]{2,1,0:T(8,128)(2,1)S(1)} %get-tuple-element.92), channel_id=1, source_target_pairs={{0,16},{4,20},{8,24},{12,28},{16,0},{20,4},{24,8},{28,12},{1,17},{... | collective-permute-start | bytes 589832 | tf_op jit(solution)/shard_map/ppermute | solution.py:516
  83.5 17.4 %collective-permute-start.19 = (bf16[4,32,768]{2,1,0:T(8,128)(2,1)S(1)}, bf16[4,32,768]{2,1,0:T(8,128)(2,1)S(1)}, u32[]{:S(2)}, u32[]{:S(2)}) collective-permute-start(bf16[4,32,768]{2,1,0:T(8,128)(2,1)S(1)} %get-tuple-element.93), channel_id=1, source_target_pairs={{0,24},{4,28},{8,16},{12,20},{16,8},{20,12},{24,0},{28,4},{1,25},{... | collective-permute-start | bytes 589832 | tf_op jit(solution)/shard_map/ppermute | solution.py:516
  101.1 28.9 %collective-permute-start.26 = (bf16[2,512,256]{2,1,0:T(8,128)(2,1)S(1)}, bf16[2,512,256]{2,1,0:T(8,128)(2,1)S(1)}, u32[]{:S(2)}, u32[]{:S(2)}) collective-permute-start(bf16[2,512,256]{2,1,0:T(8,128)(2,1)S(1)} %get-tuple-element.101), channel_id=1, source_target_pairs={{4,0},{8,4},{12,8},{16,12},{20,16},{24,20},{28,24},{5,1},{9,5},{13... | collective-permute-start | bytes 1572872 | tf_op jit(solution)/shard_map/ppermute | solution.py:402
  102.4 27.6 %collective-permute-start.27 = (bf16[2,512,256]{2,1,0:T(8,128)(2,1)S(1)}, bf16[2,512,256]{2,1,0:T(8,128)(2,1)S(1)}, u32[]{:S(2)}, u32[]{:S(2)}) collective-permute-start(bf16[2,512,256]{2,1,0:T(8,128)(2,1)S(1)} %get-tuple-element.101), channel_id=1, source_target_pairs={{0,4},{4,8},{8,12},{12,16},{16,20},{20,24},{24,28},{1,5},{5,9},{9,... | collective-permute-start | bytes 1572872 | tf_op jit(solution)/shard_map/ppermute | solution.py:402
  105.4 4.5 %collective-permute-start.20 = (bf16[32,768]{1,0:T(8,128)(2,1)S(1)}, bf16[32,768]{1,0:T(8,128)(2,1)S(1)}, u32[]{:S(2)}, u32[]{:S(2)}) collective-permute-start(bf16[32,768]{1,0:T(8,128)(2,1)S(1)} %get-tuple-element.97), channel_id=1, source_target_pairs={{0,1},{1,0},{2,3},{3,2},{4,5},{5,4},{6,7},{7,6},{8,9},{9,8},{10,11... | collective-permute-start | bytes 147464 | tf_op jit(solution)/shard_map/ppermute | solution.py:528
  106.9 5.5 %collective-permute-start.21 = (bf16[32,768]{1,0:T(8,128)(2,1)S(1)}, bf16[32,768]{1,0:T(8,128)(2,1)S(1)}, u32[]{:S(2)}, u32[]{:S(2)}) collective-permute-start(bf16[32,768]{1,0:T(8,128)(2,1)S(1)} %get-tuple-element.98), channel_id=1, source_target_pairs={{0,2},{1,3},{2,0},{3,1},{4,6},{5,7},{6,4},{7,5},{8,10},{9,11},{10,... | collective-permute-start | bytes 147464 | tf_op jit(solution)/shard_map/ppermute | solution.py:528
  108.5 6.0 %collective-permute-start.22 = (bf16[32,768]{1,0:T(8,128)(2,1)S(1)}, bf16[32,768]{1,0:T(8,128)(2,1)S(1)}, u32[]{:S(2)}, u32[]{:S(2)}) collective-permute-start(bf16[32,768]{1,0:T(8,128)(2,1)S(1)} %get-tuple-element.99), channel_id=1, source_target_pairs={{0,3},{1,2},{2,1},{3,0},{4,7},{5,6},{6,5},{7,4},{8,11},{9,10},{10,... | collective-permute-start | bytes 147464 | tf_op jit(solution)/shard_map/ppermute | solution.py:528
  114.5 4.6 %collective-permute-start.23 = (bf16[32,768]{1,0:T(8,128)(2,1)S(1)}, bf16[32,768]{1,0:T(8,128)(2,1)S(1)}, u32[]{:S(2)}, u32[]{:S(2)}) collective-permute-start(bf16[32,768]{1,0:T(8,128)(2,1)S(1)} %line_sum.1.refs_0_), channel_id=1, source_target_pairs={{0,1},{1,0},{2,3},{3,2},{4,5},{5,4},{6,7},{7,6},{8,9},{9,8},{10,11... | collective-permute-start | bytes 147464 | tf_op jit(solution)/shard_map/ppermute | solution.py:534
  115.3 7.1 %collective-permute-start.24 = (bf16[32,768]{1,0:T(8,128)(2,1)S(1)}, bf16[32,768]{1,0:T(8,128)(2,1)S(1)}, u32[]{:S(2)}, u32[]{:S(2)}) collective-permute-start(bf16[32,768]{1,0:T(8,128)(2,1)S(1)} %line_sum.1.refs_0_), channel_id=1, source_target_pairs={{0,2},{1,3},{2,0},{3,1},{4,6},{5,7},{6,4},{7,5},{8,10},{9,11},{10,... | collective-permute-start | bytes 147464 | tf_op jit(solution)/shard_map/ppermute | solution.py:534
  117.0 5.9 %collective-permute-start.25 = (bf16[32,768]{1,0:T(8,128)(2,1)S(1)}, bf16[32,768]{1,0:T(8,128)(2,1)S(1)}, u32[]{:S(2)}, u32[]{:S(2)}) collective-permute-start(bf16[32,768]{1,0:T(8,128)(2,1)S(1)} %line_sum.1.refs_0_), channel_id=1, source_target_pairs={{0,3},{1,2},{2,1},{3,0},{4,7},{5,6},{6,5},{7,4},{8,11},{9,10},{10,... | collective-permute-start | bytes 147464 | tf_op jit(solution)/shard_map/ppermute | solution.py:534
  123.0 12.1 %collective-permute-start.28 = (bf16[4,32,768]{2,1,0:T(8,128)(2,1)S(1)}, bf16[4,32,768]{2,1,0:T(8,128)(2,1)S(1)}, u32[]{:S(2)}, u32[]{:S(2)}) collective-permute-start(bf16[4,32,768]{2,1,0:T(8,128)(2,1)S(1)} %line_place.1.refs_0_), channel_id=1, source_target_pairs={{0,8},{4,12},{8,0},{12,4},{16,24},{20,28},{24,16},{28,20},{1,9},{5... | collective-permute-start | bytes 589832 | tf_op jit(solution)/shard_map/ppermute | solution.py:538
  126.5 9.3 %collective-permute-start.29 = (bf16[4,32,768]{2,1,0:T(8,128)(2,1)S(1)}, bf16[4,32,768]{2,1,0:T(8,128)(2,1)S(1)}, u32[]{:S(2)}, u32[]{:S(2)}) collective-permute-start(bf16[4,32,768]{2,1,0:T(8,128)(2,1)S(1)} %line_place.1.refs_0_), channel_id=1, source_target_pairs={{0,16},{4,20},{8,24},{12,28},{16,0},{20,4},{24,8},{28,12},{1,17},{... | collective-permute-start | bytes 589832 | tf_op jit(solution)/shard_map/ppermute | solution.py:538
  128.5 8.7 %collective-permute-start.30 = (bf16[4,32,768]{2,1,0:T(8,128)(2,1)S(1)}, bf16[4,32,768]{2,1,0:T(8,128)(2,1)S(1)}, u32[]{:S(2)}, u32[]{:S(2)}) collective-permute-start(bf16[4,32,768]{2,1,0:T(8,128)(2,1)S(1)} %line_place.1.refs_0_), channel_id=1, source_target_pairs={{0,24},{4,28},{8,16},{12,20},{16,8},{20,12},{24,0},{28,4},{1,25},{... | collective-permute-start | bytes 589832 | tf_op jit(solution)/shard_map/ppermute | solution.py:538
  137.2 2.4 %collective-permute-start.31 = (bf16[4,4,32,768]{3,2,1,0:T(8,128)(2,1)S(1)}, bf16[4,4,32,768]{3,2,1,0:T(8,128)(2,1)S(1)}, u32[]{:S(2)}, u32[]{:S(2)}) collective-permute-start(bf16[4,4,32,768]{3,2,1,0:T(8,128)(2,1)S(1)} %plane_place.1.mine_ref), channel_id=1, source_target_pairs={{0,4},{4,0},{8,12},{12,8},{16,20},{20,16},{24,28},{28,24},{1,5},{5... | collective-permute-start | bytes 2359304 | tf_op jit(solution)/shard_map/ppermute | solution.py:550

commit v8 on v6

--- a/solution.py
+++ b/solution.py
@@ -455,7 +455,7 @@
         cot_corner.append(lax.ppermute(straight, "tm", [(3, 4), (4, 3)]))
     parts = spread_sums(sums, "space")
     if by_corner:
-        parts[0], relayed = lax.optimization_barrier((parts[0], relayed))
+        _, relayed = lax.optimization_barrier((sums, relayed))
         cot_corner.append(lax.ppermute(relayed, "tm", [(7, 4), (0, 3)]))
     x_turned = call(
         turn_kernel, "turned", [frames_in, above, below], shape((3 * channels, frames * pixels), BF16),

time: 130 us -> 129 us (level)
  waiting for transfers between devices: 34.6 us -> 33.2 us
    ppermute x1, waiting for transfers between devices: 6.16 us -> 0.01 us  [per_device(): cot_corner.append(lax.ppermute(relayed, 'tm', [(7, 4), (0, 3)]))]
    ppermute x1, waiting for transfers between devices: 0.01 us -> 2.57 us  [per_device(): relayed = lax.ppermute(relayed, 'tm', [(3, 7), (4, 0)])]
    ppermute x2, starting transfers between devices: 2.73 us -> 4.27 us  [spread_sums(): got = lax.ppermute(part, axis, [(i, i ^ step) for i in range(size)])]
  transfers between devices with their start and end apart: 32 -> 32, of which waited for: 14 -> 15; matrix products, arithmetic and copies ran while one was open for 1% -> 1% of each run, Pallas kernels for 29% -> 29%
where the time goes in v8:
time: 129 us
  starting transfers between devices  51.6 us (40%)
  Pallas kernels  39.8 us (31%)
  waiting for transfers between devices  33.2 us (26%)
  local copies, waits for them, and re-layouts  2.8 us (2%)
    pallas_call x17, Pallas kernels, call(): pl.pallas_call(kernel, in_specs=[smem if x.dtype == jnp.int32 else vmem f...  39.8 us
    ppermute x10, starting transfers between devices, neighbours(): return (lax.ppermute(high, axis, up), lax.ppermute(low, axis, down))  21 us
    ppermute x10, waiting for transfers between devices, neighbours(): return (lax.ppermute(high, axis, up), lax.ppermute(low, axis, down))  9.43 us
    ppermute x3, waiting for transfers between devices, per_device(): lax.ppermute(x, 'space', other_plane(s))  4.77 us
    ppermute x3, starting transfers between devices, per_device(): gots = [lax.ppermute(own, 'space', other_plane(s)) for s in range(1, n)]  4.45 us
    ppermute x3, starting transfers between devices, per_device(): lax.ppermute(x, 'space', other_plane(s))  4.45 us
    ppermute x2, starting transfers between devices, spread_sums(): got = lax.ppermute(part, axis, [(i, i ^ step) for i in range(size)])  4.27 us
    ppermute x3, starting transfers between devices, per_device(): gots = [lax.ppermute(own, 'tm', other_chip(s)) for s in range(1, chips)]  4.25 us
  transfers between devices with their start and end apart: 32, of which 15 were waited for; matrix products, arithmetic and copies ran while one was open for 1% of the time, Pallas kernels for 29%

profile of v8, /device:TPU:0, one launch (start us, length us, event | category | flops | bytes accessed | tf_op | source)
XLA Modules:
  0.0 128.5 jit_solution(9780073389551589443)
XLA Ops:
  0.6 1.1 fusion.1
  1.7 1.6 %collective-permute-start.4 = (bf16[8,512,256]{2,1,0:T(8,128)(2,1)}, bf16[8,512,256]{2,1,0:T(8,128)(2,1)S(1)}, u32[]{:S(2)}, u32[]{:S(2)}) collective-permute-start(bf16[8,512,256]{2,1,0:T(8,128)(2,1)} %bitcast.6), channel_id=1, source_target_pairs={{4,0},{8,4},{12,8},{20,16},{24,20},{28,24},{5,1},{9,5},{13,9},{21,... | collective-permute-start | bytes 6291464 | tf_op jit(solution)/shard_map/ppermute | solution.py:402
  3.3 3.2 %collective-permute-start.5 = (bf16[8,512,256]{2,1,0:T(8,128)(2,1)}, bf16[8,512,256]{2,1,0:T(8,128)(2,1)S(1)}, u32[]{:S(2)}, u32[]{:S(2)}) collective-permute-start(bf16[8,512,256]{2,1,0:T(8,128)(2,1)} %bitcast.7), channel_id=1, source_target_pairs={{0,4},{4,8},{8,12},{16,20},{20,24},{24,28},{1,5},{5,9},{9,13},{17,... | collective-permute-start | bytes 6291464 | tf_op jit(solution)/shard_map/ppermute | solution.py:402
  6.5 4.9 %collective-permute-start = (bf16[8,1,64,256]{3,2,1,0:T(8,128)(2,1)S(1)}, bf16[8,1,64,256]{3,2,1,0:T(8,128)(2,1)S(1)}, u32[]{:S(2)}, u32[]{:S(2)}) collective-permute-start(bf16[8,1,64,256]{3,2,1,0:T(8,128)(2,1)S(1)} %get-tuple-element.52), channel_id=1, source_target_pairs={{0,1},{1,2},{2,3},{4,5},{5,6},{6,7},{8,9},{9,10},{10,11},{12,13},{... | collective-permute-start | bytes 786440 | tf_op jit(solution)/shard_map/ppermute | solution.py:402
  11.4 1.3 %collective-permute-start.1 = (bf16[8,1,64,256]{3,2,1,0:T(8,128)(2,1)S(1)}, bf16[8,1,64,256]{3,2,1,0:T(8,128)(2,1)S(1)}, u32[]{:S(2)}, u32[]{:S(2)}) collective-permute-start(bf16[8,1,64,256]{3,2,1,0:T(8,128)(2,1)S(1)} %get-tuple-element.53), channel_id=1, source_target_pairs={{1,0},{2,1},{3,2},{5,4},{6,5},{7,6},{9,8},{10,9},{11,10},{13,12},{... | collective-permute-start | bytes 786440 | tf_op jit(solution)/shard_map/ppermute | solution.py:402
  12.7 1.7 %fusion = (bf16[4,8,64,256]{3,2,1,0:T(8,128)(2,1)S(1)}, bf16[4,8,64,256]{3,2,1,0:T(8,128)(2,1)S(1)}) fusion(bf16[8,8,64,256]{3,2,1,0:T(8,128)(2,1)} %cot_ref.1), kind=kLoop, calls=%fused_computation | loop fusion | bytes 4194304 | tf_op jit(solution)/shard_map/slice | solution.py:441
  14.4 1.4 %collective-permute-start.7 = (bf16[4,512,256]{2,1,0:T(8,128)(2,1)S(1)}, bf16[4,512,256]{2,1,0:T(8,128)(2,1)S(1)}, u32[]{:S(2)}, u32[]{:S(2)}) collective-permute-start(bf16[4,512,256]{2,1,0:T(8,128)(2,1)S(1)} %bitcast.13), channel_id=1, source_target_pairs={{12,28},{16,0},{13,29},{17,1},{14,30},{18,2},{15,31},{19,3}} | collective-permute-start | bytes 3145736 | tf_op jit(solution)/shard_map/ppermute | solution.py:442
  15.8 2.2 %collective-permute-done.above_ref = bf16[8,1,64,256]{3,2,1,0:T(8,128)(2,1)S(1)} collective-permute-done((bf16[8,1,64,256]{3,2,1,0:T(8,128)(2,1)S(1)}, bf16[8,1,64,256]{3,2,1,0:T(8,128)(2,1)S(1)}, u32[]{:S(2)}, u32[]{:S(2)}) %collective-permute-start) | collective-permute-done | bytes 262176 | tf_op jit(solution)/shard_map/ppermute | solution.py:402
  18.1 4.1 %collective-permute-done.1.below_ref = bf16[8,1,64,256]{3,2,1,0:T(8,128)(2,1)S(1)} collective-permute-done((bf16[8,1,64,256]{3,2,1,0:T(8,128)(2,1)S(1)}, bf16[8,1,64,256]{3,2,1,0:T(8,128)(2,1)S(1)}, u32[]{:S(2)}, u32[]{:S(2)}) %collective-permute-start.1) | collective-permute-done | bytes 262176 | tf_op jit(solution)/shard_map/ppermute | solution.py:402
  22.2 5.7 %conv_forward.1 = (f32[8,512,256]{2,1,0:T(8,128)S(1)}, f32[8,2,256]{2,1,0:T(2,128)S(1)}) custom-call(bf16[8,8,64,256]{3,2,1,0:T(8,128)(2,1)S(1)} %copy-done, bf16[8,1,64,256]{3,2,1,0:T(8,128)(2,1)S(1)} %collective-permute-done.above_ref, bf16[8,1,64,256]{3,2,1,0:T(8,128)(2,1)S(1)} %collective-permute-done.1.below_ref, bf16[3,3,256,256]{3,2,1,0:T(8,128)(2,1)S(1)} %copy-done.3), custom_call_target="tpu_custom_call" | custom-call | flops 26843545600 | bytes 8388608 | tf_op jit(solution)/shard_map/conv_forward/pallas_call | solution.py:20
  27.9 0.7 collective-permute-start.6
  28.7 2.6 %collective-permute-done.7 = bf16[4,512,256]{2,1,0:T(8,128)(2,1)S(1)} collective-permute-done((bf16[4,512,256]{2,1,0:T(8,128)(2,1)S(1)}, bf16[4,512,256]{2,1,0:T(8,128)(2,1)S(1)}, u32[]{:S(2)}, u32[]{:S(2)}) %collective-permute-start.7) | collective-permute-done | bytes 1048608 | tf_op jit(solution)/shard_map/ppermute | solution.py:442
  31.2 3.3 %collective-permute-start.8 = (bf16[4,512,256]{2,1,0:T(8,128)(2,1)S(1)}, bf16[4,512,256]{2,1,0:T(8,128)(2,1)S(1)}, u32[]{:S(2)}, u32[]{:S(2)}) collective-permute-start(bf16[4,512,256]{2,1,0:T(8,128)(2,1)S(1)} %collective-permute-done.7), channel_id=1, source_target_pairs={{28,16},{0,12},{29,17},{1,13},{30,18},{2,14},{31,19},{3,15}} | collective-permute-start | bytes 3145736 | tf_op jit(solution)/shard_map/ppermute | solution.py:459
  34.5 1.6 %collective-permute-start.2 = (f32[8,2,256]{2,1,0:T(2,128)S(1)}, f32[8,2,256]{2,1,0:T(2,128)S(1)}, u32[]{:S(2)}, u32[]{:S(2)}) collective-permute-start(f32[8,2,256]{2,1,0:T(2,128)S(1)} %get-tuple-element.55), channel_id=1, source_target_pairs={{0,1},{1,0},{2,3},{3,2},{4,5},{5,4},{6,7},{7,6},{8,9},{9,8},{10,11... | collective-permute-start | bytes 49160 | tf_op jit(solution)/shard_map/ppermute | solution.py:416
  36.2 2.2 %collective-permute-done.2 = f32[8,2,256]{2,1,0:T(2,128)S(1)} collective-permute-done((f32[8,2,256]{2,1,0:T(2,128)S(1)}, f32[8,2,256]{2,1,0:T(2,128)S(1)}, u32[]{:S(2)}, u32[]{:S(2)}) %collective-permute-start.2) | collective-permute-done | bytes 16416 | tf_op jit(solution)/shard_map/ppermute | solution.py:416
  38.4 2.6 %collective-permute-start.3 = (f32[8,2,256]{2,1,0:T(2,128)S(1)}, f32[8,2,256]{2,1,0:T(2,128)S(1)}, u32[]{:S(2)}, u32[]{:S(2)}) collective-permute-start(f32[8,2,256]{2,1,0:T(2,128)S(1)} %add.3.refs_0_), channel_id=1, source_target_pairs={{0,2},{1,3},{2,0},{3,1},{4,6},{5,7},{6,4},{7,5},{8,10},{9,11},{10,... | collective-permute-start | bytes 49160 | tf_op jit(solution)/shard_map/ppermute | solution.py:416
  41.0 0.5 turn_weights.1
  41.5 2.2 %turned.1.xt_ref = bf16[768,4096]{1,0:T(8,128)(2,1)S(1)} custom-call(bf16[8,8,64,256]{3,2,1,0:T(8,128)(2,1)S(1)} %copy-done, bf16[8,1,64,256]{3,2,1,0:T(8,128)(2,1)S(1)} %collective-permute-done.above_ref, bf16[8,1,64,256]{3,2,1,0:T(8,128)(2,1)S(1)} %collective-permute-done.1.below_ref), custom_call_target="tpu_custom_call" | custom-call | bytes 8388608 | tf_op jit(solution)/shard_map/turned/pallas_call | solution.py:20
  43.7 3.4 %activation.1 = (bf16[8,512,256]{2,1,0:T(8,128)(2,1)S(1)}, bf16[6,512,256]{2,1,0:T(8,128)(2,1)S(1)}, bf16[2,512,256]{2,1,0:T(8,128)(2,1)S(1)}, bf16[8,512,256]{2,1,0:T(8,128)(2,1)S(1)}, bf16[8,512,256]{2,1,0:T(8,128)(2,1)S(1)}) custom-call(s32[2]{0:T(128)S(1)} %copy-done.4, f32[8,2,256]{2,1,0:T(2,128)S(1)} %add.3.refs_0_, ...), custom_call_target="tpu_custom_call" | custom-call | flops 10485760 | bytes 10485760 | tf_op jit(solution)/shard_map/activation/pallas_call | solution.py:20
  47.1 1.4 %collective-permute-start.15 = (bf16[6,512,256]{2,1,0:T(8,128)(2,1)S(1)}, bf16[6,512,256]{2,1,0:T(8,128)(2,1)S(1)}, u32[]{:S(2)}, u32[]{:S(2)}) collective-permute-start(bf16[6,512,256]{2,1,0:T(8,128)(2,1)S(1)} %get-tuple-element.81), channel_id=1, source_target_pairs={{0,4},{4,8},{8,12},{12,16},{16,20},{20,24},{24,28},{1,5},{5,9},{9,... | collective-permute-start | bytes 4718600 | tf_op jit(solution)/shard_map/ppermute | solution.py:402
  48.5 1.3 %collective-permute-start.16 = (bf16[6,512,256]{2,1,0:T(8,128)(2,1)S(1)}, bf16[6,512,256]{2,1,0:T(8,128)(2,1)S(1)}, u32[]{:S(2)}, u32[]{:S(2)}) collective-permute-start(bf16[6,512,256]{2,1,0:T(8,128)(2,1)S(1)} %get-tuple-element.81), channel_id=1, source_target_pairs={{4,0},{8,4},{12,8},{16,12},{20,16},{24,20},{28,24},{5,1},{9,5},{13... | collective-permute-start | bytes 4718600 | tf_op jit(solution)/shard_map/ppermute | solution.py:402
  49.9 4.2 %grad_activation.1 = (bf16[8,512,256]{2,1,0:T(8,128)(2,1)S(1)}, bf16[4096,768]{1,0:T(8,128)(2,1)S(1)}, f32[8,2,256]{2,1,0:T(2,128)S(1)}) custom-call(s32[2]{0:T(128)S(1)} %copy-done.4, s32[2]{0:T(128)S(1)} %copy-done.5, bf16[8,512,256]{2,1,0:T(8,128)(2,1)S(1)} %bitcast.8, bf16[8,512,256]{2,1,0:T(8,128)(2,1)S(1)} %collective-permute-done.4.nxt, ...), custom_call_target="tpu_custom_call" | custom-call | flops 1610612736 | bytes 16777216 | tf_op jit(solution)/shard_map/grad_activation/pallas_call | solution.py:20
  54.1 2.7 %collective-permute-start.10 = (f32[8,2,256]{2,1,0:T(2,128)S(1)}, f32[8,2,256]{2,1,0:T(2,128)S(1)}, u32[]{:S(2)}, u32[]{:S(2)}) collective-permute-start(f32[8,2,256]{2,1,0:T(2,128)S(1)} %get-tuple-element.67.refs_2_), channel_id=1, source_target_pairs={{0,2},{1,3},{2,0},{3,1},{4,6},{5,7},{6,4},{7,5},{8,10},{9,11},{10,... | collective-permute-start | bytes 49160 | tf_op jit(solution)/shard_map/ppermute | solution.py:407
  56.7 1.3 %collective-permute-start.11 = (f32[8,2,256]{2,1,0:T(2,128)S(1)}, f32[8,2,256]{2,1,0:T(2,128)S(1)}, u32[]{:S(2)}, u32[]{:S(2)}) collective-permute-start(f32[8,2,256]{2,1,0:T(2,128)S(1)} %get-tuple-element.67.refs_2_), channel_id=1, source_target_pairs={{0,3},{1,2},{2,1},{3,0},{4,7},{5,6},{6,5},{7,4},{8,11},{9,10},{10,... | collective-permute-start | bytes 49160 | tf_op jit(solution)/shard_map/ppermute | solution.py:407
  58.1 0.1 collective-permute-start.9
  58.2 1.9 %temporal_grad.1.temporal_ref = f32[256,768]{1,0:T(8,128)S(1)} custom-call(bf16[8,512,256]{2,1,0:T(8,128)(2,1)S(1)} %get-tuple-element.69.act_ref.own, bf16[4096,768]{1,0:T(8,128)(2,1)S(1)} %get-tuple-element.70.cat_ref), custom_call_target="tpu_custom_call" | custom-call | flops 1610612736 | bytes 8388608 | tf_op jit(solution)/shard_map/temporal_grad/pallas_call | solution.py:20
  60.0 2.2 %collective-permute-done.11.refs_5_ = f32[8,2,256]{2,1,0:T(2,128)S(1)} collective-permute-done((f32[8,2,256]{2,1,0:T(2,128)S(1)}, f32[8,2,256]{2,1,0:T(2,128)S(1)}, u32[]{:S(2)}, u32[]{:S(2)}) %collective-permute-start.11) | collective-permute-done | bytes 16416 | tf_op jit(solution)/shard_map/ppermute | solution.py:407
  62.3 2.2 %norm_backward.1 = (bf16[8,512,256]{2,1,0:T(8,128)(2,1)S(1)}, bf16[8,1,64,256]{3,2,1,0:T(8,128)(2,1)S(1)}, bf16[8,1,64,256]{3,2,1,0:T(8,128)(2,1)S(1)}, bf16[4096,768]{1,0:T(8,128)(2,1)S(1)}) custom-call(bf16[8,512,256]{2,1,0:T(8,128)(2,1)S(1)} %get-tuple-element.60.refs_3_.normed_ref, bf16[8,512,256]{2,1,0:T(8,128)(2,1)S(1)} %get-tuple-element.61.refs_4_.slope_ref, ...), custom_call_target="tpu_custom_call" | custom-call | bytes 12582912 | tf_op jit(solution)/shard_map/norm_backward/pallas_call | solution.py:20
  64.5 1.7 %collective-permute-start.12 = (bf16[8,1,64,256]{3,2,1,0:T(8,128)(2,1)S(1)}, bf16[8,1,64,256]{3,2,1,0:T(8,128)(2,1)S(1)}, u32[]{:S(2)}, u32[]{:S(2)}) collective-permute-start(bf16[8,1,64,256]{3,2,1,0:T(8,128)(2,1)S(1)} %get-tuple-element.71), channel_id=1, source_target_pairs={{0,1},{1,2},{2,3},{4,5},{5,6},{6,7},{8,9},{9,10},{10,11},{12,13},{... | collective-permute-start | bytes 786440 | tf_op jit(solution)/shard_map/ppermute | solution.py:402
  66.2 1.3 %collective-permute-start.13 = (bf16[8,1,64,256]{3,2,1,0:T(8,128)(2,1)S(1)}, bf16[8,1,64,256]{3,2,1,0:T(8,128)(2,1)S(1)}, u32[]{:S(2)}, u32[]{:S(2)}) collective-permute-start(bf16[8,1,64,256]{3,2,1,0:T(8,128)(2,1)S(1)} %get-tuple-element.72), channel_id=1, source_target_pairs={{1,0},{2,1},{3,2},{5,4},{6,5},{7,6},{9,8},{10,9},{11,10},{13,12},{... | collective-permute-start | bytes 786440 | tf_op jit(solution)/shard_map/ppermute | solution.py:402
  67.5 5.1 %weight_grad.1.acc_ref = f32[1024,768]{1,0:T(8,128)S(1)} custom-call(bf16[768,4096]{1,0:T(8,128)(2,1)S(1)} %turned.1.xt_ref, bf16[4096,768]{1,0:T(8,128)(2,1)S(1)} %get-tuple-element.68.moved_ref, f32[256,768]{1,0:T(8,128)S(1)} %temporal_grad.1.temporal_ref), custom_call_target="tpu_custom_call" | custom-call | flops 4831838208 | bytes 12582912 | tf_op jit(solution)/shard_map/weight_grad/pallas_call | solution.py:20
  72.6 3.0 %collective-permute-done.13.below_ref = bf16[8,1,64,256]{3,2,1,0:T(8,128)(2,1)S(1)} collective-permute-done((bf16[8,1,64,256]{3,2,1,0:T(8,128)(2,1)S(1)}, bf16[8,1,64,256]{3,2,1,0:T(8,128)(2,1)S(1)}, u32[]{:S(2)}, u32[]{:S(2)}) %collective-permute-start.13) | collective-permute-done | bytes 262176 | tf_op jit(solution)/shard_map/ppermute | solution.py:402
  75.6 0.4 hand_out.1
  76.0 0.1 collective-permute-start.14
  76.1 2.3 %collective-permute-done.14.got_ref = bf16[4,4,32,768]{3,2,1,0:T(8,128)(2,1)S(1)} collective-permute-done((bf16[4,4,32,768]{3,2,1,0:T(8,128)(2,1)S(1)}, bf16[4,4,32,768]{3,2,1,0:T(8,128)(2,1)S(1)}, u32[]{:S(2)}, u32[]{:S(2)}) %collective-permute-start.14) | collective-permute-done | bytes 786464 | tf_op jit(solution)/shard_map/ppermute | solution.py:510
  78.4 0.2 core_sum.1
  78.5 0.1 collective-permute-start.17
  78.6 1.6 %collective-permute-start.18 = (bf16[4,32,768]{2,1,0:T(8,128)(2,1)S(1)}, bf16[4,32,768]{2,1,0:T(8,128)(2,1)S(1)}, u32[]{:S(2)}, u32[]{:S(2)}) collective-permute-start(bf16[4,32,768]{2,1,0:T(8,128)(2,1)S(1)} %get-tuple-element.84), channel_id=1, source_target_pairs={{0,16},{4,20},{8,24},{12,28},{16,0},{20,4},{24,8},{28,12},{1,17},{... | collective-permute-start | bytes 589832 | tf_op jit(solution)/shard_map/ppermute | solution.py:515
  80.2 1.9 %collective-permute-start.19 = (bf16[4,32,768]{2,1,0:T(8,128)(2,1)S(1)}, bf16[4,32,768]{2,1,0:T(8,128)(2,1)S(1)}, u32[]{:S(2)}, u32[]{:S(2)}) collective-permute-start(bf16[4,32,768]{2,1,0:T(8,128)(2,1)S(1)} %get-tuple-element.85), channel_id=1, source_target_pairs={{0,24},{4,28},{8,16},{12,20},{16,8},{20,12},{24,0},{28,4},{1,25},{... | collective-permute-start | bytes 589832 | tf_op jit(solution)/shard_map/ppermute | solution.py:515
  82.1 7.0 %conv_backward.1 = bf16[8,8,64,256]{3,2,1,0:T(8,128)(2,1)} custom-call(bf16[8,512,256]{2,1,0:T(8,128)(2,1)S(1)} %get-tuple-element.77.g_ref, bf16[8,1,64,256]{3,2,1,0:T(8,128)(2,1)S(1)} %collective-permute-done.12.above_ref, bf16[8,1,64,256]{3,2,1,0:T(8,128)(2,1)S(1)} %collective-permute-done.13.below_ref, bf16[8,8,64,256]{3,2,1,0:T(8,128)(2,1)S(1)} %copy-done.1, ...), custom_call_target="tpu_custom_call" | custom-call | flops 4831838208 | bytes 8388608 | tf_op jit(solution)/shard_map/conv_backward/pallas_call | solution.py:20
  89.1 1.3 %collective-permute-done.19.refs_2_ = bf16[4,32,768]{2,1,0:T(8,128)(2,1)S(1)} collective-permute-done((bf16[4,32,768]{2,1,0:T(8,128)(2,1)S(1)}, bf16[4,32,768]{2,1,0:T(8,128)(2,1)S(1)}, u32[]{:S(2)}, u32[]{:S(2)}) %collective-permute-start.19) | collective-permute-done | bytes 196640 | tf_op jit(solution)/shard_map/ppermute | solution.py:515
  90.4 0.1 plane_sum.1
  90.5 1.3 %collective-permute-start.26 = (bf16[2,512,256]{2,1,0:T(8,128)(2,1)S(1)}, bf16[2,512,256]{2,1,0:T(8,128)(2,1)S(1)}, u32[]{:S(2)}, u32[]{:S(2)}) collective-permute-start(bf16[2,512,256]{2,1,0:T(8,128)(2,1)S(1)} %get-tuple-element.93), channel_id=1, source_target_pairs={{4,0},{8,4},{12,8},{16,12},{20,16},{24,20},{28,24},{5,1},{9,5},{13... | collective-permute-start | bytes 1572872 | tf_op jit(solution)/shard_map/ppermute | solution.py:402
  91.8 3.1 %collective-permute-start.27 = (bf16[2,512,256]{2,1,0:T(8,128)(2,1)S(1)}, bf16[2,512,256]{2,1,0:T(8,128)(2,1)S(1)}, u32[]{:S(2)}, u32[]{:S(2)}) collective-permute-start(bf16[2,512,256]{2,1,0:T(8,128)(2,1)S(1)} %get-tuple-element.93), channel_id=1, source_target_pairs={{0,4},{4,8},{8,12},{12,16},{16,20},{20,24},{24,28},{1,5},{5,9},{9,... | collective-permute-start | bytes 1572872 | tf_op jit(solution)/shard_map/ppermute | solution.py:402
  94.9 1.5 %collective-permute-start.20 = (bf16[32,768]{1,0:T(8,128)(2,1)S(1)}, bf16[32,768]{1,0:T(8,128)(2,1)S(1)}, u32[]{:S(2)}, u32[]{:S(2)}) collective-permute-start(bf16[32,768]{1,0:T(8,128)(2,1)S(1)} %get-tuple-element.89), channel_id=1, source_target_pairs={{0,1},{1,0},{2,3},{3,2},{4,5},{5,4},{6,7},{7,6},{8,9},{9,8},{10,11... | collective-permute-start | bytes 147464 | tf_op jit(solution)/shard_map/ppermute | solution.py:527
  96.4 1.7 %collective-permute-start.21 = (bf16[32,768]{1,0:T(8,128)(2,1)S(1)}, bf16[32,768]{1,0:T(8,128)(2,1)S(1)}, u32[]{:S(2)}, u32[]{:S(2)}) collective-permute-start(bf16[32,768]{1,0:T(8,128)(2,1)S(1)} %get-tuple-element.90), channel_id=1, source_target_pairs={{0,2},{1,3},{2,0},{3,1},{4,6},{5,7},{6,4},{7,5},{8,10},{9,11},{10,... | collective-permute-start | bytes 147464 | tf_op jit(solution)/shard_map/ppermute | solution.py:527
  98.1 1.2 collective-permute-start.22
  99.3 0.1 collective-permute-done.20.refs_0_
  99.5 3.9 %collective-permute-done.21.refs_1_ = bf16[32,768]{1,0:T(8,128)(2,1)S(1)} collective-permute-done((bf16[32,768]{1,0:T(8,128)(2,1)S(1)}, bf16[32,768]{1,0:T(8,128)(2,1)S(1)}, u32[]{:S(2)}, u32[]{:S(2)}) %collective-permute-start.21) | collective-permute-done | bytes 49184 | tf_op jit(solution)/shard_map/ppermute | solution.py:527
  103.4 0.7 collective-permute-done.22.refs_2_
  104.1 1.2 collective-permute-start.23
  105.3 1.4 %collective-permute-start.24 = (bf16[32,768]{1,0:T(8,128)(2,1)S(1)}, bf16[32,768]{1,0:T(8,128)(2,1)S(1)}, u32[]{:S(2)}, u32[]{:S(2)}) collective-permute-start(bf16[32,768]{1,0:T(8,128)(2,1)S(1)} %line_sum.1.refs_0_), channel_id=1, source_target_pairs={{0,2},{1,3},{2,0},{3,1},{4,6},{5,7},{6,4},{7,5},{8,10},{9,11},{10,... | collective-permute-start | bytes 147464 | tf_op jit(solution)/shard_map/ppermute | solution.py:533
  106.6 1.9 %collective-permute-start.25 = (bf16[32,768]{1,0:T(8,128)(2,1)S(1)}, bf16[32,768]{1,0:T(8,128)(2,1)S(1)}, u32[]{:S(2)}, u32[]{:S(2)}) collective-permute-start(bf16[32,768]{1,0:T(8,128)(2,1)S(1)} %line_sum.1.refs_0_), channel_id=1, source_target_pairs={{0,3},{1,2},{2,1},{3,0},{4,7},{5,6},{6,5},{7,4},{8,11},{9,10},{10,... | collective-permute-start | bytes 147464 | tf_op jit(solution)/shard_map/ppermute | solution.py:533
  108.6 2.9 %collective-permute-done.24.refs_2_ = bf16[32,768]{1,0:T(8,128)(2,1)S(1)} collective-permute-done((bf16[32,768]{1,0:T(8,128)(2,1)S(1)}, bf16[32,768]{1,0:T(8,128)(2,1)S(1)}, u32[]{:S(2)}, u32[]{:S(2)}) %collective-permute-start.24) | collective-permute-done | bytes 49184 | tf_op jit(solution)/shard_map/ppermute | solution.py:533
  111.5 1.1 collective-permute-done.25.refs_3_
  112.6 1.2 collective-permute-start.28
  113.7 2.0 %collective-permute-start.29 = (bf16[4,32,768]{2,1,0:T(8,128)(2,1)S(1)}, bf16[4,32,768]{2,1,0:T(8,128)(2,1)S(1)}, u32[]{:S(2)}, u32[]{:S(2)}) collective-permute-start(bf16[4,32,768]{2,1,0:T(8,128)(2,1)S(1)} %line_place.1.refs_0_), channel_id=1, source_target_pairs={{0,16},{4,20},{8,24},{12,28},{16,0},{20,4},{24,8},{28,12},{1,17},{... | collective-permute-start | bytes 589832 | tf_op jit(solution)/shard_map/ppermute | solution.py:537
  115.7 1.1 collective-permute-start.30
  116.8 5.2 %temporal_forward.1 = bf16[8,8,64,256]{3,2,1,0:T(8,128)(2,1)} custom-call(s32[2]{0:T(128)S(1)} %copy-done.4, s32[2]{0:T(128)S(1)} %copy-done.5, bf16[8,512,256]{2,1,0:T(8,128)(2,1)S(1)} %get-tuple-element.69.act_ref.own, bf16[6,512,256]{2,1,0:T(8,128)(2,1)S(1)} %collective-permute-done.16.nxt_a, bf16[2,512,256]{2,1,0:T(8,128)(2,1)S(1)} %collective-permute-done.26.nxt_b, ...), custom_call_target="tpu_custom_call" | custom-call | flops 1610612736 | bytes 10485760 | tf_op jit(solution)/shard_map/temporal_forward/pallas_call | solution.py:20
  122.0 2.2 %collective-permute-done.29.refs_2_ = bf16[4,32,768]{2,1,0:T(8,128)(2,1)S(1)} collective-permute-done((bf16[4,32,768]{2,1,0:T(8,128)(2,1)S(1)}, bf16[4,32,768]{2,1,0:T(8,128)(2,1)S(1)}, u32[]{:S(2)}, u32[]{:S(2)}) %collective-permute-start.29) | collective-permute-done | bytes 196640 | tf_op jit(solution)/shard_map/ppermute | solution.py:537
  124.2 0.1 plane_place.1.mine_ref
  124.3 0.1 collective-permute-start.31
  124.4 2.3 %collective-permute-done.31.got_ref = bf16[4,4,32,768]{3,2,1,0:T(8,128)(2,1)S(1)} collective-permute-done((bf16[4,4,32,768]{3,2,1,0:T(8,128)(2,1)S(1)}, bf16[4,4,32,768]{3,2,1,0:T(8,128)(2,1)S(1)}, u32[]{:S(2)}, u32[]{:S(2)}) %collective-permute-start.31) | collective-permute-done | bytes 786464 | tf_op jit(solution)/shard_map/ppermute | solution.py:549
  126.6 1.9 %finish.1 = (f32[3,3,256,256]{3,2,1,0:T(8,128)}, f32[3,256,256]{2,1,0:T(8,128)}) custom-call(bf16[4,4,32,768]{3,2,1,0:T(8,128)(2,1)S(1)} %plane_place.1.mine_ref, bf16[4,4,32,768]{3,2,1,0:T(8,128)(2,1)S(1)} %collective-permute-done.31.got_ref), custom_call_target="tpu_custom_call" | custom-call | bytes 4194304 | tf_op jit(solution)/shard_map/finish/pallas_call | solution.py:20
  (36 shorter events, 0.2 us)
Async XLA Ops:
  1.7 20.5 %copy-start = (bf16[8,8,64,256]{3,2,1,0:T(8,128)(2,1)S(1)}, bf16[8,8,64,256]{3,2,1,0:T(8,128)(2,1)}, u32[]{:S(2)}) copy-start(bf16[8,8,64,256]{3,2,1,0:T(8,128)(2,1)} %x_ref.5) | copy-start | bytes 6291460
  1.7 20.5 %copy-start.3 = (bf16[3,3,256,256]{3,2,1,0:T(8,128)(2,1)S(1)}, bf16[3,3,256,256]{3,2,1,0:T(8,128)(2,1)}, u32[]{:S(2)}) copy-start(bf16[3,3,256,256]{3,2,1,0:T(8,128)(2,1)} %spatial_ref.1) | copy-start | bytes 3538948
  1.7 48.1 %collective-permute-start.4 = (bf16[8,512,256]{2,1,0:T(8,128)(2,1)}, bf16[8,512,256]{2,1,0:T(8,128)(2,1)S(1)}, u32[]{:S(2)}, u32[]{:S(2)}) collective-permute-start(bf16[8,512,256]{2,1,0:T(8,128)(2,1)} %bitcast.6), channel_id=1, source_target_pairs={{4,0},{8,4},{12,8},{20,16},{24,20},{28,24},{5,1},{9,5},{13,9},{21,... | collective-permute-start | bytes 6291464 | tf_op jit(solution)/shard_map/ppermute | solution.py:402
  3.3 46.5 %collective-permute-start.5 = (bf16[8,512,256]{2,1,0:T(8,128)(2,1)}, bf16[8,512,256]{2,1,0:T(8,128)(2,1)S(1)}, u32[]{:S(2)}, u32[]{:S(2)}) collective-permute-start(bf16[8,512,256]{2,1,0:T(8,128)(2,1)} %bitcast.7), channel_id=1, source_target_pairs={{0,4},{4,8},{8,12},{16,20},{20,24},{24,28},{1,5},{5,9},{9,13},{17,... | collective-permute-start | bytes 6291464 | tf_op jit(solution)/shard_map/ppermute | solution.py:402
  6.5 11.6 %collective-permute-start = (bf16[8,1,64,256]{3,2,1,0:T(8,128)(2,1)S(1)}, bf16[8,1,64,256]{3,2,1,0:T(8,128)(2,1)S(1)}, u32[]{:S(2)}, u32[]{:S(2)}) collective-permute-start(bf16[8,1,64,256]{3,2,1,0:T(8,128)(2,1)S(1)} %get-tuple-element.52), channel_id=1, source_target_pairs={{0,1},{1,2},{2,3},{4,5},{5,6},{6,7},{8,9},{9,10},{10,11},{12,13},{... | collective-permute-start | bytes 786440 | tf_op jit(solution)/shard_map/ppermute | solution.py:402
  11.4 10.8 %collective-permute-start.1 = (bf16[8,1,64,256]{3,2,1,0:T(8,128)(2,1)S(1)}, bf16[8,1,64,256]{3,2,1,0:T(8,128)(2,1)S(1)}, u32[]{:S(2)}, u32[]{:S(2)}) collective-permute-start(bf16[8,1,64,256]{3,2,1,0:T(8,128)(2,1)S(1)} %get-tuple-element.53), channel_id=1, source_target_pairs={{1,0},{2,1},{3,2},{5,4},{6,5},{7,6},{9,8},{10,9},{11,10},{13,12},{... | collective-permute-start | bytes 786440 | tf_op jit(solution)/shard_map/ppermute | solution.py:402
  14.4 26.6 %copy-start.2 = (bf16[3,256,256]{2,1,0:T(8,128)(2,1)S(1)}, bf16[3,256,256]{2,1,0:T(8,128)(2,1)}, u32[]{:S(2)}) copy-start(bf16[3,256,256]{2,1,0:T(8,128)(2,1)} %temporal_ref.1) | copy-start | bytes 1179652
  14.4 16.8 %collective-permute-start.7 = (bf16[4,512,256]{2,1,0:T(8,128)(2,1)S(1)}, bf16[4,512,256]{2,1,0:T(8,128)(2,1)S(1)}, u32[]{:S(2)}, u32[]{:S(2)}) collective-permute-start(bf16[4,512,256]{2,1,0:T(8,128)(2,1)S(1)} %bitcast.13), channel_id=1, source_target_pairs={{12,28},{16,0},{13,29},{17,1},{14,30},{18,2},{15,31},{19,3}} | collective-permute-start | bytes 3145736 | tf_op jit(solution)/shard_map/ppermute | solution.py:442
  27.9 20.6 %collective-permute-start.6 = (bf16[4,512,256]{2,1,0:T(8,128)(2,1)S(1)}, bf16[4,512,256]{2,1,0:T(8,128)(2,1)S(1)}, u32[]{:S(2)}, u32[]{:S(2)}) collective-permute-start(bf16[4,512,256]{2,1,0:T(8,128)(2,1)S(1)} %bitcast.12), channel_id=1, source_target_pairs={{12,16},{16,12},{13,17},{17,13},{14,18},{18,14},{15,19},{19,15}} | collective-permute-start | bytes 3145736 | tf_op jit(solution)/shard_map/ppermute | solution.py:455
  31.2 18.6 %collective-permute-start.8 = (bf16[4,512,256]{2,1,0:T(8,128)(2,1)S(1)}, bf16[4,512,256]{2,1,0:T(8,128)(2,1)S(1)}, u32[]{:S(2)}, u32[]{:S(2)}) collective-permute-start(bf16[4,512,256]{2,1,0:T(8,128)(2,1)S(1)} %collective-permute-done.7), channel_id=1, source_target_pairs={{28,16},{0,12},{29,17},{1,13},{30,18},{2,14},{31,19},{3,15}} | collective-permute-start | bytes 3145736 | tf_op jit(solution)/shard_map/ppermute | solution.py:459
  34.5 3.8 %collective-permute-start.2 = (f32[8,2,256]{2,1,0:T(2,128)S(1)}, f32[8,2,256]{2,1,0:T(2,128)S(1)}, u32[]{:S(2)}, u32[]{:S(2)}) collective-permute-start(f32[8,2,256]{2,1,0:T(2,128)S(1)} %get-tuple-element.55), channel_id=1, source_target_pairs={{0,1},{1,0},{2,3},{3,2},{4,5},{5,4},{6,7},{7,6},{8,9},{9,8},{10,11... | collective-permute-start | bytes 49160 | tf_op jit(solution)/shard_map/ppermute | solution.py:416
  38.4 5.3 %collective-permute-start.3 = (f32[8,2,256]{2,1,0:T(2,128)S(1)}, f32[8,2,256]{2,1,0:T(2,128)S(1)}, u32[]{:S(2)}, u32[]{:S(2)}) collective-permute-start(f32[8,2,256]{2,1,0:T(2,128)S(1)} %add.3.refs_0_), channel_id=1, source_target_pairs={{0,2},{1,3},{2,0},{3,1},{4,6},{5,7},{6,4},{7,5},{8,10},{9,11},{10,... | collective-permute-start | bytes 49160 | tf_op jit(solution)/shard_map/ppermute | solution.py:416
  41.5 2.2 %copy-start.4 = (s32[2]{0:T(128)S(1)}, s32[2]{0:T(128)}, u32[]{:S(2)}) copy-start(s32[2]{0:T(128)} %clip_ref.5) | copy-start | bytes 28
  41.5 2.2 %copy-start.6 = (f32[256]{0:T(256)S(1)}, f32[256]{0:T(256)}, u32[]{:S(2)}) copy-start(f32[256]{0:T(256)} %param.12) | copy-start | bytes 3076
  41.5 2.2 %copy-start.7 = (f32[256]{0:T(256)S(1)}, f32[256]{0:T(256)}, u32[]{:S(2)}) copy-start(f32[256]{0:T(256)} %param.13) | copy-start | bytes 3076
  43.7 6.1 %copy-start.1 = (bf16[8,8,64,256]{3,2,1,0:T(8,128)(2,1)S(1)}, bf16[8,8,64,256]{3,2,1,0:T(8,128)(2,1)}, u32[]{:S(2)}) copy-start(bf16[8,8,64,256]{3,2,1,0:T(8,128)(2,1)} %cot_ref.1) | copy-start | bytes 6291460
  43.7 6.1 %copy-start.5 = (s32[2]{0:T(128)S(1)}, s32[2]{0:T(128)}, u32[]{:S(2)}) copy-start(s32[2]{0:T(128)} %dil_ref.3) | copy-start | bytes 28
  47.1 42.0 %collective-permute-start.15 = (bf16[6,512,256]{2,1,0:T(8,128)(2,1)S(1)}, bf16[6,512,256]{2,1,0:T(8,128)(2,1)S(1)}, u32[]{:S(2)}, u32[]{:S(2)}) collective-permute-start(bf16[6,512,256]{2,1,0:T(8,128)(2,1)S(1)} %get-tuple-element.81), channel_id=1, source_target_pairs={{0,4},{4,8},{8,12},{12,16},{16,20},{20,24},{24,28},{1,5},{5,9},{9,... | collective-permute-start | bytes 4718600 | tf_op jit(solution)/shard_map/ppermute | solution.py:402
  48.5 40.6 %collective-permute-start.16 = (bf16[6,512,256]{2,1,0:T(8,128)(2,1)S(1)}, bf16[6,512,256]{2,1,0:T(8,128)(2,1)S(1)}, u32[]{:S(2)}, u32[]{:S(2)}) collective-permute-start(bf16[6,512,256]{2,1,0:T(8,128)(2,1)S(1)} %get-tuple-element.81), channel_id=1, source_target_pairs={{4,0},{8,4},{12,8},{16,12},{20,16},{24,20},{28,24},{5,1},{9,5},{13... | collective-permute-start | bytes 4718600 | tf_op jit(solution)/shard_map/ppermute | solution.py:402
  54.1 6.0 %collective-permute-start.10 = (f32[8,2,256]{2,1,0:T(2,128)S(1)}, f32[8,2,256]{2,1,0:T(2,128)S(1)}, u32[]{:S(2)}, u32[]{:S(2)}) collective-permute-start(f32[8,2,256]{2,1,0:T(2,128)S(1)} %get-tuple-element.67.refs_2_), channel_id=1, source_target_pairs={{0,2},{1,3},{2,0},{3,1},{4,6},{5,7},{6,4},{7,5},{8,10},{9,11},{10,... | collective-permute-start | bytes 49160 | tf_op jit(solution)/shard_map/ppermute | solution.py:407
  56.7 5.5 %collective-permute-start.11 = (f32[8,2,256]{2,1,0:T(2,128)S(1)}, f32[8,2,256]{2,1,0:T(2,128)S(1)}, u32[]{:S(2)}, u32[]{:S(2)}) collective-permute-start(f32[8,2,256]{2,1,0:T(2,128)S(1)} %get-tuple-element.67.refs_2_), channel_id=1, source_target_pairs={{0,3},{1,2},{2,1},{3,0},{4,7},{5,6},{6,5},{7,4},{8,11},{9,10},{10,... | collective-permute-start | bytes 49160 | tf_op jit(solution)/shard_map/ppermute | solution.py:407
  58.1 4.2 %collective-permute-start.9 = (f32[8,2,256]{2,1,0:T(2,128)S(1)}, f32[8,2,256]{2,1,0:T(2,128)S(1)}, u32[]{:S(2)}, u32[]{:S(2)}) collective-permute-start(f32[8,2,256]{2,1,0:T(2,128)S(1)} %get-tuple-element.67.refs_2_), channel_id=1, source_target_pairs={{0,1},{1,0},{2,3},{3,2},{4,5},{5,4},{6,7},{7,6},{8,9},{9,8},{10,11... | collective-permute-start | bytes 49160 | tf_op jit(solution)/shard_map/ppermute | solution.py:407
  64.5 8.1 %collective-permute-start.12 = (bf16[8,1,64,256]{3,2,1,0:T(8,128)(2,1)S(1)}, bf16[8,1,64,256]{3,2,1,0:T(8,128)(2,1)S(1)}, u32[]{:S(2)}, u32[]{:S(2)}) collective-permute-start(bf16[8,1,64,256]{3,2,1,0:T(8,128)(2,1)S(1)} %get-tuple-element.71), channel_id=1, source_target_pairs={{0,1},{1,2},{2,3},{4,5},{5,6},{6,7},{8,9},{9,10},{10,11},{12,13},{... | collective-permute-start | bytes 786440 | tf_op jit(solution)/shard_map/ppermute | solution.py:402
  66.2 9.5 %collective-permute-start.13 = (bf16[8,1,64,256]{3,2,1,0:T(8,128)(2,1)S(1)}, bf16[8,1,64,256]{3,2,1,0:T(8,128)(2,1)S(1)}, u32[]{:S(2)}, u32[]{:S(2)}) collective-permute-start(bf16[8,1,64,256]{3,2,1,0:T(8,128)(2,1)S(1)} %get-tuple-element.72), channel_id=1, source_target_pairs={{1,0},{2,1},{3,2},{5,4},{6,5},{7,6},{9,8},{10,9},{11,10},{13,12},{... | collective-permute-start | bytes 786440 | tf_op jit(solution)/shard_map/ppermute | solution.py:402
  76.0 2.4 %collective-permute-start.14 = (bf16[4,4,32,768]{3,2,1,0:T(8,128)(2,1)S(1)}, bf16[4,4,32,768]{3,2,1,0:T(8,128)(2,1)S(1)}, u32[]{:S(2)}, u32[]{:S(2)}) collective-permute-start(bf16[4,4,32,768]{3,2,1,0:T(8,128)(2,1)S(1)} %get-tuple-element.75), channel_id=1, source_target_pairs={{0,4},{4,0},{8,12},{12,8},{16,20},{20,16},{24,28},{28,24},{1,5},{5... | collective-permute-start | bytes 2359304 | tf_op jit(solution)/shard_map/ppermute | solution.py:510
  78.5 10.6 %collective-permute-start.17 = (bf16[4,32,768]{2,1,0:T(8,128)(2,1)S(1)}, bf16[4,32,768]{2,1,0:T(8,128)(2,1)S(1)}, u32[]{:S(2)}, u32[]{:S(2)}) collective-permute-start(bf16[4,32,768]{2,1,0:T(8,128)(2,1)S(1)} %get-tuple-element.83), channel_id=1, source_target_pairs={{0,8},{4,12},{8,0},{12,4},{16,24},{20,28},{24,16},{28,20},{1,9},{5... | collective-permute-start | bytes 589832 | tf_op jit(solution)/shard_map/ppermute | solution.py:515
  78.6 10.5 %collective-permute-start.18 = (bf16[4,32,768]{2,1,0:T(8,128)(2,1)S(1)}, bf16[4,32,768]{2,1,0:T(8,128)(2,1)S(1)}, u32[]{:S(2)}, u32[]{:S(2)}) collective-permute-start(bf16[4,32,768]{2,1,0:T(8,128)(2,1)S(1)} %get-tuple-element.84), channel_id=1, source_target_pairs={{0,16},{4,20},{8,24},{12,28},{16,0},{20,4},{24,8},{28,12},{1,17},{... | collective-permute-start | bytes 589832 | tf_op jit(solution)/shard_map/ppermute | solution.py:515
  80.2 10.2 %collective-permute-start.19 = (bf16[4,32,768]{2,1,0:T(8,128)(2,1)S(1)}, bf16[4,32,768]{2,1,0:T(8,128)(2,1)S(1)}, u32[]{:S(2)}, u32[]{:S(2)}) collective-permute-start(bf16[4,32,768]{2,1,0:T(8,128)(2,1)S(1)} %get-tuple-element.85), channel_id=1, source_target_pairs={{0,24},{4,28},{8,16},{12,20},{16,8},{20,12},{24,0},{28,4},{1,25},{... | collective-permute-start | bytes 589832 | tf_op jit(solution)/shard_map/ppermute | solution.py:515
  90.5 26.3 %collective-permute-start.26 = (bf16[2,512,256]{2,1,0:T(8,128)(2,1)S(1)}, bf16[2,512,256]{2,1,0:T(8,128)(2,1)S(1)}, u32[]{:S(2)}, u32[]{:S(2)}) collective-permute-start(bf16[2,512,256]{2,1,0:T(8,128)(2,1)S(1)} %get-tuple-element.93), channel_id=1, source_target_pairs={{4,0},{8,4},{12,8},{16,12},{20,16},{24,20},{28,24},{5,1},{9,5},{13... | collective-permute-start | bytes 1572872 | tf_op jit(solution)/shard_map/ppermute | solution.py:402
  91.8 25.0 %collective-permute-start.27 = (bf16[2,512,256]{2,1,0:T(8,128)(2,1)S(1)}, bf16[2,512,256]{2,1,0:T(8,128)(2,1)S(1)}, u32[]{:S(2)}, u32[]{:S(2)}) collective-permute-start(bf16[2,512,256]{2,1,0:T(8,128)(2,1)S(1)} %get-tuple-element.93), channel_id=1, source_target_pairs={{0,4},{4,8},{8,12},{12,16},{16,20},{20,24},{24,28},{1,5},{5,9},{9,... | collective-permute-start | bytes 1572872 | tf_op jit(solution)/shard_map/ppermute | solution.py:402
  94.9 4.6 %collective-permute-start.20 = (bf16[32,768]{1,0:T(8,128)(2,1)S(1)}, bf16[32,768]{1,0:T(8,128)(2,1)S(1)}, u32[]{:S(2)}, u32[]{:S(2)}) collective-permute-start(bf16[32,768]{1,0:T(8,128)(2,1)S(1)} %get-tuple-element.89), channel_id=1, source_target_pairs={{0,1},{1,0},{2,3},{3,2},{4,5},{5,4},{6,7},{7,6},{8,9},{9,8},{10,11... | collective-permute-start | bytes 147464 | tf_op jit(solution)/shard_map/ppermute | solution.py:527
  96.4 7.0 %collective-permute-start.21 = (bf16[32,768]{1,0:T(8,128)(2,1)S(1)}, bf16[32,768]{1,0:T(8,128)(2,1)S(1)}, u32[]{:S(2)}, u32[]{:S(2)}) collective-permute-start(bf16[32,768]{1,0:T(8,128)(2,1)S(1)} %get-tuple-element.90), channel_id=1, source_target_pairs={{0,2},{1,3},{2,0},{3,1},{4,6},{5,7},{6,4},{7,5},{8,10},{9,11},{10,... | collective-permute-start | bytes 147464 | tf_op jit(solution)/shard_map/ppermute | solution.py:527
  98.1 6.0 %collective-permute-start.22 = (bf16[32,768]{1,0:T(8,128)(2,1)S(1)}, bf16[32,768]{1,0:T(8,128)(2,1)S(1)}, u32[]{:S(2)}, u32[]{:S(2)}) collective-permute-start(bf16[32,768]{1,0:T(8,128)(2,1)S(1)} %get-tuple-element.91), channel_id=1, source_target_pairs={{0,3},{1,2},{2,1},{3,0},{4,7},{5,6},{6,5},{7,4},{8,11},{9,10},{10,... | collective-permute-start | bytes 147464 | tf_op jit(solution)/shard_map/ppermute | solution.py:527
  104.1 4.5 %collective-permute-start.23 = (bf16[32,768]{1,0:T(8,128)(2,1)S(1)}, bf16[32,768]{1,0:T(8,128)(2,1)S(1)}, u32[]{:S(2)}, u32[]{:S(2)}) collective-permute-start(bf16[32,768]{1,0:T(8,128)(2,1)S(1)} %line_sum.1.refs_0_), channel_id=1, source_target_pairs={{0,1},{1,0},{2,3},{3,2},{4,5},{5,4},{6,7},{7,6},{8,9},{9,8},{10,11... | collective-permute-start | bytes 147464 | tf_op jit(solution)/shard_map/ppermute | solution.py:533
  105.3 6.2 %collective-permute-start.24 = (bf16[32,768]{1,0:T(8,128)(2,1)S(1)}, bf16[32,768]{1,0:T(8,128)(2,1)S(1)}, u32[]{:S(2)}, u32[]{:S(2)}) collective-permute-start(bf16[32,768]{1,0:T(8,128)(2,1)S(1)} %line_sum.1.refs_0_), channel_id=1, source_target_pairs={{0,2},{1,3},{2,0},{3,1},{4,6},{5,7},{6,4},{7,5},{8,10},{9,11},{10,... | collective-permute-start | bytes 147464 | tf_op jit(solution)/shard_map/ppermute | solution.py:533
  106.6 5.9 %collective-permute-start.25 = (bf16[32,768]{1,0:T(8,128)(2,1)S(1)}, bf16[32,768]{1,0:T(8,128)(2,1)S(1)}, u32[]{:S(2)}, u32[]{:S(2)}) collective-permute-start(bf16[32,768]{1,0:T(8,128)(2,1)S(1)} %line_sum.1.refs_0_), channel_id=1, source_target_pairs={{0,3},{1,2},{2,1},{3,0},{4,7},{5,6},{6,5},{7,4},{8,11},{9,10},{10,... | collective-permute-start | bytes 147464 | tf_op jit(solution)/shard_map/ppermute | solution.py:533
  112.6 9.4 %collective-permute-start.28 = (bf16[4,32,768]{2,1,0:T(8,128)(2,1)S(1)}, bf16[4,32,768]{2,1,0:T(8,128)(2,1)S(1)}, u32[]{:S(2)}, u32[]{:S(2)}) collective-permute-start(bf16[4,32,768]{2,1,0:T(8,128)(2,1)S(1)} %line_place.1.refs_0_), channel_id=1, source_target_pairs={{0,8},{4,12},{8,0},{12,4},{16,24},{20,28},{24,16},{28,20},{1,9},{5... | collective-permute-start | bytes 589832 | tf_op jit(solution)/shard_map/ppermute | solution.py:537
  113.7 10.5 %collective-permute-start.29 = (bf16[4,32,768]{2,1,0:T(8,128)(2,1)S(1)}, bf16[4,32,768]{2,1,0:T(8,128)(2,1)S(1)}, u32[]{:S(2)}, u32[]{:S(2)}) collective-permute-start(bf16[4,32,768]{2,1,0:T(8,128)(2,1)S(1)} %line_place.1.refs_0_), channel_id=1, source_target_pairs={{0,16},{4,20},{8,24},{12,28},{16,0},{20,4},{24,8},{28,12},{1,17},{... | collective-permute-start | bytes 589832 | tf_op jit(solution)/shard_map/ppermute | solution.py:537
  115.7 8.5 %collective-permute-start.30 = (bf16[4,32,768]{2,1,0:T(8,128)(2,1)S(1)}, bf16[4,32,768]{2,1,0:T(8,128)(2,1)S(1)}, u32[]{:S(2)}, u32[]{:S(2)}) collective-permute-start(bf16[4,32,768]{2,1,0:T(8,128)(2,1)S(1)} %line_place.1.refs_0_), channel_id=1, source_target_pairs={{0,24},{4,28},{8,16},{12,20},{16,8},{20,12},{24,0},{28,4},{1,25},{... | collective-permute-start | bytes 589832 | tf_op jit(solution)/shard_map/ppermute | solution.py:537
  124.3 2.4 %collective-permute-start.31 = (bf16[4,4,32,768]{3,2,1,0:T(8,128)(2,1)S(1)}, bf16[4,4,32,768]{3,2,1,0:T(8,128)(2,1)S(1)}, u32[]{:S(2)}, u32[]{:S(2)}) collective-permute-start(bf16[4,4,32,768]{3,2,1,0:T(8,128)(2,1)S(1)} %plane_place.1.mine_ref), channel_id=1, source_target_pairs={{0,4},{4,0},{8,12},{12,8},{16,20},{20,16},{24,28},{28,24},{1,5},{5... | collective-permute-start | bytes 2359304 | tf_op jit(solution)/shard_map/ppermute | solution.py:549
